TPU v7x, 32 devices: a whole 2x2x4 slice. The times are simulated.
32 devices in a mesh: seq: 8 (over z, y), chan: 4 (over x, core).
Axes of the slice: x: 2, y: 2, z: 4, core: 2. Of those that a mesh axis runs over, the one named last changes fastest.
Arguments:
- features: bfloat16 [4096, 512], P('seq', 'chan'), may hold values from -600 to 600
- pre_gate: bfloat16 [4096, 512], P('seq', 'chan'), may hold values from -6 to 6
- post_gate: bfloat16 [4096, 512], P('seq', 'chan'), may hold values from -6 to 6
- norm_gain: float32 [512], P('chan'), may hold values from 0.1 to 1.9
- skip_weight: float32 [512], P('chan'), may hold values from -4 to 4
- spectrum: float32 [2, 16, 512, 512], P(None, 'seq', None, 'chan'), may hold values from -6 to 6
Outputs:
- gated_out: bfloat16 [4096, 512], P('seq', 'chan')
All inputs are finite; a program needn't handle non-finite values.
Results may differ from a plain program's by a relative error of at most 0.007.
Values may be sent and summed in bfloat16 or wider, within the bound.
No kernel may reach another device: no remote copies, remote signals or barrier semaphores. Data moves between devices by JAX's collectives and lax.ppermute only.
A program may use at most 64 MiB of HBM per device.

v0:
```python
import functools

import jax
import jax.numpy as jnp
import numpy as np
from jax import lax
from jax.experimental import pallas as pl
from jax.experimental.pallas import tpu as pltpu
from jax.sharding import PartitionSpec as P

EPS = 1e-06
BF16 = jnp.bfloat16
F32 = jnp.float32
VMEM_LIMIT = 48 * 1024 * 1024
WHOLE_VMEM = 63 * 1024 * 1024 + 512 * 1024


def order_of(places):
    return (0, 3, 4, 7, 1, 2, 5, 6) if places == 8 else tuple(range(places))


def reverse_bits(index, levels):
    return sum((index >> bit & 1) << levels - 1 - bit for bit in range(levels))


@functools.lru_cache(maxsize=None)
def tables(places, rows, width):
    levels = places.bit_length() - 1
    stride = 2 * places
    bins = stride * rows
    residues = np.array([2 * reverse_bits(place, levels) + parity for place in range(places) for parity in range(2)])
    angle = 2.0 * np.pi * ((residues[:, None] * np.arange(places)[None, :]) % stride) / stride
    same = np.eye(width)
    first = np.concatenate([np.kron(np.cos(angle), same), np.kron(-np.sin(angle), same)])
    last = first.T / bins
    angle = 2.0 * np.pi * ((residues[:, None] * np.arange(rows)[None, :]) % bins) / bins
    twist = np.repeat(np.stack([np.cos(angle), np.sin(angle)]), width, axis=1)
    series = np.arange(rows)
    angle = 2.0 * np.pi * ((series[:, None] * series[None, :]) % rows) / rows
    dft = np.concatenate([np.cos(angle), np.sin(angle)])
    return (
        first.astype(jnp.bfloat16),
        last.astype(jnp.bfloat16),
        twist.astype(np.float32),
        dft.astype(jnp.bfloat16),
    )


def pair_rows(places):
    levels = places.bit_length() - 1

    def holder(residue):
        return order_of(places).index(reverse_bits(residue // 2, levels)), residue % 2

    mirrors = [None if residue % places == 0 else holder(2 * places - residue) for residue in range(places + 1)]
    return [holder(residue) for residue in range(places + 1)], mirrors


@functools.lru_cache(maxsize=None)
def folded_tables(places, rows, width):
    stride = 2 * places
    bins = stride * rows
    residues = np.arange(places + 1)
    angle = 2.0 * np.pi * ((residues[:, None] * np.arange(places)[None, :]) % stride) / stride
    parts = np.stack([np.cos(angle), -np.sin(angle)], axis=1)
    first = np.kron(parts.reshape(-1, places), np.eye(width))
    last = first.T / bins
    angle = 2.0 * np.pi * ((residues[:, None] * np.arange(rows)[None, :]) % bins) / bins
    twist = np.stack([np.cos(angle), np.sin(angle)])
    block = rows // 4
    series = np.arange(block)
    angle = 2.0 * np.pi * ((np.arange(4)[:, None] * series[None, :]) % rows) / rows
    spin = np.stack([np.cos(angle), np.sin(angle)])
    angle = 2.0 * np.pi * ((series[:, None] * series[None, :]) % block) / block
    cos, sin = np.cos(angle), np.sin(angle)
    there = np.block([[cos, -sin], [sin, cos]])
    back = np.block([[cos, sin], [-sin, cos]])
    reverse = np.eye(block)[::-1]
    return (
        first.astype(jnp.bfloat16),
        last.astype(jnp.bfloat16),
        twist.astype(np.float32),
        spin.astype(np.float32),
        np.stack([there, back]).astype(jnp.bfloat16),
        reverse.astype(jnp.bfloat16),
    )


def hops(places):
    return [[apart, apart + 1] for apart in range(0, places, 2)]


def prepare_kernel(
    features_ref,
    pre_ref,
    gain_ref,
    skip_ref,
    spectrum_ref,
    squares_ref,
    skipped_ref,
    packed_ref,
    features_in,
    pre_in,
    gain_in,
    skip_in,
    spectrum_in,
    squares_out,
    skipped_out,
    packed_out,
    in_sems,
    out_sems,
):
    blocks = [(part, parity) for part in range(2) for parity in range(2)]
    pairs = [(features_ref, features_in), (pre_ref, pre_in), (gain_ref, gain_in), (skip_ref, skip_in)]
    pairs += [(spectrum_ref.at[block], spectrum_in.at[block]) for block in blocks]
    arriving = [pltpu.make_async_copy(*pair, in_sems.at[slot]) for slot, pair in enumerate(pairs)]
    for copy in arriving:
        copy.start()
    leaving = []

    def leave(source, target):
        copy = pltpu.make_async_copy(source, target, out_sems.at[len(leaving)])
        copy.start()
        leaving.append(copy)

    def pack(slot, turned):
        if len(packed_ref.shape) == 4:
            places, width = packed_out.shape[1:3]
            for rank, place in enumerate(order_of(places)):
                packed_out[slot, rank] = turned[place * width : (place + 1) * width]
            leave(packed_out.at[slot], packed_ref.at[:, slot])
        else:
            packed_out[slot] = turned
            leave(packed_out.at[slot], packed_ref.at[slot])

    for copy in arriving[:4]:
        copy.wait()
    features = features_in[...].astype(F32)
    scaled = features * gain_in[...] * pre_in[...].astype(F32)
    pack(4, scaled.astype(BF16).T)
    skipped_out[...] = (scaled * skip_in[...]).astype(BF16).T
    leave(skipped_out, skipped_ref)
    turned = features_in[...].T.astype(F32)
    squares_out[...] = jnp.sum(turned * turned, axis=0, keepdims=True)
    leave(squares_out, squares_ref)
    for slot, block in enumerate(blocks):
        arriving[4 + slot].wait()
        if len(packed_ref.shape) == 4:
            quarter = spectrum_in.shape[2] // 4
            rows = [spectrum_in[(*block, pl.ds(turn, quarter, stride=4), slice(None))] for turn in range(4)]
            pack(slot, jnp.concatenate([row.astype(BF16).T for row in rows], axis=1))
        else:
            pack(slot, spectrum_in[block].astype(BF16).T)
    for copy in leaving:
        copy.wait()


def scale_kernel(channels, *refs):
    square_refs, scale_ref = refs[:-1], refs[-1]
    total = square_refs[0][...]
    for square_ref in square_refs[1:]:
        total = total + square_ref[...]
    scale_ref[...] = lax.rsqrt(total / channels + EPS)


def matmul(left, right):
    return jnp.dot(left, right, preferred_element_type=F32)


def butterfly(values, direction):
    (real0, imag0), (real1, imag1), (real2, imag2), (real3, imag3) = values
    even, odd = (real0 + real2, imag0 + imag2), (real1 + real3, imag1 + imag3)
    even_gap, odd_gap = (real0 - real2, imag0 - imag2), (real1 - real3, imag1 - imag3)
    lower = (even_gap[0] + odd_gap[1], even_gap[1] - odd_gap[0])
    upper = (even_gap[0] - odd_gap[1], even_gap[1] + odd_gap[0])
    total, gap = (even[0] + odd[0], even[1] + odd[1]), (even[0] - odd[0], even[1] - odd[1])
    return [total, lower, gap, upper] if direction > 0 else [total, upper, gap, lower]


def folded_kernel(packed_ref, first_ref, last_ref, twist_ref, spin_ref, dft_ref, reverse_ref, *refs):
    scale_refs, (out_ref, scales, signal, mirror, forward, backward, both) = refs[:-7], refs[-7:]
    wide, rows = out_ref.shape
    places, width = scales.shape[0], wide // scales.shape[0]
    block, inner = rows // 4, mirror.shape[0] // 8
    order = order_of(places)
    direct, mirrors = pair_rows(places)
    quarters = [pl.ds(turn * block, block) for turn in range(4)]
    groups = [range(begin, min(begin + 3, places + 1)) for begin in range(0, places + 1, 3)]
    for row, holder in enumerate(mirrors[1:places]):
        for part in range(2):
            for turn in range(4):
                at = pl.ds((part * 4 + 3 - turn) * inner + row * width, width)
                mirror[at, :] = packed_ref[holder[0], 2 * part + holder[1], :, quarters[turn]]
    reversed_bins = matmul(mirror[...], reverse_ref[...])
    place = lax.axis_index("seq")
    for scale_ref, steps in zip(scale_refs, hops(places)):
        for at, step in enumerate(steps):
            scales[place ^ step] = scale_ref[pl.ds(at, 1), :]
    for rank, at in enumerate(order):
        signal[pl.ds(at * width, width), :] = (packed_ref[rank, 4].astype(F32) * scales[at]).astype(BF16)
    spectral = []
    for group in groups:
        begin = group[0] * width
        mixed = matmul(first_ref[pl.ds(2 * begin, 2 * len(group) * width), :], signal[...])
        for at, residue in enumerate(group):
            over, under = mixed[2 * at * width : (2 * at + 1) * width], mixed[(2 * at + 1) * width : (2 * at + 2) * width]
            values = []
            for turn in range(4):
                real, imag = (part[:, turn * block : (turn + 1) * block] for part in (over, under))
                cos, sin = (twist_ref[part, pl.ds(residue, 1), quarters[turn]] for part in range(2))
                values.append((real * cos + imag * sin, imag * cos - real * sin))
            for turn, (real, imag) in enumerate(butterfly(values, 1)):
                if turn > 0:
                    cos, sin = spin_ref[0, pl.ds(turn, 1), :], spin_ref[1, pl.ds(turn, 1), :]
                    real, imag = real * cos + imag * sin, imag * cos - real * sin
                row = pl.ds(4 * begin + (turn * len(group) + at) * width, width)
                forward[row, pl.ds(0, block)] = real.astype(BF16)
                forward[row, pl.ds(block, block)] = imag.astype(BF16)
        spectral.append(matmul(forward[pl.ds(4 * begin, 4 * len(group) * width), :], dft_ref[0]))
    restored = []
    for group, values in zip(groups, spectral):
        begin = group[0] * width
        for turn in range(4):
            for at, residue in enumerate(group):
                row = (turn * len(group) + at) * width
                real, imag = values[row : row + width, :block], values[row : row + width, block:]
                holder = direct[residue]
                response_real = packed_ref[holder[0], holder[1], :, quarters[turn]].astype(F32)
                response_imag = packed_ref[holder[0], 2 + holder[1], :, quarters[turn]].astype(F32)
                if mirrors[residue] is not None:
                    other = turn * inner + (residue - 1) * width
                    response_real = response_real + reversed_bins[other : other + width]
                    other = other + 4 * inner
                    response_imag = response_imag - reversed_bins[other : other + width]
                target = pl.ds(4 * begin + row, width)
                backward[target, pl.ds(0, block)] = (real * response_real - imag * response_imag).astype(BF16)
                backward[target, pl.ds(block, block)] = (real * response_imag + imag * response_real).astype(BF16)
        restored.append(matmul(backward[pl.ds(4 * begin, 4 * len(group) * width), :], dft_ref[1]))
    for group, turned in zip(groups, restored):
        for at, residue in enumerate(group):
            values = []
            for turn in range(4):
                row = (turn * len(group) + at) * width
                real, imag = turned[row : row + width, :block], turned[row : row + width, block:]
                if turn > 0:
                    cos, sin = spin_ref[0, pl.ds(turn, 1), :], spin_ref[1, pl.ds(turn, 1), :]
                    real, imag = real * cos - imag * sin, imag * cos + real * sin
                values.append((real, imag))
            for lanes, (real, imag) in zip(quarters, butterfly(values, -1)):
                cos, sin = twist_ref[0, pl.ds(residue, 1), lanes], twist_ref[1, pl.ds(residue, 1), lanes]
                both[pl.ds(2 * residue * width, width), lanes] = (real * cos - imag * sin).astype(BF16)
                both[pl.ds((2 * residue + 1) * width, width), lanes] = (imag * cos + real * sin).astype(BF16)
    result = matmul(last_ref[...], both[...]).astype(BF16)
    for rank, at in enumerate(order):
        out_ref[pl.ds(rank * width, width), :] = result[at * width : (at + 1) * width]


def convolve_kernel(packed_ref, first_ref, last_ref, twist_ref, dft_ref, scale_ref, out_ref, left, right):
    wide, rows = out_ref.shape
    half = 2 * wide
    signal = (packed_ref[4].astype(F32) * scale_ref[...]).astype(BF16)
    mixed = matmul(first_ref[...], signal)
    real, imag = mixed[:half], mixed[half:]
    cos_twist, sin_twist = twist_ref[0], twist_ref[1]
    turned_real = (real * cos_twist + imag * sin_twist).astype(BF16)
    turned_imag = (imag * cos_twist - real * sin_twist).astype(BF16)
    left[pl.ds(0, half), pl.ds(0, rows)] = turned_real
    left[pl.ds(0, half), pl.ds(rows, rows)] = turned_imag
    left[pl.ds(half, half), pl.ds(0, rows)] = turned_imag
    left[pl.ds(half, half), pl.ds(rows, rows)] = -turned_real
    mixed = matmul(left[...], dft_ref[...])
    real, imag = mixed[:half], mixed[half:]
    response_real = packed_ref[0:2].reshape(half, rows).astype(F32)
    response_imag = packed_ref[2:4].reshape(half, rows).astype(F32)
    product_real = (real * response_real - imag * response_imag).astype(BF16)
    product_imag = (real * response_imag + imag * response_real).astype(BF16)
    right[pl.ds(0, half), pl.ds(0, rows)] = product_real
    right[pl.ds(0, half), pl.ds(rows, rows)] = -product_imag
    right[pl.ds(half, half), pl.ds(0, rows)] = product_imag
    right[pl.ds(half, half), pl.ds(rows, rows)] = product_real
    mixed = matmul(right[...], dft_ref[...])
    real, imag = mixed[:half], mixed[half:]
    turned_real = (real * cos_twist - imag * sin_twist).astype(BF16)
    turned_imag = (imag * cos_twist + real * sin_twist).astype(BF16)
    both = jnp.concatenate([turned_real, turned_imag], axis=0)
    out_ref[...] = matmul(last_ref[...], both).astype(BF16)


def finish_kernel(conv_ref, skipped_ref, scale_ref, post_ref, out_ref):
    conv = conv_ref[...]
    if len(conv_ref.shape) == 3:
        order = order_of(conv_ref.shape[0])
        conv = jnp.concatenate([conv_ref[order.index(place)] for place in range(len(order))])
    turned = conv.astype(F32) + skipped_ref[...].astype(F32) * scale_ref[...]
    out_ref[...] = (post_ref[...].astype(F32) * turned.T).astype(BF16)


def call(kernel, out_shape, flops, moved, *operands, limit=VMEM_LIMIT, **options):
    return pl.pallas_call(
        kernel,
        out_shape=out_shape,
        compiler_params=pltpu.CompilerParams(vmem_limit_bytes=limit),
        cost_estimate=pl.CostEstimate(flops=flops, bytes_accessed=moved, transcendentals=0),
        **options,
    )(*operands)


def exchange(value):
    ranks = [list(order_of(lax.axis_size("seq")))]
    return lax.all_to_all(value, "seq", split_axis=0, concat_axis=0, tiled=True, axis_index_groups=ranks)


def swap(value, axis, apart):
    return lax.ppermute(value, axis, [(place, place ^ apart) for place in range(lax.axis_size(axis))])


def local(features, pre_gate, post_gate, norm_gain, skip_weight, spectrum):
    rows, wide = features.shape
    places = lax.axis_size("seq")
    groups = lax.axis_size("chan")
    width = wide // places
    piled = width % 16 == 0
    cells = rows * wide
    shape = jax.ShapeDtypeStruct
    vmem, anywhere = pl.BlockSpec(memory_space=pltpu.VMEM), pl.BlockSpec(memory_space=pl.ANY)
    squares, skipped, packed = call(
        prepare_kernel,
        (
            shape((1, rows), F32),
            shape((wide, rows), BF16),
            shape((places, 5, width, rows) if piled else (5, wide, rows), BF16),
        ),
        10 * cells,
        32 * cells,
        features,
        pre_gate,
        norm_gain[None, :],
        skip_weight[None, :],
        spectrum,
        limit=WHOLE_VMEM,
        in_specs=[anywhere] * 5,
        out_specs=(anywhere, anywhere, anywhere),
        scratch_shapes=[
            pltpu.VMEM(features.shape, BF16),
            pltpu.VMEM(pre_gate.shape, BF16),
            pltpu.VMEM((1, wide), F32),
            pltpu.VMEM((1, wide), F32),
            pltpu.VMEM(spectrum.shape, F32),
            pltpu.VMEM((1, rows), F32),
            pltpu.VMEM((wide, rows), BF16),
            pltpu.VMEM((5, places, width, rows) if piled else (5, wide, rows), BF16),
            pltpu.SemaphoreType.DMA((8,)),
            pltpu.SemaphoreType.DMA((7,)),
        ],
    )
    if not piled:
        packed = packed.reshape(5, places, width, rows).transpose(1, 0, 2, 3)
    gathered = exchange(packed)
    others = [swap(squares, "chan", apart) for apart in range(1, groups)]
    scale = call(
        functools.partial(scale_kernel, wide * groups), shape((1, rows), F32), 8 * rows, 32 * rows, squares, *others
    )
    if piled:
        near = jnp.concatenate([scale, swap(scale, "seq", 1)])
        scales = [near] + [swap(near, "seq", steps[0]) for steps in hops(places)[1:]]
    else:
        scales = [jnp.repeat(lax.all_gather(scale, "seq", axis=0, tiled=True), width, axis=0)]
        response = gathered[:, :4].reshape(places, 2, 2, width, rows).transpose(1, 0, 2, 3, 4)
        gathered = jnp.concatenate([response.reshape(4, wide, rows), gathered[:, 4].reshape(1, wide, rows)])
    if piled:
        constants = folded_tables(places, rows, width)
        half = constants[0].shape[0] // 2
        scratch = [
            pltpu.VMEM((places, 1, rows), F32),
            pltpu.VMEM((wide, rows), BF16),
            pltpu.VMEM((8 * (half - 2 * width), rows // 4), BF16),
            pltpu.VMEM((4 * half, rows // 2), BF16),
            pltpu.VMEM((4 * half, rows // 2), BF16),
            pltpu.VMEM((2 * half, rows), BF16),
        ]
    else:
        constants = tables(places, rows, width)
        scratch = [pltpu.VMEM((4 * wide, 2 * rows), BF16)] * 2
    conv = call(
        folded_kernel if piled else convolve_kernel,
        shape((wide, rows), BF16),
        20 * cells * rows,
        20 * cells,
        gathered,
        *constants,
        *scales,
        scratch_shapes=scratch,
    )
    conv = exchange(conv.reshape(places, width, rows))
    if not piled:
        conv = conv.reshape(wide, rows)
    return call(finish_kernel, shape((rows, wide), BF16), 10 * cells, 8 * cells, conv, skipped, scale, post_gate)


def solution(mesh):
    return jax.shard_map(
        local,
        mesh=mesh,
        in_specs=(
            P("seq", "chan"),
            P("seq", "chan"),
            P("seq", "chan"),
            P("chan"),
            P("chan"),
            P(None, "seq", None, "chan"),
        ),
        out_specs=P("seq", "chan"),
        check_vma=False,
    )
```

profile of v0, /device:TPU:0, one launch (start us, length us, event | category | flops | bytes accessed | tf_op | source)
XLA Modules:
  0.0 40.4 jit_solution(3442739128505587589)
XLA Ops:
  0.0 2.3 %shard_map.118 = (f32[1,512]{1,0:T(1,128)}, bf16[128,512]{1,0:T(8,128)(2,1)}, bf16[8,5,16,512]{3,2,1,0:T(8,128)(2,1)}) custom-call(bf16[512,128]{1,0:T(8,128)(2,1)} %features_ref.1, bf16[512,128]{1,0:T(8,128)(2,1)} %pre_ref.1, f32[1,128]{1,0:T(1,128)} %bitcast.4, f32[1,128]{1,0:T(1,128)} %bitcast.5, f32[2,2,512,128]{3,2,1,0:T(8,128)} %spectrum_ref.1), custom_call_target="tpu_custom_call" | custom-call | flops 655360 | bytes 2097152 | tf_op jit(solution)/shard_map/pallas_call | solution.py:299
  2.3 0.0 copy-start.3
  2.3 0.0 copy-start.4
  2.3 0.0 copy-start.5
  2.3 0.0 copy-start.6
  2.4 0.0 copy-start.7
  2.4 7.4 %all-to-all-start = ((bf16[8,5,16,512]{3,2,1,0:T(8,128)(2,1)}), bf16[8,5,16,512]{3,2,1,0:T(8,128)(2,1)S(1)}, u32[]{:S(2)}, u32[]{:S(2)}) async-start(bf16[8,5,16,512]{3,2,1,0:T(8,128)(2,1)} %get-tuple-element.8), calls=%async_computation | async-start | bytes 1310720 | tf_op jit(solution)/shard_map/all_to_all | solution.py:310
  9.8 0.7 %collective-permute-start.2 = (f32[1,512]{1,0:T(1,128)S(1)}, f32[1,512]{1,0:T(1,128)S(1)}, u32[]{:S(2)}, u32[]{:S(2)}) collective-permute-start(f32[1,512]{1,0:T(1,128)S(1)} %copy-done.2), channel_id=1, source_target_pairs={{0,3},{1,2},{2,1},{3,0},{4,7},{5,6},{6,5},{7,4},{8,11},{9,10},{10,... | collective-permute-start | bytes 6152 | tf_op jit(solution)/shard_map/ppermute | solution.py:314
  10.5 0.9 %collective-permute-start.1 = (f32[1,512]{1,0:T(1,128)S(1)}, f32[1,512]{1,0:T(1,128)S(1)}, u32[]{:S(2)}, u32[]{:S(2)}) collective-permute-start(f32[1,512]{1,0:T(1,128)S(1)} %copy-done.2), channel_id=1, source_target_pairs={{0,2},{1,3},{2,0},{3,1},{4,6},{5,7},{6,4},{7,5},{8,10},{9,11},{10,... | collective-permute-start | bytes 6152 | tf_op jit(solution)/shard_map/ppermute | solution.py:314
  11.4 0.3 collective-permute-start
  11.7 1.1 %collective-permute-done.2.refs_3_ = f32[1,512]{1,0:T(1,128)S(1)} collective-permute-done((f32[1,512]{1,0:T(1,128)S(1)}, f32[1,512]{1,0:T(1,128)S(1)}, u32[]{:S(2)}, u32[]{:S(2)}) %collective-permute-start.2) | collective-permute-done | bytes 2080 | tf_op jit(solution)/shard_map/ppermute | solution.py:314
  12.9 1.2 %collective-permute-done.1.refs_2_ = f32[1,512]{1,0:T(1,128)S(1)} collective-permute-done((f32[1,512]{1,0:T(1,128)S(1)}, f32[1,512]{1,0:T(1,128)S(1)}, u32[]{:S(2)}, u32[]{:S(2)}) %collective-permute-start.1) | collective-permute-done | bytes 2080 | tf_op jit(solution)/shard_map/ppermute | solution.py:314
  14.1 0.0 collective-permute-done.refs_1_
  14.1 0.0 copy-start.8
  14.1 1.8 %collective-permute-start.3 = (f32[1,512]{1,0:T(1,128)S(1)}, f32[1,512]{1,0:T(1,128)S(1)}, u32[]{:S(2)}, u32[]{:S(2)}) collective-permute-start(f32[1,512]{1,0:T(1,128)S(1)} %shard_map.119.scale_ref), channel_id=1, source_target_pairs={{0,4},{4,0},{8,12},{12,8},{16,20},{20,16},{24,28},{28,24},{1,5},{5... | collective-permute-start | bytes 6152 | tf_op jit(solution)/shard_map/ppermute | solution.py:314
  15.9 1.9 %collective-permute-done.3 = f32[1,512]{1,0:T(1,128)S(1)} collective-permute-done((f32[1,512]{1,0:T(1,128)S(1)}, f32[1,512]{1,0:T(1,128)S(1)}, u32[]{:S(2)}, u32[]{:S(2)}) %collective-permute-start.3) | collective-permute-done | bytes 2080 | tf_op jit(solution)/shard_map/ppermute | solution.py:314
  17.8 3.8 %collective-permute-start.6 = (f32[2,512]{1,0:T(2,128)S(1)}, f32[2,512]{1,0:T(2,128)S(1)}, u32[]{:S(2)}, u32[]{:S(2)}) collective-permute-start(f32[2,512]{1,0:T(2,128)S(1)} %pad_maximum_fusion.refs_0_), channel_id=1, source_target_pairs={{0,24},{4,28},{8,16},{12,20},{16,8},{20,12},{24,0},{28,4},{1,25},{... | collective-permute-start | bytes 12296 | tf_op jit(solution)/shard_map/ppermute | solution.py:314
  21.6 0.0 collective-permute-start.5
  21.6 0.7 %collective-permute-start.4 = (f32[2,512]{1,0:T(2,128)S(1)}, f32[2,512]{1,0:T(2,128)S(1)}, u32[]{:S(2)}, u32[]{:S(2)}) collective-permute-start(f32[2,512]{1,0:T(2,128)S(1)} %pad_maximum_fusion.refs_0_), channel_id=1, source_target_pairs={{0,8},{4,12},{8,0},{12,4},{16,24},{20,28},{24,16},{28,20},{1,9},{5... | collective-permute-start | bytes 12296 | tf_op jit(solution)/shard_map/ppermute | solution.py:314
  22.3 2.5 %collective-permute-done.6.refs_3_ = f32[2,512]{1,0:T(2,128)S(1)} collective-permute-done((f32[2,512]{1,0:T(2,128)S(1)}, f32[2,512]{1,0:T(2,128)S(1)}, u32[]{:S(2)}, u32[]{:S(2)}) %collective-permute-start.6) | collective-permute-done | bytes 4128 | tf_op jit(solution)/shard_map/ppermute | solution.py:314
  24.7 2.7 %collective-permute-done.5.refs_2_ = f32[2,512]{1,0:T(2,128)S(1)} collective-permute-done((f32[2,512]{1,0:T(2,128)S(1)}, f32[2,512]{1,0:T(2,128)S(1)}, u32[]{:S(2)}, u32[]{:S(2)}) %collective-permute-start.5) | collective-permute-done | bytes 4128 | tf_op jit(solution)/shard_map/ppermute | solution.py:314
  27.4 0.0 collective-permute-done.4.refs_1_
  27.4 0.8 %all-to-all-done.packed_ref = bf16[8,5,16,512]{3,2,1,0:T(8,128)(2,1)S(1)} async-done(((bf16[8,5,16,512]{3,2,1,0:T(8,128)(2,1)}), bf16[8,5,16,512]{3,2,1,0:T(8,128)(2,1)S(1)}, u32[]{:S(2)}, u32[]{:S(2)}) %all-to-all-start) | async-done | bytes 655392 | tf_op jit(solution)/shard_map/all_to_all | solution.py:310
  28.3 0.0 copy-done.6
  28.3 0.0 copy-done.7
  28.3 0.0 copy-done.8
  28.3 1.1 %shard_map.120 = bf16[128,512]{1,0:T(8,128)(2,1)S(1)} custom-call(bf16[8,5,16,512]{3,2,1,0:T(8,128)(2,1)S(1)} %all-to-all-done.packed_ref, bf16[288,128]{1,0:T(8,128)(2,1)S(1)} %copy-done.5, bf16[128,288]{1,0:T(8,128)(2,1)S(1)} %copy-done.4, f32[2,9,512]{2,1,0:T(8,128)S(1)} %copy-done.6, f32[2,4,128]{2,1,0:T(4,128)S(1)} %copy-done.8, ...), custom_call_target="tpu_custom_call" | custom-call | flops 671088640 | bytes 1310720 | tf_op jit(solution)/shard_map/pallas_call | solution.py:299
  29.4 0.0 copy-start
  29.4 0.0 copy-start.1
  29.4 10.2 %all_to_all.10.conv_ref = bf16[8,16,512]{2,1,0:T(8,128)(2,1)S(1)} all-to-all(bf16[8,16,512]{2,1,0:T(8,128)(2,1)S(1)} %bitcast.3), channel_id=1, replica_groups={{0,12,16,28,4,8,20,24},{1,13,17,29,5,9,21,25},{2,14,18,30,6,10,22,26},{..., dimensions={0} | all-to-all | bytes 262144 | tf_op jit(solution)/shard_map/all_to_all | solution.py:310
  39.6 0.0 copy-done.1
  39.6 0.8 %shard_map.121 = bf16[512,128]{1,0:T(8,128)(2,1)} custom-call(bf16[8,16,512]{2,1,0:T(8,128)(2,1)S(1)} %all_to_all.10.conv_ref, bf16[128,512]{1,0:T(8,128)(2,1)S(1)} %copy-done.1, f32[1,512]{1,0:T(1,128)S(1)} %shard_map.119.scale_ref, bf16[512,128]{1,0:T(8,128)(2,1)S(1)} %copy-done), custom_call_target="tpu_custom_call" | custom-call | flops 655360 | bytes 524288 | tf_op jit(solution)/shard_map/pallas_call | solution.py:299
  (8 shorter events, 0.0 us)
Async XLA Ops:
  2.3 7.5 %copy-start.2 = (f32[1,512]{1,0:T(1,128)S(1)}, f32[1,512]{1,0:T(1,128)}, u32[]{:S(2)}) copy-start(f32[1,512]{1,0:T(1,128)} %get-tuple-element.9.refs_0_) | copy-start | bytes 6148
  2.3 25.9 %copy-start.3 = (bf16[2,256,256]{2,1,0:T(8,128)(2,1)S(1)}, bf16[2,256,256]{2,1,0:T(8,128)(2,1)}, u32[]{:S(2)}) copy-start(bf16[2,256,256]{2,1,0:T(8,128)(2,1)} %constant.16.clone.dft_ref) | copy-start | bytes 786436
  2.3 25.9 %copy-start.4 = (bf16[128,288]{1,0:T(8,128)(2,1)S(1)}, bf16[128,288]{1,0:T(8,128)(2,1)}, u32[]{:S(2)}) copy-start(bf16[128,288]{1,0:T(8,128)(2,1)} %constant.13.clone.last_ref) | copy-start | bytes 221188
  2.3 25.9 %copy-start.5 = (bf16[288,128]{1,0:T(8,128)(2,1)S(1)}, bf16[288,128]{1,0:T(8,128)(2,1)}, u32[]{:S(2)}) copy-start(bf16[288,128]{1,0:T(8,128)(2,1)} %constant.12.clone.first_ref) | copy-start | bytes 221188
  2.3 25.9 %copy-start.6 = (f32[2,9,512]{2,1,0:T(8,128)S(1)}, f32[2,9,512]{2,1,0:T(8,128)}, u32[]{:S(2)}) copy-start(f32[2,9,512]{2,1,0:T(8,128)} %constant.14.clone.twist_ref) | copy-start | bytes 110596
  2.4 25.9 %copy-start.7 = (bf16[128,128]{1,0:T(8,128)(2,1)S(1)}, bf16[128,128]{1,0:T(8,128)(2,1)}, u32[]{:S(2)}) copy-start(bf16[128,128]{1,0:T(8,128)(2,1)} %constant.17.clone.reverse_ref) | copy-start | bytes 98308
  2.4 25.9 %all-to-all-start = ((bf16[8,5,16,512]{3,2,1,0:T(8,128)(2,1)}), bf16[8,5,16,512]{3,2,1,0:T(8,128)(2,1)S(1)}, u32[]{:S(2)}, u32[]{:S(2)}) async-start(bf16[8,5,16,512]{3,2,1,0:T(8,128)(2,1)} %get-tuple-element.8), calls=%async_computation | async-start | bytes 1310720 | tf_op jit(solution)/shard_map/all_to_all | solution.py:310
  9.8 3.1 %collective-permute-start.2 = (f32[1,512]{1,0:T(1,128)S(1)}, f32[1,512]{1,0:T(1,128)S(1)}, u32[]{:S(2)}, u32[]{:S(2)}) collective-permute-start(f32[1,512]{1,0:T(1,128)S(1)} %copy-done.2), channel_id=1, source_target_pairs={{0,3},{1,2},{2,1},{3,0},{4,7},{5,6},{6,5},{7,4},{8,11},{9,10},{10,... | collective-permute-start | bytes 6152 | tf_op jit(solution)/shard_map/ppermute | solution.py:314
  10.5 3.6 %collective-permute-start.1 = (f32[1,512]{1,0:T(1,128)S(1)}, f32[1,512]{1,0:T(1,128)S(1)}, u32[]{:S(2)}, u32[]{:S(2)}) collective-permute-start(f32[1,512]{1,0:T(1,128)S(1)} %copy-done.2), channel_id=1, source_target_pairs={{0,2},{1,3},{2,0},{3,1},{4,6},{5,7},{6,4},{7,5},{8,10},{9,11},{10,... | collective-permute-start | bytes 6152 | tf_op jit(solution)/shard_map/ppermute | solution.py:314
  11.4 2.7 %collective-permute-start = (f32[1,512]{1,0:T(1,128)S(1)}, f32[1,512]{1,0:T(1,128)S(1)}, u32[]{:S(2)}, u32[]{:S(2)}) collective-permute-start(f32[1,512]{1,0:T(1,128)S(1)} %copy-done.2), channel_id=1, source_target_pairs={{0,1},{1,0},{2,3},{3,2},{4,5},{5,4},{6,7},{7,6},{8,9},{9,8},{10,11... | collective-permute-start | bytes 6152 | tf_op jit(solution)/shard_map/ppermute | solution.py:314
  14.1 14.2 %copy-start.8 = (f32[2,4,128]{2,1,0:T(4,128)S(1)}, f32[2,4,128]{2,1,0:T(4,128)}, u32[]{:S(2)}) copy-start(f32[2,4,128]{2,1,0:T(4,128)} %constant.15.clone.spin_ref) | copy-start | bytes 12292
  14.1 3.7 %collective-permute-start.3 = (f32[1,512]{1,0:T(1,128)S(1)}, f32[1,512]{1,0:T(1,128)S(1)}, u32[]{:S(2)}, u32[]{:S(2)}) collective-permute-start(f32[1,512]{1,0:T(1,128)S(1)} %shard_map.119.scale_ref), channel_id=1, source_target_pairs={{0,4},{4,0},{8,12},{12,8},{16,20},{20,16},{24,28},{28,24},{1,5},{5... | collective-permute-start | bytes 6152 | tf_op jit(solution)/shard_map/ppermute | solution.py:314
  17.8 6.9 %collective-permute-start.6 = (f32[2,512]{1,0:T(2,128)S(1)}, f32[2,512]{1,0:T(2,128)S(1)}, u32[]{:S(2)}, u32[]{:S(2)}) collective-permute-start(f32[2,512]{1,0:T(2,128)S(1)} %pad_maximum_fusion.refs_0_), channel_id=1, source_target_pairs={{0,24},{4,28},{8,16},{12,20},{16,8},{20,12},{24,0},{28,4},{1,25},{... | collective-permute-start | bytes 12296 | tf_op jit(solution)/shard_map/ppermute | solution.py:314
  21.6 5.9 %collective-permute-start.5 = (f32[2,512]{1,0:T(2,128)S(1)}, f32[2,512]{1,0:T(2,128)S(1)}, u32[]{:S(2)}, u32[]{:S(2)}) collective-permute-start(f32[2,512]{1,0:T(2,128)S(1)} %pad_maximum_fusion.refs_0_), channel_id=1, source_target_pairs={{0,16},{4,20},{8,24},{12,28},{16,0},{20,4},{24,8},{28,12},{1,17},{... | collective-permute-start | bytes 12296 | tf_op jit(solution)/shard_map/ppermute | solution.py:314
  21.6 5.9 %collective-permute-start.4 = (f32[2,512]{1,0:T(2,128)S(1)}, f32[2,512]{1,0:T(2,128)S(1)}, u32[]{:S(2)}, u32[]{:S(2)}) collective-permute-start(f32[2,512]{1,0:T(2,128)S(1)} %pad_maximum_fusion.refs_0_), channel_id=1, source_target_pairs={{0,8},{4,12},{8,0},{12,4},{16,24},{20,28},{24,16},{28,20},{1,9},{5... | collective-permute-start | bytes 12296 | tf_op jit(solution)/shard_map/ppermute | solution.py:314
  29.4 10.2 %copy-start = (bf16[512,128]{1,0:T(8,128)(2,1)S(1)}, bf16[512,128]{1,0:T(8,128)(2,1)}, u32[]{:S(2)}) copy-start(bf16[512,128]{1,0:T(8,128)(2,1)} %post_ref.1) | copy-start | bytes 393220
  29.4 10.2 %copy-start.1 = (bf16[128,512]{1,0:T(8,128)(2,1)S(1)}, bf16[128,512]{1,0:T(8,128)(2,1)}, u32[]{:S(2)}) copy-start(bf16[128,512]{1,0:T(8,128)(2,1)} %get-tuple-element.10.skipped_ref) | copy-start | bytes 393220
where the time goes:
time: 40.6 us; the launch traced here: 40.4 us
  starting transfers between devices  15.6 us (38%)
  waiting for transfers between devices  10.3 us (25%)
  blocking collectives  10.2 us (25%)
  Pallas kernels  4.18 us (10%)
    all_to_all x1, blocking collectives, exchange(): lax.all_to_all(value, 'seq', split_axis=0, concat_axis=0, tiled=True, axi...  10.2 us
    ppermute x7, waiting for transfers between devices, swap(): lax.ppermute(value, axis, [(place, place ^ apart) for place in range(lax....  9.47 us
    ppermute x7, starting transfers between devices, swap(): lax.ppermute(value, axis, [(place, place ^ apart) for place in range(lax....  8.13 us
    all_to_all x1, starting transfers between devices, exchange(): lax.all_to_all(value, 'seq', split_axis=0, concat_axis=0, tiled=True, axi...  7.42 us
    pallas_call x4, Pallas kernels, call(): pl.pallas_call(kernel, out_shape=out_shape, compiler_params=pltpu.Compile...  4.18 us
  transfers between devices with their start and end apart: 8, of which 6 were waited for; matrix products, arithmetic and copies ran while one was open for 0% of the time, Pallas kernels for 0%

commit v1 on v0

--- a/solution.py
+++ b/solution.py
@@ -16,7 +16,7 @@
 
 
 def order_of(places):
-    return (0, 3, 4, 7, 1, 2, 5, 6) if places == 8 else tuple(range(places))
+    return (0, 2, 6, 4, 1, 5, 3, 7) if places == 8 else tuple(range(places))
 
 
 def reverse_bits(index, levels):

time: 40.6 us -> 40.6 us (level)
  waiting for transfers between devices: 10.3 us -> 9.48 us
  blocking collectives: 10.2 us -> 10.9 us
    all_to_all x1, waiting for transfers between devices: 0.81 us -> 0.01 us  [exchange(): lax.all_to_all(value, 'seq', split_axis=0, concat_axis=0, tiled=True, axi...]
    all_to_all x1, blocking collectives: 10.2 us -> 10.9 us  [exchange(): lax.all_to_all(value, 'seq', split_axis=0, concat_axis=0, tiled=True, axi...]
  transfers between devices with their start and end apart: 8 -> 8, of which waited for: 6 -> 5; matrix products, arithmetic and copies ran while one was open for 0% -> 0% of each run, Pallas kernels for 0% -> 0%
where the time goes in v1:
time: 40.6 us; the launch traced here: 40.3 us
  starting transfers between devices  15.6 us (38%)
  blocking collectives  10.9 us (27%)
  waiting for transfers between devices  9.48 us (23%)
  Pallas kernels  4.18 us (10%)
    all_to_all x1, blocking collectives, exchange(): lax.all_to_all(value, 'seq', split_axis=0, concat_axis=0, tiled=True, axi...  10.9 us
    ppermute x7, waiting for transfers between devices, swap(): lax.ppermute(value, axis, [(place, place ^ apart) for place in range(lax....  9.47 us
    ppermute x7, starting transfers between devices, swap(): lax.ppermute(value, axis, [(place, place ^ apart) for place in range(lax....  8.13 us
    all_to_all x1, starting transfers between devices, exchange(): lax.all_to_all(value, 'seq', split_axis=0, concat_axis=0, tiled=True, axi...  7.42 us
    pallas_call x4, Pallas kernels, call(): pl.pallas_call(kernel, out_shape=out_shape, compiler_params=pltpu.Compile...  4.18 us
  transfers between devices with their start and end apart: 8, of which 5 were waited for; matrix products, arithmetic and copies ran while one was open for 0% of the time, Pallas kernels for 0%

profile of v1, /device:TPU:0, one launch (start us, length us, event | category | flops | bytes accessed | tf_op | source)
XLA Modules:
  0.0 40.3 jit_solution(1492350569337658455)
XLA Ops:
  0.0 2.3 %shard_map.118 = (f32[1,512]{1,0:T(1,128)}, bf16[128,512]{1,0:T(8,128)(2,1)}, bf16[8,5,16,512]{3,2,1,0:T(8,128)(2,1)}) custom-call(bf16[512,128]{1,0:T(8,128)(2,1)} %features_ref.1, bf16[512,128]{1,0:T(8,128)(2,1)} %pre_ref.1, f32[1,128]{1,0:T(1,128)} %bitcast.4, f32[1,128]{1,0:T(1,128)} %bitcast.5, f32[2,2,512,128]{3,2,1,0:T(8,128)} %spectrum_ref.1), custom_call_target="tpu_custom_call" | custom-call | flops 655360 | bytes 2097152 | tf_op jit(solution)/shard_map/pallas_call | solution.py:299
  2.3 0.0 copy-start.2
  2.3 0.0 copy-start.3
  2.3 0.0 copy-start.4
  2.3 0.0 copy-start.5
  2.3 0.0 copy-start.6
  2.4 0.0 copy-start.7
  2.4 7.4 %all-to-all-start = ((bf16[8,5,16,512]{3,2,1,0:T(8,128)(2,1)}), bf16[8,5,16,512]{3,2,1,0:T(8,128)(2,1)S(1)}, u32[]{:S(2)}, u32[]{:S(2)}) async-start(bf16[8,5,16,512]{3,2,1,0:T(8,128)(2,1)} %get-tuple-element.8), calls=%async_computation | async-start | bytes 1310720 | tf_op jit(solution)/shard_map/all_to_all | solution.py:310
  9.8 0.0 copy-done.2
  9.8 0.7 %collective-permute-start.2 = (f32[1,512]{1,0:T(1,128)S(1)}, f32[1,512]{1,0:T(1,128)S(1)}, u32[]{:S(2)}, u32[]{:S(2)}) collective-permute-start(f32[1,512]{1,0:T(1,128)S(1)} %copy-done.2), channel_id=1, source_target_pairs={{0,3},{1,2},{2,1},{3,0},{4,7},{5,6},{6,5},{7,4},{8,11},{9,10},{10,... | collective-permute-start | bytes 6152 | tf_op jit(solution)/shard_map/ppermute | solution.py:314
  10.5 0.9 %collective-permute-start.1 = (f32[1,512]{1,0:T(1,128)S(1)}, f32[1,512]{1,0:T(1,128)S(1)}, u32[]{:S(2)}, u32[]{:S(2)}) collective-permute-start(f32[1,512]{1,0:T(1,128)S(1)} %copy-done.2), channel_id=1, source_target_pairs={{0,2},{1,3},{2,0},{3,1},{4,6},{5,7},{6,4},{7,5},{8,10},{9,11},{10,... | collective-permute-start | bytes 6152 | tf_op jit(solution)/shard_map/ppermute | solution.py:314
  11.4 0.3 collective-permute-start
  11.7 1.1 %collective-permute-done.2.refs_3_ = f32[1,512]{1,0:T(1,128)S(1)} collective-permute-done((f32[1,512]{1,0:T(1,128)S(1)}, f32[1,512]{1,0:T(1,128)S(1)}, u32[]{:S(2)}, u32[]{:S(2)}) %collective-permute-start.2) | collective-permute-done | bytes 2080 | tf_op jit(solution)/shard_map/ppermute | solution.py:314
  12.9 1.2 %collective-permute-done.1.refs_2_ = f32[1,512]{1,0:T(1,128)S(1)} collective-permute-done((f32[1,512]{1,0:T(1,128)S(1)}, f32[1,512]{1,0:T(1,128)S(1)}, u32[]{:S(2)}, u32[]{:S(2)}) %collective-permute-start.1) | collective-permute-done | bytes 2080 | tf_op jit(solution)/shard_map/ppermute | solution.py:314
  14.1 0.0 collective-permute-done.refs_1_
  14.1 0.0 copy-start.8
  14.1 1.8 %collective-permute-start.3 = (f32[1,512]{1,0:T(1,128)S(1)}, f32[1,512]{1,0:T(1,128)S(1)}, u32[]{:S(2)}, u32[]{:S(2)}) collective-permute-start(f32[1,512]{1,0:T(1,128)S(1)} %shard_map.119.scale_ref), channel_id=1, source_target_pairs={{0,4},{4,0},{8,12},{12,8},{16,20},{20,16},{24,28},{28,24},{1,5},{5... | collective-permute-start | bytes 6152 | tf_op jit(solution)/shard_map/ppermute | solution.py:314
  15.9 2.1 %collective-permute-done.3 = f32[1,512]{1,0:T(1,128)S(1)} collective-permute-done((f32[1,512]{1,0:T(1,128)S(1)}, f32[1,512]{1,0:T(1,128)S(1)}, u32[]{:S(2)}, u32[]{:S(2)}) %collective-permute-start.3) | collective-permute-done | bytes 2080 | tf_op jit(solution)/shard_map/ppermute | solution.py:314
  18.0 3.5 %collective-permute-start.6 = (f32[2,512]{1,0:T(2,128)S(1)}, f32[2,512]{1,0:T(2,128)S(1)}, u32[]{:S(2)}, u32[]{:S(2)}) collective-permute-start(f32[2,512]{1,0:T(2,128)S(1)} %pad_maximum_fusion.refs_0_), channel_id=1, source_target_pairs={{0,24},{4,28},{8,16},{12,20},{16,8},{20,12},{24,0},{28,4},{1,25},{... | collective-permute-start | bytes 12296 | tf_op jit(solution)/shard_map/ppermute | solution.py:314
  21.5 0.0 collective-permute-start.5
  21.6 0.9 %collective-permute-start.4 = (f32[2,512]{1,0:T(2,128)S(1)}, f32[2,512]{1,0:T(2,128)S(1)}, u32[]{:S(2)}, u32[]{:S(2)}) collective-permute-start(f32[2,512]{1,0:T(2,128)S(1)} %pad_maximum_fusion.refs_0_), channel_id=1, source_target_pairs={{0,8},{4,12},{8,0},{12,4},{16,24},{20,28},{24,16},{28,20},{1,9},{5... | collective-permute-start | bytes 12296 | tf_op jit(solution)/shard_map/ppermute | solution.py:314
  22.5 2.3 %collective-permute-done.6.refs_3_ = f32[2,512]{1,0:T(2,128)S(1)} collective-permute-done((f32[2,512]{1,0:T(2,128)S(1)}, f32[2,512]{1,0:T(2,128)S(1)}, u32[]{:S(2)}, u32[]{:S(2)}) %collective-permute-start.6) | collective-permute-done | bytes 4128 | tf_op jit(solution)/shard_map/ppermute | solution.py:314
  24.8 2.7 %collective-permute-done.5.refs_2_ = f32[2,512]{1,0:T(2,128)S(1)} collective-permute-done((f32[2,512]{1,0:T(2,128)S(1)}, f32[2,512]{1,0:T(2,128)S(1)}, u32[]{:S(2)}, u32[]{:S(2)}) %collective-permute-start.5) | collective-permute-done | bytes 4128 | tf_op jit(solution)/shard_map/ppermute | solution.py:314
  27.4 0.0 collective-permute-done.4.refs_1_
  27.4 0.0 all-to-all-done.packed_ref
  27.5 0.0 copy-done.3
  27.5 1.1 %shard_map.120 = bf16[128,512]{1,0:T(8,128)(2,1)S(1)} custom-call(bf16[8,5,16,512]{3,2,1,0:T(8,128)(2,1)S(1)} %all-to-all-done.packed_ref, bf16[288,128]{1,0:T(8,128)(2,1)S(1)} %copy-done.5, bf16[128,288]{1,0:T(8,128)(2,1)S(1)} %copy-done.4, f32[2,9,512]{2,1,0:T(8,128)S(1)} %copy-done.6, f32[2,4,128]{2,1,0:T(4,128)S(1)} %copy-done.8, ...), custom_call_target="tpu_custom_call" | custom-call | flops 671088640 | bytes 1310720 | tf_op jit(solution)/shard_map/pallas_call | solution.py:299
  28.6 0.0 copy-start
  28.6 0.0 copy-start.1
  28.6 10.9 %all_to_all.10.conv_ref = bf16[8,16,512]{2,1,0:T(8,128)(2,1)S(1)} all-to-all(bf16[8,16,512]{2,1,0:T(8,128)(2,1)S(1)} %bitcast.3), channel_id=1, replica_groups={{0,8,24,16,4,20,12,28},{1,9,25,17,5,21,13,29},{2,10,26,18,6,22,14,30},{..., dimensions={0} | all-to-all | bytes 262144 | tf_op jit(solution)/shard_map/all_to_all | solution.py:310
  39.5 0.0 copy-done.1
  39.5 0.8 %shard_map.121 = bf16[512,128]{1,0:T(8,128)(2,1)} custom-call(bf16[8,16,512]{2,1,0:T(8,128)(2,1)S(1)} %all_to_all.10.conv_ref, bf16[128,512]{1,0:T(8,128)(2,1)S(1)} %copy-done.1, f32[1,512]{1,0:T(1,128)S(1)} %shard_map.119.scale_ref, bf16[512,128]{1,0:T(8,128)(2,1)S(1)} %copy-done), custom_call_target="tpu_custom_call" | custom-call | flops 655360 | bytes 524288 | tf_op jit(solution)/shard_map/pallas_call | solution.py:299
  (8 shorter events, 0.0 us)
Async XLA Ops:
  2.3 7.5 %copy-start.2 = (f32[1,512]{1,0:T(1,128)S(1)}, f32[1,512]{1,0:T(1,128)}, u32[]{:S(2)}) copy-start(f32[1,512]{1,0:T(1,128)} %get-tuple-element.9.refs_0_) | copy-start | bytes 6148
  2.3 25.1 %copy-start.3 = (bf16[2,256,256]{2,1,0:T(8,128)(2,1)S(1)}, bf16[2,256,256]{2,1,0:T(8,128)(2,1)}, u32[]{:S(2)}) copy-start(bf16[2,256,256]{2,1,0:T(8,128)(2,1)} %constant.16.clone.dft_ref) | copy-start | bytes 786436
  2.3 25.1 %copy-start.4 = (bf16[128,288]{1,0:T(8,128)(2,1)S(1)}, bf16[128,288]{1,0:T(8,128)(2,1)}, u32[]{:S(2)}) copy-start(bf16[128,288]{1,0:T(8,128)(2,1)} %constant.13.clone.last_ref) | copy-start | bytes 221188
  2.3 25.1 %copy-start.5 = (bf16[288,128]{1,0:T(8,128)(2,1)S(1)}, bf16[288,128]{1,0:T(8,128)(2,1)}, u32[]{:S(2)}) copy-start(bf16[288,128]{1,0:T(8,128)(2,1)} %constant.12.clone.first_ref) | copy-start | bytes 221188
  2.3 25.1 %copy-start.6 = (f32[2,9,512]{2,1,0:T(8,128)S(1)}, f32[2,9,512]{2,1,0:T(8,128)}, u32[]{:S(2)}) copy-start(f32[2,9,512]{2,1,0:T(8,128)} %constant.14.clone.twist_ref) | copy-start | bytes 110596
  2.4 25.1 %copy-start.7 = (bf16[128,128]{1,0:T(8,128)(2,1)S(1)}, bf16[128,128]{1,0:T(8,128)(2,1)}, u32[]{:S(2)}) copy-start(bf16[128,128]{1,0:T(8,128)(2,1)} %constant.17.clone.reverse_ref) | copy-start | bytes 98308
  2.4 25.1 %all-to-all-start = ((bf16[8,5,16,512]{3,2,1,0:T(8,128)(2,1)}), bf16[8,5,16,512]{3,2,1,0:T(8,128)(2,1)S(1)}, u32[]{:S(2)}, u32[]{:S(2)}) async-start(bf16[8,5,16,512]{3,2,1,0:T(8,128)(2,1)} %get-tuple-element.8), calls=%async_computation | async-start | bytes 1310720 | tf_op jit(solution)/shard_map/all_to_all | solution.py:310
  9.8 3.1 %collective-permute-start.2 = (f32[1,512]{1,0:T(1,128)S(1)}, f32[1,512]{1,0:T(1,128)S(1)}, u32[]{:S(2)}, u32[]{:S(2)}) collective-permute-start(f32[1,512]{1,0:T(1,128)S(1)} %copy-done.2), channel_id=1, source_target_pairs={{0,3},{1,2},{2,1},{3,0},{4,7},{5,6},{6,5},{7,4},{8,11},{9,10},{10,... | collective-permute-start | bytes 6152 | tf_op jit(solution)/shard_map/ppermute | solution.py:314
  10.5 3.6 %collective-permute-start.1 = (f32[1,512]{1,0:T(1,128)S(1)}, f32[1,512]{1,0:T(1,128)S(1)}, u32[]{:S(2)}, u32[]{:S(2)}) collective-permute-start(f32[1,512]{1,0:T(1,128)S(1)} %copy-done.2), channel_id=1, source_target_pairs={{0,2},{1,3},{2,0},{3,1},{4,6},{5,7},{6,4},{7,5},{8,10},{9,11},{10,... | collective-permute-start | bytes 6152 | tf_op jit(solution)/shard_map/ppermute | solution.py:314
  11.4 2.7 %collective-permute-start = (f32[1,512]{1,0:T(1,128)S(1)}, f32[1,512]{1,0:T(1,128)S(1)}, u32[]{:S(2)}, u32[]{:S(2)}) collective-permute-start(f32[1,512]{1,0:T(1,128)S(1)} %copy-done.2), channel_id=1, source_target_pairs={{0,1},{1,0},{2,3},{3,2},{4,5},{5,4},{6,7},{7,6},{8,9},{9,8},{10,11... | collective-permute-start | bytes 6152 | tf_op jit(solution)/shard_map/ppermute | solution.py:314
  14.1 13.4 %copy-start.8 = (f32[2,4,128]{2,1,0:T(4,128)S(1)}, f32[2,4,128]{2,1,0:T(4,128)}, u32[]{:S(2)}) copy-start(f32[2,4,128]{2,1,0:T(4,128)} %constant.15.clone.spin_ref) | copy-start | bytes 12292
  14.1 3.9 %collective-permute-start.3 = (f32[1,512]{1,0:T(1,128)S(1)}, f32[1,512]{1,0:T(1,128)S(1)}, u32[]{:S(2)}, u32[]{:S(2)}) collective-permute-start(f32[1,512]{1,0:T(1,128)S(1)} %shard_map.119.scale_ref), channel_id=1, source_target_pairs={{0,4},{4,0},{8,12},{12,8},{16,20},{20,16},{24,28},{28,24},{1,5},{5... | collective-permute-start | bytes 6152 | tf_op jit(solution)/shard_map/ppermute | solution.py:314
  18.0 6.8 %collective-permute-start.6 = (f32[2,512]{1,0:T(2,128)S(1)}, f32[2,512]{1,0:T(2,128)S(1)}, u32[]{:S(2)}, u32[]{:S(2)}) collective-permute-start(f32[2,512]{1,0:T(2,128)S(1)} %pad_maximum_fusion.refs_0_), channel_id=1, source_target_pairs={{0,24},{4,28},{8,16},{12,20},{16,8},{20,12},{24,0},{28,4},{1,25},{... | collective-permute-start | bytes 12296 | tf_op jit(solution)/shard_map/ppermute | solution.py:314
  21.5 5.9 %collective-permute-start.5 = (f32[2,512]{1,0:T(2,128)S(1)}, f32[2,512]{1,0:T(2,128)S(1)}, u32[]{:S(2)}, u32[]{:S(2)}) collective-permute-start(f32[2,512]{1,0:T(2,128)S(1)} %pad_maximum_fusion.refs_0_), channel_id=1, source_target_pairs={{0,16},{4,20},{8,24},{12,28},{16,0},{20,4},{24,8},{28,12},{1,17},{... | collective-permute-start | bytes 12296 | tf_op jit(solution)/shard_map/ppermute | solution.py:314
  21.6 5.9 %collective-permute-start.4 = (f32[2,512]{1,0:T(2,128)S(1)}, f32[2,512]{1,0:T(2,128)S(1)}, u32[]{:S(2)}, u32[]{:S(2)}) collective-permute-start(f32[2,512]{1,0:T(2,128)S(1)} %pad_maximum_fusion.refs_0_), channel_id=1, source_target_pairs={{0,8},{4,12},{8,0},{12,4},{16,24},{20,28},{24,16},{28,20},{1,9},{5... | collective-permute-start | bytes 12296 | tf_op jit(solution)/shard_map/ppermute | solution.py:314
  28.6 10.9 %copy-start = (bf16[512,128]{1,0:T(8,128)(2,1)S(1)}, bf16[512,128]{1,0:T(8,128)(2,1)}, u32[]{:S(2)}) copy-start(bf16[512,128]{1,0:T(8,128)(2,1)} %post_ref.1) | copy-start | bytes 393220
  28.6 10.9 %copy-start.1 = (bf16[128,512]{1,0:T(8,128)(2,1)S(1)}, bf16[128,512]{1,0:T(8,128)(2,1)}, u32[]{:S(2)}) copy-start(bf16[128,512]{1,0:T(8,128)(2,1)} %get-tuple-element.10.skipped_ref) | copy-start | bytes 393220

commit v2 on v1

--- a/solution.py
+++ b/solution.py
@@ -16,7 +16,7 @@
 
 
 def order_of(places):
-    return (0, 2, 6, 4, 1, 5, 3, 7) if places == 8 else tuple(range(places))
+    return (7, 5, 1, 3, 6, 2, 4, 0) if places == 8 else tuple(range(places))
 
 
 def reverse_bits(index, levels):

time: 40.6 us -> 39.2 us (0.966)
  blocking collectives: 10.9 us -> 9.46 us
  starting transfers between devices: 15.6 us -> 16.5 us
  waiting for transfers between devices: 9.48 us -> 8.6 us
    all_to_all x1, starting transfers between devices: 7.42 us -> 9.63 us  [exchange(): lax.all_to_all(value, 'seq', split_axis=0, concat_axis=0, tiled=True, axi...]
    all_to_all x1, blocking collectives: 10.9 us -> 9.46 us  [exchange(): lax.all_to_all(value, 'seq', split_axis=0, concat_axis=0, tiled=True, axi...]
    ppermute x7, starting transfers between devices: 8.13 us -> 6.91 us  [swap(): lax.ppermute(value, axis, [(place, place ^ apart) for place in range(lax....]
    ppermute x7, waiting for transfers between devices: 9.47 us -> 8.6 us  [swap(): lax.ppermute(value, axis, [(place, place ^ apart) for place in range(lax....]
where the time goes in v2:
time: 39.2 us; the launch traced here: 39 us
  starting transfers between devices  16.5 us (42%)
  blocking collectives  9.46 us (24%)
  waiting for transfers between devices  8.6 us (22%)
  Pallas kernels  4.18 us (11%)
    all_to_all x1, starting transfers between devices, exchange(): lax.all_to_all(value, 'seq', split_axis=0, concat_axis=0, tiled=True, axi...  9.63 us
    all_to_all x1, blocking collectives, exchange(): lax.all_to_all(value, 'seq', split_axis=0, concat_axis=0, tiled=True, axi...  9.46 us
    ppermute x7, waiting for transfers between devices, swap(): lax.ppermute(value, axis, [(place, place ^ apart) for place in range(lax....  8.6 us
    ppermute x7, starting transfers between devices, swap(): lax.ppermute(value, axis, [(place, place ^ apart) for place in range(lax....  6.91 us
    pallas_call x4, Pallas kernels, call(): pl.pallas_call(kernel, out_shape=out_shape, compiler_params=pltpu.Compile...  4.18 us
  transfers between devices with their start and end apart: 8, of which 5 were waited for; matrix products, arithmetic and copies ran while one was open for 0% of the time, Pallas kernels for 0%

profile of v2, /device:TPU:0, one launch (start us, length us, event | category | flops | bytes accessed | tf_op | source)
XLA Modules:
  0.0 39.0 jit_solution(1643712016142510597)
XLA Ops:
  0.0 2.3 %shard_map.118 = (f32[1,512]{1,0:T(1,128)}, bf16[128,512]{1,0:T(8,128)(2,1)}, bf16[8,5,16,512]{3,2,1,0:T(8,128)(2,1)}) custom-call(bf16[512,128]{1,0:T(8,128)(2,1)} %features_ref.1, bf16[512,128]{1,0:T(8,128)(2,1)} %pre_ref.1, f32[1,128]{1,0:T(1,128)} %bitcast.4, f32[1,128]{1,0:T(1,128)} %bitcast.5, f32[2,2,512,128]{3,2,1,0:T(8,128)} %spectrum_ref.1), custom_call_target="tpu_custom_call" | custom-call | flops 655360 | bytes 2097152 | tf_op jit(solution)/shard_map/pallas_call | solution.py:299
  2.3 0.0 copy-start.2
  2.3 0.0 copy-start.3
  2.3 0.0 copy-start.4
  2.3 0.0 copy-start.5
  2.3 0.0 copy-start.6
  2.4 0.0 copy-start.7
  2.4 9.6 %all-to-all-start = ((bf16[8,5,16,512]{3,2,1,0:T(8,128)(2,1)}), bf16[8,5,16,512]{3,2,1,0:T(8,128)(2,1)S(1)}, u32[]{:S(2)}, u32[]{:S(2)}) async-start(bf16[8,5,16,512]{3,2,1,0:T(8,128)(2,1)} %get-tuple-element.8), calls=%async_computation | async-start | bytes 1310720 | tf_op jit(solution)/shard_map/all_to_all | solution.py:310
  12.0 0.0 copy-done.2
  12.0 0.7 %collective-permute-start.2 = (f32[1,512]{1,0:T(1,128)S(1)}, f32[1,512]{1,0:T(1,128)S(1)}, u32[]{:S(2)}, u32[]{:S(2)}) collective-permute-start(f32[1,512]{1,0:T(1,128)S(1)} %copy-done.2), channel_id=1, source_target_pairs={{0,3},{1,2},{2,1},{3,0},{4,7},{5,6},{6,5},{7,4},{8,11},{9,10},{10,... | collective-permute-start | bytes 6152 | tf_op jit(solution)/shard_map/ppermute | solution.py:314
  12.7 0.9 %collective-permute-start.1 = (f32[1,512]{1,0:T(1,128)S(1)}, f32[1,512]{1,0:T(1,128)S(1)}, u32[]{:S(2)}, u32[]{:S(2)}) collective-permute-start(f32[1,512]{1,0:T(1,128)S(1)} %copy-done.2), channel_id=1, source_target_pairs={{0,2},{1,3},{2,0},{3,1},{4,6},{5,7},{6,4},{7,5},{8,10},{9,11},{10,... | collective-permute-start | bytes 6152 | tf_op jit(solution)/shard_map/ppermute | solution.py:314
  13.6 0.3 collective-permute-start
  13.9 1.1 %collective-permute-done.2.refs_3_ = f32[1,512]{1,0:T(1,128)S(1)} collective-permute-done((f32[1,512]{1,0:T(1,128)S(1)}, f32[1,512]{1,0:T(1,128)S(1)}, u32[]{:S(2)}, u32[]{:S(2)}) %collective-permute-start.2) | collective-permute-done | bytes 2080 | tf_op jit(solution)/shard_map/ppermute | solution.py:314
  15.0 1.2 %collective-permute-done.1.refs_2_ = f32[1,512]{1,0:T(1,128)S(1)} collective-permute-done((f32[1,512]{1,0:T(1,128)S(1)}, f32[1,512]{1,0:T(1,128)S(1)}, u32[]{:S(2)}, u32[]{:S(2)}) %collective-permute-start.1) | collective-permute-done | bytes 2080 | tf_op jit(solution)/shard_map/ppermute | solution.py:314
  16.3 0.0 collective-permute-done.refs_1_
  16.3 0.0 copy-start.8
  16.3 0.6 %collective-permute-start.3 = (f32[1,512]{1,0:T(1,128)S(1)}, f32[1,512]{1,0:T(1,128)S(1)}, u32[]{:S(2)}, u32[]{:S(2)}) collective-permute-start(f32[1,512]{1,0:T(1,128)S(1)} %shard_map.119.scale_ref), channel_id=1, source_target_pairs={{0,4},{4,0},{8,12},{12,8},{16,20},{20,16},{24,28},{28,24},{1,5},{5... | collective-permute-start | bytes 6152 | tf_op jit(solution)/shard_map/ppermute | solution.py:314
  16.9 3.1 %collective-permute-done.3 = f32[1,512]{1,0:T(1,128)S(1)} collective-permute-done((f32[1,512]{1,0:T(1,128)S(1)}, f32[1,512]{1,0:T(1,128)S(1)}, u32[]{:S(2)}, u32[]{:S(2)}) %collective-permute-start.3) | collective-permute-done | bytes 2080 | tf_op jit(solution)/shard_map/ppermute | solution.py:314
  20.0 0.6 %collective-permute-start.6 = (f32[2,512]{1,0:T(2,128)S(1)}, f32[2,512]{1,0:T(2,128)S(1)}, u32[]{:S(2)}, u32[]{:S(2)}) collective-permute-start(f32[2,512]{1,0:T(2,128)S(1)} %pad_maximum_fusion.refs_0_), channel_id=1, source_target_pairs={{0,24},{4,28},{8,16},{12,20},{16,8},{20,12},{24,0},{28,4},{1,25},{... | collective-permute-start | bytes 12296 | tf_op jit(solution)/shard_map/ppermute | solution.py:314
  20.5 1.5 %collective-permute-start.5 = (f32[2,512]{1,0:T(2,128)S(1)}, f32[2,512]{1,0:T(2,128)S(1)}, u32[]{:S(2)}, u32[]{:S(2)}) collective-permute-start(f32[2,512]{1,0:T(2,128)S(1)} %pad_maximum_fusion.refs_0_), channel_id=1, source_target_pairs={{0,16},{4,20},{8,24},{12,28},{16,0},{20,4},{24,8},{28,12},{1,17},{... | collective-permute-start | bytes 12296 | tf_op jit(solution)/shard_map/ppermute | solution.py:314
  22.0 2.4 %collective-permute-start.4 = (f32[2,512]{1,0:T(2,128)S(1)}, f32[2,512]{1,0:T(2,128)S(1)}, u32[]{:S(2)}, u32[]{:S(2)}) collective-permute-start(f32[2,512]{1,0:T(2,128)S(1)} %pad_maximum_fusion.refs_0_), channel_id=1, source_target_pairs={{0,8},{4,12},{8,0},{12,4},{16,24},{20,28},{24,16},{28,20},{1,9},{5... | collective-permute-start | bytes 12296 | tf_op jit(solution)/shard_map/ppermute | solution.py:314
  24.4 1.2 %collective-permute-done.6.refs_3_ = f32[2,512]{1,0:T(2,128)S(1)} collective-permute-done((f32[2,512]{1,0:T(2,128)S(1)}, f32[2,512]{1,0:T(2,128)S(1)}, u32[]{:S(2)}, u32[]{:S(2)}) %collective-permute-start.6) | collective-permute-done | bytes 4128 | tf_op jit(solution)/shard_map/ppermute | solution.py:314
  25.6 2.0 %collective-permute-done.5.refs_2_ = f32[2,512]{1,0:T(2,128)S(1)} collective-permute-done((f32[2,512]{1,0:T(2,128)S(1)}, f32[2,512]{1,0:T(2,128)S(1)}, u32[]{:S(2)}, u32[]{:S(2)}) %collective-permute-start.5) | collective-permute-done | bytes 4128 | tf_op jit(solution)/shard_map/ppermute | solution.py:314
  27.6 0.0 collective-permute-done.4.refs_1_
  27.6 0.0 all-to-all-done.packed_ref
  27.6 0.0 copy-done.3
  27.6 0.0 copy-done.4
  27.6 1.1 %shard_map.120 = bf16[128,512]{1,0:T(8,128)(2,1)S(1)} custom-call(bf16[8,5,16,512]{3,2,1,0:T(8,128)(2,1)S(1)} %all-to-all-done.packed_ref, bf16[288,128]{1,0:T(8,128)(2,1)S(1)} %copy-done.5, bf16[128,288]{1,0:T(8,128)(2,1)S(1)} %copy-done.4, f32[2,9,512]{2,1,0:T(8,128)S(1)} %copy-done.6, f32[2,4,128]{2,1,0:T(4,128)S(1)} %copy-done.8, ...), custom_call_target="tpu_custom_call" | custom-call | flops 671088640 | bytes 1310720 | tf_op jit(solution)/shard_map/pallas_call | solution.py:299
  28.7 0.0 copy-start
  28.7 0.0 copy-start.1
  28.7 9.5 %all_to_all.10.conv_ref = bf16[8,16,512]{2,1,0:T(8,128)(2,1)S(1)} all-to-all(bf16[8,16,512]{2,1,0:T(8,128)(2,1)S(1)} %bitcast.3), channel_id=1, replica_groups={{28,20,4,12,24,8,16,0},{29,21,5,13,25,9,17,1},{30,22,6,14,26,10,18,2},{..., dimensions={0} | all-to-all | bytes 262144 | tf_op jit(solution)/shard_map/all_to_all | solution.py:310
  38.2 0.8 %shard_map.121 = bf16[512,128]{1,0:T(8,128)(2,1)} custom-call(bf16[8,16,512]{2,1,0:T(8,128)(2,1)S(1)} %all_to_all.10.conv_ref, bf16[128,512]{1,0:T(8,128)(2,1)S(1)} %copy-done.1, f32[1,512]{1,0:T(1,128)S(1)} %shard_map.119.scale_ref, bf16[512,128]{1,0:T(8,128)(2,1)S(1)} %copy-done), custom_call_target="tpu_custom_call" | custom-call | flops 655360 | bytes 524288 | tf_op jit(solution)/shard_map/pallas_call | solution.py:299
  (8 shorter events, 0.0 us)
Async XLA Ops:
  2.3 9.7 %copy-start.2 = (f32[1,512]{1,0:T(1,128)S(1)}, f32[1,512]{1,0:T(1,128)}, u32[]{:S(2)}) copy-start(f32[1,512]{1,0:T(1,128)} %get-tuple-element.9.refs_0_) | copy-start | bytes 6148
  2.3 25.3 %copy-start.3 = (bf16[2,256,256]{2,1,0:T(8,128)(2,1)S(1)}, bf16[2,256,256]{2,1,0:T(8,128)(2,1)}, u32[]{:S(2)}) copy-start(bf16[2,256,256]{2,1,0:T(8,128)(2,1)} %constant.16.clone.dft_ref) | copy-start | bytes 786436
  2.3 25.2 %copy-start.4 = (bf16[128,288]{1,0:T(8,128)(2,1)S(1)}, bf16[128,288]{1,0:T(8,128)(2,1)}, u32[]{:S(2)}) copy-start(bf16[128,288]{1,0:T(8,128)(2,1)} %constant.13.clone.last_ref) | copy-start | bytes 221188
  2.3 25.2 %copy-start.5 = (bf16[288,128]{1,0:T(8,128)(2,1)S(1)}, bf16[288,128]{1,0:T(8,128)(2,1)}, u32[]{:S(2)}) copy-start(bf16[288,128]{1,0:T(8,128)(2,1)} %constant.12.clone.first_ref) | copy-start | bytes 221188
  2.3 25.2 %copy-start.6 = (f32[2,9,512]{2,1,0:T(8,128)S(1)}, f32[2,9,512]{2,1,0:T(8,128)}, u32[]{:S(2)}) copy-start(f32[2,9,512]{2,1,0:T(8,128)} %constant.14.clone.twist_ref) | copy-start | bytes 110596
  2.4 25.2 %copy-start.7 = (bf16[128,128]{1,0:T(8,128)(2,1)S(1)}, bf16[128,128]{1,0:T(8,128)(2,1)}, u32[]{:S(2)}) copy-start(bf16[128,128]{1,0:T(8,128)(2,1)} %constant.17.clone.reverse_ref) | copy-start | bytes 98308
  2.4 25.2 %all-to-all-start = ((bf16[8,5,16,512]{3,2,1,0:T(8,128)(2,1)}), bf16[8,5,16,512]{3,2,1,0:T(8,128)(2,1)S(1)}, u32[]{:S(2)}, u32[]{:S(2)}) async-start(bf16[8,5,16,512]{3,2,1,0:T(8,128)(2,1)} %get-tuple-element.8), calls=%async_computation | async-start | bytes 1310720 | tf_op jit(solution)/shard_map/all_to_all | solution.py:310
  12.0 3.0 %collective-permute-start.2 = (f32[1,512]{1,0:T(1,128)S(1)}, f32[1,512]{1,0:T(1,128)S(1)}, u32[]{:S(2)}, u32[]{:S(2)}) collective-permute-start(f32[1,512]{1,0:T(1,128)S(1)} %copy-done.2), channel_id=1, source_target_pairs={{0,3},{1,2},{2,1},{3,0},{4,7},{5,6},{6,5},{7,4},{8,11},{9,10},{10,... | collective-permute-start | bytes 6152 | tf_op jit(solution)/shard_map/ppermute | solution.py:314
  12.7 3.6 %collective-permute-start.1 = (f32[1,512]{1,0:T(1,128)S(1)}, f32[1,512]{1,0:T(1,128)S(1)}, u32[]{:S(2)}, u32[]{:S(2)}) collective-permute-start(f32[1,512]{1,0:T(1,128)S(1)} %copy-done.2), channel_id=1, source_target_pairs={{0,2},{1,3},{2,0},{3,1},{4,6},{5,7},{6,4},{7,5},{8,10},{9,11},{10,... | collective-permute-start | bytes 6152 | tf_op jit(solution)/shard_map/ppermute | solution.py:314
  13.6 2.7 %collective-permute-start = (f32[1,512]{1,0:T(1,128)S(1)}, f32[1,512]{1,0:T(1,128)S(1)}, u32[]{:S(2)}, u32[]{:S(2)}) collective-permute-start(f32[1,512]{1,0:T(1,128)S(1)} %copy-done.2), channel_id=1, source_target_pairs={{0,1},{1,0},{2,3},{3,2},{4,5},{5,4},{6,7},{7,6},{8,9},{9,8},{10,11... | collective-permute-start | bytes 6152 | tf_op jit(solution)/shard_map/ppermute | solution.py:314
  16.3 11.3 %copy-start.8 = (f32[2,4,128]{2,1,0:T(4,128)S(1)}, f32[2,4,128]{2,1,0:T(4,128)}, u32[]{:S(2)}) copy-start(f32[2,4,128]{2,1,0:T(4,128)} %constant.15.clone.spin_ref) | copy-start | bytes 12292
  16.3 3.7 %collective-permute-start.3 = (f32[1,512]{1,0:T(1,128)S(1)}, f32[1,512]{1,0:T(1,128)S(1)}, u32[]{:S(2)}, u32[]{:S(2)}) collective-permute-start(f32[1,512]{1,0:T(1,128)S(1)} %shard_map.119.scale_ref), channel_id=1, source_target_pairs={{0,4},{4,0},{8,12},{12,8},{16,20},{20,16},{24,28},{28,24},{1,5},{5... | collective-permute-start | bytes 6152 | tf_op jit(solution)/shard_map/ppermute | solution.py:314
  20.0 5.6 %collective-permute-start.6 = (f32[2,512]{1,0:T(2,128)S(1)}, f32[2,512]{1,0:T(2,128)S(1)}, u32[]{:S(2)}, u32[]{:S(2)}) collective-permute-start(f32[2,512]{1,0:T(2,128)S(1)} %pad_maximum_fusion.refs_0_), channel_id=1, source_target_pairs={{0,24},{4,28},{8,16},{12,20},{16,8},{20,12},{24,0},{28,4},{1,25},{... | collective-permute-start | bytes 12296 | tf_op jit(solution)/shard_map/ppermute | solution.py:314
  20.5 7.0 %collective-permute-start.5 = (f32[2,512]{1,0:T(2,128)S(1)}, f32[2,512]{1,0:T(2,128)S(1)}, u32[]{:S(2)}, u32[]{:S(2)}) collective-permute-start(f32[2,512]{1,0:T(2,128)S(1)} %pad_maximum_fusion.refs_0_), channel_id=1, source_target_pairs={{0,16},{4,20},{8,24},{12,28},{16,0},{20,4},{24,8},{28,12},{1,17},{... | collective-permute-start | bytes 12296 | tf_op jit(solution)/shard_map/ppermute | solution.py:314
  22.0 5.5 %collective-permute-start.4 = (f32[2,512]{1,0:T(2,128)S(1)}, f32[2,512]{1,0:T(2,128)S(1)}, u32[]{:S(2)}, u32[]{:S(2)}) collective-permute-start(f32[2,512]{1,0:T(2,128)S(1)} %pad_maximum_fusion.refs_0_), channel_id=1, source_target_pairs={{0,8},{4,12},{8,0},{12,4},{16,24},{20,28},{24,16},{28,20},{1,9},{5... | collective-permute-start | bytes 12296 | tf_op jit(solution)/shard_map/ppermute | solution.py:314
  28.7 9.5 %copy-start = (bf16[512,128]{1,0:T(8,128)(2,1)S(1)}, bf16[512,128]{1,0:T(8,128)(2,1)}, u32[]{:S(2)}) copy-start(bf16[512,128]{1,0:T(8,128)(2,1)} %post_ref.1) | copy-start | bytes 393220
  28.7 9.5 %copy-start.1 = (bf16[128,512]{1,0:T(8,128)(2,1)S(1)}, bf16[128,512]{1,0:T(8,128)(2,1)}, u32[]{:S(2)}) copy-start(bf16[128,512]{1,0:T(8,128)(2,1)} %get-tuple-element.10.skipped_ref) | copy-start | bytes 393220

commit v3 on v2

--- a/solution.py
+++ b/solution.py
@@ -16,7 +16,7 @@
 
 
 def order_of(places):
-    return (7, 5, 1, 3, 6, 2, 4, 0) if places == 8 else tuple(range(places))
+    return (1, 3, 6, 2, 4, 0, 7, 5) if places == 8 else tuple(range(places))
 
 
 def reverse_bits(index, levels):

time: 39.2 us -> 39.2 us (level)
  starting transfers between devices: 16.5 us -> 14.7 us
  waiting for transfers between devices: 8.6 us -> 10.4 us
    ppermute x7, waiting for transfers between devices: 8.6 us -> 10.4 us  [swap(): lax.ppermute(value, axis, [(place, place ^ apart) for place in range(lax....]
    all_to_all x1, starting transfers between devices: 9.63 us -> 7.99 us  [exchange(): lax.all_to_all(value, 'seq', split_axis=0, concat_axis=0, tiled=True, axi...]
where the time goes in v3:
time: 39.2 us; the launch traced here: 38.9 us
  starting transfers between devices  14.7 us (38%)
  waiting for transfers between devices  10.4 us (27%)
  blocking collectives  9.48 us (24%)
  Pallas kernels  4.18 us (11%)
    ppermute x7, waiting for transfers between devices, swap(): lax.ppermute(value, axis, [(place, place ^ apart) for place in range(lax....  10.4 us
    all_to_all x1, blocking collectives, exchange(): lax.all_to_all(value, 'seq', split_axis=0, concat_axis=0, tiled=True, axi...  9.48 us
    all_to_all x1, starting transfers between devices, exchange(): lax.all_to_all(value, 'seq', split_axis=0, concat_axis=0, tiled=True, axi...  7.99 us
    ppermute x7, starting transfers between devices, swap(): lax.ppermute(value, axis, [(place, place ^ apart) for place in range(lax....  6.74 us
    pallas_call x4, Pallas kernels, call(): pl.pallas_call(kernel, out_shape=out_shape, compiler_params=pltpu.Compile...  4.18 us
  transfers between devices with their start and end apart: 8, of which 5 were waited for; matrix products, arithmetic and copies ran while one was open for 0% of the time, Pallas kernels for 0%

profile of v3, /device:TPU:0, one launch (start us, length us, event | category | flops | bytes accessed | tf_op | source)
XLA Modules:
  0.0 38.9 jit_solution(10640003116639714633)
XLA Ops:
  0.0 2.3 %shard_map.118 = (f32[1,512]{1,0:T(1,128)}, bf16[128,512]{1,0:T(8,128)(2,1)}, bf16[8,5,16,512]{3,2,1,0:T(8,128)(2,1)}) custom-call(bf16[512,128]{1,0:T(8,128)(2,1)} %features_ref.1, bf16[512,128]{1,0:T(8,128)(2,1)} %pre_ref.1, f32[1,128]{1,0:T(1,128)} %bitcast.4, f32[1,128]{1,0:T(1,128)} %bitcast.5, f32[2,2,512,128]{3,2,1,0:T(8,128)} %spectrum_ref.1), custom_call_target="tpu_custom_call" | custom-call | flops 655360 | bytes 2097152 | tf_op jit(solution)/shard_map/pallas_call | solution.py:299
  2.3 0.0 copy-start.2
  2.3 0.0 copy-start.3
  2.3 0.0 copy-start.4
  2.3 0.0 copy-start.5
  2.3 0.0 copy-start.6
  2.4 0.0 copy-start.7
  2.4 8.0 %all-to-all-start = ((bf16[8,5,16,512]{3,2,1,0:T(8,128)(2,1)}), bf16[8,5,16,512]{3,2,1,0:T(8,128)(2,1)S(1)}, u32[]{:S(2)}, u32[]{:S(2)}) async-start(bf16[8,5,16,512]{3,2,1,0:T(8,128)(2,1)} %get-tuple-element.8), calls=%async_computation | async-start | bytes 1310720 | tf_op jit(solution)/shard_map/all_to_all | solution.py:310
  10.4 0.0 copy-done.2
  10.4 0.4 collective-permute-start.2
  10.7 1.2 %collective-permute-start.1 = (f32[1,512]{1,0:T(1,128)S(1)}, f32[1,512]{1,0:T(1,128)S(1)}, u32[]{:S(2)}, u32[]{:S(2)}) collective-permute-start(f32[1,512]{1,0:T(1,128)S(1)} %copy-done.2), channel_id=1, source_target_pairs={{0,2},{1,3},{2,0},{3,1},{4,6},{5,7},{6,4},{7,5},{8,10},{9,11},{10,... | collective-permute-start | bytes 6152 | tf_op jit(solution)/shard_map/ppermute | solution.py:314
  11.9 0.3 collective-permute-start
  12.2 1.1 %collective-permute-done.2.refs_3_ = f32[1,512]{1,0:T(1,128)S(1)} collective-permute-done((f32[1,512]{1,0:T(1,128)S(1)}, f32[1,512]{1,0:T(1,128)S(1)}, u32[]{:S(2)}, u32[]{:S(2)}) %collective-permute-start.2) | collective-permute-done | bytes 2080 | tf_op jit(solution)/shard_map/ppermute | solution.py:314
  13.4 0.9 %collective-permute-done.1.refs_2_ = f32[1,512]{1,0:T(1,128)S(1)} collective-permute-done((f32[1,512]{1,0:T(1,128)S(1)}, f32[1,512]{1,0:T(1,128)S(1)}, u32[]{:S(2)}, u32[]{:S(2)}) %collective-permute-start.1) | collective-permute-done | bytes 2080 | tf_op jit(solution)/shard_map/ppermute | solution.py:314
  14.3 0.0 collective-permute-done.refs_1_
  14.3 0.0 copy-start.8
  14.3 0.4 %collective-permute-start.3 = (f32[1,512]{1,0:T(1,128)S(1)}, f32[1,512]{1,0:T(1,128)S(1)}, u32[]{:S(2)}, u32[]{:S(2)}) collective-permute-start(f32[1,512]{1,0:T(1,128)S(1)} %shard_map.119.scale_ref), channel_id=1, source_target_pairs={{0,4},{4,0},{8,12},{12,8},{16,20},{20,16},{24,28},{28,24},{1,5},{5... | collective-permute-start | bytes 6152 | tf_op jit(solution)/shard_map/ppermute | solution.py:314
  14.8 3.3 %collective-permute-done.3 = f32[1,512]{1,0:T(1,128)S(1)} collective-permute-done((f32[1,512]{1,0:T(1,128)S(1)}, f32[1,512]{1,0:T(1,128)S(1)}, u32[]{:S(2)}, u32[]{:S(2)}) %collective-permute-start.3) | collective-permute-done | bytes 2080 | tf_op jit(solution)/shard_map/ppermute | solution.py:314
  18.0 3.3 %collective-permute-start.6 = (f32[2,512]{1,0:T(2,128)S(1)}, f32[2,512]{1,0:T(2,128)S(1)}, u32[]{:S(2)}, u32[]{:S(2)}) collective-permute-start(f32[2,512]{1,0:T(2,128)S(1)} %pad_maximum_fusion.refs_0_), channel_id=1, source_target_pairs={{0,24},{4,28},{8,16},{12,20},{16,8},{20,12},{24,0},{28,4},{1,25},{... | collective-permute-start | bytes 12296 | tf_op jit(solution)/shard_map/ppermute | solution.py:314
  21.4 0.0 collective-permute-start.5
  21.4 1.1 %collective-permute-start.4 = (f32[2,512]{1,0:T(2,128)S(1)}, f32[2,512]{1,0:T(2,128)S(1)}, u32[]{:S(2)}, u32[]{:S(2)}) collective-permute-start(f32[2,512]{1,0:T(2,128)S(1)} %pad_maximum_fusion.refs_0_), channel_id=1, source_target_pairs={{0,8},{4,12},{8,0},{12,4},{16,24},{20,28},{24,16},{28,20},{1,9},{5... | collective-permute-start | bytes 12296 | tf_op jit(solution)/shard_map/ppermute | solution.py:314
  22.5 2.3 %collective-permute-done.6.refs_3_ = f32[2,512]{1,0:T(2,128)S(1)} collective-permute-done((f32[2,512]{1,0:T(2,128)S(1)}, f32[2,512]{1,0:T(2,128)S(1)}, u32[]{:S(2)}, u32[]{:S(2)}) %collective-permute-start.6) | collective-permute-done | bytes 4128 | tf_op jit(solution)/shard_map/ppermute | solution.py:314
  24.8 2.7 %collective-permute-done.5.refs_2_ = f32[2,512]{1,0:T(2,128)S(1)} collective-permute-done((f32[2,512]{1,0:T(2,128)S(1)}, f32[2,512]{1,0:T(2,128)S(1)}, u32[]{:S(2)}, u32[]{:S(2)}) %collective-permute-start.5) | collective-permute-done | bytes 4128 | tf_op jit(solution)/shard_map/ppermute | solution.py:314
  27.5 0.0 collective-permute-done.4.refs_1_
  27.5 0.0 all-to-all-done.packed_ref
  27.5 0.0 copy-done.3
  27.5 0.0 copy-done.4
  27.6 1.1 %shard_map.120 = bf16[128,512]{1,0:T(8,128)(2,1)S(1)} custom-call(bf16[8,5,16,512]{3,2,1,0:T(8,128)(2,1)S(1)} %all-to-all-done.packed_ref, bf16[288,128]{1,0:T(8,128)(2,1)S(1)} %copy-done.5, bf16[128,288]{1,0:T(8,128)(2,1)S(1)} %copy-done.4, f32[2,9,512]{2,1,0:T(8,128)S(1)} %copy-done.6, f32[2,4,128]{2,1,0:T(4,128)S(1)} %copy-done.8, ...), custom_call_target="tpu_custom_call" | custom-call | flops 671088640 | bytes 1310720 | tf_op jit(solution)/shard_map/pallas_call | solution.py:299
  28.6 0.0 copy-start
  28.7 0.0 copy-start.1
  28.7 9.5 %all_to_all.10.conv_ref = bf16[8,16,512]{2,1,0:T(8,128)(2,1)S(1)} all-to-all(bf16[8,16,512]{2,1,0:T(8,128)(2,1)S(1)} %bitcast.3), channel_id=1, replica_groups={{4,12,24,8,16,0,28,20},{5,13,25,9,17,1,29,21},{6,14,26,10,18,2,30,22},{..., dimensions={0} | all-to-all | bytes 262144 | tf_op jit(solution)/shard_map/all_to_all | solution.py:310
  38.2 0.8 %shard_map.121 = bf16[512,128]{1,0:T(8,128)(2,1)} custom-call(bf16[8,16,512]{2,1,0:T(8,128)(2,1)S(1)} %all_to_all.10.conv_ref, bf16[128,512]{1,0:T(8,128)(2,1)S(1)} %copy-done.1, f32[1,512]{1,0:T(1,128)S(1)} %shard_map.119.scale_ref, bf16[512,128]{1,0:T(8,128)(2,1)S(1)} %copy-done), custom_call_target="tpu_custom_call" | custom-call | flops 655360 | bytes 524288 | tf_op jit(solution)/shard_map/pallas_call | solution.py:299
  (8 shorter events, 0.0 us)
Async XLA Ops:
  2.3 8.1 %copy-start.2 = (f32[1,512]{1,0:T(1,128)S(1)}, f32[1,512]{1,0:T(1,128)}, u32[]{:S(2)}) copy-start(f32[1,512]{1,0:T(1,128)} %get-tuple-element.9.refs_0_) | copy-start | bytes 6148
  2.3 25.2 %copy-start.3 = (bf16[2,256,256]{2,1,0:T(8,128)(2,1)S(1)}, bf16[2,256,256]{2,1,0:T(8,128)(2,1)}, u32[]{:S(2)}) copy-start(bf16[2,256,256]{2,1,0:T(8,128)(2,1)} %constant.16.clone.dft_ref) | copy-start | bytes 786436
  2.3 25.2 %copy-start.4 = (bf16[128,288]{1,0:T(8,128)(2,1)S(1)}, bf16[128,288]{1,0:T(8,128)(2,1)}, u32[]{:S(2)}) copy-start(bf16[128,288]{1,0:T(8,128)(2,1)} %constant.13.clone.last_ref) | copy-start | bytes 221188
  2.3 25.2 %copy-start.5 = (bf16[288,128]{1,0:T(8,128)(2,1)S(1)}, bf16[288,128]{1,0:T(8,128)(2,1)}, u32[]{:S(2)}) copy-start(bf16[288,128]{1,0:T(8,128)(2,1)} %constant.12.clone.first_ref) | copy-start | bytes 221188
  2.3 25.2 %copy-start.6 = (f32[2,9,512]{2,1,0:T(8,128)S(1)}, f32[2,9,512]{2,1,0:T(8,128)}, u32[]{:S(2)}) copy-start(f32[2,9,512]{2,1,0:T(8,128)} %constant.14.clone.twist_ref) | copy-start | bytes 110596
  2.4 25.2 %copy-start.7 = (bf16[128,128]{1,0:T(8,128)(2,1)S(1)}, bf16[128,128]{1,0:T(8,128)(2,1)}, u32[]{:S(2)}) copy-start(bf16[128,128]{1,0:T(8,128)(2,1)} %constant.17.clone.reverse_ref) | copy-start | bytes 98308
  2.4 25.1 %all-to-all-start = ((bf16[8,5,16,512]{3,2,1,0:T(8,128)(2,1)}), bf16[8,5,16,512]{3,2,1,0:T(8,128)(2,1)S(1)}, u32[]{:S(2)}, u32[]{:S(2)}) async-start(bf16[8,5,16,512]{3,2,1,0:T(8,128)(2,1)} %get-tuple-element.8), calls=%async_computation | async-start | bytes 1310720 | tf_op jit(solution)/shard_map/all_to_all | solution.py:310
  10.4 3.0 %collective-permute-start.2 = (f32[1,512]{1,0:T(1,128)S(1)}, f32[1,512]{1,0:T(1,128)S(1)}, u32[]{:S(2)}, u32[]{:S(2)}) collective-permute-start(f32[1,512]{1,0:T(1,128)S(1)} %copy-done.2), channel_id=1, source_target_pairs={{0,3},{1,2},{2,1},{3,0},{4,7},{5,6},{6,5},{7,4},{8,11},{9,10},{10,... | collective-permute-start | bytes 6152 | tf_op jit(solution)/shard_map/ppermute | solution.py:314
  10.7 3.6 %collective-permute-start.1 = (f32[1,512]{1,0:T(1,128)S(1)}, f32[1,512]{1,0:T(1,128)S(1)}, u32[]{:S(2)}, u32[]{:S(2)}) collective-permute-start(f32[1,512]{1,0:T(1,128)S(1)} %copy-done.2), channel_id=1, source_target_pairs={{0,2},{1,3},{2,0},{3,1},{4,6},{5,7},{6,4},{7,5},{8,10},{9,11},{10,... | collective-permute-start | bytes 6152 | tf_op jit(solution)/shard_map/ppermute | solution.py:314
  11.9 2.4 %collective-permute-start = (f32[1,512]{1,0:T(1,128)S(1)}, f32[1,512]{1,0:T(1,128)S(1)}, u32[]{:S(2)}, u32[]{:S(2)}) collective-permute-start(f32[1,512]{1,0:T(1,128)S(1)} %copy-done.2), channel_id=1, source_target_pairs={{0,1},{1,0},{2,3},{3,2},{4,5},{5,4},{6,7},{7,6},{8,9},{9,8},{10,11... | collective-permute-start | bytes 6152 | tf_op jit(solution)/shard_map/ppermute | solution.py:314
  14.3 13.2 %copy-start.8 = (f32[2,4,128]{2,1,0:T(4,128)S(1)}, f32[2,4,128]{2,1,0:T(4,128)}, u32[]{:S(2)}) copy-start(f32[2,4,128]{2,1,0:T(4,128)} %constant.15.clone.spin_ref) | copy-start | bytes 12292
  14.3 3.7 %collective-permute-start.3 = (f32[1,512]{1,0:T(1,128)S(1)}, f32[1,512]{1,0:T(1,128)S(1)}, u32[]{:S(2)}, u32[]{:S(2)}) collective-permute-start(f32[1,512]{1,0:T(1,128)S(1)} %shard_map.119.scale_ref), channel_id=1, source_target_pairs={{0,4},{4,0},{8,12},{12,8},{16,20},{20,16},{24,28},{28,24},{1,5},{5... | collective-permute-start | bytes 6152 | tf_op jit(solution)/shard_map/ppermute | solution.py:314
  18.0 6.8 %collective-permute-start.6 = (f32[2,512]{1,0:T(2,128)S(1)}, f32[2,512]{1,0:T(2,128)S(1)}, u32[]{:S(2)}, u32[]{:S(2)}) collective-permute-start(f32[2,512]{1,0:T(2,128)S(1)} %pad_maximum_fusion.refs_0_), channel_id=1, source_target_pairs={{0,24},{4,28},{8,16},{12,20},{16,8},{20,12},{24,0},{28,4},{1,25},{... | collective-permute-start | bytes 12296 | tf_op jit(solution)/shard_map/ppermute | solution.py:314
  21.4 6.1 %collective-permute-start.5 = (f32[2,512]{1,0:T(2,128)S(1)}, f32[2,512]{1,0:T(2,128)S(1)}, u32[]{:S(2)}, u32[]{:S(2)}) collective-permute-start(f32[2,512]{1,0:T(2,128)S(1)} %pad_maximum_fusion.refs_0_), channel_id=1, source_target_pairs={{0,16},{4,20},{8,24},{12,28},{16,0},{20,4},{24,8},{28,12},{1,17},{... | collective-permute-start | bytes 12296 | tf_op jit(solution)/shard_map/ppermute | solution.py:314
  21.4 6.1 %collective-permute-start.4 = (f32[2,512]{1,0:T(2,128)S(1)}, f32[2,512]{1,0:T(2,128)S(1)}, u32[]{:S(2)}, u32[]{:S(2)}) collective-permute-start(f32[2,512]{1,0:T(2,128)S(1)} %pad_maximum_fusion.refs_0_), channel_id=1, source_target_pairs={{0,8},{4,12},{8,0},{12,4},{16,24},{20,28},{24,16},{28,20},{1,9},{5... | collective-permute-start | bytes 12296 | tf_op jit(solution)/shard_map/ppermute | solution.py:314
  28.6 9.5 %copy-start = (bf16[512,128]{1,0:T(8,128)(2,1)S(1)}, bf16[512,128]{1,0:T(8,128)(2,1)}, u32[]{:S(2)}) copy-start(bf16[512,128]{1,0:T(8,128)(2,1)} %post_ref.1) | copy-start | bytes 393220
  28.7 9.5 %copy-start.1 = (bf16[128,512]{1,0:T(8,128)(2,1)S(1)}, bf16[128,512]{1,0:T(8,128)(2,1)}, u32[]{:S(2)}) copy-start(bf16[128,512]{1,0:T(8,128)(2,1)} %get-tuple-element.10.skipped_ref) | copy-start | bytes 393220

commit v4 on v3

--- a/solution.py
+++ b/solution.py
@@ -16,7 +16,7 @@
 
 
 def order_of(places):
-    return (1, 3, 6, 2, 4, 0, 7, 5) if places == 8 else tuple(range(places))
+    return (5, 1, 3, 6, 2, 4, 0, 7) if places == 8 else tuple(range(places))
 
 
 def reverse_bits(index, levels):

time: 39.2 us -> 37.4 us (0.954)
  waiting for transfers between devices: 10.4 us -> 8.62 us
  blocking collectives: 9.48 us -> 8.58 us
  starting transfers between devices: 14.7 us -> 15.5 us
    ppermute x7, waiting for transfers between devices: 10.4 us -> 8.61 us  [swap(): lax.ppermute(value, axis, [(place, place ^ apart) for place in range(lax....]
    all_to_all x1, blocking collectives: 9.48 us -> 8.58 us  [exchange(): lax.all_to_all(value, 'seq', split_axis=0, concat_axis=0, tiled=True, axi...]
    all_to_all x1, starting transfers between devices: 7.99 us -> 8.61 us  [exchange(): lax.all_to_all(value, 'seq', split_axis=0, concat_axis=0, tiled=True, axi...]
where the time goes in v4:
time: 37.4 us; the launch traced here: 37.1 us
  starting transfers between devices  15.5 us (41%)
  waiting for transfers between devices  8.62 us (23%)
  blocking collectives  8.58 us (23%)
  Pallas kernels  4.18 us (11%)
    ppermute x7, waiting for transfers between devices, swap(): lax.ppermute(value, axis, [(place, place ^ apart) for place in range(lax....  8.61 us
    all_to_all x1, starting transfers between devices, exchange(): lax.all_to_all(value, 'seq', split_axis=0, concat_axis=0, tiled=True, axi...  8.61 us
    all_to_all x1, blocking collectives, exchange(): lax.all_to_all(value, 'seq', split_axis=0, concat_axis=0, tiled=True, axi...  8.58 us
    ppermute x7, starting transfers between devices, swap(): lax.ppermute(value, axis, [(place, place ^ apart) for place in range(lax....  6.91 us
    pallas_call x4, Pallas kernels, call(): pl.pallas_call(kernel, out_shape=out_shape, compiler_params=pltpu.Compile...  4.18 us
  transfers between devices with their start and end apart: 8, of which 5 were waited for; matrix products, arithmetic and copies ran while one was open for 0% of the time, Pallas kernels for 0%

profile of v4, /device:TPU:0, one launch (start us, length us, event | category | flops | bytes accessed | tf_op | source)
XLA Modules:
  0.0 37.1 jit_solution(6029475151303755966)
XLA Ops:
  0.0 2.3 %shard_map.118 = (f32[1,512]{1,0:T(1,128)}, bf16[128,512]{1,0:T(8,128)(2,1)}, bf16[8,5,16,512]{3,2,1,0:T(8,128)(2,1)}) custom-call(bf16[512,128]{1,0:T(8,128)(2,1)} %features_ref.1, bf16[512,128]{1,0:T(8,128)(2,1)} %pre_ref.1, f32[1,128]{1,0:T(1,128)} %bitcast.4, f32[1,128]{1,0:T(1,128)} %bitcast.5, f32[2,2,512,128]{3,2,1,0:T(8,128)} %spectrum_ref.1), custom_call_target="tpu_custom_call" | custom-call | flops 655360 | bytes 2097152 | tf_op jit(solution)/shard_map/pallas_call | solution.py:299
  2.3 0.0 copy-start.2
  2.3 0.0 copy-start.3
  2.3 0.0 copy-start.4
  2.3 0.0 copy-start.5
  2.3 0.0 copy-start.6
  2.4 0.0 copy-start.7
  2.4 8.6 %all-to-all-start = ((bf16[8,5,16,512]{3,2,1,0:T(8,128)(2,1)}), bf16[8,5,16,512]{3,2,1,0:T(8,128)(2,1)S(1)}, u32[]{:S(2)}, u32[]{:S(2)}) async-start(bf16[8,5,16,512]{3,2,1,0:T(8,128)(2,1)} %get-tuple-element.8), calls=%async_computation | async-start | bytes 1310720 | tf_op jit(solution)/shard_map/all_to_all | solution.py:310
  11.0 0.0 copy-done.2
  11.0 0.7 %collective-permute-start.2 = (f32[1,512]{1,0:T(1,128)S(1)}, f32[1,512]{1,0:T(1,128)S(1)}, u32[]{:S(2)}, u32[]{:S(2)}) collective-permute-start(f32[1,512]{1,0:T(1,128)S(1)} %copy-done.2), channel_id=1, source_target_pairs={{0,3},{1,2},{2,1},{3,0},{4,7},{5,6},{6,5},{7,4},{8,11},{9,10},{10,... | collective-permute-start | bytes 6152 | tf_op jit(solution)/shard_map/ppermute | solution.py:314
  11.6 0.9 %collective-permute-start.1 = (f32[1,512]{1,0:T(1,128)S(1)}, f32[1,512]{1,0:T(1,128)S(1)}, u32[]{:S(2)}, u32[]{:S(2)}) collective-permute-start(f32[1,512]{1,0:T(1,128)S(1)} %copy-done.2), channel_id=1, source_target_pairs={{0,2},{1,3},{2,0},{3,1},{4,6},{5,7},{6,4},{7,5},{8,10},{9,11},{10,... | collective-permute-start | bytes 6152 | tf_op jit(solution)/shard_map/ppermute | solution.py:314
  12.6 0.3 collective-permute-start
  12.9 1.1 %collective-permute-done.2.refs_3_ = f32[1,512]{1,0:T(1,128)S(1)} collective-permute-done((f32[1,512]{1,0:T(1,128)S(1)}, f32[1,512]{1,0:T(1,128)S(1)}, u32[]{:S(2)}, u32[]{:S(2)}) %collective-permute-start.2) | collective-permute-done | bytes 2080 | tf_op jit(solution)/shard_map/ppermute | solution.py:314
  14.0 1.2 %collective-permute-done.1.refs_2_ = f32[1,512]{1,0:T(1,128)S(1)} collective-permute-done((f32[1,512]{1,0:T(1,128)S(1)}, f32[1,512]{1,0:T(1,128)S(1)}, u32[]{:S(2)}, u32[]{:S(2)}) %collective-permute-start.1) | collective-permute-done | bytes 2080 | tf_op jit(solution)/shard_map/ppermute | solution.py:314
  15.2 0.0 collective-permute-done.refs_1_
  15.2 0.0 copy-start.8
  15.3 0.6 %collective-permute-start.3 = (f32[1,512]{1,0:T(1,128)S(1)}, f32[1,512]{1,0:T(1,128)S(1)}, u32[]{:S(2)}, u32[]{:S(2)}) collective-permute-start(f32[1,512]{1,0:T(1,128)S(1)} %shard_map.119.scale_ref), channel_id=1, source_target_pairs={{0,4},{4,0},{8,12},{12,8},{16,20},{20,16},{24,28},{28,24},{1,5},{5... | collective-permute-start | bytes 6152 | tf_op jit(solution)/shard_map/ppermute | solution.py:314
  15.9 3.1 %collective-permute-done.3 = f32[1,512]{1,0:T(1,128)S(1)} collective-permute-done((f32[1,512]{1,0:T(1,128)S(1)}, f32[1,512]{1,0:T(1,128)S(1)}, u32[]{:S(2)}, u32[]{:S(2)}) %collective-permute-start.3) | collective-permute-done | bytes 2080 | tf_op jit(solution)/shard_map/ppermute | solution.py:314
  18.9 1.5 %collective-permute-start.6 = (f32[2,512]{1,0:T(2,128)S(1)}, f32[2,512]{1,0:T(2,128)S(1)}, u32[]{:S(2)}, u32[]{:S(2)}) collective-permute-start(f32[2,512]{1,0:T(2,128)S(1)} %pad_maximum_fusion.refs_0_), channel_id=1, source_target_pairs={{0,24},{4,28},{8,16},{12,20},{16,8},{20,12},{24,0},{28,4},{1,25},{... | collective-permute-start | bytes 12296 | tf_op jit(solution)/shard_map/ppermute | solution.py:314
  20.4 0.6 %collective-permute-start.5 = (f32[2,512]{1,0:T(2,128)S(1)}, f32[2,512]{1,0:T(2,128)S(1)}, u32[]{:S(2)}, u32[]{:S(2)}) collective-permute-start(f32[2,512]{1,0:T(2,128)S(1)} %pad_maximum_fusion.refs_0_), channel_id=1, source_target_pairs={{0,16},{4,20},{8,24},{12,28},{16,0},{20,4},{24,8},{28,12},{1,17},{... | collective-permute-start | bytes 12296 | tf_op jit(solution)/shard_map/ppermute | solution.py:314
  21.0 2.4 %collective-permute-start.4 = (f32[2,512]{1,0:T(2,128)S(1)}, f32[2,512]{1,0:T(2,128)S(1)}, u32[]{:S(2)}, u32[]{:S(2)}) collective-permute-start(f32[2,512]{1,0:T(2,128)S(1)} %pad_maximum_fusion.refs_0_), channel_id=1, source_target_pairs={{0,8},{4,12},{8,0},{12,4},{16,24},{20,28},{24,16},{28,20},{1,9},{5... | collective-permute-start | bytes 12296 | tf_op jit(solution)/shard_map/ppermute | solution.py:314
  23.4 1.1 %collective-permute-done.6.refs_3_ = f32[2,512]{1,0:T(2,128)S(1)} collective-permute-done((f32[2,512]{1,0:T(2,128)S(1)}, f32[2,512]{1,0:T(2,128)S(1)}, u32[]{:S(2)}, u32[]{:S(2)}) %collective-permute-start.6) | collective-permute-done | bytes 4128 | tf_op jit(solution)/shard_map/ppermute | solution.py:314
  24.5 2.0 %collective-permute-done.5.refs_2_ = f32[2,512]{1,0:T(2,128)S(1)} collective-permute-done((f32[2,512]{1,0:T(2,128)S(1)}, f32[2,512]{1,0:T(2,128)S(1)}, u32[]{:S(2)}, u32[]{:S(2)}) %collective-permute-start.5) | collective-permute-done | bytes 4128 | tf_op jit(solution)/shard_map/ppermute | solution.py:314
  26.5 0.0 collective-permute-done.4.refs_1_
  26.6 0.0 all-to-all-done.packed_ref
  26.6 0.0 copy-done.3
  26.6 0.0 copy-done.4
  26.6 1.1 %shard_map.120 = bf16[128,512]{1,0:T(8,128)(2,1)S(1)} custom-call(bf16[8,5,16,512]{3,2,1,0:T(8,128)(2,1)S(1)} %all-to-all-done.packed_ref, bf16[288,128]{1,0:T(8,128)(2,1)S(1)} %copy-done.5, bf16[128,288]{1,0:T(8,128)(2,1)S(1)} %copy-done.4, f32[2,9,512]{2,1,0:T(8,128)S(1)} %copy-done.6, f32[2,4,128]{2,1,0:T(4,128)S(1)} %copy-done.8, ...), custom_call_target="tpu_custom_call" | custom-call | flops 671088640 | bytes 1310720 | tf_op jit(solution)/shard_map/pallas_call | solution.py:299
  27.7 0.0 copy-start
  27.7 0.0 copy-start.1
  27.7 8.6 %all_to_all.10.conv_ref = bf16[8,16,512]{2,1,0:T(8,128)(2,1)S(1)} all-to-all(bf16[8,16,512]{2,1,0:T(8,128)(2,1)S(1)} %bitcast.3), channel_id=1, replica_groups={{20,4,12,24,8,16,0,28},{21,5,13,25,9,17,1,29},{22,6,14,26,10,18,2,30},{..., dimensions={0} | all-to-all | bytes 262144 | tf_op jit(solution)/shard_map/all_to_all | solution.py:310
  36.3 0.8 %shard_map.121 = bf16[512,128]{1,0:T(8,128)(2,1)} custom-call(bf16[8,16,512]{2,1,0:T(8,128)(2,1)S(1)} %all_to_all.10.conv_ref, bf16[128,512]{1,0:T(8,128)(2,1)S(1)} %copy-done.1, f32[1,512]{1,0:T(1,128)S(1)} %shard_map.119.scale_ref, bf16[512,128]{1,0:T(8,128)(2,1)S(1)} %copy-done), custom_call_target="tpu_custom_call" | custom-call | flops 655360 | bytes 524288 | tf_op jit(solution)/shard_map/pallas_call | solution.py:299
  (8 shorter events, 0.0 us)
Async XLA Ops:
  2.3 8.7 %copy-start.2 = (f32[1,512]{1,0:T(1,128)S(1)}, f32[1,512]{1,0:T(1,128)}, u32[]{:S(2)}) copy-start(f32[1,512]{1,0:T(1,128)} %get-tuple-element.9.refs_0_) | copy-start | bytes 6148
  2.3 24.2 %copy-start.3 = (bf16[2,256,256]{2,1,0:T(8,128)(2,1)S(1)}, bf16[2,256,256]{2,1,0:T(8,128)(2,1)}, u32[]{:S(2)}) copy-start(bf16[2,256,256]{2,1,0:T(8,128)(2,1)} %constant.16.clone.dft_ref) | copy-start | bytes 786436
  2.3 24.2 %copy-start.4 = (bf16[128,288]{1,0:T(8,128)(2,1)S(1)}, bf16[128,288]{1,0:T(8,128)(2,1)}, u32[]{:S(2)}) copy-start(bf16[128,288]{1,0:T(8,128)(2,1)} %constant.13.clone.last_ref) | copy-start | bytes 221188
  2.3 24.2 %copy-start.5 = (bf16[288,128]{1,0:T(8,128)(2,1)S(1)}, bf16[288,128]{1,0:T(8,128)(2,1)}, u32[]{:S(2)}) copy-start(bf16[288,128]{1,0:T(8,128)(2,1)} %constant.12.clone.first_ref) | copy-start | bytes 221188
  2.3 24.2 %copy-start.6 = (f32[2,9,512]{2,1,0:T(8,128)S(1)}, f32[2,9,512]{2,1,0:T(8,128)}, u32[]{:S(2)}) copy-start(f32[2,9,512]{2,1,0:T(8,128)} %constant.14.clone.twist_ref) | copy-start | bytes 110596
  2.4 24.2 %copy-start.7 = (bf16[128,128]{1,0:T(8,128)(2,1)S(1)}, bf16[128,128]{1,0:T(8,128)(2,1)}, u32[]{:S(2)}) copy-start(bf16[128,128]{1,0:T(8,128)(2,1)} %constant.17.clone.reverse_ref) | copy-start | bytes 98308
  2.4 24.2 %all-to-all-start = ((bf16[8,5,16,512]{3,2,1,0:T(8,128)(2,1)}), bf16[8,5,16,512]{3,2,1,0:T(8,128)(2,1)S(1)}, u32[]{:S(2)}, u32[]{:S(2)}) async-start(bf16[8,5,16,512]{3,2,1,0:T(8,128)(2,1)} %get-tuple-element.8), calls=%async_computation | async-start | bytes 1310720 | tf_op jit(solution)/shard_map/all_to_all | solution.py:310
  11.0 3.0 %collective-permute-start.2 = (f32[1,512]{1,0:T(1,128)S(1)}, f32[1,512]{1,0:T(1,128)S(1)}, u32[]{:S(2)}, u32[]{:S(2)}) collective-permute-start(f32[1,512]{1,0:T(1,128)S(1)} %copy-done.2), channel_id=1, source_target_pairs={{0,3},{1,2},{2,1},{3,0},{4,7},{5,6},{6,5},{7,4},{8,11},{9,10},{10,... | collective-permute-start | bytes 6152 | tf_op jit(solution)/shard_map/ppermute | solution.py:314
  11.6 3.6 %collective-permute-start.1 = (f32[1,512]{1,0:T(1,128)S(1)}, f32[1,512]{1,0:T(1,128)S(1)}, u32[]{:S(2)}, u32[]{:S(2)}) collective-permute-start(f32[1,512]{1,0:T(1,128)S(1)} %copy-done.2), channel_id=1, source_target_pairs={{0,2},{1,3},{2,0},{3,1},{4,6},{5,7},{6,4},{7,5},{8,10},{9,11},{10,... | collective-permute-start | bytes 6152 | tf_op jit(solution)/shard_map/ppermute | solution.py:314
  12.6 2.7 %collective-permute-start = (f32[1,512]{1,0:T(1,128)S(1)}, f32[1,512]{1,0:T(1,128)S(1)}, u32[]{:S(2)}, u32[]{:S(2)}) collective-permute-start(f32[1,512]{1,0:T(1,128)S(1)} %copy-done.2), channel_id=1, source_target_pairs={{0,1},{1,0},{2,3},{3,2},{4,5},{5,4},{6,7},{7,6},{8,9},{9,8},{10,11... | collective-permute-start | bytes 6152 | tf_op jit(solution)/shard_map/ppermute | solution.py:314
  15.2 11.4 %copy-start.8 = (f32[2,4,128]{2,1,0:T(4,128)S(1)}, f32[2,4,128]{2,1,0:T(4,128)}, u32[]{:S(2)}) copy-start(f32[2,4,128]{2,1,0:T(4,128)} %constant.15.clone.spin_ref) | copy-start | bytes 12292
  15.3 3.7 %collective-permute-start.3 = (f32[1,512]{1,0:T(1,128)S(1)}, f32[1,512]{1,0:T(1,128)S(1)}, u32[]{:S(2)}, u32[]{:S(2)}) collective-permute-start(f32[1,512]{1,0:T(1,128)S(1)} %shard_map.119.scale_ref), channel_id=1, source_target_pairs={{0,4},{4,0},{8,12},{12,8},{16,20},{20,16},{24,28},{28,24},{1,5},{5... | collective-permute-start | bytes 6152 | tf_op jit(solution)/shard_map/ppermute | solution.py:314
  18.9 5.6 %collective-permute-start.6 = (f32[2,512]{1,0:T(2,128)S(1)}, f32[2,512]{1,0:T(2,128)S(1)}, u32[]{:S(2)}, u32[]{:S(2)}) collective-permute-start(f32[2,512]{1,0:T(2,128)S(1)} %pad_maximum_fusion.refs_0_), channel_id=1, source_target_pairs={{0,24},{4,28},{8,16},{12,20},{16,8},{20,12},{24,0},{28,4},{1,25},{... | collective-permute-start | bytes 12296 | tf_op jit(solution)/shard_map/ppermute | solution.py:314
  20.4 6.1 %collective-permute-start.5 = (f32[2,512]{1,0:T(2,128)S(1)}, f32[2,512]{1,0:T(2,128)S(1)}, u32[]{:S(2)}, u32[]{:S(2)}) collective-permute-start(f32[2,512]{1,0:T(2,128)S(1)} %pad_maximum_fusion.refs_0_), channel_id=1, source_target_pairs={{0,16},{4,20},{8,24},{12,28},{16,0},{20,4},{24,8},{28,12},{1,17},{... | collective-permute-start | bytes 12296 | tf_op jit(solution)/shard_map/ppermute | solution.py:314
  21.0 5.6 %collective-permute-start.4 = (f32[2,512]{1,0:T(2,128)S(1)}, f32[2,512]{1,0:T(2,128)S(1)}, u32[]{:S(2)}, u32[]{:S(2)}) collective-permute-start(f32[2,512]{1,0:T(2,128)S(1)} %pad_maximum_fusion.refs_0_), channel_id=1, source_target_pairs={{0,8},{4,12},{8,0},{12,4},{16,24},{20,28},{24,16},{28,20},{1,9},{5... | collective-permute-start | bytes 12296 | tf_op jit(solution)/shard_map/ppermute | solution.py:314
  27.7 8.6 %copy-start = (bf16[512,128]{1,0:T(8,128)(2,1)S(1)}, bf16[512,128]{1,0:T(8,128)(2,1)}, u32[]{:S(2)}) copy-start(bf16[512,128]{1,0:T(8,128)(2,1)} %post_ref.1) | copy-start | bytes 393220
  27.7 8.6 %copy-start.1 = (bf16[128,512]{1,0:T(8,128)(2,1)S(1)}, bf16[128,512]{1,0:T(8,128)(2,1)}, u32[]{:S(2)}) copy-start(bf16[128,512]{1,0:T(8,128)(2,1)} %get-tuple-element.10.skipped_ref) | copy-start | bytes 393220

commit v5 on v4

--- a/solution.py
+++ b/solution.py
@@ -16,7 +16,7 @@
 
 
 def order_of(places):
-    return (5, 1, 3, 6, 2, 4, 0, 7) if places == 8 else tuple(range(places))
+    return (5, 2, 1, 7, 4, 3, 0, 6) if places == 8 else tuple(range(places))
 
 
 def reverse_bits(index, levels):

time: 37.4 us -> 37.4 us (level)
  no operation moved by 1% of the time
where the time goes in v5:
time: 37.4 us; the launch traced here: 37.1 us
  starting transfers between devices  15.5 us (41%)
  waiting for transfers between devices  8.65 us (23%)
  blocking collectives  8.58 us (23%)
  Pallas kernels  4.18 us (11%)
    ppermute x7, waiting for transfers between devices, swap(): lax.ppermute(value, axis, [(place, place ^ apart) for place in range(lax....  8.65 us
    all_to_all x1, starting transfers between devices, exchange(): lax.all_to_all(value, 'seq', split_axis=0, concat_axis=0, tiled=True, axi...  8.61 us
    all_to_all x1, blocking collectives, exchange(): lax.all_to_all(value, 'seq', split_axis=0, concat_axis=0, tiled=True, axi...  8.58 us
    ppermute x7, starting transfers between devices, swap(): lax.ppermute(value, axis, [(place, place ^ apart) for place in range(lax....  6.92 us
    pallas_call x4, Pallas kernels, call(): pl.pallas_call(kernel, out_shape=out_shape, compiler_params=pltpu.Compile...  4.18 us
  transfers between devices with their start and end apart: 8, of which 5 were waited for; matrix products, arithmetic and copies ran while one was open for 0% of the time, Pallas kernels for 0%

profile of v5, /device:TPU:0, one launch (start us, length us, event | category | flops | bytes accessed | tf_op | source)
XLA Modules:
  0.0 37.1 jit_solution(1846239329998791922)
XLA Ops:
  0.0 2.3 %shard_map.118 = (f32[1,512]{1,0:T(1,128)}, bf16[128,512]{1,0:T(8,128)(2,1)}, bf16[8,5,16,512]{3,2,1,0:T(8,128)(2,1)}) custom-call(bf16[512,128]{1,0:T(8,128)(2,1)} %features_ref.1, bf16[512,128]{1,0:T(8,128)(2,1)} %pre_ref.1, f32[1,128]{1,0:T(1,128)} %bitcast.4, f32[1,128]{1,0:T(1,128)} %bitcast.5, f32[2,2,512,128]{3,2,1,0:T(8,128)} %spectrum_ref.1), custom_call_target="tpu_custom_call" | custom-call | flops 655360 | bytes 2097152 | tf_op jit(solution)/shard_map/pallas_call | solution.py:299
  2.3 0.0 copy-start.3
  2.3 0.0 copy-start.4
  2.3 0.0 copy-start.5
  2.3 0.0 copy-start.6
  2.4 0.0 copy-start.7
  2.4 8.6 %all-to-all-start = ((bf16[8,5,16,512]{3,2,1,0:T(8,128)(2,1)}), bf16[8,5,16,512]{3,2,1,0:T(8,128)(2,1)S(1)}, u32[]{:S(2)}, u32[]{:S(2)}) async-start(bf16[8,5,16,512]{3,2,1,0:T(8,128)(2,1)} %get-tuple-element.8), calls=%async_computation | async-start | bytes 1310720 | tf_op jit(solution)/shard_map/all_to_all | solution.py:310
  11.0 0.7 %collective-permute-start.2 = (f32[1,512]{1,0:T(1,128)S(1)}, f32[1,512]{1,0:T(1,128)S(1)}, u32[]{:S(2)}, u32[]{:S(2)}) collective-permute-start(f32[1,512]{1,0:T(1,128)S(1)} %copy-done.2), channel_id=1, source_target_pairs={{0,3},{1,2},{2,1},{3,0},{4,7},{5,6},{6,5},{7,4},{8,11},{9,10},{10,... | collective-permute-start | bytes 6152 | tf_op jit(solution)/shard_map/ppermute | solution.py:314
  11.6 0.9 %collective-permute-start.1 = (f32[1,512]{1,0:T(1,128)S(1)}, f32[1,512]{1,0:T(1,128)S(1)}, u32[]{:S(2)}, u32[]{:S(2)}) collective-permute-start(f32[1,512]{1,0:T(1,128)S(1)} %copy-done.2), channel_id=1, source_target_pairs={{0,2},{1,3},{2,0},{3,1},{4,6},{5,7},{6,4},{7,5},{8,10},{9,11},{10,... | collective-permute-start | bytes 6152 | tf_op jit(solution)/shard_map/ppermute | solution.py:314
  12.6 0.3 collective-permute-start
  12.9 1.1 %collective-permute-done.2.refs_3_ = f32[1,512]{1,0:T(1,128)S(1)} collective-permute-done((f32[1,512]{1,0:T(1,128)S(1)}, f32[1,512]{1,0:T(1,128)S(1)}, u32[]{:S(2)}, u32[]{:S(2)}) %collective-permute-start.2) | collective-permute-done | bytes 2080 | tf_op jit(solution)/shard_map/ppermute | solution.py:314
  14.0 1.2 %collective-permute-done.1.refs_2_ = f32[1,512]{1,0:T(1,128)S(1)} collective-permute-done((f32[1,512]{1,0:T(1,128)S(1)}, f32[1,512]{1,0:T(1,128)S(1)}, u32[]{:S(2)}, u32[]{:S(2)}) %collective-permute-start.1) | collective-permute-done | bytes 2080 | tf_op jit(solution)/shard_map/ppermute | solution.py:314
  15.2 0.0 collective-permute-done.refs_1_
  15.2 0.0 copy-start.8
  15.3 0.6 %collective-permute-start.3 = (f32[1,512]{1,0:T(1,128)S(1)}, f32[1,512]{1,0:T(1,128)S(1)}, u32[]{:S(2)}, u32[]{:S(2)}) collective-permute-start(f32[1,512]{1,0:T(1,128)S(1)} %shard_map.119.scale_ref), channel_id=1, source_target_pairs={{0,4},{4,0},{8,12},{12,8},{16,20},{20,16},{24,28},{28,24},{1,5},{5... | collective-permute-start | bytes 6152 | tf_op jit(solution)/shard_map/ppermute | solution.py:314
  15.9 3.3 %collective-permute-done.3 = f32[1,512]{1,0:T(1,128)S(1)} collective-permute-done((f32[1,512]{1,0:T(1,128)S(1)}, f32[1,512]{1,0:T(1,128)S(1)}, u32[]{:S(2)}, u32[]{:S(2)}) %collective-permute-start.3) | collective-permute-done | bytes 2080 | tf_op jit(solution)/shard_map/ppermute | solution.py:314
  19.1 1.3 %collective-permute-start.6 = (f32[2,512]{1,0:T(2,128)S(1)}, f32[2,512]{1,0:T(2,128)S(1)}, u32[]{:S(2)}, u32[]{:S(2)}) collective-permute-start(f32[2,512]{1,0:T(2,128)S(1)} %pad_maximum_fusion.refs_0_), channel_id=1, source_target_pairs={{0,24},{4,28},{8,16},{12,20},{16,8},{20,12},{24,0},{28,4},{1,25},{... | collective-permute-start | bytes 12296 | tf_op jit(solution)/shard_map/ppermute | solution.py:314
  20.5 0.5 %collective-permute-start.5 = (f32[2,512]{1,0:T(2,128)S(1)}, f32[2,512]{1,0:T(2,128)S(1)}, u32[]{:S(2)}, u32[]{:S(2)}) collective-permute-start(f32[2,512]{1,0:T(2,128)S(1)} %pad_maximum_fusion.refs_0_), channel_id=1, source_target_pairs={{0,16},{4,20},{8,24},{12,28},{16,0},{20,4},{24,8},{28,12},{1,17},{... | collective-permute-start | bytes 12296 | tf_op jit(solution)/shard_map/ppermute | solution.py:314
  21.0 2.6 %collective-permute-start.4 = (f32[2,512]{1,0:T(2,128)S(1)}, f32[2,512]{1,0:T(2,128)S(1)}, u32[]{:S(2)}, u32[]{:S(2)}) collective-permute-start(f32[2,512]{1,0:T(2,128)S(1)} %pad_maximum_fusion.refs_0_), channel_id=1, source_target_pairs={{0,8},{4,12},{8,0},{12,4},{16,24},{20,28},{24,16},{28,20},{1,9},{5... | collective-permute-start | bytes 12296 | tf_op jit(solution)/shard_map/ppermute | solution.py:314
  23.6 1.1 %collective-permute-done.6.refs_3_ = f32[2,512]{1,0:T(2,128)S(1)} collective-permute-done((f32[2,512]{1,0:T(2,128)S(1)}, f32[2,512]{1,0:T(2,128)S(1)}, u32[]{:S(2)}, u32[]{:S(2)}) %collective-permute-start.6) | collective-permute-done | bytes 4128 | tf_op jit(solution)/shard_map/ppermute | solution.py:314
  24.7 1.9 %collective-permute-done.5.refs_2_ = f32[2,512]{1,0:T(2,128)S(1)} collective-permute-done((f32[2,512]{1,0:T(2,128)S(1)}, f32[2,512]{1,0:T(2,128)S(1)}, u32[]{:S(2)}, u32[]{:S(2)}) %collective-permute-start.5) | collective-permute-done | bytes 4128 | tf_op jit(solution)/shard_map/ppermute | solution.py:314
  26.6 0.0 collective-permute-done.4.refs_1_
  26.6 0.0 all-to-all-done.packed_ref
  26.6 0.0 copy-done.4
  26.6 0.0 copy-done.5
  26.6 0.0 copy-done.6
  26.6 0.0 copy-done.7
  26.6 1.1 %shard_map.120 = bf16[128,512]{1,0:T(8,128)(2,1)S(1)} custom-call(bf16[8,5,16,512]{3,2,1,0:T(8,128)(2,1)S(1)} %all-to-all-done.packed_ref, bf16[288,128]{1,0:T(8,128)(2,1)S(1)} %copy-done.5, bf16[128,288]{1,0:T(8,128)(2,1)S(1)} %copy-done.4, f32[2,9,512]{2,1,0:T(8,128)S(1)} %copy-done.6, f32[2,4,128]{2,1,0:T(4,128)S(1)} %copy-done.8, ...), custom_call_target="tpu_custom_call" | custom-call | flops 671088640 | bytes 1310720 | tf_op jit(solution)/shard_map/pallas_call | solution.py:299
  27.7 0.0 copy-start
  27.8 0.0 copy-start.1
  27.8 8.6 %all_to_all.10.conv_ref = bf16[8,16,512]{2,1,0:T(8,128)(2,1)S(1)} all-to-all(bf16[8,16,512]{2,1,0:T(8,128)(2,1)S(1)} %bitcast.3), channel_id=1, replica_groups={{20,8,4,28,16,12,0,24},{21,9,5,29,17,13,1,25},{22,10,6,30,18,14,2,26},{..., dimensions={0} | all-to-all | bytes 262144 | tf_op jit(solution)/shard_map/all_to_all | solution.py:310
  36.4 0.8 %shard_map.121 = bf16[512,128]{1,0:T(8,128)(2,1)} custom-call(bf16[8,16,512]{2,1,0:T(8,128)(2,1)S(1)} %all_to_all.10.conv_ref, bf16[128,512]{1,0:T(8,128)(2,1)S(1)} %copy-done.1, f32[1,512]{1,0:T(1,128)S(1)} %shard_map.119.scale_ref, bf16[512,128]{1,0:T(8,128)(2,1)S(1)} %copy-done), custom_call_target="tpu_custom_call" | custom-call | flops 655360 | bytes 524288 | tf_op jit(solution)/shard_map/pallas_call | solution.py:299
  (8 shorter events, 0.0 us)
Async XLA Ops:
  2.3 8.7 %copy-start.2 = (f32[1,512]{1,0:T(1,128)S(1)}, f32[1,512]{1,0:T(1,128)}, u32[]{:S(2)}) copy-start(f32[1,512]{1,0:T(1,128)} %get-tuple-element.9.refs_0_) | copy-start | bytes 6148
  2.3 24.3 %copy-start.3 = (bf16[2,256,256]{2,1,0:T(8,128)(2,1)S(1)}, bf16[2,256,256]{2,1,0:T(8,128)(2,1)}, u32[]{:S(2)}) copy-start(bf16[2,256,256]{2,1,0:T(8,128)(2,1)} %constant.16.clone.dft_ref) | copy-start | bytes 786436
  2.3 24.3 %copy-start.4 = (bf16[128,288]{1,0:T(8,128)(2,1)S(1)}, bf16[128,288]{1,0:T(8,128)(2,1)}, u32[]{:S(2)}) copy-start(bf16[128,288]{1,0:T(8,128)(2,1)} %constant.13.clone.last_ref) | copy-start | bytes 221188
  2.3 24.3 %copy-start.5 = (bf16[288,128]{1,0:T(8,128)(2,1)S(1)}, bf16[288,128]{1,0:T(8,128)(2,1)}, u32[]{:S(2)}) copy-start(bf16[288,128]{1,0:T(8,128)(2,1)} %constant.12.clone.first_ref) | copy-start | bytes 221188
  2.3 24.3 %copy-start.6 = (f32[2,9,512]{2,1,0:T(8,128)S(1)}, f32[2,9,512]{2,1,0:T(8,128)}, u32[]{:S(2)}) copy-start(f32[2,9,512]{2,1,0:T(8,128)} %constant.14.clone.twist_ref) | copy-start | bytes 110596
  2.4 24.3 %copy-start.7 = (bf16[128,128]{1,0:T(8,128)(2,1)S(1)}, bf16[128,128]{1,0:T(8,128)(2,1)}, u32[]{:S(2)}) copy-start(bf16[128,128]{1,0:T(8,128)(2,1)} %constant.17.clone.reverse_ref) | copy-start | bytes 98308
  2.4 24.2 %all-to-all-start = ((bf16[8,5,16,512]{3,2,1,0:T(8,128)(2,1)}), bf16[8,5,16,512]{3,2,1,0:T(8,128)(2,1)S(1)}, u32[]{:S(2)}, u32[]{:S(2)}) async-start(bf16[8,5,16,512]{3,2,1,0:T(8,128)(2,1)} %get-tuple-element.8), calls=%async_computation | async-start | bytes 1310720 | tf_op jit(solution)/shard_map/all_to_all | solution.py:310
  11.0 3.0 %collective-permute-start.2 = (f32[1,512]{1,0:T(1,128)S(1)}, f32[1,512]{1,0:T(1,128)S(1)}, u32[]{:S(2)}, u32[]{:S(2)}) collective-permute-start(f32[1,512]{1,0:T(1,128)S(1)} %copy-done.2), channel_id=1, source_target_pairs={{0,3},{1,2},{2,1},{3,0},{4,7},{5,6},{6,5},{7,4},{8,11},{9,10},{10,... | collective-permute-start | bytes 6152 | tf_op jit(solution)/shard_map/ppermute | solution.py:314
  11.6 3.6 %collective-permute-start.1 = (f32[1,512]{1,0:T(1,128)S(1)}, f32[1,512]{1,0:T(1,128)S(1)}, u32[]{:S(2)}, u32[]{:S(2)}) collective-permute-start(f32[1,512]{1,0:T(1,128)S(1)} %copy-done.2), channel_id=1, source_target_pairs={{0,2},{1,3},{2,0},{3,1},{4,6},{5,7},{6,4},{7,5},{8,10},{9,11},{10,... | collective-permute-start | bytes 6152 | tf_op jit(solution)/shard_map/ppermute | solution.py:314
  12.6 2.7 %collective-permute-start = (f32[1,512]{1,0:T(1,128)S(1)}, f32[1,512]{1,0:T(1,128)S(1)}, u32[]{:S(2)}, u32[]{:S(2)}) collective-permute-start(f32[1,512]{1,0:T(1,128)S(1)} %copy-done.2), channel_id=1, source_target_pairs={{0,1},{1,0},{2,3},{3,2},{4,5},{5,4},{6,7},{7,6},{8,9},{9,8},{10,11... | collective-permute-start | bytes 6152 | tf_op jit(solution)/shard_map/ppermute | solution.py:314
  15.2 11.4 %copy-start.8 = (f32[2,4,128]{2,1,0:T(4,128)S(1)}, f32[2,4,128]{2,1,0:T(4,128)}, u32[]{:S(2)}) copy-start(f32[2,4,128]{2,1,0:T(4,128)} %constant.15.clone.spin_ref) | copy-start | bytes 12292
  15.3 3.9 %collective-permute-start.3 = (f32[1,512]{1,0:T(1,128)S(1)}, f32[1,512]{1,0:T(1,128)S(1)}, u32[]{:S(2)}, u32[]{:S(2)}) collective-permute-start(f32[1,512]{1,0:T(1,128)S(1)} %shard_map.119.scale_ref), channel_id=1, source_target_pairs={{0,4},{4,0},{8,12},{12,8},{16,20},{20,16},{24,28},{28,24},{1,5},{5... | collective-permute-start | bytes 6152 | tf_op jit(solution)/shard_map/ppermute | solution.py:314
  19.1 5.6 %collective-permute-start.6 = (f32[2,512]{1,0:T(2,128)S(1)}, f32[2,512]{1,0:T(2,128)S(1)}, u32[]{:S(2)}, u32[]{:S(2)}) collective-permute-start(f32[2,512]{1,0:T(2,128)S(1)} %pad_maximum_fusion.refs_0_), channel_id=1, source_target_pairs={{0,24},{4,28},{8,16},{12,20},{16,8},{20,12},{24,0},{28,4},{1,25},{... | collective-permute-start | bytes 12296 | tf_op jit(solution)/shard_map/ppermute | solution.py:314
  20.5 6.1 %collective-permute-start.5 = (f32[2,512]{1,0:T(2,128)S(1)}, f32[2,512]{1,0:T(2,128)S(1)}, u32[]{:S(2)}, u32[]{:S(2)}) collective-permute-start(f32[2,512]{1,0:T(2,128)S(1)} %pad_maximum_fusion.refs_0_), channel_id=1, source_target_pairs={{0,16},{4,20},{8,24},{12,28},{16,0},{20,4},{24,8},{28,12},{1,17},{... | collective-permute-start | bytes 12296 | tf_op jit(solution)/shard_map/ppermute | solution.py:314
  21.0 5.6 %collective-permute-start.4 = (f32[2,512]{1,0:T(2,128)S(1)}, f32[2,512]{1,0:T(2,128)S(1)}, u32[]{:S(2)}, u32[]{:S(2)}) collective-permute-start(f32[2,512]{1,0:T(2,128)S(1)} %pad_maximum_fusion.refs_0_), channel_id=1, source_target_pairs={{0,8},{4,12},{8,0},{12,4},{16,24},{20,28},{24,16},{28,20},{1,9},{5... | collective-permute-start | bytes 12296 | tf_op jit(solution)/shard_map/ppermute | solution.py:314
  27.7 8.6 %copy-start = (bf16[512,128]{1,0:T(8,128)(2,1)S(1)}, bf16[512,128]{1,0:T(8,128)(2,1)}, u32[]{:S(2)}) copy-start(bf16[512,128]{1,0:T(8,128)(2,1)} %post_ref.1) | copy-start | bytes 393220
  27.8 8.6 %copy-start.1 = (bf16[128,512]{1,0:T(8,128)(2,1)S(1)}, bf16[128,512]{1,0:T(8,128)(2,1)}, u32[]{:S(2)}) copy-start(bf16[128,512]{1,0:T(8,128)(2,1)} %get-tuple-element.10.skipped_ref) | copy-start | bytes 393220

commit v6 on v5

--- a/solution.py
+++ b/solution.py
@@ -15,8 +15,10 @@
 WHOLE_VMEM = 63 * 1024 * 1024 + 512 * 1024
 
 
-def order_of(places):
-    return (5, 2, 1, 7, 4, 3, 0, 6) if places == 8 else tuple(range(places))
+def order_of(places, back=False):
+    if places != 8:
+        return tuple(range(places))
+    return (2, 1, 7, 4, 3, 0, 6, 5) if back else (5, 2, 1, 7, 4, 3, 0, 6)
 
 
 def reverse_bits(index, levels):
@@ -251,7 +253,7 @@
                 both[pl.ds(2 * residue * width, width), lanes] = (real * cos - imag * sin).astype(BF16)
                 both[pl.ds((2 * residue + 1) * width, width), lanes] = (imag * cos + real * sin).astype(BF16)
     result = matmul(last_ref[...], both[...]).astype(BF16)
-    for rank, at in enumerate(order):
+    for rank, at in enumerate(order_of(places, back=True)):
         out_ref[pl.ds(rank * width, width), :] = result[at * width : (at + 1) * width]
 
 
@@ -289,7 +291,7 @@
 def finish_kernel(conv_ref, skipped_ref, scale_ref, post_ref, out_ref):
     conv = conv_ref[...]
     if len(conv_ref.shape) == 3:
-        order = order_of(conv_ref.shape[0])
+        order = order_of(conv_ref.shape[0], back=True)
         conv = jnp.concatenate([conv_ref[order.index(place)] for place in range(len(order))])
     turned = conv.astype(F32) + skipped_ref[...].astype(F32) * scale_ref[...]
     out_ref[...] = (post_ref[...].astype(F32) * turned.T).astype(BF16)
@@ -305,8 +307,8 @@
     )(*operands)
 
 
-def exchange(value):
-    ranks = [list(order_of(lax.axis_size("seq")))]
+def exchange(value, back=False):
+    ranks = [list(order_of(lax.axis_size("seq"), back))]
     return lax.all_to_all(value, "seq", split_axis=0, concat_axis=0, tiled=True, axis_index_groups=ranks)
 
 
@@ -391,7 +393,7 @@
         *scales,
         scratch_shapes=scratch,
     )
-    conv = exchange(conv.reshape(places, width, rows))
+    conv = exchange(conv.reshape(places, width, rows), back=True)
     if not piled:
         conv = conv.reshape(wide, rows)
     return call(finish_kernel, shape((rows, wide), BF16), 10 * cells, 8 * cells, conv, skipped, scale, post_gate)

time: 37.4 us -> 39 us (1.043)
  blocking collectives: 8.58 us -> 10.2 us
    all_to_all x1, blocking collectives: 8.58 us -> 10.2 us  [exchange(): lax.all_to_all(value, 'seq', split_axis=0, concat_axis=0, tiled=True, axi...]
where the time goes in v6:
time: 39 us; the launch traced here: 38.8 us
  starting transfers between devices  15.5 us (40%)
  blocking collectives  10.2 us (26%)
  waiting for transfers between devices  8.65 us (22%)
  Pallas kernels  4.18 us (11%)
    all_to_all x1, blocking collectives, exchange(): lax.all_to_all(value, 'seq', split_axis=0, concat_axis=0, tiled=True, axi...  10.2 us
    ppermute x7, waiting for transfers between devices, swap(): lax.ppermute(value, axis, [(place, place ^ apart) for place in range(lax....  8.65 us
    all_to_all x1, starting transfers between devices, exchange(): lax.all_to_all(value, 'seq', split_axis=0, concat_axis=0, tiled=True, axi...  8.61 us
    ppermute x7, starting transfers between devices, swap(): lax.ppermute(value, axis, [(place, place ^ apart) for place in range(lax....  6.92 us
    pallas_call x4, Pallas kernels, call(): pl.pallas_call(kernel, out_shape=out_shape, compiler_params=pltpu.Compile...  4.18 us
  transfers between devices with their start and end apart: 8, of which 5 were waited for; matrix products, arithmetic and copies ran while one was open for 0% of the time, Pallas kernels for 0%

profile of v6, /device:TPU:0, one launch (start us, length us, event | category | flops | bytes accessed | tf_op | source)
XLA Modules:
  0.0 38.8 jit_solution(15306596824953639156)
XLA Ops:
  0.0 2.3 %shard_map.118 = (f32[1,512]{1,0:T(1,128)}, bf16[128,512]{1,0:T(8,128)(2,1)}, bf16[8,5,16,512]{3,2,1,0:T(8,128)(2,1)}) custom-call(bf16[512,128]{1,0:T(8,128)(2,1)} %features_ref.1, bf16[512,128]{1,0:T(8,128)(2,1)} %pre_ref.1, f32[1,128]{1,0:T(1,128)} %bitcast.4, f32[1,128]{1,0:T(1,128)} %bitcast.5, f32[2,2,512,128]{3,2,1,0:T(8,128)} %spectrum_ref.1), custom_call_target="tpu_custom_call" | custom-call | flops 655360 | bytes 2097152 | tf_op jit(solution)/shard_map/pallas_call | solution.py:301
  2.3 0.0 copy-start.2
  2.3 0.0 copy-start.3
  2.3 0.0 copy-start.4
  2.3 0.0 copy-start.5
  2.3 0.0 copy-start.6
  2.4 0.0 copy-start.7
  2.4 8.6 %all-to-all-start = ((bf16[8,5,16,512]{3,2,1,0:T(8,128)(2,1)}), bf16[8,5,16,512]{3,2,1,0:T(8,128)(2,1)S(1)}, u32[]{:S(2)}, u32[]{:S(2)}) async-start(bf16[8,5,16,512]{3,2,1,0:T(8,128)(2,1)} %get-tuple-element.8), calls=%async_computation | async-start | bytes 1310720 | tf_op jit(solution)/shard_map/all_to_all | solution.py:312
  11.0 0.0 copy-done.2
  11.0 0.7 %collective-permute-start.2 = (f32[1,512]{1,0:T(1,128)S(1)}, f32[1,512]{1,0:T(1,128)S(1)}, u32[]{:S(2)}, u32[]{:S(2)}) collective-permute-start(f32[1,512]{1,0:T(1,128)S(1)} %copy-done.2), channel_id=1, source_target_pairs={{0,3},{1,2},{2,1},{3,0},{4,7},{5,6},{6,5},{7,4},{8,11},{9,10},{10,... | collective-permute-start | bytes 6152 | tf_op jit(solution)/shard_map/ppermute | solution.py:316
  11.6 0.9 %collective-permute-start.1 = (f32[1,512]{1,0:T(1,128)S(1)}, f32[1,512]{1,0:T(1,128)S(1)}, u32[]{:S(2)}, u32[]{:S(2)}) collective-permute-start(f32[1,512]{1,0:T(1,128)S(1)} %copy-done.2), channel_id=1, source_target_pairs={{0,2},{1,3},{2,0},{3,1},{4,6},{5,7},{6,4},{7,5},{8,10},{9,11},{10,... | collective-permute-start | bytes 6152 | tf_op jit(solution)/shard_map/ppermute | solution.py:316
  12.6 0.3 collective-permute-start
  12.9 1.1 %collective-permute-done.2.refs_3_ = f32[1,512]{1,0:T(1,128)S(1)} collective-permute-done((f32[1,512]{1,0:T(1,128)S(1)}, f32[1,512]{1,0:T(1,128)S(1)}, u32[]{:S(2)}, u32[]{:S(2)}) %collective-permute-start.2) | collective-permute-done | bytes 2080 | tf_op jit(solution)/shard_map/ppermute | solution.py:316
  14.0 1.2 %collective-permute-done.1.refs_2_ = f32[1,512]{1,0:T(1,128)S(1)} collective-permute-done((f32[1,512]{1,0:T(1,128)S(1)}, f32[1,512]{1,0:T(1,128)S(1)}, u32[]{:S(2)}, u32[]{:S(2)}) %collective-permute-start.1) | collective-permute-done | bytes 2080 | tf_op jit(solution)/shard_map/ppermute | solution.py:316
  15.2 0.0 collective-permute-done.refs_1_
  15.2 0.0 copy-start.8
  15.3 0.6 %collective-permute-start.3 = (f32[1,512]{1,0:T(1,128)S(1)}, f32[1,512]{1,0:T(1,128)S(1)}, u32[]{:S(2)}, u32[]{:S(2)}) collective-permute-start(f32[1,512]{1,0:T(1,128)S(1)} %shard_map.119.scale_ref), channel_id=1, source_target_pairs={{0,4},{4,0},{8,12},{12,8},{16,20},{20,16},{24,28},{28,24},{1,5},{5... | collective-permute-start | bytes 6152 | tf_op jit(solution)/shard_map/ppermute | solution.py:316
  15.9 3.3 %collective-permute-done.3 = f32[1,512]{1,0:T(1,128)S(1)} collective-permute-done((f32[1,512]{1,0:T(1,128)S(1)}, f32[1,512]{1,0:T(1,128)S(1)}, u32[]{:S(2)}, u32[]{:S(2)}) %collective-permute-start.3) | collective-permute-done | bytes 2080 | tf_op jit(solution)/shard_map/ppermute | solution.py:316
  19.1 1.3 %collective-permute-start.6 = (f32[2,512]{1,0:T(2,128)S(1)}, f32[2,512]{1,0:T(2,128)S(1)}, u32[]{:S(2)}, u32[]{:S(2)}) collective-permute-start(f32[2,512]{1,0:T(2,128)S(1)} %pad_maximum_fusion.refs_0_), channel_id=1, source_target_pairs={{0,24},{4,28},{8,16},{12,20},{16,8},{20,12},{24,0},{28,4},{1,25},{... | collective-permute-start | bytes 12296 | tf_op jit(solution)/shard_map/ppermute | solution.py:316
  20.5 0.5 %collective-permute-start.5 = (f32[2,512]{1,0:T(2,128)S(1)}, f32[2,512]{1,0:T(2,128)S(1)}, u32[]{:S(2)}, u32[]{:S(2)}) collective-permute-start(f32[2,512]{1,0:T(2,128)S(1)} %pad_maximum_fusion.refs_0_), channel_id=1, source_target_pairs={{0,16},{4,20},{8,24},{12,28},{16,0},{20,4},{24,8},{28,12},{1,17},{... | collective-permute-start | bytes 12296 | tf_op jit(solution)/shard_map/ppermute | solution.py:316
  21.0 2.6 %collective-permute-start.4 = (f32[2,512]{1,0:T(2,128)S(1)}, f32[2,512]{1,0:T(2,128)S(1)}, u32[]{:S(2)}, u32[]{:S(2)}) collective-permute-start(f32[2,512]{1,0:T(2,128)S(1)} %pad_maximum_fusion.refs_0_), channel_id=1, source_target_pairs={{0,8},{4,12},{8,0},{12,4},{16,24},{20,28},{24,16},{28,20},{1,9},{5... | collective-permute-start | bytes 12296 | tf_op jit(solution)/shard_map/ppermute | solution.py:316
  23.6 1.1 %collective-permute-done.6.refs_3_ = f32[2,512]{1,0:T(2,128)S(1)} collective-permute-done((f32[2,512]{1,0:T(2,128)S(1)}, f32[2,512]{1,0:T(2,128)S(1)}, u32[]{:S(2)}, u32[]{:S(2)}) %collective-permute-start.6) | collective-permute-done | bytes 4128 | tf_op jit(solution)/shard_map/ppermute | solution.py:316
  24.7 1.9 %collective-permute-done.5.refs_2_ = f32[2,512]{1,0:T(2,128)S(1)} collective-permute-done((f32[2,512]{1,0:T(2,128)S(1)}, f32[2,512]{1,0:T(2,128)S(1)}, u32[]{:S(2)}, u32[]{:S(2)}) %collective-permute-start.5) | collective-permute-done | bytes 4128 | tf_op jit(solution)/shard_map/ppermute | solution.py:316
  26.6 0.0 collective-permute-done.4.refs_1_
  26.6 0.0 all-to-all-done.packed_ref
  26.6 0.0 copy-done.3
  26.6 1.1 %shard_map.120 = bf16[128,512]{1,0:T(8,128)(2,1)S(1)} custom-call(bf16[8,5,16,512]{3,2,1,0:T(8,128)(2,1)S(1)} %all-to-all-done.packed_ref, bf16[288,128]{1,0:T(8,128)(2,1)S(1)} %copy-done.5, bf16[128,288]{1,0:T(8,128)(2,1)S(1)} %copy-done.4, f32[2,9,512]{2,1,0:T(8,128)S(1)} %copy-done.6, f32[2,4,128]{2,1,0:T(4,128)S(1)} %copy-done.8, ...), custom_call_target="tpu_custom_call" | custom-call | flops 671088640 | bytes 1310720 | tf_op jit(solution)/shard_map/pallas_call | solution.py:301
  27.7 0.0 copy-start
  27.8 0.0 copy-start.1
  27.8 10.2 %all_to_all.10.conv_ref = bf16[8,16,512]{2,1,0:T(8,128)(2,1)S(1)} all-to-all(bf16[8,16,512]{2,1,0:T(8,128)(2,1)S(1)} %bitcast.3), channel_id=1, replica_groups={{8,4,28,16,12,0,24,20},{9,5,29,17,13,1,25,21},{10,6,30,18,14,2,26,22},{..., dimensions={0} | all-to-all | bytes 262144 | tf_op jit(solution)/shard_map/all_to_all | solution.py:312
  38.0 0.0 copy-done.1
  38.0 0.8 %shard_map.121 = bf16[512,128]{1,0:T(8,128)(2,1)} custom-call(bf16[8,16,512]{2,1,0:T(8,128)(2,1)S(1)} %all_to_all.10.conv_ref, bf16[128,512]{1,0:T(8,128)(2,1)S(1)} %copy-done.1, f32[1,512]{1,0:T(1,128)S(1)} %shard_map.119.scale_ref, bf16[512,128]{1,0:T(8,128)(2,1)S(1)} %copy-done), custom_call_target="tpu_custom_call" | custom-call | flops 655360 | bytes 524288 | tf_op jit(solution)/shard_map/pallas_call | solution.py:301
  (8 shorter events, 0.0 us)
Async XLA Ops:
  2.3 8.7 %copy-start.2 = (f32[1,512]{1,0:T(1,128)S(1)}, f32[1,512]{1,0:T(1,128)}, u32[]{:S(2)}) copy-start(f32[1,512]{1,0:T(1,128)} %get-tuple-element.9.refs_0_) | copy-start | bytes 6148
  2.3 24.3 %copy-start.3 = (bf16[2,256,256]{2,1,0:T(8,128)(2,1)S(1)}, bf16[2,256,256]{2,1,0:T(8,128)(2,1)}, u32[]{:S(2)}) copy-start(bf16[2,256,256]{2,1,0:T(8,128)(2,1)} %constant.16.clone.dft_ref) | copy-start | bytes 786436
  2.3 24.3 %copy-start.4 = (bf16[128,288]{1,0:T(8,128)(2,1)S(1)}, bf16[128,288]{1,0:T(8,128)(2,1)}, u32[]{:S(2)}) copy-start(bf16[128,288]{1,0:T(8,128)(2,1)} %constant.13.clone.last_ref) | copy-start | bytes 221188
  2.3 24.3 %copy-start.5 = (bf16[288,128]{1,0:T(8,128)(2,1)S(1)}, bf16[288,128]{1,0:T(8,128)(2,1)}, u32[]{:S(2)}) copy-start(bf16[288,128]{1,0:T(8,128)(2,1)} %constant.12.clone.first_ref) | copy-start | bytes 221188
  2.3 24.3 %copy-start.6 = (f32[2,9,512]{2,1,0:T(8,128)S(1)}, f32[2,9,512]{2,1,0:T(8,128)}, u32[]{:S(2)}) copy-start(f32[2,9,512]{2,1,0:T(8,128)} %constant.14.clone.twist_ref) | copy-start | bytes 110596
  2.4 24.3 %copy-start.7 = (bf16[128,128]{1,0:T(8,128)(2,1)S(1)}, bf16[128,128]{1,0:T(8,128)(2,1)}, u32[]{:S(2)}) copy-start(bf16[128,128]{1,0:T(8,128)(2,1)} %constant.17.clone.reverse_ref) | copy-start | bytes 98308
  2.4 24.2 %all-to-all-start = ((bf16[8,5,16,512]{3,2,1,0:T(8,128)(2,1)}), bf16[8,5,16,512]{3,2,1,0:T(8,128)(2,1)S(1)}, u32[]{:S(2)}, u32[]{:S(2)}) async-start(bf16[8,5,16,512]{3,2,1,0:T(8,128)(2,1)} %get-tuple-element.8), calls=%async_computation | async-start | bytes 1310720 | tf_op jit(solution)/shard_map/all_to_all | solution.py:312
  11.0 3.0 %collective-permute-start.2 = (f32[1,512]{1,0:T(1,128)S(1)}, f32[1,512]{1,0:T(1,128)S(1)}, u32[]{:S(2)}, u32[]{:S(2)}) collective-permute-start(f32[1,512]{1,0:T(1,128)S(1)} %copy-done.2), channel_id=1, source_target_pairs={{0,3},{1,2},{2,1},{3,0},{4,7},{5,6},{6,5},{7,4},{8,11},{9,10},{10,... | collective-permute-start | bytes 6152 | tf_op jit(solution)/shard_map/ppermute | solution.py:316
  11.6 3.6 %collective-permute-start.1 = (f32[1,512]{1,0:T(1,128)S(1)}, f32[1,512]{1,0:T(1,128)S(1)}, u32[]{:S(2)}, u32[]{:S(2)}) collective-permute-start(f32[1,512]{1,0:T(1,128)S(1)} %copy-done.2), channel_id=1, source_target_pairs={{0,2},{1,3},{2,0},{3,1},{4,6},{5,7},{6,4},{7,5},{8,10},{9,11},{10,... | collective-permute-start | bytes 6152 | tf_op jit(solution)/shard_map/ppermute | solution.py:316
  12.6 2.7 %collective-permute-start = (f32[1,512]{1,0:T(1,128)S(1)}, f32[1,512]{1,0:T(1,128)S(1)}, u32[]{:S(2)}, u32[]{:S(2)}) collective-permute-start(f32[1,512]{1,0:T(1,128)S(1)} %copy-done.2), channel_id=1, source_target_pairs={{0,1},{1,0},{2,3},{3,2},{4,5},{5,4},{6,7},{7,6},{8,9},{9,8},{10,11... | collective-permute-start | bytes 6152 | tf_op jit(solution)/shard_map/ppermute | solution.py:316
  15.2 11.4 %copy-start.8 = (f32[2,4,128]{2,1,0:T(4,128)S(1)}, f32[2,4,128]{2,1,0:T(4,128)}, u32[]{:S(2)}) copy-start(f32[2,4,128]{2,1,0:T(4,128)} %constant.15.clone.spin_ref) | copy-start | bytes 12292
  15.3 3.9 %collective-permute-start.3 = (f32[1,512]{1,0:T(1,128)S(1)}, f32[1,512]{1,0:T(1,128)S(1)}, u32[]{:S(2)}, u32[]{:S(2)}) collective-permute-start(f32[1,512]{1,0:T(1,128)S(1)} %shard_map.119.scale_ref), channel_id=1, source_target_pairs={{0,4},{4,0},{8,12},{12,8},{16,20},{20,16},{24,28},{28,24},{1,5},{5... | collective-permute-start | bytes 6152 | tf_op jit(solution)/shard_map/ppermute | solution.py:316
  19.1 5.6 %collective-permute-start.6 = (f32[2,512]{1,0:T(2,128)S(1)}, f32[2,512]{1,0:T(2,128)S(1)}, u32[]{:S(2)}, u32[]{:S(2)}) collective-permute-start(f32[2,512]{1,0:T(2,128)S(1)} %pad_maximum_fusion.refs_0_), channel_id=1, source_target_pairs={{0,24},{4,28},{8,16},{12,20},{16,8},{20,12},{24,0},{28,4},{1,25},{... | collective-permute-start | bytes 12296 | tf_op jit(solution)/shard_map/ppermute | solution.py:316
  20.5 6.1 %collective-permute-start.5 = (f32[2,512]{1,0:T(2,128)S(1)}, f32[2,512]{1,0:T(2,128)S(1)}, u32[]{:S(2)}, u32[]{:S(2)}) collective-permute-start(f32[2,512]{1,0:T(2,128)S(1)} %pad_maximum_fusion.refs_0_), channel_id=1, source_target_pairs={{0,16},{4,20},{8,24},{12,28},{16,0},{20,4},{24,8},{28,12},{1,17},{... | collective-permute-start | bytes 12296 | tf_op jit(solution)/shard_map/ppermute | solution.py:316
  21.0 5.6 %collective-permute-start.4 = (f32[2,512]{1,0:T(2,128)S(1)}, f32[2,512]{1,0:T(2,128)S(1)}, u32[]{:S(2)}, u32[]{:S(2)}) collective-permute-start(f32[2,512]{1,0:T(2,128)S(1)} %pad_maximum_fusion.refs_0_), channel_id=1, source_target_pairs={{0,8},{4,12},{8,0},{12,4},{16,24},{20,28},{24,16},{28,20},{1,9},{5... | collective-permute-start | bytes 12296 | tf_op jit(solution)/shard_map/ppermute | solution.py:316
  27.7 10.2 %copy-start = (bf16[512,128]{1,0:T(8,128)(2,1)S(1)}, bf16[512,128]{1,0:T(8,128)(2,1)}, u32[]{:S(2)}) copy-start(bf16[512,128]{1,0:T(8,128)(2,1)} %post_ref.1) | copy-start | bytes 393220
  27.8 10.2 %copy-start.1 = (bf16[128,512]{1,0:T(8,128)(2,1)S(1)}, bf16[128,512]{1,0:T(8,128)(2,1)}, u32[]{:S(2)}) copy-start(bf16[128,512]{1,0:T(8,128)(2,1)} %get-tuple-element.10.skipped_ref) | copy-start | bytes 393220

commit v7 on v5

--- a/solution.py
+++ b/solution.py
@@ -16,7 +16,7 @@
 
 
 def order_of(places):
-    return (5, 2, 1, 7, 4, 3, 0, 6) if places == 8 else tuple(range(places))
+    return (4, 7, 1, 2, 5, 6, 0, 3) if places == 8 else tuple(range(places))
 
 
 def reverse_bits(index, levels):

time: 37.4 us -> 37.9 us (1.013)
  blocking collectives: 8.58 us -> 9.26 us
  waiting for transfers between devices: 8.65 us -> 8.21 us
    ppermute x7, waiting for transfers between devices: 8.65 us -> 7.11 us  [swap(): lax.ppermute(value, axis, [(place, place ^ apart) for place in range(lax....]
    all_to_all x1, waiting for transfers between devices: 0.01 us -> 1.1 us  [exchange(): lax.all_to_all(value, 'seq', split_axis=0, concat_axis=0, tiled=True, axi...]
    ppermute x7, starting transfers between devices: 6.92 us -> 7.86 us  [swap(): lax.ppermute(value, axis, [(place, place ^ apart) for place in range(lax....]
    all_to_all x1, blocking collectives: 8.58 us -> 9.26 us  [exchange(): lax.all_to_all(value, 'seq', split_axis=0, concat_axis=0, tiled=True, axi...]
    all_to_all x1, starting transfers between devices: 8.61 us -> 7.99 us  [exchange(): lax.all_to_all(value, 'seq', split_axis=0, concat_axis=0, tiled=True, axi...]
  transfers between devices with their start and end apart: 8 -> 8, of which waited for: 5 -> 6; matrix products, arithmetic and copies ran while one was open for 0% -> 0% of each run, Pallas kernels for 0% -> 0%
where the time goes in v7:
time: 37.9 us; the launch traced here: 37.7 us
  starting transfers between devices  15.8 us (42%)
  blocking collectives  9.26 us (24%)
  waiting for transfers between devices  8.21 us (22%)
  Pallas kernels  4.18 us (11%)
    all_to_all x1, blocking collectives, exchange(): lax.all_to_all(value, 'seq', split_axis=0, concat_axis=0, tiled=True, axi...  9.26 us
    all_to_all x1, starting transfers between devices, exchange(): lax.all_to_all(value, 'seq', split_axis=0, concat_axis=0, tiled=True, axi...  7.99 us
    ppermute x7, starting transfers between devices, swap(): lax.ppermute(value, axis, [(place, place ^ apart) for place in range(lax....  7.86 us
    ppermute x7, waiting for transfers between devices, swap(): lax.ppermute(value, axis, [(place, place ^ apart) for place in range(lax....  7.11 us
    pallas_call x4, Pallas kernels, call(): pl.pallas_call(kernel, out_shape=out_shape, compiler_params=pltpu.Compile...  4.18 us
    all_to_all x1, waiting for transfers between devices, exchange(): lax.all_to_all(value, 'seq', split_axis=0, concat_axis=0, tiled=True, axi...  1.1 us
  transfers between devices with their start and end apart: 8, of which 6 were waited for; matrix products, arithmetic and copies ran while one was open for 0% of the time, Pallas kernels for 0%

profile of v7, /device:TPU:0, one launch (start us, length us, event | category | flops | bytes accessed | tf_op | source)
XLA Modules:
  0.0 37.7 jit_solution(8621164456209704747)
XLA Ops:
  0.0 2.3 %shard_map.118 = (f32[1,512]{1,0:T(1,128)}, bf16[128,512]{1,0:T(8,128)(2,1)}, bf16[8,5,16,512]{3,2,1,0:T(8,128)(2,1)}) custom-call(bf16[512,128]{1,0:T(8,128)(2,1)} %features_ref.1, bf16[512,128]{1,0:T(8,128)(2,1)} %pre_ref.1, f32[1,128]{1,0:T(1,128)} %bitcast.4, f32[1,128]{1,0:T(1,128)} %bitcast.5, f32[2,2,512,128]{3,2,1,0:T(8,128)} %spectrum_ref.1), custom_call_target="tpu_custom_call" | custom-call | flops 655360 | bytes 2097152 | tf_op jit(solution)/shard_map/pallas_call | solution.py:299
  2.3 0.0 copy-start.2
  2.3 0.0 copy-start.3
  2.3 0.0 copy-start.4
  2.3 0.0 copy-start.5
  2.3 0.0 copy-start.6
  2.4 0.0 copy-start.7
  2.4 8.0 %all-to-all-start = ((bf16[8,5,16,512]{3,2,1,0:T(8,128)(2,1)}), bf16[8,5,16,512]{3,2,1,0:T(8,128)(2,1)S(1)}, u32[]{:S(2)}, u32[]{:S(2)}) async-start(bf16[8,5,16,512]{3,2,1,0:T(8,128)(2,1)} %get-tuple-element.8), calls=%async_computation | async-start | bytes 1310720 | tf_op jit(solution)/shard_map/all_to_all | solution.py:310
  10.4 0.0 copy-done.2
  10.4 0.4 collective-permute-start.2
  10.7 1.2 %collective-permute-start.1 = (f32[1,512]{1,0:T(1,128)S(1)}, f32[1,512]{1,0:T(1,128)S(1)}, u32[]{:S(2)}, u32[]{:S(2)}) collective-permute-start(f32[1,512]{1,0:T(1,128)S(1)} %copy-done.2), channel_id=1, source_target_pairs={{0,2},{1,3},{2,0},{3,1},{4,6},{5,7},{6,4},{7,5},{8,10},{9,11},{10,... | collective-permute-start | bytes 6152 | tf_op jit(solution)/shard_map/ppermute | solution.py:314
  11.9 0.3 collective-permute-start
  12.2 1.1 %collective-permute-done.2.refs_3_ = f32[1,512]{1,0:T(1,128)S(1)} collective-permute-done((f32[1,512]{1,0:T(1,128)S(1)}, f32[1,512]{1,0:T(1,128)S(1)}, u32[]{:S(2)}, u32[]{:S(2)}) %collective-permute-start.2) | collective-permute-done | bytes 2080 | tf_op jit(solution)/shard_map/ppermute | solution.py:314
  13.4 0.9 %collective-permute-done.1.refs_2_ = f32[1,512]{1,0:T(1,128)S(1)} collective-permute-done((f32[1,512]{1,0:T(1,128)S(1)}, f32[1,512]{1,0:T(1,128)S(1)}, u32[]{:S(2)}, u32[]{:S(2)}) %collective-permute-start.1) | collective-permute-done | bytes 2080 | tf_op jit(solution)/shard_map/ppermute | solution.py:314
  14.3 0.0 collective-permute-done.refs_1_
  14.3 0.0 copy-start.8
  14.3 1.5 %collective-permute-start.3 = (f32[1,512]{1,0:T(1,128)S(1)}, f32[1,512]{1,0:T(1,128)S(1)}, u32[]{:S(2)}, u32[]{:S(2)}) collective-permute-start(f32[1,512]{1,0:T(1,128)S(1)} %shard_map.119.scale_ref), channel_id=1, source_target_pairs={{0,4},{4,0},{8,12},{12,8},{16,20},{20,16},{24,28},{28,24},{1,5},{5... | collective-permute-start | bytes 6152 | tf_op jit(solution)/shard_map/ppermute | solution.py:314
  15.9 2.1 %collective-permute-done.3 = f32[1,512]{1,0:T(1,128)S(1)} collective-permute-done((f32[1,512]{1,0:T(1,128)S(1)}, f32[1,512]{1,0:T(1,128)S(1)}, u32[]{:S(2)}, u32[]{:S(2)}) %collective-permute-start.3) | collective-permute-done | bytes 2080 | tf_op jit(solution)/shard_map/ppermute | solution.py:314
  18.0 1.6 %collective-permute-start.6 = (f32[2,512]{1,0:T(2,128)S(1)}, f32[2,512]{1,0:T(2,128)S(1)}, u32[]{:S(2)}, u32[]{:S(2)}) collective-permute-start(f32[2,512]{1,0:T(2,128)S(1)} %pad_maximum_fusion.refs_0_), channel_id=1, source_target_pairs={{0,24},{4,28},{8,16},{12,20},{16,8},{20,12},{24,0},{28,4},{1,25},{... | collective-permute-start | bytes 12296 | tf_op jit(solution)/shard_map/ppermute | solution.py:314
  19.6 0.5 %collective-permute-start.5 = (f32[2,512]{1,0:T(2,128)S(1)}, f32[2,512]{1,0:T(2,128)S(1)}, u32[]{:S(2)}, u32[]{:S(2)}) collective-permute-start(f32[2,512]{1,0:T(2,128)S(1)} %pad_maximum_fusion.refs_0_), channel_id=1, source_target_pairs={{0,16},{4,20},{8,24},{12,28},{16,0},{20,4},{24,8},{28,12},{1,17},{... | collective-permute-start | bytes 12296 | tf_op jit(solution)/shard_map/ppermute | solution.py:314
  20.1 2.4 %collective-permute-start.4 = (f32[2,512]{1,0:T(2,128)S(1)}, f32[2,512]{1,0:T(2,128)S(1)}, u32[]{:S(2)}, u32[]{:S(2)}) collective-permute-start(f32[2,512]{1,0:T(2,128)S(1)} %pad_maximum_fusion.refs_0_), channel_id=1, source_target_pairs={{0,8},{4,12},{8,0},{12,4},{16,24},{20,28},{24,16},{28,20},{1,9},{5... | collective-permute-start | bytes 12296 | tf_op jit(solution)/shard_map/ppermute | solution.py:314
  22.5 1.2 %collective-permute-done.6.refs_3_ = f32[2,512]{1,0:T(2,128)S(1)} collective-permute-done((f32[2,512]{1,0:T(2,128)S(1)}, f32[2,512]{1,0:T(2,128)S(1)}, u32[]{:S(2)}, u32[]{:S(2)}) %collective-permute-start.6) | collective-permute-done | bytes 4128 | tf_op jit(solution)/shard_map/ppermute | solution.py:314
  23.6 1.7 %collective-permute-done.5.refs_2_ = f32[2,512]{1,0:T(2,128)S(1)} collective-permute-done((f32[2,512]{1,0:T(2,128)S(1)}, f32[2,512]{1,0:T(2,128)S(1)}, u32[]{:S(2)}, u32[]{:S(2)}) %collective-permute-start.5) | collective-permute-done | bytes 4128 | tf_op jit(solution)/shard_map/ppermute | solution.py:314
  25.4 0.0 collective-permute-done.4.refs_1_
  25.4 1.1 %all-to-all-done.packed_ref = bf16[8,5,16,512]{3,2,1,0:T(8,128)(2,1)S(1)} async-done(((bf16[8,5,16,512]{3,2,1,0:T(8,128)(2,1)}), bf16[8,5,16,512]{3,2,1,0:T(8,128)(2,1)S(1)}, u32[]{:S(2)}, u32[]{:S(2)}) %all-to-all-start) | async-done | bytes 655392 | tf_op jit(solution)/shard_map/all_to_all | solution.py:310
  26.5 0.0 copy-done.5
  26.5 0.0 copy-done.6
  26.5 1.1 %shard_map.120 = bf16[128,512]{1,0:T(8,128)(2,1)S(1)} custom-call(bf16[8,5,16,512]{3,2,1,0:T(8,128)(2,1)S(1)} %all-to-all-done.packed_ref, bf16[288,128]{1,0:T(8,128)(2,1)S(1)} %copy-done.5, bf16[128,288]{1,0:T(8,128)(2,1)S(1)} %copy-done.4, f32[2,9,512]{2,1,0:T(8,128)S(1)} %copy-done.6, f32[2,4,128]{2,1,0:T(4,128)S(1)} %copy-done.8, ...), custom_call_target="tpu_custom_call" | custom-call | flops 671088640 | bytes 1310720 | tf_op jit(solution)/shard_map/pallas_call | solution.py:299
  27.6 0.0 copy-start
  27.6 0.0 copy-start.1
  27.6 9.3 %all_to_all.10.conv_ref = bf16[8,16,512]{2,1,0:T(8,128)(2,1)S(1)} all-to-all(bf16[8,16,512]{2,1,0:T(8,128)(2,1)S(1)} %bitcast.3), channel_id=1, replica_groups={{16,28,4,8,20,24,0,12},{17,29,5,9,21,25,1,13},{18,30,6,10,22,26,2,14},{..., dimensions={0} | all-to-all | bytes 262144 | tf_op jit(solution)/shard_map/all_to_all | solution.py:310
  36.9 0.8 %shard_map.121 = bf16[512,128]{1,0:T(8,128)(2,1)} custom-call(bf16[8,16,512]{2,1,0:T(8,128)(2,1)S(1)} %all_to_all.10.conv_ref, bf16[128,512]{1,0:T(8,128)(2,1)S(1)} %copy-done.1, f32[1,512]{1,0:T(1,128)S(1)} %shard_map.119.scale_ref, bf16[512,128]{1,0:T(8,128)(2,1)S(1)} %copy-done), custom_call_target="tpu_custom_call" | custom-call | flops 655360 | bytes 524288 | tf_op jit(solution)/shard_map/pallas_call | solution.py:299
  (8 shorter events, 0.0 us)
Async XLA Ops:
  2.3 8.1 %copy-start.2 = (f32[1,512]{1,0:T(1,128)S(1)}, f32[1,512]{1,0:T(1,128)}, u32[]{:S(2)}) copy-start(f32[1,512]{1,0:T(1,128)} %get-tuple-element.9.refs_0_) | copy-start | bytes 6148
  2.3 24.2 %copy-start.3 = (bf16[2,256,256]{2,1,0:T(8,128)(2,1)S(1)}, bf16[2,256,256]{2,1,0:T(8,128)(2,1)}, u32[]{:S(2)}) copy-start(bf16[2,256,256]{2,1,0:T(8,128)(2,1)} %constant.16.clone.dft_ref) | copy-start | bytes 786436
  2.3 24.2 %copy-start.4 = (bf16[128,288]{1,0:T(8,128)(2,1)S(1)}, bf16[128,288]{1,0:T(8,128)(2,1)}, u32[]{:S(2)}) copy-start(bf16[128,288]{1,0:T(8,128)(2,1)} %constant.13.clone.last_ref) | copy-start | bytes 221188
  2.3 24.1 %copy-start.5 = (bf16[288,128]{1,0:T(8,128)(2,1)S(1)}, bf16[288,128]{1,0:T(8,128)(2,1)}, u32[]{:S(2)}) copy-start(bf16[288,128]{1,0:T(8,128)(2,1)} %constant.12.clone.first_ref) | copy-start | bytes 221188
  2.3 24.1 %copy-start.6 = (f32[2,9,512]{2,1,0:T(8,128)S(1)}, f32[2,9,512]{2,1,0:T(8,128)}, u32[]{:S(2)}) copy-start(f32[2,9,512]{2,1,0:T(8,128)} %constant.14.clone.twist_ref) | copy-start | bytes 110596
  2.4 24.1 %copy-start.7 = (bf16[128,128]{1,0:T(8,128)(2,1)S(1)}, bf16[128,128]{1,0:T(8,128)(2,1)}, u32[]{:S(2)}) copy-start(bf16[128,128]{1,0:T(8,128)(2,1)} %constant.17.clone.reverse_ref) | copy-start | bytes 98308
  2.4 24.1 %all-to-all-start = ((bf16[8,5,16,512]{3,2,1,0:T(8,128)(2,1)}), bf16[8,5,16,512]{3,2,1,0:T(8,128)(2,1)S(1)}, u32[]{:S(2)}, u32[]{:S(2)}) async-start(bf16[8,5,16,512]{3,2,1,0:T(8,128)(2,1)} %get-tuple-element.8), calls=%async_computation | async-start | bytes 1310720 | tf_op jit(solution)/shard_map/all_to_all | solution.py:310
  10.4 3.0 %collective-permute-start.2 = (f32[1,512]{1,0:T(1,128)S(1)}, f32[1,512]{1,0:T(1,128)S(1)}, u32[]{:S(2)}, u32[]{:S(2)}) collective-permute-start(f32[1,512]{1,0:T(1,128)S(1)} %copy-done.2), channel_id=1, source_target_pairs={{0,3},{1,2},{2,1},{3,0},{4,7},{5,6},{6,5},{7,4},{8,11},{9,10},{10,... | collective-permute-start | bytes 6152 | tf_op jit(solution)/shard_map/ppermute | solution.py:314
  10.7 3.6 %collective-permute-start.1 = (f32[1,512]{1,0:T(1,128)S(1)}, f32[1,512]{1,0:T(1,128)S(1)}, u32[]{:S(2)}, u32[]{:S(2)}) collective-permute-start(f32[1,512]{1,0:T(1,128)S(1)} %copy-done.2), channel_id=1, source_target_pairs={{0,2},{1,3},{2,0},{3,1},{4,6},{5,7},{6,4},{7,5},{8,10},{9,11},{10,... | collective-permute-start | bytes 6152 | tf_op jit(solution)/shard_map/ppermute | solution.py:314
  11.9 2.4 %collective-permute-start = (f32[1,512]{1,0:T(1,128)S(1)}, f32[1,512]{1,0:T(1,128)S(1)}, u32[]{:S(2)}, u32[]{:S(2)}) collective-permute-start(f32[1,512]{1,0:T(1,128)S(1)} %copy-done.2), channel_id=1, source_target_pairs={{0,1},{1,0},{2,3},{3,2},{4,5},{5,4},{6,7},{7,6},{8,9},{9,8},{10,11... | collective-permute-start | bytes 6152 | tf_op jit(solution)/shard_map/ppermute | solution.py:314
  14.3 12.2 %copy-start.8 = (f32[2,4,128]{2,1,0:T(4,128)S(1)}, f32[2,4,128]{2,1,0:T(4,128)}, u32[]{:S(2)}) copy-start(f32[2,4,128]{2,1,0:T(4,128)} %constant.15.clone.spin_ref) | copy-start | bytes 12292
  14.3 3.7 %collective-permute-start.3 = (f32[1,512]{1,0:T(1,128)S(1)}, f32[1,512]{1,0:T(1,128)S(1)}, u32[]{:S(2)}, u32[]{:S(2)}) collective-permute-start(f32[1,512]{1,0:T(1,128)S(1)} %shard_map.119.scale_ref), channel_id=1, source_target_pairs={{0,4},{4,0},{8,12},{12,8},{16,20},{20,16},{24,28},{28,24},{1,5},{5... | collective-permute-start | bytes 6152 | tf_op jit(solution)/shard_map/ppermute | solution.py:314
  18.0 5.6 %collective-permute-start.6 = (f32[2,512]{1,0:T(2,128)S(1)}, f32[2,512]{1,0:T(2,128)S(1)}, u32[]{:S(2)}, u32[]{:S(2)}) collective-permute-start(f32[2,512]{1,0:T(2,128)S(1)} %pad_maximum_fusion.refs_0_), channel_id=1, source_target_pairs={{0,24},{4,28},{8,16},{12,20},{16,8},{20,12},{24,0},{28,4},{1,25},{... | collective-permute-start | bytes 12296 | tf_op jit(solution)/shard_map/ppermute | solution.py:314
  19.6 5.8 %collective-permute-start.5 = (f32[2,512]{1,0:T(2,128)S(1)}, f32[2,512]{1,0:T(2,128)S(1)}, u32[]{:S(2)}, u32[]{:S(2)}) collective-permute-start(f32[2,512]{1,0:T(2,128)S(1)} %pad_maximum_fusion.refs_0_), channel_id=1, source_target_pairs={{0,16},{4,20},{8,24},{12,28},{16,0},{20,4},{24,8},{28,12},{1,17},{... | collective-permute-start | bytes 12296 | tf_op jit(solution)/shard_map/ppermute | solution.py:314
  20.1 5.2 %collective-permute-start.4 = (f32[2,512]{1,0:T(2,128)S(1)}, f32[2,512]{1,0:T(2,128)S(1)}, u32[]{:S(2)}, u32[]{:S(2)}) collective-permute-start(f32[2,512]{1,0:T(2,128)S(1)} %pad_maximum_fusion.refs_0_), channel_id=1, source_target_pairs={{0,8},{4,12},{8,0},{12,4},{16,24},{20,28},{24,16},{28,20},{1,9},{5... | collective-permute-start | bytes 12296 | tf_op jit(solution)/shard_map/ppermute | solution.py:314
  27.6 9.3 %copy-start = (bf16[512,128]{1,0:T(8,128)(2,1)S(1)}, bf16[512,128]{1,0:T(8,128)(2,1)}, u32[]{:S(2)}) copy-start(bf16[512,128]{1,0:T(8,128)(2,1)} %post_ref.1) | copy-start | bytes 393220
  27.6 9.3 %copy-start.1 = (bf16[128,512]{1,0:T(8,128)(2,1)S(1)}, bf16[128,512]{1,0:T(8,128)(2,1)}, u32[]{:S(2)}) copy-start(bf16[128,512]{1,0:T(8,128)(2,1)} %get-tuple-element.10.skipped_ref) | copy-start | bytes 393220

commit v8 on v6

--- a/solution.py
+++ b/solution.py
@@ -18,7 +18,7 @@
 def order_of(places, back=False):
     if places != 8:
         return tuple(range(places))
-    return (2, 1, 7, 4, 3, 0, 6, 5) if back else (5, 2, 1, 7, 4, 3, 0, 6)
+    return (5, 1, 3, 6, 2, 4, 0, 7) if back else (4, 7, 1, 2, 5, 6, 0, 3)
 
 
 def reverse_bits(index, levels):

time: 39 us -> 37.3 us (0.956)
  blocking collectives: 10.2 us -> 8.58 us
  waiting for transfers between devices: 8.65 us -> 8.21 us
    all_to_all x1, blocking collectives: 10.2 us -> 8.58 us  [exchange(): lax.all_to_all(value, 'seq', split_axis=0, concat_axis=0, tiled=True, axi...]
    ppermute x7, waiting for transfers between devices: 8.65 us -> 7.11 us  [swap(): lax.ppermute(value, axis, [(place, place ^ apart) for place in range(lax....]
    all_to_all x1, waiting for transfers between devices: 0.01 us -> 1.1 us  [exchange(): lax.all_to_all(value, 'seq', split_axis=0, concat_axis=0, tiled=True, axi...]
    ppermute x7, starting transfers between devices: 6.92 us -> 7.86 us  [swap(): lax.ppermute(value, axis, [(place, place ^ apart) for place in range(lax....]
    all_to_all x1, starting transfers between devices: 8.61 us -> 7.99 us  [exchange(): lax.all_to_all(value, 'seq', split_axis=0, concat_axis=0, tiled=True, axi...]
  transfers between devices with their start and end apart: 8 -> 8, of which waited for: 5 -> 6; matrix products, arithmetic and copies ran while one was open for 0% -> 0% of each run, Pallas kernels for 0% -> 0%
where the time goes in v8:
time: 37.3 us; the launch traced here: 37 us
  starting transfers between devices  15.8 us (42%)
  blocking collectives  8.58 us (23%)
  waiting for transfers between devices  8.21 us (22%)
  Pallas kernels  4.18 us (11%)
    all_to_all x1, blocking collectives, exchange(): lax.all_to_all(value, 'seq', split_axis=0, concat_axis=0, tiled=True, axi...  8.58 us
    all_to_all x1, starting transfers between devices, exchange(): lax.all_to_all(value, 'seq', split_axis=0, concat_axis=0, tiled=True, axi...  7.99 us
    ppermute x7, starting transfers between devices, swap(): lax.ppermute(value, axis, [(place, place ^ apart) for place in range(lax....  7.86 us
    ppermute x7, waiting for transfers between devices, swap(): lax.ppermute(value, axis, [(place, place ^ apart) for place in range(lax....  7.11 us
    pallas_call x4, Pallas kernels, call(): pl.pallas_call(kernel, out_shape=out_shape, compiler_params=pltpu.Compile...  4.18 us
    all_to_all x1, waiting for transfers between devices, exchange(): lax.all_to_all(value, 'seq', split_axis=0, concat_axis=0, tiled=True, axi...  1.1 us
  transfers between devices with their start and end apart: 8, of which 6 were waited for; matrix products, arithmetic and copies ran while one was open for 0% of the time, Pallas kernels for 0%

profile of v8, /device:TPU:0, one launch (start us, length us, event | category | flops | bytes accessed | tf_op | source)
XLA Modules:
  0.0 37.0 jit_solution(11368502404291801542)
XLA Ops:
  0.0 2.3 %shard_map.118 = (f32[1,512]{1,0:T(1,128)}, bf16[128,512]{1,0:T(8,128)(2,1)}, bf16[8,5,16,512]{3,2,1,0:T(8,128)(2,1)}) custom-call(bf16[512,128]{1,0:T(8,128)(2,1)} %features_ref.1, bf16[512,128]{1,0:T(8,128)(2,1)} %pre_ref.1, f32[1,128]{1,0:T(1,128)} %bitcast.4, f32[1,128]{1,0:T(1,128)} %bitcast.5, f32[2,2,512,128]{3,2,1,0:T(8,128)} %spectrum_ref.1), custom_call_target="tpu_custom_call" | custom-call | flops 655360 | bytes 2097152 | tf_op jit(solution)/shard_map/pallas_call | solution.py:301
  2.3 0.0 copy-start.3
  2.3 0.0 copy-start.4
  2.3 0.0 copy-start.5
  2.3 0.0 copy-start.6
  2.4 0.0 copy-start.7
  2.4 8.0 %all-to-all-start = ((bf16[8,5,16,512]{3,2,1,0:T(8,128)(2,1)}), bf16[8,5,16,512]{3,2,1,0:T(8,128)(2,1)S(1)}, u32[]{:S(2)}, u32[]{:S(2)}) async-start(bf16[8,5,16,512]{3,2,1,0:T(8,128)(2,1)} %get-tuple-element.8), calls=%async_computation | async-start | bytes 1310720 | tf_op jit(solution)/shard_map/all_to_all | solution.py:312
  10.4 0.4 %collective-permute-start.2 = (f32[1,512]{1,0:T(1,128)S(1)}, f32[1,512]{1,0:T(1,128)S(1)}, u32[]{:S(2)}, u32[]{:S(2)}) collective-permute-start(f32[1,512]{1,0:T(1,128)S(1)} %copy-done.2), channel_id=1, source_target_pairs={{0,3},{1,2},{2,1},{3,0},{4,7},{5,6},{6,5},{7,4},{8,11},{9,10},{10,... | collective-permute-start | bytes 6152 | tf_op jit(solution)/shard_map/ppermute | solution.py:316
  10.7 1.2 %collective-permute-start.1 = (f32[1,512]{1,0:T(1,128)S(1)}, f32[1,512]{1,0:T(1,128)S(1)}, u32[]{:S(2)}, u32[]{:S(2)}) collective-permute-start(f32[1,512]{1,0:T(1,128)S(1)} %copy-done.2), channel_id=1, source_target_pairs={{0,2},{1,3},{2,0},{3,1},{4,6},{5,7},{6,4},{7,5},{8,10},{9,11},{10,... | collective-permute-start | bytes 6152 | tf_op jit(solution)/shard_map/ppermute | solution.py:316
  11.9 0.3 collective-permute-start
  12.2 1.1 %collective-permute-done.2.refs_3_ = f32[1,512]{1,0:T(1,128)S(1)} collective-permute-done((f32[1,512]{1,0:T(1,128)S(1)}, f32[1,512]{1,0:T(1,128)S(1)}, u32[]{:S(2)}, u32[]{:S(2)}) %collective-permute-start.2) | collective-permute-done | bytes 2080 | tf_op jit(solution)/shard_map/ppermute | solution.py:316
  13.4 0.9 %collective-permute-done.1.refs_2_ = f32[1,512]{1,0:T(1,128)S(1)} collective-permute-done((f32[1,512]{1,0:T(1,128)S(1)}, f32[1,512]{1,0:T(1,128)S(1)}, u32[]{:S(2)}, u32[]{:S(2)}) %collective-permute-start.1) | collective-permute-done | bytes 2080 | tf_op jit(solution)/shard_map/ppermute | solution.py:316
  14.3 0.0 collective-permute-done.refs_1_
  14.3 0.0 copy-start.8
  14.3 1.5 %collective-permute-start.3 = (f32[1,512]{1,0:T(1,128)S(1)}, f32[1,512]{1,0:T(1,128)S(1)}, u32[]{:S(2)}, u32[]{:S(2)}) collective-permute-start(f32[1,512]{1,0:T(1,128)S(1)} %shard_map.119.scale_ref), channel_id=1, source_target_pairs={{0,4},{4,0},{8,12},{12,8},{16,20},{20,16},{24,28},{28,24},{1,5},{5... | collective-permute-start | bytes 6152 | tf_op jit(solution)/shard_map/ppermute | solution.py:316
  15.9 2.1 %collective-permute-done.3 = f32[1,512]{1,0:T(1,128)S(1)} collective-permute-done((f32[1,512]{1,0:T(1,128)S(1)}, f32[1,512]{1,0:T(1,128)S(1)}, u32[]{:S(2)}, u32[]{:S(2)}) %collective-permute-start.3) | collective-permute-done | bytes 2080 | tf_op jit(solution)/shard_map/ppermute | solution.py:316
  18.0 1.6 %collective-permute-start.6 = (f32[2,512]{1,0:T(2,128)S(1)}, f32[2,512]{1,0:T(2,128)S(1)}, u32[]{:S(2)}, u32[]{:S(2)}) collective-permute-start(f32[2,512]{1,0:T(2,128)S(1)} %pad_maximum_fusion.refs_0_), channel_id=1, source_target_pairs={{0,24},{4,28},{8,16},{12,20},{16,8},{20,12},{24,0},{28,4},{1,25},{... | collective-permute-start | bytes 12296 | tf_op jit(solution)/shard_map/ppermute | solution.py:316
  19.6 0.5 %collective-permute-start.5 = (f32[2,512]{1,0:T(2,128)S(1)}, f32[2,512]{1,0:T(2,128)S(1)}, u32[]{:S(2)}, u32[]{:S(2)}) collective-permute-start(f32[2,512]{1,0:T(2,128)S(1)} %pad_maximum_fusion.refs_0_), channel_id=1, source_target_pairs={{0,16},{4,20},{8,24},{12,28},{16,0},{20,4},{24,8},{28,12},{1,17},{... | collective-permute-start | bytes 12296 | tf_op jit(solution)/shard_map/ppermute | solution.py:316
  20.1 2.4 %collective-permute-start.4 = (f32[2,512]{1,0:T(2,128)S(1)}, f32[2,512]{1,0:T(2,128)S(1)}, u32[]{:S(2)}, u32[]{:S(2)}) collective-permute-start(f32[2,512]{1,0:T(2,128)S(1)} %pad_maximum_fusion.refs_0_), channel_id=1, source_target_pairs={{0,8},{4,12},{8,0},{12,4},{16,24},{20,28},{24,16},{28,20},{1,9},{5... | collective-permute-start | bytes 12296 | tf_op jit(solution)/shard_map/ppermute | solution.py:316
  22.5 1.2 %collective-permute-done.6.refs_3_ = f32[2,512]{1,0:T(2,128)S(1)} collective-permute-done((f32[2,512]{1,0:T(2,128)S(1)}, f32[2,512]{1,0:T(2,128)S(1)}, u32[]{:S(2)}, u32[]{:S(2)}) %collective-permute-start.6) | collective-permute-done | bytes 4128 | tf_op jit(solution)/shard_map/ppermute | solution.py:316
  23.6 1.7 %collective-permute-done.5.refs_2_ = f32[2,512]{1,0:T(2,128)S(1)} collective-permute-done((f32[2,512]{1,0:T(2,128)S(1)}, f32[2,512]{1,0:T(2,128)S(1)}, u32[]{:S(2)}, u32[]{:S(2)}) %collective-permute-start.5) | collective-permute-done | bytes 4128 | tf_op jit(solution)/shard_map/ppermute | solution.py:316
  25.4 0.0 collective-permute-done.4.refs_1_
  25.4 1.1 %all-to-all-done.packed_ref = bf16[8,5,16,512]{3,2,1,0:T(8,128)(2,1)S(1)} async-done(((bf16[8,5,16,512]{3,2,1,0:T(8,128)(2,1)}), bf16[8,5,16,512]{3,2,1,0:T(8,128)(2,1)S(1)}, u32[]{:S(2)}, u32[]{:S(2)}) %all-to-all-start) | async-done | bytes 655392 | tf_op jit(solution)/shard_map/all_to_all | solution.py:312
  26.5 0.0 copy-done.6
  26.5 0.0 copy-done.7
  26.5 0.0 copy-done.8
  26.5 1.1 %shard_map.120 = bf16[128,512]{1,0:T(8,128)(2,1)S(1)} custom-call(bf16[8,5,16,512]{3,2,1,0:T(8,128)(2,1)S(1)} %all-to-all-done.packed_ref, bf16[288,128]{1,0:T(8,128)(2,1)S(1)} %copy-done.5, bf16[128,288]{1,0:T(8,128)(2,1)S(1)} %copy-done.4, f32[2,9,512]{2,1,0:T(8,128)S(1)} %copy-done.6, f32[2,4,128]{2,1,0:T(4,128)S(1)} %copy-done.8, ...), custom_call_target="tpu_custom_call" | custom-call | flops 671088640 | bytes 1310720 | tf_op jit(solution)/shard_map/pallas_call | solution.py:301
  27.6 0.0 copy-start
  27.6 0.0 copy-start.1
  27.6 8.6 %all_to_all.10.conv_ref = bf16[8,16,512]{2,1,0:T(8,128)(2,1)S(1)} all-to-all(bf16[8,16,512]{2,1,0:T(8,128)(2,1)S(1)} %bitcast.3), channel_id=1, replica_groups={{20,4,12,24,8,16,0,28},{21,5,13,25,9,17,1,29},{22,6,14,26,10,18,2,30},{..., dimensions={0} | all-to-all | bytes 262144 | tf_op jit(solution)/shard_map/all_to_all | solution.py:312
  36.2 0.0 copy-done.1
  36.2 0.8 %shard_map.121 = bf16[512,128]{1,0:T(8,128)(2,1)} custom-call(bf16[8,16,512]{2,1,0:T(8,128)(2,1)S(1)} %all_to_all.10.conv_ref, bf16[128,512]{1,0:T(8,128)(2,1)S(1)} %copy-done.1, f32[1,512]{1,0:T(1,128)S(1)} %shard_map.119.scale_ref, bf16[512,128]{1,0:T(8,128)(2,1)S(1)} %copy-done), custom_call_target="tpu_custom_call" | custom-call | flops 655360 | bytes 524288 | tf_op jit(solution)/shard_map/pallas_call | solution.py:301
  (8 shorter events, 0.0 us)
Async XLA Ops:
  2.3 8.1 %copy-start.2 = (f32[1,512]{1,0:T(1,128)S(1)}, f32[1,512]{1,0:T(1,128)}, u32[]{:S(2)}) copy-start(f32[1,512]{1,0:T(1,128)} %get-tuple-element.9.refs_0_) | copy-start | bytes 6148
  2.3 24.2 %copy-start.3 = (bf16[2,256,256]{2,1,0:T(8,128)(2,1)S(1)}, bf16[2,256,256]{2,1,0:T(8,128)(2,1)}, u32[]{:S(2)}) copy-start(bf16[2,256,256]{2,1,0:T(8,128)(2,1)} %constant.16.clone.dft_ref) | copy-start | bytes 786436
  2.3 24.2 %copy-start.4 = (bf16[128,288]{1,0:T(8,128)(2,1)S(1)}, bf16[128,288]{1,0:T(8,128)(2,1)}, u32[]{:S(2)}) copy-start(bf16[128,288]{1,0:T(8,128)(2,1)} %constant.13.clone.last_ref) | copy-start | bytes 221188
  2.3 24.1 %copy-start.5 = (bf16[288,128]{1,0:T(8,128)(2,1)S(1)}, bf16[288,128]{1,0:T(8,128)(2,1)}, u32[]{:S(2)}) copy-start(bf16[288,128]{1,0:T(8,128)(2,1)} %constant.12.clone.first_ref) | copy-start | bytes 221188
  2.3 24.1 %copy-start.6 = (f32[2,9,512]{2,1,0:T(8,128)S(1)}, f32[2,9,512]{2,1,0:T(8,128)}, u32[]{:S(2)}) copy-start(f32[2,9,512]{2,1,0:T(8,128)} %constant.14.clone.twist_ref) | copy-start | bytes 110596
  2.4 24.1 %copy-start.7 = (bf16[128,128]{1,0:T(8,128)(2,1)S(1)}, bf16[128,128]{1,0:T(8,128)(2,1)}, u32[]{:S(2)}) copy-start(bf16[128,128]{1,0:T(8,128)(2,1)} %constant.17.clone.reverse_ref) | copy-start | bytes 98308
  2.4 24.1 %all-to-all-start = ((bf16[8,5,16,512]{3,2,1,0:T(8,128)(2,1)}), bf16[8,5,16,512]{3,2,1,0:T(8,128)(2,1)S(1)}, u32[]{:S(2)}, u32[]{:S(2)}) async-start(bf16[8,5,16,512]{3,2,1,0:T(8,128)(2,1)} %get-tuple-element.8), calls=%async_computation | async-start | bytes 1310720 | tf_op jit(solution)/shard_map/all_to_all | solution.py:312
  10.4 3.0 %collective-permute-start.2 = (f32[1,512]{1,0:T(1,128)S(1)}, f32[1,512]{1,0:T(1,128)S(1)}, u32[]{:S(2)}, u32[]{:S(2)}) collective-permute-start(f32[1,512]{1,0:T(1,128)S(1)} %copy-done.2), channel_id=1, source_target_pairs={{0,3},{1,2},{2,1},{3,0},{4,7},{5,6},{6,5},{7,4},{8,11},{9,10},{10,... | collective-permute-start | bytes 6152 | tf_op jit(solution)/shard_map/ppermute | solution.py:316
  10.7 3.6 %collective-permute-start.1 = (f32[1,512]{1,0:T(1,128)S(1)}, f32[1,512]{1,0:T(1,128)S(1)}, u32[]{:S(2)}, u32[]{:S(2)}) collective-permute-start(f32[1,512]{1,0:T(1,128)S(1)} %copy-done.2), channel_id=1, source_target_pairs={{0,2},{1,3},{2,0},{3,1},{4,6},{5,7},{6,4},{7,5},{8,10},{9,11},{10,... | collective-permute-start | bytes 6152 | tf_op jit(solution)/shard_map/ppermute | solution.py:316
  11.9 2.4 %collective-permute-start = (f32[1,512]{1,0:T(1,128)S(1)}, f32[1,512]{1,0:T(1,128)S(1)}, u32[]{:S(2)}, u32[]{:S(2)}) collective-permute-start(f32[1,512]{1,0:T(1,128)S(1)} %copy-done.2), channel_id=1, source_target_pairs={{0,1},{1,0},{2,3},{3,2},{4,5},{5,4},{6,7},{7,6},{8,9},{9,8},{10,11... | collective-permute-start | bytes 6152 | tf_op jit(solution)/shard_map/ppermute | solution.py:316
  14.3 12.2 %copy-start.8 = (f32[2,4,128]{2,1,0:T(4,128)S(1)}, f32[2,4,128]{2,1,0:T(4,128)}, u32[]{:S(2)}) copy-start(f32[2,4,128]{2,1,0:T(4,128)} %constant.15.clone.spin_ref) | copy-start | bytes 12292
  14.3 3.7 %collective-permute-start.3 = (f32[1,512]{1,0:T(1,128)S(1)}, f32[1,512]{1,0:T(1,128)S(1)}, u32[]{:S(2)}, u32[]{:S(2)}) collective-permute-start(f32[1,512]{1,0:T(1,128)S(1)} %shard_map.119.scale_ref), channel_id=1, source_target_pairs={{0,4},{4,0},{8,12},{12,8},{16,20},{20,16},{24,28},{28,24},{1,5},{5... | collective-permute-start | bytes 6152 | tf_op jit(solution)/shard_map/ppermute | solution.py:316
  18.0 5.6 %collective-permute-start.6 = (f32[2,512]{1,0:T(2,128)S(1)}, f32[2,512]{1,0:T(2,128)S(1)}, u32[]{:S(2)}, u32[]{:S(2)}) collective-permute-start(f32[2,512]{1,0:T(2,128)S(1)} %pad_maximum_fusion.refs_0_), channel_id=1, source_target_pairs={{0,24},{4,28},{8,16},{12,20},{16,8},{20,12},{24,0},{28,4},{1,25},{... | collective-permute-start | bytes 12296 | tf_op jit(solution)/shard_map/ppermute | solution.py:316
  19.6 5.8 %collective-permute-start.5 = (f32[2,512]{1,0:T(2,128)S(1)}, f32[2,512]{1,0:T(2,128)S(1)}, u32[]{:S(2)}, u32[]{:S(2)}) collective-permute-start(f32[2,512]{1,0:T(2,128)S(1)} %pad_maximum_fusion.refs_0_), channel_id=1, source_target_pairs={{0,16},{4,20},{8,24},{12,28},{16,0},{20,4},{24,8},{28,12},{1,17},{... | collective-permute-start | bytes 12296 | tf_op jit(solution)/shard_map/ppermute | solution.py:316
  20.1 5.2 %collective-permute-start.4 = (f32[2,512]{1,0:T(2,128)S(1)}, f32[2,512]{1,0:T(2,128)S(1)}, u32[]{:S(2)}, u32[]{:S(2)}) collective-permute-start(f32[2,512]{1,0:T(2,128)S(1)} %pad_maximum_fusion.refs_0_), channel_id=1, source_target_pairs={{0,8},{4,12},{8,0},{12,4},{16,24},{20,28},{24,16},{28,20},{1,9},{5... | collective-permute-start | bytes 12296 | tf_op jit(solution)/shard_map/ppermute | solution.py:316
  27.6 8.6 %copy-start = (bf16[512,128]{1,0:T(8,128)(2,1)S(1)}, bf16[512,128]{1,0:T(8,128)(2,1)}, u32[]{:S(2)}) copy-start(bf16[512,128]{1,0:T(8,128)(2,1)} %post_ref.1) | copy-start | bytes 393220
  27.6 8.6 %copy-start.1 = (bf16[128,512]{1,0:T(8,128)(2,1)S(1)}, bf16[128,512]{1,0:T(8,128)(2,1)}, u32[]{:S(2)}) copy-start(bf16[128,512]{1,0:T(8,128)(2,1)} %get-tuple-element.10.skipped_ref) | copy-start | bytes 393220

commit v9 on v8

--- a/solution.py
+++ b/solution.py
@@ -15,10 +15,19 @@
 WHOLE_VMEM = 63 * 1024 * 1024 + 512 * 1024
 
 
-def order_of(places, back=False):
+def order_of(places, odd, back=False):
     if places != 8:
         return tuple(range(places))
-    return (5, 1, 3, 6, 2, 4, 0, 7) if back else (4, 7, 1, 2, 5, 6, 0, 3)
+    order = (5, 1, 3, 6, 2, 4, 0, 7) if back else (4, 7, 1, 2, 5, 6, 0, 3)
+    return tuple(place ^ (4 if odd and not back else 0) for place in order)
+
+
+def rank_of(place, places, odd, back=False):
+    return jnp.where(odd, order_of(places, True, back).index(place), order_of(places, False, back).index(place))
+
+
+def is_odd():
+    return lax.axis_index("chan") % 2 == 1
 
 
 def reverse_bits(index, levels):
@@ -52,7 +61,7 @@
     levels = places.bit_length() - 1
 
     def holder(residue):
-        return order_of(places).index(reverse_bits(residue // 2, levels)), residue % 2
+        return reverse_bits(residue // 2, levels), residue % 2
 
     mirrors = [None if residue % places == 0 else holder(2 * places - residue) for residue in range(places + 1)]
     return [holder(residue) for residue in range(places + 1)], mirrors
@@ -125,11 +134,13 @@
         copy.start()
         leaving.append(copy)
 
+    odd = is_odd()
+
     def pack(slot, turned):
         if len(packed_ref.shape) == 4:
             places, width = packed_out.shape[1:3]
-            for rank, place in enumerate(order_of(places)):
-                packed_out[slot, rank] = turned[place * width : (place + 1) * width]
+            for place in range(places):
+                packed_out[slot, rank_of(place, places, odd)] = turned[place * width : (place + 1) * width]
             leave(packed_out.at[slot], packed_ref.at[:, slot])
         else:
             packed_out[slot] = turned
@@ -184,7 +195,8 @@
     wide, rows = out_ref.shape
     places, width = scales.shape[0], wide // scales.shape[0]
     block, inner = rows // 4, mirror.shape[0] // 8
-    order = order_of(places)
+    odd = is_odd()
+    ranks = [rank_of(at, places, odd) for at in range(places)]
     direct, mirrors = pair_rows(places)
     quarters = [pl.ds(turn * block, block) for turn in range(4)]
     groups = [range(begin, min(begin + 3, places + 1)) for begin in range(0, places + 1, 3)]
@@ -192,14 +204,14 @@
         for part in range(2):
             for turn in range(4):
                 at = pl.ds((part * 4 + 3 - turn) * inner + row * width, width)
-                mirror[at, :] = packed_ref[holder[0], 2 * part + holder[1], :, quarters[turn]]
+                mirror[at, :] = packed_ref[ranks[holder[0]], 2 * part + holder[1], :, quarters[turn]]
     reversed_bins = matmul(mirror[...], reverse_ref[...])
     place = lax.axis_index("seq")
     for scale_ref, steps in zip(scale_refs, hops(places)):
         for at, step in enumerate(steps):
             scales[place ^ step] = scale_ref[pl.ds(at, 1), :]
-    for rank, at in enumerate(order):
-        signal[pl.ds(at * width, width), :] = (packed_ref[rank, 4].astype(F32) * scales[at]).astype(BF16)
+    for at in range(places):
+        signal[pl.ds(at * width, width), :] = (packed_ref[ranks[at], 4].astype(F32) * scales[at]).astype(BF16)
     spectral = []
     for group in groups:
         begin = group[0] * width
@@ -227,8 +239,8 @@
                 row = (turn * len(group) + at) * width
                 real, imag = values[row : row + width, :block], values[row : row + width, block:]
                 holder = direct[residue]
-                response_real = packed_ref[holder[0], holder[1], :, quarters[turn]].astype(F32)
-                response_imag = packed_ref[holder[0], 2 + holder[1], :, quarters[turn]].astype(F32)
+                response_real = packed_ref[ranks[holder[0]], holder[1], :, quarters[turn]].astype(F32)
+                response_imag = packed_ref[ranks[holder[0]], 2 + holder[1], :, quarters[turn]].astype(F32)
                 if mirrors[residue] is not None:
                     other = turn * inner + (residue - 1) * width
                     response_real = response_real + reversed_bins[other : other + width]
@@ -253,7 +265,7 @@
                 both[pl.ds(2 * residue * width, width), lanes] = (real * cos - imag * sin).astype(BF16)
                 both[pl.ds((2 * residue + 1) * width, width), lanes] = (imag * cos + real * sin).astype(BF16)
     result = matmul(last_ref[...], both[...]).astype(BF16)
-    for rank, at in enumerate(order_of(places, back=True)):
+    for rank, at in enumerate(order_of(places, False, back=True)):
         out_ref[pl.ds(rank * width, width), :] = result[at * width : (at + 1) * width]
 
 
@@ -291,7 +303,7 @@
 def finish_kernel(conv_ref, skipped_ref, scale_ref, post_ref, out_ref):
     conv = conv_ref[...]
     if len(conv_ref.shape) == 3:
-        order = order_of(conv_ref.shape[0], back=True)
+        order = order_of(conv_ref.shape[0], False, back=True)
         conv = jnp.concatenate([conv_ref[order.index(place)] for place in range(len(order))])
     turned = conv.astype(F32) + skipped_ref[...].astype(F32) * scale_ref[...]
     out_ref[...] = (post_ref[...].astype(F32) * turned.T).astype(BF16)
@@ -308,8 +320,10 @@
 
 
 def exchange(value, back=False):
-    ranks = [list(order_of(lax.axis_size("seq"), back))]
-    return lax.all_to_all(value, "seq", split_axis=0, concat_axis=0, tiled=True, axis_index_groups=ranks)
+    places, groups = lax.axis_size("seq"), lax.axis_size("chan")
+    lists = [[place * groups + index for place in order_of(places, index % 2, back)] for index in range(groups)]
+    both = ("seq", "chan")
+    return lax.all_to_all(value, both, split_axis=0, concat_axis=0, tiled=True, axis_index_groups=lists)
 
 
 def swap(value, axis, apart):

time: 37.3 us -> 38.3 us (1.027)
  waiting for transfers between devices: 8.21 us -> 9.02 us
    all_to_all x1, waiting for transfers between devices: 1.1 us -> 1.54 us  [exchange(): lax.all_to_all(value, both, split_axis=0, concat_axis=0, tiled=True, axis...]
where the time goes in v9:
time: 38.3 us; the launch traced here: 38 us
  starting transfers between devices  16.1 us (42%)
  waiting for transfers between devices  9.02 us (24%)
  blocking collectives  8.58 us (22%)
  Pallas kernels  4.17 us (11%)
    all_to_all x1, blocking collectives, exchange(): lax.all_to_all(value, both, split_axis=0, concat_axis=0, tiled=True, axis...  8.58 us
    ppermute x7, starting transfers between devices, swap(): lax.ppermute(value, axis, [(place, place ^ apart) for place in range(lax....  8.07 us
    all_to_all x1, starting transfers between devices, exchange(): lax.all_to_all(value, both, split_axis=0, concat_axis=0, tiled=True, axis...  7.99 us
    ppermute x7, waiting for transfers between devices, swap(): lax.ppermute(value, axis, [(place, place ^ apart) for place in range(lax....  7.48 us
    pallas_call x4, Pallas kernels, call(): pl.pallas_call(kernel, out_shape=out_shape, compiler_params=pltpu.Compile...  4.17 us
    all_to_all x1, waiting for transfers between devices, exchange(): lax.all_to_all(value, both, split_axis=0, concat_axis=0, tiled=True, axis...  1.54 us
  transfers between devices with their start and end apart: 8, of which 6 were waited for; matrix products, arithmetic and copies ran while one was open for 0% of the time, Pallas kernels for 0%

profile of v9, /device:TPU:0, one launch (start us, length us, event | category | flops | bytes accessed | tf_op | source)
XLA Modules:
  0.0 38.0 jit_solution(5420310030261186203)
XLA Ops:
  0.0 2.3 %shard_map.118 = (f32[1,512]{1,0:T(1,128)}, bf16[128,512]{1,0:T(8,128)(2,1)}, bf16[8,5,16,512]{3,2,1,0:T(8,128)(2,1)}) custom-call(bf16[512,128]{1,0:T(8,128)(2,1)} %features_ref.1, bf16[512,128]{1,0:T(8,128)(2,1)} %pre_ref.1, f32[1,128]{1,0:T(1,128)} %bitcast.4, f32[1,128]{1,0:T(1,128)} %bitcast.5, f32[2,2,512,128]{3,2,1,0:T(8,128)} %spectrum_ref.1), custom_call_target="tpu_custom_call" | custom-call | flops 655360 | bytes 2097152 | tf_op jit(solution)/shard_map/pallas_call | solution.py:313
  2.3 0.0 copy-start.2
  2.3 0.0 copy-start.3
  2.3 0.0 copy-start.4
  2.3 0.0 copy-start.5
  2.3 0.0 copy-start.6
  2.4 0.0 copy-start.7
  2.4 8.0 %all-to-all-start = ((bf16[8,5,16,512]{3,2,1,0:T(8,128)(2,1)}), bf16[8,5,16,512]{3,2,1,0:T(8,128)(2,1)S(1)}, u32[]{:S(2)}, u32[]{:S(2)}) async-start(bf16[8,5,16,512]{3,2,1,0:T(8,128)(2,1)} %get-tuple-element.8), calls=%async_computation | async-start | bytes 1310720 | tf_op jit(solution)/shard_map/all_to_all | solution.py:326
  10.4 0.0 copy-done.2
  10.4 0.2 collective-permute-start.2
  10.5 1.4 %collective-permute-start.1 = (f32[1,512]{1,0:T(1,128)S(1)}, f32[1,512]{1,0:T(1,128)S(1)}, u32[]{:S(2)}, u32[]{:S(2)}) collective-permute-start(f32[1,512]{1,0:T(1,128)S(1)} %copy-done.2), channel_id=1, source_target_pairs={{0,2},{1,3},{2,0},{3,1},{4,6},{5,7},{6,4},{7,5},{8,10},{9,11},{10,... | collective-permute-start | bytes 6152 | tf_op jit(solution)/shard_map/ppermute | solution.py:330
  11.9 0.3 collective-permute-start
  12.2 1.1 %collective-permute-done.2.refs_3_ = f32[1,512]{1,0:T(1,128)S(1)} collective-permute-done((f32[1,512]{1,0:T(1,128)S(1)}, f32[1,512]{1,0:T(1,128)S(1)}, u32[]{:S(2)}, u32[]{:S(2)}) %collective-permute-start.2) | collective-permute-done | bytes 2080 | tf_op jit(solution)/shard_map/ppermute | solution.py:330
  13.4 0.7 %collective-permute-done.1.refs_2_ = f32[1,512]{1,0:T(1,128)S(1)} collective-permute-done((f32[1,512]{1,0:T(1,128)S(1)}, f32[1,512]{1,0:T(1,128)S(1)}, u32[]{:S(2)}, u32[]{:S(2)}) %collective-permute-start.1) | collective-permute-done | bytes 2080 | tf_op jit(solution)/shard_map/ppermute | solution.py:330
  14.1 0.0 collective-permute-done.refs_1_
  14.1 0.0 copy-start.8
  14.1 1.8 %collective-permute-start.3 = (f32[1,512]{1,0:T(1,128)S(1)}, f32[1,512]{1,0:T(1,128)S(1)}, u32[]{:S(2)}, u32[]{:S(2)}) collective-permute-start(f32[1,512]{1,0:T(1,128)S(1)} %shard_map.119.scale_ref), channel_id=1, source_target_pairs={{0,4},{4,0},{8,12},{12,8},{16,20},{20,16},{24,28},{28,24},{1,5},{5... | collective-permute-start | bytes 6152 | tf_op jit(solution)/shard_map/ppermute | solution.py:330
  15.9 1.9 %collective-permute-done.3 = f32[1,512]{1,0:T(1,128)S(1)} collective-permute-done((f32[1,512]{1,0:T(1,128)S(1)}, f32[1,512]{1,0:T(1,128)S(1)}, u32[]{:S(2)}, u32[]{:S(2)}) %collective-permute-start.3) | collective-permute-done | bytes 2080 | tf_op jit(solution)/shard_map/ppermute | solution.py:330
  17.8 3.5 %collective-permute-start.6 = (f32[2,512]{1,0:T(2,128)S(1)}, f32[2,512]{1,0:T(2,128)S(1)}, u32[]{:S(2)}, u32[]{:S(2)}) collective-permute-start(f32[2,512]{1,0:T(2,128)S(1)} %pad_maximum_fusion.refs_0_), channel_id=1, source_target_pairs={{0,24},{4,28},{8,16},{12,20},{16,8},{20,12},{24,0},{28,4},{1,25},{... | collective-permute-start | bytes 12296 | tf_op jit(solution)/shard_map/ppermute | solution.py:330
  21.3 0.0 collective-permute-start.5
  21.3 0.9 %collective-permute-start.4 = (f32[2,512]{1,0:T(2,128)S(1)}, f32[2,512]{1,0:T(2,128)S(1)}, u32[]{:S(2)}, u32[]{:S(2)}) collective-permute-start(f32[2,512]{1,0:T(2,128)S(1)} %pad_maximum_fusion.refs_0_), channel_id=1, source_target_pairs={{0,8},{4,12},{8,0},{12,4},{16,24},{20,28},{24,16},{28,20},{1,9},{5... | collective-permute-start | bytes 12296 | tf_op jit(solution)/shard_map/ppermute | solution.py:330
  22.3 1.8 %collective-permute-done.6.refs_3_ = f32[2,512]{1,0:T(2,128)S(1)} collective-permute-done((f32[2,512]{1,0:T(2,128)S(1)}, f32[2,512]{1,0:T(2,128)S(1)}, u32[]{:S(2)}, u32[]{:S(2)}) %collective-permute-start.6) | collective-permute-done | bytes 4128 | tf_op jit(solution)/shard_map/ppermute | solution.py:330
  24.1 1.9 %collective-permute-done.5.refs_2_ = f32[2,512]{1,0:T(2,128)S(1)} collective-permute-done((f32[2,512]{1,0:T(2,128)S(1)}, f32[2,512]{1,0:T(2,128)S(1)}, u32[]{:S(2)}, u32[]{:S(2)}) %collective-permute-start.5) | collective-permute-done | bytes 4128 | tf_op jit(solution)/shard_map/ppermute | solution.py:330
  26.0 0.0 collective-permute-done.4.refs_1_
  26.0 1.5 %all-to-all-done.packed_ref = bf16[8,5,16,512]{3,2,1,0:T(8,128)(2,1)S(1)} async-done(((bf16[8,5,16,512]{3,2,1,0:T(8,128)(2,1)}), bf16[8,5,16,512]{3,2,1,0:T(8,128)(2,1)S(1)}, u32[]{:S(2)}, u32[]{:S(2)}) %all-to-all-start) | async-done | bytes 655392 | tf_op jit(solution)/shard_map/all_to_all | solution.py:326
  27.5 0.0 copy-done.3
  27.5 0.0 copy-done.4
  27.5 1.1 %shard_map.120 = bf16[128,512]{1,0:T(8,128)(2,1)S(1)} custom-call(bf16[8,5,16,512]{3,2,1,0:T(8,128)(2,1)S(1)} %all-to-all-done.packed_ref, bf16[288,128]{1,0:T(8,128)(2,1)S(1)} %copy-done.5, bf16[128,288]{1,0:T(8,128)(2,1)S(1)} %copy-done.4, f32[2,9,512]{2,1,0:T(8,128)S(1)} %copy-done.6, f32[2,4,128]{2,1,0:T(4,128)S(1)} %copy-done.8, ...), custom_call_target="tpu_custom_call" | custom-call | flops 671088640 | bytes 1310720 | tf_op jit(solution)/shard_map/pallas_call | solution.py:313
  28.6 0.0 copy-start
  28.6 0.0 copy-start.1
  28.6 8.6 %all_to_all.10.conv_ref = bf16[8,16,512]{2,1,0:T(8,128)(2,1)S(1)} all-to-all(bf16[8,16,512]{2,1,0:T(8,128)(2,1)S(1)} %bitcast.3), channel_id=1, replica_groups={{20,4,12,24,8,16,0,28},{21,5,13,25,9,17,1,29},{22,6,14,26,10,18,2,30},{..., dimensions={0} | all-to-all | bytes 262144 | tf_op jit(solution)/shard_map/all_to_all | solution.py:326
  37.2 0.8 %shard_map.121 = bf16[512,128]{1,0:T(8,128)(2,1)} custom-call(bf16[8,16,512]{2,1,0:T(8,128)(2,1)S(1)} %all_to_all.10.conv_ref, bf16[128,512]{1,0:T(8,128)(2,1)S(1)} %copy-done.1, f32[1,512]{1,0:T(1,128)S(1)} %shard_map.119.scale_ref, bf16[512,128]{1,0:T(8,128)(2,1)S(1)} %copy-done), custom_call_target="tpu_custom_call" | custom-call | flops 655360 | bytes 524288 | tf_op jit(solution)/shard_map/pallas_call | solution.py:313
  (8 shorter events, 0.0 us)
Async XLA Ops:
  2.3 8.1 %copy-start.2 = (f32[1,512]{1,0:T(1,128)S(1)}, f32[1,512]{1,0:T(1,128)}, u32[]{:S(2)}) copy-start(f32[1,512]{1,0:T(1,128)} %get-tuple-element.9.refs_0_) | copy-start | bytes 6148
  2.3 25.2 %copy-start.3 = (bf16[2,256,256]{2,1,0:T(8,128)(2,1)S(1)}, bf16[2,256,256]{2,1,0:T(8,128)(2,1)}, u32[]{:S(2)}) copy-start(bf16[2,256,256]{2,1,0:T(8,128)(2,1)} %constant.16.clone.dft_ref) | copy-start | bytes 786436
  2.3 25.2 %copy-start.4 = (bf16[128,288]{1,0:T(8,128)(2,1)S(1)}, bf16[128,288]{1,0:T(8,128)(2,1)}, u32[]{:S(2)}) copy-start(bf16[128,288]{1,0:T(8,128)(2,1)} %constant.13.clone.last_ref) | copy-start | bytes 221188
  2.3 25.2 %copy-start.5 = (bf16[288,128]{1,0:T(8,128)(2,1)S(1)}, bf16[288,128]{1,0:T(8,128)(2,1)}, u32[]{:S(2)}) copy-start(bf16[288,128]{1,0:T(8,128)(2,1)} %constant.12.clone.first_ref) | copy-start | bytes 221188
  2.3 25.2 %copy-start.6 = (f32[2,9,512]{2,1,0:T(8,128)S(1)}, f32[2,9,512]{2,1,0:T(8,128)}, u32[]{:S(2)}) copy-start(f32[2,9,512]{2,1,0:T(8,128)} %constant.14.clone.twist_ref) | copy-start | bytes 110596
  2.4 25.2 %copy-start.7 = (bf16[128,128]{1,0:T(8,128)(2,1)S(1)}, bf16[128,128]{1,0:T(8,128)(2,1)}, u32[]{:S(2)}) copy-start(bf16[128,128]{1,0:T(8,128)(2,1)} %constant.17.clone.reverse_ref) | copy-start | bytes 98308
  2.4 25.1 %all-to-all-start = ((bf16[8,5,16,512]{3,2,1,0:T(8,128)(2,1)}), bf16[8,5,16,512]{3,2,1,0:T(8,128)(2,1)S(1)}, u32[]{:S(2)}, u32[]{:S(2)}) async-start(bf16[8,5,16,512]{3,2,1,0:T(8,128)(2,1)} %get-tuple-element.8), calls=%async_computation | async-start | bytes 1310720 | tf_op jit(solution)/shard_map/all_to_all | solution.py:326
  10.4 3.0 %collective-permute-start.2 = (f32[1,512]{1,0:T(1,128)S(1)}, f32[1,512]{1,0:T(1,128)S(1)}, u32[]{:S(2)}, u32[]{:S(2)}) collective-permute-start(f32[1,512]{1,0:T(1,128)S(1)} %copy-done.2), channel_id=1, source_target_pairs={{0,3},{1,2},{2,1},{3,0},{4,7},{5,6},{6,5},{7,4},{8,11},{9,10},{10,... | collective-permute-start | bytes 6152 | tf_op jit(solution)/shard_map/ppermute | solution.py:330
  10.5 3.6 %collective-permute-start.1 = (f32[1,512]{1,0:T(1,128)S(1)}, f32[1,512]{1,0:T(1,128)S(1)}, u32[]{:S(2)}, u32[]{:S(2)}) collective-permute-start(f32[1,512]{1,0:T(1,128)S(1)} %copy-done.2), channel_id=1, source_target_pairs={{0,2},{1,3},{2,0},{3,1},{4,6},{5,7},{6,4},{7,5},{8,10},{9,11},{10,... | collective-permute-start | bytes 6152 | tf_op jit(solution)/shard_map/ppermute | solution.py:330
  11.9 2.2 %collective-permute-start = (f32[1,512]{1,0:T(1,128)S(1)}, f32[1,512]{1,0:T(1,128)S(1)}, u32[]{:S(2)}, u32[]{:S(2)}) collective-permute-start(f32[1,512]{1,0:T(1,128)S(1)} %copy-done.2), channel_id=1, source_target_pairs={{0,1},{1,0},{2,3},{3,2},{4,5},{5,4},{6,7},{7,6},{8,9},{9,8},{10,11... | collective-permute-start | bytes 6152 | tf_op jit(solution)/shard_map/ppermute | solution.py:330
  14.1 13.4 %copy-start.8 = (f32[2,4,128]{2,1,0:T(4,128)S(1)}, f32[2,4,128]{2,1,0:T(4,128)}, u32[]{:S(2)}) copy-start(f32[2,4,128]{2,1,0:T(4,128)} %constant.15.clone.spin_ref) | copy-start | bytes 12292
  14.1 3.7 %collective-permute-start.3 = (f32[1,512]{1,0:T(1,128)S(1)}, f32[1,512]{1,0:T(1,128)S(1)}, u32[]{:S(2)}, u32[]{:S(2)}) collective-permute-start(f32[1,512]{1,0:T(1,128)S(1)} %shard_map.119.scale_ref), channel_id=1, source_target_pairs={{0,4},{4,0},{8,12},{12,8},{16,20},{20,16},{24,28},{28,24},{1,5},{5... | collective-permute-start | bytes 6152 | tf_op jit(solution)/shard_map/ppermute | solution.py:330
  17.8 6.3 %collective-permute-start.6 = (f32[2,512]{1,0:T(2,128)S(1)}, f32[2,512]{1,0:T(2,128)S(1)}, u32[]{:S(2)}, u32[]{:S(2)}) collective-permute-start(f32[2,512]{1,0:T(2,128)S(1)} %pad_maximum_fusion.refs_0_), channel_id=1, source_target_pairs={{0,24},{4,28},{8,16},{12,20},{16,8},{20,12},{24,0},{28,4},{1,25},{... | collective-permute-start | bytes 12296 | tf_op jit(solution)/shard_map/ppermute | solution.py:330
  21.3 4.6 %collective-permute-start.5 = (f32[2,512]{1,0:T(2,128)S(1)}, f32[2,512]{1,0:T(2,128)S(1)}, u32[]{:S(2)}, u32[]{:S(2)}) collective-permute-start(f32[2,512]{1,0:T(2,128)S(1)} %pad_maximum_fusion.refs_0_), channel_id=1, source_target_pairs={{0,16},{4,20},{8,24},{12,28},{16,0},{20,4},{24,8},{28,12},{1,17},{... | collective-permute-start | bytes 12296 | tf_op jit(solution)/shard_map/ppermute | solution.py:330
  21.3 4.6 %collective-permute-start.4 = (f32[2,512]{1,0:T(2,128)S(1)}, f32[2,512]{1,0:T(2,128)S(1)}, u32[]{:S(2)}, u32[]{:S(2)}) collective-permute-start(f32[2,512]{1,0:T(2,128)S(1)} %pad_maximum_fusion.refs_0_), channel_id=1, source_target_pairs={{0,8},{4,12},{8,0},{12,4},{16,24},{20,28},{24,16},{28,20},{1,9},{5... | collective-permute-start | bytes 12296 | tf_op jit(solution)/shard_map/ppermute | solution.py:330
  28.6 8.6 %copy-start = (bf16[512,128]{1,0:T(8,128)(2,1)S(1)}, bf16[512,128]{1,0:T(8,128)(2,1)}, u32[]{:S(2)}) copy-start(bf16[512,128]{1,0:T(8,128)(2,1)} %post_ref.1) | copy-start | bytes 393220
  28.6 8.6 %copy-start.1 = (bf16[128,512]{1,0:T(8,128)(2,1)S(1)}, bf16[128,512]{1,0:T(8,128)(2,1)}, u32[]{:S(2)}) copy-start(bf16[128,512]{1,0:T(8,128)(2,1)} %get-tuple-element.10.skipped_ref) | copy-start | bytes 393220

commit v10 on v8

--- a/solution.py
+++ b/solution.py
@@ -18,7 +18,7 @@
 def order_of(places, back=False):
     if places != 8:
         return tuple(range(places))
-    return (5, 1, 3, 6, 2, 4, 0, 7) if back else (4, 7, 1, 2, 5, 6, 0, 3)
+    return (5, 3, 4, 6, 7, 0, 1, 2) if back else (4, 7, 1, 2, 5, 6, 0, 3)
 
 
 def reverse_bits(index, levels):

time: 37.3 us -> 37.8 us (1.013)
  blocking collectives: 8.58 us -> 9.11 us
    all_to_all x1, blocking collectives: 8.58 us -> 9.11 us  [exchange(): lax.all_to_all(value, 'seq', split_axis=0, concat_axis=0, tiled=True, axi...]
where the time goes in v10:
time: 37.8 us; the launch traced here: 37.5 us
  starting transfers between devices  15.8 us (42%)
  blocking collectives  9.11 us (24%)
  waiting for transfers between devices  8.21 us (22%)
  Pallas kernels  4.18 us (11%)
    all_to_all x1, blocking collectives, exchange(): lax.all_to_all(value, 'seq', split_axis=0, concat_axis=0, tiled=True, axi...  9.11 us
    all_to_all x1, starting transfers between devices, exchange(): lax.all_to_all(value, 'seq', split_axis=0, concat_axis=0, tiled=True, axi...  7.99 us
    ppermute x7, starting transfers between devices, swap(): lax.ppermute(value, axis, [(place, place ^ apart) for place in range(lax....  7.86 us
    ppermute x7, waiting for transfers between devices, swap(): lax.ppermute(value, axis, [(place, place ^ apart) for place in range(lax....  7.11 us
    pallas_call x4, Pallas kernels, call(): pl.pallas_call(kernel, out_shape=out_shape, compiler_params=pltpu.Compile...  4.18 us
    all_to_all x1, waiting for transfers between devices, exchange(): lax.all_to_all(value, 'seq', split_axis=0, concat_axis=0, tiled=True, axi...  1.1 us
  transfers between devices with their start and end apart: 8, of which 6 were waited for; matrix products, arithmetic and copies ran while one was open for 0% of the time, Pallas kernels for 0%

profile of v10, /device:TPU:0, one launch (start us, length us, event | category | flops | bytes accessed | tf_op | source)
XLA Modules:
  0.0 37.5 jit_solution(6206337862083025667)
XLA Ops:
  0.0 2.3 %shard_map.118 = (f32[1,512]{1,0:T(1,128)}, bf16[128,512]{1,0:T(8,128)(2,1)}, bf16[8,5,16,512]{3,2,1,0:T(8,128)(2,1)}) custom-call(bf16[512,128]{1,0:T(8,128)(2,1)} %features_ref.1, bf16[512,128]{1,0:T(8,128)(2,1)} %pre_ref.1, f32[1,128]{1,0:T(1,128)} %bitcast.4, f32[1,128]{1,0:T(1,128)} %bitcast.5, f32[2,2,512,128]{3,2,1,0:T(8,128)} %spectrum_ref.1), custom_call_target="tpu_custom_call" | custom-call | flops 655360 | bytes 2097152 | tf_op jit(solution)/shard_map/pallas_call | solution.py:301
  2.3 0.0 copy-start.2
  2.3 0.0 copy-start.3
  2.3 0.0 copy-start.4
  2.3 0.0 copy-start.5
  2.3 0.0 copy-start.6
  2.4 0.0 copy-start.7
  2.4 8.0 %all-to-all-start = ((bf16[8,5,16,512]{3,2,1,0:T(8,128)(2,1)}), bf16[8,5,16,512]{3,2,1,0:T(8,128)(2,1)S(1)}, u32[]{:S(2)}, u32[]{:S(2)}) async-start(bf16[8,5,16,512]{3,2,1,0:T(8,128)(2,1)} %get-tuple-element.8), calls=%async_computation | async-start | bytes 1310720 | tf_op jit(solution)/shard_map/all_to_all | solution.py:312
  10.4 0.4 collective-permute-start.2
  10.7 1.2 %collective-permute-start.1 = (f32[1,512]{1,0:T(1,128)S(1)}, f32[1,512]{1,0:T(1,128)S(1)}, u32[]{:S(2)}, u32[]{:S(2)}) collective-permute-start(f32[1,512]{1,0:T(1,128)S(1)} %copy-done.2), channel_id=1, source_target_pairs={{0,2},{1,3},{2,0},{3,1},{4,6},{5,7},{6,4},{7,5},{8,10},{9,11},{10,... | collective-permute-start | bytes 6152 | tf_op jit(solution)/shard_map/ppermute | solution.py:316
  11.9 0.3 collective-permute-start
  12.2 1.1 %collective-permute-done.2.refs_3_ = f32[1,512]{1,0:T(1,128)S(1)} collective-permute-done((f32[1,512]{1,0:T(1,128)S(1)}, f32[1,512]{1,0:T(1,128)S(1)}, u32[]{:S(2)}, u32[]{:S(2)}) %collective-permute-start.2) | collective-permute-done | bytes 2080 | tf_op jit(solution)/shard_map/ppermute | solution.py:316
  13.4 0.9 %collective-permute-done.1.refs_2_ = f32[1,512]{1,0:T(1,128)S(1)} collective-permute-done((f32[1,512]{1,0:T(1,128)S(1)}, f32[1,512]{1,0:T(1,128)S(1)}, u32[]{:S(2)}, u32[]{:S(2)}) %collective-permute-start.1) | collective-permute-done | bytes 2080 | tf_op jit(solution)/shard_map/ppermute | solution.py:316
  14.3 0.0 collective-permute-done.refs_1_
  14.3 0.0 copy-start.8
  14.3 1.5 %collective-permute-start.3 = (f32[1,512]{1,0:T(1,128)S(1)}, f32[1,512]{1,0:T(1,128)S(1)}, u32[]{:S(2)}, u32[]{:S(2)}) collective-permute-start(f32[1,512]{1,0:T(1,128)S(1)} %shard_map.119.scale_ref), channel_id=1, source_target_pairs={{0,4},{4,0},{8,12},{12,8},{16,20},{20,16},{24,28},{28,24},{1,5},{5... | collective-permute-start | bytes 6152 | tf_op jit(solution)/shard_map/ppermute | solution.py:316
  15.9 2.1 %collective-permute-done.3 = f32[1,512]{1,0:T(1,128)S(1)} collective-permute-done((f32[1,512]{1,0:T(1,128)S(1)}, f32[1,512]{1,0:T(1,128)S(1)}, u32[]{:S(2)}, u32[]{:S(2)}) %collective-permute-start.3) | collective-permute-done | bytes 2080 | tf_op jit(solution)/shard_map/ppermute | solution.py:316
  18.0 1.6 %collective-permute-start.6 = (f32[2,512]{1,0:T(2,128)S(1)}, f32[2,512]{1,0:T(2,128)S(1)}, u32[]{:S(2)}, u32[]{:S(2)}) collective-permute-start(f32[2,512]{1,0:T(2,128)S(1)} %pad_maximum_fusion.refs_0_), channel_id=1, source_target_pairs={{0,24},{4,28},{8,16},{12,20},{16,8},{20,12},{24,0},{28,4},{1,25},{... | collective-permute-start | bytes 12296 | tf_op jit(solution)/shard_map/ppermute | solution.py:316
  19.6 0.5 %collective-permute-start.5 = (f32[2,512]{1,0:T(2,128)S(1)}, f32[2,512]{1,0:T(2,128)S(1)}, u32[]{:S(2)}, u32[]{:S(2)}) collective-permute-start(f32[2,512]{1,0:T(2,128)S(1)} %pad_maximum_fusion.refs_0_), channel_id=1, source_target_pairs={{0,16},{4,20},{8,24},{12,28},{16,0},{20,4},{24,8},{28,12},{1,17},{... | collective-permute-start | bytes 12296 | tf_op jit(solution)/shard_map/ppermute | solution.py:316
  20.1 2.4 %collective-permute-start.4 = (f32[2,512]{1,0:T(2,128)S(1)}, f32[2,512]{1,0:T(2,128)S(1)}, u32[]{:S(2)}, u32[]{:S(2)}) collective-permute-start(f32[2,512]{1,0:T(2,128)S(1)} %pad_maximum_fusion.refs_0_), channel_id=1, source_target_pairs={{0,8},{4,12},{8,0},{12,4},{16,24},{20,28},{24,16},{28,20},{1,9},{5... | collective-permute-start | bytes 12296 | tf_op jit(solution)/shard_map/ppermute | solution.py:316
  22.5 1.2 %collective-permute-done.6.refs_3_ = f32[2,512]{1,0:T(2,128)S(1)} collective-permute-done((f32[2,512]{1,0:T(2,128)S(1)}, f32[2,512]{1,0:T(2,128)S(1)}, u32[]{:S(2)}, u32[]{:S(2)}) %collective-permute-start.6) | collective-permute-done | bytes 4128 | tf_op jit(solution)/shard_map/ppermute | solution.py:316
  23.6 1.7 %collective-permute-done.5.refs_2_ = f32[2,512]{1,0:T(2,128)S(1)} collective-permute-done((f32[2,512]{1,0:T(2,128)S(1)}, f32[2,512]{1,0:T(2,128)S(1)}, u32[]{:S(2)}, u32[]{:S(2)}) %collective-permute-start.5) | collective-permute-done | bytes 4128 | tf_op jit(solution)/shard_map/ppermute | solution.py:316
  25.4 0.0 collective-permute-done.4.refs_1_
  25.4 1.1 %all-to-all-done.packed_ref = bf16[8,5,16,512]{3,2,1,0:T(8,128)(2,1)S(1)} async-done(((bf16[8,5,16,512]{3,2,1,0:T(8,128)(2,1)}), bf16[8,5,16,512]{3,2,1,0:T(8,128)(2,1)S(1)}, u32[]{:S(2)}, u32[]{:S(2)}) %all-to-all-start) | async-done | bytes 655392 | tf_op jit(solution)/shard_map/all_to_all | solution.py:312
  26.5 0.0 copy-done.6
  26.5 0.0 copy-done.7
  26.5 0.0 copy-done.8
  26.5 1.1 %shard_map.120 = bf16[128,512]{1,0:T(8,128)(2,1)S(1)} custom-call(bf16[8,5,16,512]{3,2,1,0:T(8,128)(2,1)S(1)} %all-to-all-done.packed_ref, bf16[288,128]{1,0:T(8,128)(2,1)S(1)} %copy-done.5, bf16[128,288]{1,0:T(8,128)(2,1)S(1)} %copy-done.4, f32[2,9,512]{2,1,0:T(8,128)S(1)} %copy-done.6, f32[2,4,128]{2,1,0:T(4,128)S(1)} %copy-done.8, ...), custom_call_target="tpu_custom_call" | custom-call | flops 671088640 | bytes 1310720 | tf_op jit(solution)/shard_map/pallas_call | solution.py:301
  27.6 0.0 copy-start
  27.6 0.0 copy-start.1
  27.6 9.1 %all_to_all.10.conv_ref = bf16[8,16,512]{2,1,0:T(8,128)(2,1)S(1)} all-to-all(bf16[8,16,512]{2,1,0:T(8,128)(2,1)S(1)} %bitcast.3), channel_id=1, replica_groups={{20,12,16,24,28,0,4,8},{21,13,17,25,29,1,5,9},{22,14,18,26,30,2,6,10},{..., dimensions={0} | all-to-all | bytes 262144 | tf_op jit(solution)/shard_map/all_to_all | solution.py:312
  36.7 0.8 %shard_map.121 = bf16[512,128]{1,0:T(8,128)(2,1)} custom-call(bf16[8,16,512]{2,1,0:T(8,128)(2,1)S(1)} %all_to_all.10.conv_ref, bf16[128,512]{1,0:T(8,128)(2,1)S(1)} %copy-done.1, f32[1,512]{1,0:T(1,128)S(1)} %shard_map.119.scale_ref, bf16[512,128]{1,0:T(8,128)(2,1)S(1)} %copy-done), custom_call_target="tpu_custom_call" | custom-call | flops 655360 | bytes 524288 | tf_op jit(solution)/shard_map/pallas_call | solution.py:301
  (8 shorter events, 0.0 us)
Async XLA Ops:
  2.3 8.1 %copy-start.2 = (f32[1,512]{1,0:T(1,128)S(1)}, f32[1,512]{1,0:T(1,128)}, u32[]{:S(2)}) copy-start(f32[1,512]{1,0:T(1,128)} %get-tuple-element.9.refs_0_) | copy-start | bytes 6148
  2.3 24.2 %copy-start.3 = (bf16[2,256,256]{2,1,0:T(8,128)(2,1)S(1)}, bf16[2,256,256]{2,1,0:T(8,128)(2,1)}, u32[]{:S(2)}) copy-start(bf16[2,256,256]{2,1,0:T(8,128)(2,1)} %constant.16.clone.dft_ref) | copy-start | bytes 786436
  2.3 24.2 %copy-start.4 = (bf16[128,288]{1,0:T(8,128)(2,1)S(1)}, bf16[128,288]{1,0:T(8,128)(2,1)}, u32[]{:S(2)}) copy-start(bf16[128,288]{1,0:T(8,128)(2,1)} %constant.13.clone.last_ref) | copy-start | bytes 221188
  2.3 24.1 %copy-start.5 = (bf16[288,128]{1,0:T(8,128)(2,1)S(1)}, bf16[288,128]{1,0:T(8,128)(2,1)}, u32[]{:S(2)}) copy-start(bf16[288,128]{1,0:T(8,128)(2,1)} %constant.12.clone.first_ref) | copy-start | bytes 221188
  2.3 24.1 %copy-start.6 = (f32[2,9,512]{2,1,0:T(8,128)S(1)}, f32[2,9,512]{2,1,0:T(8,128)}, u32[]{:S(2)}) copy-start(f32[2,9,512]{2,1,0:T(8,128)} %constant.14.clone.twist_ref) | copy-start | bytes 110596
  2.4 24.1 %copy-start.7 = (bf16[128,128]{1,0:T(8,128)(2,1)S(1)}, bf16[128,128]{1,0:T(8,128)(2,1)}, u32[]{:S(2)}) copy-start(bf16[128,128]{1,0:T(8,128)(2,1)} %constant.17.clone.reverse_ref) | copy-start | bytes 98308
  2.4 24.1 %all-to-all-start = ((bf16[8,5,16,512]{3,2,1,0:T(8,128)(2,1)}), bf16[8,5,16,512]{3,2,1,0:T(8,128)(2,1)S(1)}, u32[]{:S(2)}, u32[]{:S(2)}) async-start(bf16[8,5,16,512]{3,2,1,0:T(8,128)(2,1)} %get-tuple-element.8), calls=%async_computation | async-start | bytes 1310720 | tf_op jit(solution)/shard_map/all_to_all | solution.py:312
  10.4 3.0 %collective-permute-start.2 = (f32[1,512]{1,0:T(1,128)S(1)}, f32[1,512]{1,0:T(1,128)S(1)}, u32[]{:S(2)}, u32[]{:S(2)}) collective-permute-start(f32[1,512]{1,0:T(1,128)S(1)} %copy-done.2), channel_id=1, source_target_pairs={{0,3},{1,2},{2,1},{3,0},{4,7},{5,6},{6,5},{7,4},{8,11},{9,10},{10,... | collective-permute-start | bytes 6152 | tf_op jit(solution)/shard_map/ppermute | solution.py:316
  10.7 3.6 %collective-permute-start.1 = (f32[1,512]{1,0:T(1,128)S(1)}, f32[1,512]{1,0:T(1,128)S(1)}, u32[]{:S(2)}, u32[]{:S(2)}) collective-permute-start(f32[1,512]{1,0:T(1,128)S(1)} %copy-done.2), channel_id=1, source_target_pairs={{0,2},{1,3},{2,0},{3,1},{4,6},{5,7},{6,4},{7,5},{8,10},{9,11},{10,... | collective-permute-start | bytes 6152 | tf_op jit(solution)/shard_map/ppermute | solution.py:316
  11.9 2.4 %collective-permute-start = (f32[1,512]{1,0:T(1,128)S(1)}, f32[1,512]{1,0:T(1,128)S(1)}, u32[]{:S(2)}, u32[]{:S(2)}) collective-permute-start(f32[1,512]{1,0:T(1,128)S(1)} %copy-done.2), channel_id=1, source_target_pairs={{0,1},{1,0},{2,3},{3,2},{4,5},{5,4},{6,7},{7,6},{8,9},{9,8},{10,11... | collective-permute-start | bytes 6152 | tf_op jit(solution)/shard_map/ppermute | solution.py:316
  14.3 12.2 %copy-start.8 = (f32[2,4,128]{2,1,0:T(4,128)S(1)}, f32[2,4,128]{2,1,0:T(4,128)}, u32[]{:S(2)}) copy-start(f32[2,4,128]{2,1,0:T(4,128)} %constant.15.clone.spin_ref) | copy-start | bytes 12292
  14.3 3.7 %collective-permute-start.3 = (f32[1,512]{1,0:T(1,128)S(1)}, f32[1,512]{1,0:T(1,128)S(1)}, u32[]{:S(2)}, u32[]{:S(2)}) collective-permute-start(f32[1,512]{1,0:T(1,128)S(1)} %shard_map.119.scale_ref), channel_id=1, source_target_pairs={{0,4},{4,0},{8,12},{12,8},{16,20},{20,16},{24,28},{28,24},{1,5},{5... | collective-permute-start | bytes 6152 | tf_op jit(solution)/shard_map/ppermute | solution.py:316
  18.0 5.6 %collective-permute-start.6 = (f32[2,512]{1,0:T(2,128)S(1)}, f32[2,512]{1,0:T(2,128)S(1)}, u32[]{:S(2)}, u32[]{:S(2)}) collective-permute-start(f32[2,512]{1,0:T(2,128)S(1)} %pad_maximum_fusion.refs_0_), channel_id=1, source_target_pairs={{0,24},{4,28},{8,16},{12,20},{16,8},{20,12},{24,0},{28,4},{1,25},{... | collective-permute-start | bytes 12296 | tf_op jit(solution)/shard_map/ppermute | solution.py:316
  19.6 5.8 %collective-permute-start.5 = (f32[2,512]{1,0:T(2,128)S(1)}, f32[2,512]{1,0:T(2,128)S(1)}, u32[]{:S(2)}, u32[]{:S(2)}) collective-permute-start(f32[2,512]{1,0:T(2,128)S(1)} %pad_maximum_fusion.refs_0_), channel_id=1, source_target_pairs={{0,16},{4,20},{8,24},{12,28},{16,0},{20,4},{24,8},{28,12},{1,17},{... | collective-permute-start | bytes 12296 | tf_op jit(solution)/shard_map/ppermute | solution.py:316
  20.1 5.2 %collective-permute-start.4 = (f32[2,512]{1,0:T(2,128)S(1)}, f32[2,512]{1,0:T(2,128)S(1)}, u32[]{:S(2)}, u32[]{:S(2)}) collective-permute-start(f32[2,512]{1,0:T(2,128)S(1)} %pad_maximum_fusion.refs_0_), channel_id=1, source_target_pairs={{0,8},{4,12},{8,0},{12,4},{16,24},{20,28},{24,16},{28,20},{1,9},{5... | collective-permute-start | bytes 12296 | tf_op jit(solution)/shard_map/ppermute | solution.py:316
  27.6 9.1 %copy-start = (bf16[512,128]{1,0:T(8,128)(2,1)S(1)}, bf16[512,128]{1,0:T(8,128)(2,1)}, u32[]{:S(2)}) copy-start(bf16[512,128]{1,0:T(8,128)(2,1)} %post_ref.1) | copy-start | bytes 393220
  27.6 9.1 %copy-start.1 = (bf16[128,512]{1,0:T(8,128)(2,1)S(1)}, bf16[128,512]{1,0:T(8,128)(2,1)}, u32[]{:S(2)}) copy-start(bf16[128,512]{1,0:T(8,128)(2,1)} %get-tuple-element.10.skipped_ref) | copy-start | bytes 393220

commit v11 on v10

--- a/solution.py
+++ b/solution.py
@@ -18,7 +18,7 @@
 def order_of(places, back=False):
     if places != 8:
         return tuple(range(places))
-    return (5, 3, 4, 6, 7, 0, 1, 2) if back else (4, 7, 1, 2, 5, 6, 0, 3)
+    return (5, 4, 3, 2, 1, 0, 7, 6) if back else (4, 7, 1, 2, 5, 6, 0, 3)
 
 
 def reverse_bits(index, levels):

time: 37.8 us -> 37.3 us (0.987)
  blocking collectives: 9.11 us -> 8.59 us
    all_to_all x1, blocking collectives: 9.11 us -> 8.59 us  [exchange(): lax.all_to_all(value, 'seq', split_axis=0, concat_axis=0, tiled=True, axi...]
where the time goes in v11:
time: 37.3 us; the launch traced here: 37 us
  starting transfers between devices  15.8 us (42%)
  blocking collectives  8.59 us (23%)
  waiting for transfers between devices  8.21 us (22%)
  Pallas kernels  4.18 us (11%)
    all_to_all x1, blocking collectives, exchange(): lax.all_to_all(value, 'seq', split_axis=0, concat_axis=0, tiled=True, axi...  8.59 us
    all_to_all x1, starting transfers between devices, exchange(): lax.all_to_all(value, 'seq', split_axis=0, concat_axis=0, tiled=True, axi...  7.99 us
    ppermute x7, starting transfers between devices, swap(): lax.ppermute(value, axis, [(place, place ^ apart) for place in range(lax....  7.86 us
    ppermute x7, waiting for transfers between devices, swap(): lax.ppermute(value, axis, [(place, place ^ apart) for place in range(lax....  7.11 us
    pallas_call x4, Pallas kernels, call(): pl.pallas_call(kernel, out_shape=out_shape, compiler_params=pltpu.Compile...  4.18 us
    all_to_all x1, waiting for transfers between devices, exchange(): lax.all_to_all(value, 'seq', split_axis=0, concat_axis=0, tiled=True, axi...  1.1 us
  transfers between devices with their start and end apart: 8, of which 6 were waited for; matrix products, arithmetic and copies ran while one was open for 0% of the time, Pallas kernels for 0%

profile of v11, /device:TPU:0, one launch (start us, length us, event | category | flops | bytes accessed | tf_op | source)
XLA Modules:
  0.0 37.0 jit_solution(10355732457581789619)
XLA Ops:
  0.0 2.3 %shard_map.118 = (f32[1,512]{1,0:T(1,128)}, bf16[128,512]{1,0:T(8,128)(2,1)}, bf16[8,5,16,512]{3,2,1,0:T(8,128)(2,1)}) custom-call(bf16[512,128]{1,0:T(8,128)(2,1)} %features_ref.1, bf16[512,128]{1,0:T(8,128)(2,1)} %pre_ref.1, f32[1,128]{1,0:T(1,128)} %bitcast.4, f32[1,128]{1,0:T(1,128)} %bitcast.5, f32[2,2,512,128]{3,2,1,0:T(8,128)} %spectrum_ref.1), custom_call_target="tpu_custom_call" | custom-call | flops 655360 | bytes 2097152 | tf_op jit(solution)/shard_map/pallas_call | solution.py:301
  2.3 0.0 copy-start.2
  2.3 0.0 copy-start.3
  2.3 0.0 copy-start.4
  2.3 0.0 copy-start.5
  2.3 0.0 copy-start.6
  2.4 0.0 copy-start.7
  2.4 8.0 %all-to-all-start = ((bf16[8,5,16,512]{3,2,1,0:T(8,128)(2,1)}), bf16[8,5,16,512]{3,2,1,0:T(8,128)(2,1)S(1)}, u32[]{:S(2)}, u32[]{:S(2)}) async-start(bf16[8,5,16,512]{3,2,1,0:T(8,128)(2,1)} %get-tuple-element.8), calls=%async_computation | async-start | bytes 1310720 | tf_op jit(solution)/shard_map/all_to_all | solution.py:312
  10.4 0.0 copy-done.2
  10.4 0.4 %collective-permute-start.2 = (f32[1,512]{1,0:T(1,128)S(1)}, f32[1,512]{1,0:T(1,128)S(1)}, u32[]{:S(2)}, u32[]{:S(2)}) collective-permute-start(f32[1,512]{1,0:T(1,128)S(1)} %copy-done.2), channel_id=1, source_target_pairs={{0,3},{1,2},{2,1},{3,0},{4,7},{5,6},{6,5},{7,4},{8,11},{9,10},{10,... | collective-permute-start | bytes 6152 | tf_op jit(solution)/shard_map/ppermute | solution.py:316
  10.7 1.2 %collective-permute-start.1 = (f32[1,512]{1,0:T(1,128)S(1)}, f32[1,512]{1,0:T(1,128)S(1)}, u32[]{:S(2)}, u32[]{:S(2)}) collective-permute-start(f32[1,512]{1,0:T(1,128)S(1)} %copy-done.2), channel_id=1, source_target_pairs={{0,2},{1,3},{2,0},{3,1},{4,6},{5,7},{6,4},{7,5},{8,10},{9,11},{10,... | collective-permute-start | bytes 6152 | tf_op jit(solution)/shard_map/ppermute | solution.py:316
  11.9 0.3 collective-permute-start
  12.2 1.1 %collective-permute-done.2.refs_3_ = f32[1,512]{1,0:T(1,128)S(1)} collective-permute-done((f32[1,512]{1,0:T(1,128)S(1)}, f32[1,512]{1,0:T(1,128)S(1)}, u32[]{:S(2)}, u32[]{:S(2)}) %collective-permute-start.2) | collective-permute-done | bytes 2080 | tf_op jit(solution)/shard_map/ppermute | solution.py:316
  13.4 0.9 %collective-permute-done.1.refs_2_ = f32[1,512]{1,0:T(1,128)S(1)} collective-permute-done((f32[1,512]{1,0:T(1,128)S(1)}, f32[1,512]{1,0:T(1,128)S(1)}, u32[]{:S(2)}, u32[]{:S(2)}) %collective-permute-start.1) | collective-permute-done | bytes 2080 | tf_op jit(solution)/shard_map/ppermute | solution.py:316
  14.3 0.0 collective-permute-done.refs_1_
  14.3 0.0 copy-start.8
  14.3 1.5 %collective-permute-start.3 = (f32[1,512]{1,0:T(1,128)S(1)}, f32[1,512]{1,0:T(1,128)S(1)}, u32[]{:S(2)}, u32[]{:S(2)}) collective-permute-start(f32[1,512]{1,0:T(1,128)S(1)} %shard_map.119.scale_ref), channel_id=1, source_target_pairs={{0,4},{4,0},{8,12},{12,8},{16,20},{20,16},{24,28},{28,24},{1,5},{5... | collective-permute-start | bytes 6152 | tf_op jit(solution)/shard_map/ppermute | solution.py:316
  15.9 2.1 %collective-permute-done.3 = f32[1,512]{1,0:T(1,128)S(1)} collective-permute-done((f32[1,512]{1,0:T(1,128)S(1)}, f32[1,512]{1,0:T(1,128)S(1)}, u32[]{:S(2)}, u32[]{:S(2)}) %collective-permute-start.3) | collective-permute-done | bytes 2080 | tf_op jit(solution)/shard_map/ppermute | solution.py:316
  18.0 1.6 %collective-permute-start.6 = (f32[2,512]{1,0:T(2,128)S(1)}, f32[2,512]{1,0:T(2,128)S(1)}, u32[]{:S(2)}, u32[]{:S(2)}) collective-permute-start(f32[2,512]{1,0:T(2,128)S(1)} %pad_maximum_fusion.refs_0_), channel_id=1, source_target_pairs={{0,24},{4,28},{8,16},{12,20},{16,8},{20,12},{24,0},{28,4},{1,25},{... | collective-permute-start | bytes 12296 | tf_op jit(solution)/shard_map/ppermute | solution.py:316
  19.6 0.5 %collective-permute-start.5 = (f32[2,512]{1,0:T(2,128)S(1)}, f32[2,512]{1,0:T(2,128)S(1)}, u32[]{:S(2)}, u32[]{:S(2)}) collective-permute-start(f32[2,512]{1,0:T(2,128)S(1)} %pad_maximum_fusion.refs_0_), channel_id=1, source_target_pairs={{0,16},{4,20},{8,24},{12,28},{16,0},{20,4},{24,8},{28,12},{1,17},{... | collective-permute-start | bytes 12296 | tf_op jit(solution)/shard_map/ppermute | solution.py:316
  20.1 2.4 %collective-permute-start.4 = (f32[2,512]{1,0:T(2,128)S(1)}, f32[2,512]{1,0:T(2,128)S(1)}, u32[]{:S(2)}, u32[]{:S(2)}) collective-permute-start(f32[2,512]{1,0:T(2,128)S(1)} %pad_maximum_fusion.refs_0_), channel_id=1, source_target_pairs={{0,8},{4,12},{8,0},{12,4},{16,24},{20,28},{24,16},{28,20},{1,9},{5... | collective-permute-start | bytes 12296 | tf_op jit(solution)/shard_map/ppermute | solution.py:316
  22.5 1.2 %collective-permute-done.6.refs_3_ = f32[2,512]{1,0:T(2,128)S(1)} collective-permute-done((f32[2,512]{1,0:T(2,128)S(1)}, f32[2,512]{1,0:T(2,128)S(1)}, u32[]{:S(2)}, u32[]{:S(2)}) %collective-permute-start.6) | collective-permute-done | bytes 4128 | tf_op jit(solution)/shard_map/ppermute | solution.py:316
  23.6 1.7 %collective-permute-done.5.refs_2_ = f32[2,512]{1,0:T(2,128)S(1)} collective-permute-done((f32[2,512]{1,0:T(2,128)S(1)}, f32[2,512]{1,0:T(2,128)S(1)}, u32[]{:S(2)}, u32[]{:S(2)}) %collective-permute-start.5) | collective-permute-done | bytes 4128 | tf_op jit(solution)/shard_map/ppermute | solution.py:316
  25.4 0.0 collective-permute-done.4.refs_1_
  25.4 1.1 %all-to-all-done.packed_ref = bf16[8,5,16,512]{3,2,1,0:T(8,128)(2,1)S(1)} async-done(((bf16[8,5,16,512]{3,2,1,0:T(8,128)(2,1)}), bf16[8,5,16,512]{3,2,1,0:T(8,128)(2,1)S(1)}, u32[]{:S(2)}, u32[]{:S(2)}) %all-to-all-start) | async-done | bytes 655392 | tf_op jit(solution)/shard_map/all_to_all | solution.py:312
  26.5 0.0 copy-done.3
  26.5 1.1 %shard_map.120 = bf16[128,512]{1,0:T(8,128)(2,1)S(1)} custom-call(bf16[8,5,16,512]{3,2,1,0:T(8,128)(2,1)S(1)} %all-to-all-done.packed_ref, bf16[288,128]{1,0:T(8,128)(2,1)S(1)} %copy-done.5, bf16[128,288]{1,0:T(8,128)(2,1)S(1)} %copy-done.4, f32[2,9,512]{2,1,0:T(8,128)S(1)} %copy-done.6, f32[2,4,128]{2,1,0:T(4,128)S(1)} %copy-done.8, ...), custom_call_target="tpu_custom_call" | custom-call | flops 671088640 | bytes 1310720 | tf_op jit(solution)/shard_map/pallas_call | solution.py:301
  27.6 0.0 copy-start
  27.6 0.0 copy-start.1
  27.6 8.6 %all_to_all.10.conv_ref = bf16[8,16,512]{2,1,0:T(8,128)(2,1)S(1)} all-to-all(bf16[8,16,512]{2,1,0:T(8,128)(2,1)S(1)} %bitcast.3), channel_id=1, replica_groups={{20,16,12,8,4,0,28,24},{21,17,13,9,5,1,29,25},{22,18,14,10,6,2,30,26},{..., dimensions={0} | all-to-all | bytes 262144 | tf_op jit(solution)/shard_map/all_to_all | solution.py:312
  36.2 0.0 copy-done.1
  36.2 0.8 %shard_map.121 = bf16[512,128]{1,0:T(8,128)(2,1)} custom-call(bf16[8,16,512]{2,1,0:T(8,128)(2,1)S(1)} %all_to_all.10.conv_ref, bf16[128,512]{1,0:T(8,128)(2,1)S(1)} %copy-done.1, f32[1,512]{1,0:T(1,128)S(1)} %shard_map.119.scale_ref, bf16[512,128]{1,0:T(8,128)(2,1)S(1)} %copy-done), custom_call_target="tpu_custom_call" | custom-call | flops 655360 | bytes 524288 | tf_op jit(solution)/shard_map/pallas_call | solution.py:301
  (8 shorter events, 0.0 us)
Async XLA Ops:
  2.3 8.1 %copy-start.2 = (f32[1,512]{1,0:T(1,128)S(1)}, f32[1,512]{1,0:T(1,128)}, u32[]{:S(2)}) copy-start(f32[1,512]{1,0:T(1,128)} %get-tuple-element.9.refs_0_) | copy-start | bytes 6148
  2.3 24.2 %copy-start.3 = (bf16[2,256,256]{2,1,0:T(8,128)(2,1)S(1)}, bf16[2,256,256]{2,1,0:T(8,128)(2,1)}, u32[]{:S(2)}) copy-start(bf16[2,256,256]{2,1,0:T(8,128)(2,1)} %constant.16.clone.dft_ref) | copy-start | bytes 786436
  2.3 24.2 %copy-start.4 = (bf16[128,288]{1,0:T(8,128)(2,1)S(1)}, bf16[128,288]{1,0:T(8,128)(2,1)}, u32[]{:S(2)}) copy-start(bf16[128,288]{1,0:T(8,128)(2,1)} %constant.13.clone.last_ref) | copy-start | bytes 221188
  2.3 24.1 %copy-start.5 = (bf16[288,128]{1,0:T(8,128)(2,1)S(1)}, bf16[288,128]{1,0:T(8,128)(2,1)}, u32[]{:S(2)}) copy-start(bf16[288,128]{1,0:T(8,128)(2,1)} %constant.12.clone.first_ref) | copy-start | bytes 221188
  2.3 24.1 %copy-start.6 = (f32[2,9,512]{2,1,0:T(8,128)S(1)}, f32[2,9,512]{2,1,0:T(8,128)}, u32[]{:S(2)}) copy-start(f32[2,9,512]{2,1,0:T(8,128)} %constant.14.clone.twist_ref) | copy-start | bytes 110596
  2.4 24.1 %copy-start.7 = (bf16[128,128]{1,0:T(8,128)(2,1)S(1)}, bf16[128,128]{1,0:T(8,128)(2,1)}, u32[]{:S(2)}) copy-start(bf16[128,128]{1,0:T(8,128)(2,1)} %constant.17.clone.reverse_ref) | copy-start | bytes 98308
  2.4 24.1 %all-to-all-start = ((bf16[8,5,16,512]{3,2,1,0:T(8,128)(2,1)}), bf16[8,5,16,512]{3,2,1,0:T(8,128)(2,1)S(1)}, u32[]{:S(2)}, u32[]{:S(2)}) async-start(bf16[8,5,16,512]{3,2,1,0:T(8,128)(2,1)} %get-tuple-element.8), calls=%async_computation | async-start | bytes 1310720 | tf_op jit(solution)/shard_map/all_to_all | solution.py:312
  10.4 3.0 %collective-permute-start.2 = (f32[1,512]{1,0:T(1,128)S(1)}, f32[1,512]{1,0:T(1,128)S(1)}, u32[]{:S(2)}, u32[]{:S(2)}) collective-permute-start(f32[1,512]{1,0:T(1,128)S(1)} %copy-done.2), channel_id=1, source_target_pairs={{0,3},{1,2},{2,1},{3,0},{4,7},{5,6},{6,5},{7,4},{8,11},{9,10},{10,... | collective-permute-start | bytes 6152 | tf_op jit(solution)/shard_map/ppermute | solution.py:316
  10.7 3.6 %collective-permute-start.1 = (f32[1,512]{1,0:T(1,128)S(1)}, f32[1,512]{1,0:T(1,128)S(1)}, u32[]{:S(2)}, u32[]{:S(2)}) collective-permute-start(f32[1,512]{1,0:T(1,128)S(1)} %copy-done.2), channel_id=1, source_target_pairs={{0,2},{1,3},{2,0},{3,1},{4,6},{5,7},{6,4},{7,5},{8,10},{9,11},{10,... | collective-permute-start | bytes 6152 | tf_op jit(solution)/shard_map/ppermute | solution.py:316
  11.9 2.4 %collective-permute-start = (f32[1,512]{1,0:T(1,128)S(1)}, f32[1,512]{1,0:T(1,128)S(1)}, u32[]{:S(2)}, u32[]{:S(2)}) collective-permute-start(f32[1,512]{1,0:T(1,128)S(1)} %copy-done.2), channel_id=1, source_target_pairs={{0,1},{1,0},{2,3},{3,2},{4,5},{5,4},{6,7},{7,6},{8,9},{9,8},{10,11... | collective-permute-start | bytes 6152 | tf_op jit(solution)/shard_map/ppermute | solution.py:316
  14.3 12.2 %copy-start.8 = (f32[2,4,128]{2,1,0:T(4,128)S(1)}, f32[2,4,128]{2,1,0:T(4,128)}, u32[]{:S(2)}) copy-start(f32[2,4,128]{2,1,0:T(4,128)} %constant.15.clone.spin_ref) | copy-start | bytes 12292
  14.3 3.7 %collective-permute-start.3 = (f32[1,512]{1,0:T(1,128)S(1)}, f32[1,512]{1,0:T(1,128)S(1)}, u32[]{:S(2)}, u32[]{:S(2)}) collective-permute-start(f32[1,512]{1,0:T(1,128)S(1)} %shard_map.119.scale_ref), channel_id=1, source_target_pairs={{0,4},{4,0},{8,12},{12,8},{16,20},{20,16},{24,28},{28,24},{1,5},{5... | collective-permute-start | bytes 6152 | tf_op jit(solution)/shard_map/ppermute | solution.py:316
  18.0 5.6 %collective-permute-start.6 = (f32[2,512]{1,0:T(2,128)S(1)}, f32[2,512]{1,0:T(2,128)S(1)}, u32[]{:S(2)}, u32[]{:S(2)}) collective-permute-start(f32[2,512]{1,0:T(2,128)S(1)} %pad_maximum_fusion.refs_0_), channel_id=1, source_target_pairs={{0,24},{4,28},{8,16},{12,20},{16,8},{20,12},{24,0},{28,4},{1,25},{... | collective-permute-start | bytes 12296 | tf_op jit(solution)/shard_map/ppermute | solution.py:316
  19.6 5.8 %collective-permute-start.5 = (f32[2,512]{1,0:T(2,128)S(1)}, f32[2,512]{1,0:T(2,128)S(1)}, u32[]{:S(2)}, u32[]{:S(2)}) collective-permute-start(f32[2,512]{1,0:T(2,128)S(1)} %pad_maximum_fusion.refs_0_), channel_id=1, source_target_pairs={{0,16},{4,20},{8,24},{12,28},{16,0},{20,4},{24,8},{28,12},{1,17},{... | collective-permute-start | bytes 12296 | tf_op jit(solution)/shard_map/ppermute | solution.py:316
  20.1 5.2 %collective-permute-start.4 = (f32[2,512]{1,0:T(2,128)S(1)}, f32[2,512]{1,0:T(2,128)S(1)}, u32[]{:S(2)}, u32[]{:S(2)}) collective-permute-start(f32[2,512]{1,0:T(2,128)S(1)} %pad_maximum_fusion.refs_0_), channel_id=1, source_target_pairs={{0,8},{4,12},{8,0},{12,4},{16,24},{20,28},{24,16},{28,20},{1,9},{5... | collective-permute-start | bytes 12296 | tf_op jit(solution)/shard_map/ppermute | solution.py:316
  27.6 8.6 %copy-start = (bf16[512,128]{1,0:T(8,128)(2,1)S(1)}, bf16[512,128]{1,0:T(8,128)(2,1)}, u32[]{:S(2)}) copy-start(bf16[512,128]{1,0:T(8,128)(2,1)} %post_ref.1) | copy-start | bytes 393220
  27.6 8.6 %copy-start.1 = (bf16[128,512]{1,0:T(8,128)(2,1)S(1)}, bf16[128,512]{1,0:T(8,128)(2,1)}, u32[]{:S(2)}) copy-start(bf16[128,512]{1,0:T(8,128)(2,1)} %get-tuple-element.10.skipped_ref) | copy-start | bytes 393220

commit v12 on v11

--- a/solution.py
+++ b/solution.py
@@ -18,7 +18,7 @@
 def order_of(places, back=False):
     if places != 8:
         return tuple(range(places))
-    return (5, 4, 3, 2, 1, 0, 7, 6) if back else (4, 7, 1, 2, 5, 6, 0, 3)
+    return (5, 1, 3, 6, 2, 4, 0, 7) if back else (4, 7, 3, 6, 2, 1, 5, 0)
 
 
 def reverse_bits(index, levels):

time: 37.3 us -> 37.1 us (level)
  no operation moved by 1% of the time
where the time goes in v12:
time: 37.1 us; the launch traced here: 36.9 us
  starting transfers between devices  15.8 us (43%)
  blocking collectives  8.67 us (23%)
  waiting for transfers between devices  7.97 us (21%)
  Pallas kernels  4.18 us (11%)
    all_to_all x1, blocking collectives, exchange(): lax.all_to_all(value, 'seq', split_axis=0, concat_axis=0, tiled=True, axi...  8.67 us
    all_to_all x1, starting transfers between devices, exchange(): lax.all_to_all(value, 'seq', split_axis=0, concat_axis=0, tiled=True, axi...  7.99 us
    ppermute x7, starting transfers between devices, swap(): lax.ppermute(value, axis, [(place, place ^ apart) for place in range(lax....  7.86 us
    ppermute x7, waiting for transfers between devices, swap(): lax.ppermute(value, axis, [(place, place ^ apart) for place in range(lax....  7.11 us
    pallas_call x4, Pallas kernels, call(): pl.pallas_call(kernel, out_shape=out_shape, compiler_params=pltpu.Compile...  4.18 us
    all_to_all x1, waiting for transfers between devices, exchange(): lax.all_to_all(value, 'seq', split_axis=0, concat_axis=0, tiled=True, axi...  0.87 us
  transfers between devices with their start and end apart: 8, of which 6 were waited for; matrix products, arithmetic and copies ran while one was open for 0% of the time, Pallas kernels for 0%

profile of v12, /device:TPU:0, one launch (start us, length us, event | category | flops | bytes accessed | tf_op | source)
XLA Modules:
  0.0 36.9 jit_solution(9063521748070271470)
XLA Ops:
  0.0 2.3 %shard_map.118 = (f32[1,512]{1,0:T(1,128)}, bf16[128,512]{1,0:T(8,128)(2,1)}, bf16[8,5,16,512]{3,2,1,0:T(8,128)(2,1)}) custom-call(bf16[512,128]{1,0:T(8,128)(2,1)} %features_ref.1, bf16[512,128]{1,0:T(8,128)(2,1)} %pre_ref.1, f32[1,128]{1,0:T(1,128)} %bitcast.4, f32[1,128]{1,0:T(1,128)} %bitcast.5, f32[2,2,512,128]{3,2,1,0:T(8,128)} %spectrum_ref.1), custom_call_target="tpu_custom_call" | custom-call | flops 655360 | bytes 2097152 | tf_op jit(solution)/shard_map/pallas_call | solution.py:301
  2.3 0.0 copy-start.2
  2.3 0.0 copy-start.3
  2.3 0.0 copy-start.4
  2.3 0.0 copy-start.5
  2.3 0.0 copy-start.6
  2.4 0.0 copy-start.7
  2.4 8.0 %all-to-all-start = ((bf16[8,5,16,512]{3,2,1,0:T(8,128)(2,1)}), bf16[8,5,16,512]{3,2,1,0:T(8,128)(2,1)S(1)}, u32[]{:S(2)}, u32[]{:S(2)}) async-start(bf16[8,5,16,512]{3,2,1,0:T(8,128)(2,1)} %get-tuple-element.8), calls=%async_computation | async-start | bytes 1310720 | tf_op jit(solution)/shard_map/all_to_all | solution.py:312
  10.4 0.0 copy-done.2
  10.4 0.4 %collective-permute-start.2 = (f32[1,512]{1,0:T(1,128)S(1)}, f32[1,512]{1,0:T(1,128)S(1)}, u32[]{:S(2)}, u32[]{:S(2)}) collective-permute-start(f32[1,512]{1,0:T(1,128)S(1)} %copy-done.2), channel_id=1, source_target_pairs={{0,3},{1,2},{2,1},{3,0},{4,7},{5,6},{6,5},{7,4},{8,11},{9,10},{10,... | collective-permute-start | bytes 6152 | tf_op jit(solution)/shard_map/ppermute | solution.py:316
  10.7 1.2 %collective-permute-start.1 = (f32[1,512]{1,0:T(1,128)S(1)}, f32[1,512]{1,0:T(1,128)S(1)}, u32[]{:S(2)}, u32[]{:S(2)}) collective-permute-start(f32[1,512]{1,0:T(1,128)S(1)} %copy-done.2), channel_id=1, source_target_pairs={{0,2},{1,3},{2,0},{3,1},{4,6},{5,7},{6,4},{7,5},{8,10},{9,11},{10,... | collective-permute-start | bytes 6152 | tf_op jit(solution)/shard_map/ppermute | solution.py:316
  11.9 0.3 collective-permute-start
  12.2 1.1 %collective-permute-done.2.refs_3_ = f32[1,512]{1,0:T(1,128)S(1)} collective-permute-done((f32[1,512]{1,0:T(1,128)S(1)}, f32[1,512]{1,0:T(1,128)S(1)}, u32[]{:S(2)}, u32[]{:S(2)}) %collective-permute-start.2) | collective-permute-done | bytes 2080 | tf_op jit(solution)/shard_map/ppermute | solution.py:316
  13.4 0.9 %collective-permute-done.1.refs_2_ = f32[1,512]{1,0:T(1,128)S(1)} collective-permute-done((f32[1,512]{1,0:T(1,128)S(1)}, f32[1,512]{1,0:T(1,128)S(1)}, u32[]{:S(2)}, u32[]{:S(2)}) %collective-permute-start.1) | collective-permute-done | bytes 2080 | tf_op jit(solution)/shard_map/ppermute | solution.py:316
  14.3 0.0 collective-permute-done.refs_1_
  14.3 0.0 copy-start.8
  14.3 1.5 %collective-permute-start.3 = (f32[1,512]{1,0:T(1,128)S(1)}, f32[1,512]{1,0:T(1,128)S(1)}, u32[]{:S(2)}, u32[]{:S(2)}) collective-permute-start(f32[1,512]{1,0:T(1,128)S(1)} %shard_map.119.scale_ref), channel_id=1, source_target_pairs={{0,4},{4,0},{8,12},{12,8},{16,20},{20,16},{24,28},{28,24},{1,5},{5... | collective-permute-start | bytes 6152 | tf_op jit(solution)/shard_map/ppermute | solution.py:316
  15.9 2.2 %collective-permute-done.3 = f32[1,512]{1,0:T(1,128)S(1)} collective-permute-done((f32[1,512]{1,0:T(1,128)S(1)}, f32[1,512]{1,0:T(1,128)S(1)}, u32[]{:S(2)}, u32[]{:S(2)}) %collective-permute-start.3) | collective-permute-done | bytes 2080 | tf_op jit(solution)/shard_map/ppermute | solution.py:316
  18.1 1.5 %collective-permute-start.6 = (f32[2,512]{1,0:T(2,128)S(1)}, f32[2,512]{1,0:T(2,128)S(1)}, u32[]{:S(2)}, u32[]{:S(2)}) collective-permute-start(f32[2,512]{1,0:T(2,128)S(1)} %pad_maximum_fusion.refs_0_), channel_id=1, source_target_pairs={{0,24},{4,28},{8,16},{12,20},{16,8},{20,12},{24,0},{28,4},{1,25},{... | collective-permute-start | bytes 12296 | tf_op jit(solution)/shard_map/ppermute | solution.py:316
  19.6 0.8 %collective-permute-start.5 = (f32[2,512]{1,0:T(2,128)S(1)}, f32[2,512]{1,0:T(2,128)S(1)}, u32[]{:S(2)}, u32[]{:S(2)}) collective-permute-start(f32[2,512]{1,0:T(2,128)S(1)} %pad_maximum_fusion.refs_0_), channel_id=1, source_target_pairs={{0,16},{4,20},{8,24},{12,28},{16,0},{20,4},{24,8},{28,12},{1,17},{... | collective-permute-start | bytes 12296 | tf_op jit(solution)/shard_map/ppermute | solution.py:316
  20.4 2.1 %collective-permute-start.4 = (f32[2,512]{1,0:T(2,128)S(1)}, f32[2,512]{1,0:T(2,128)S(1)}, u32[]{:S(2)}, u32[]{:S(2)}) collective-permute-start(f32[2,512]{1,0:T(2,128)S(1)} %pad_maximum_fusion.refs_0_), channel_id=1, source_target_pairs={{0,8},{4,12},{8,0},{12,4},{16,24},{20,28},{24,16},{28,20},{1,9},{5... | collective-permute-start | bytes 12296 | tf_op jit(solution)/shard_map/ppermute | solution.py:316
  22.5 1.1 %collective-permute-done.6.refs_3_ = f32[2,512]{1,0:T(2,128)S(1)} collective-permute-done((f32[2,512]{1,0:T(2,128)S(1)}, f32[2,512]{1,0:T(2,128)S(1)}, u32[]{:S(2)}, u32[]{:S(2)}) %collective-permute-start.6) | collective-permute-done | bytes 4128 | tf_op jit(solution)/shard_map/ppermute | solution.py:316
  23.7 1.7 %collective-permute-done.5.refs_2_ = f32[2,512]{1,0:T(2,128)S(1)} collective-permute-done((f32[2,512]{1,0:T(2,128)S(1)}, f32[2,512]{1,0:T(2,128)S(1)}, u32[]{:S(2)}, u32[]{:S(2)}) %collective-permute-start.5) | collective-permute-done | bytes 4128 | tf_op jit(solution)/shard_map/ppermute | solution.py:316
  25.4 0.0 collective-permute-done.4.refs_1_
  25.4 0.9 %all-to-all-done.packed_ref = bf16[8,5,16,512]{3,2,1,0:T(8,128)(2,1)S(1)} async-done(((bf16[8,5,16,512]{3,2,1,0:T(8,128)(2,1)}), bf16[8,5,16,512]{3,2,1,0:T(8,128)(2,1)S(1)}, u32[]{:S(2)}, u32[]{:S(2)}) %all-to-all-start) | async-done | bytes 655392 | tf_op jit(solution)/shard_map/all_to_all | solution.py:312
  26.2 0.0 copy-done.3
  26.2 0.0 copy-done.4
  26.3 1.1 %shard_map.120 = bf16[128,512]{1,0:T(8,128)(2,1)S(1)} custom-call(bf16[8,5,16,512]{3,2,1,0:T(8,128)(2,1)S(1)} %all-to-all-done.packed_ref, bf16[288,128]{1,0:T(8,128)(2,1)S(1)} %copy-done.5, bf16[128,288]{1,0:T(8,128)(2,1)S(1)} %copy-done.4, f32[2,9,512]{2,1,0:T(8,128)S(1)} %copy-done.6, f32[2,4,128]{2,1,0:T(4,128)S(1)} %copy-done.8, ...), custom_call_target="tpu_custom_call" | custom-call | flops 671088640 | bytes 1310720 | tf_op jit(solution)/shard_map/pallas_call | solution.py:301
  27.4 0.0 copy-start
  27.4 0.0 copy-start.1
  27.4 8.7 %all_to_all.10.conv_ref = bf16[8,16,512]{2,1,0:T(8,128)(2,1)S(1)} all-to-all(bf16[8,16,512]{2,1,0:T(8,128)(2,1)S(1)} %bitcast.3), channel_id=1, replica_groups={{20,4,12,24,8,16,0,28},{21,5,13,25,9,17,1,29},{22,6,14,26,10,18,2,30},{..., dimensions={0} | all-to-all | bytes 262144 | tf_op jit(solution)/shard_map/all_to_all | solution.py:312
  36.1 0.8 %shard_map.121 = bf16[512,128]{1,0:T(8,128)(2,1)} custom-call(bf16[8,16,512]{2,1,0:T(8,128)(2,1)S(1)} %all_to_all.10.conv_ref, bf16[128,512]{1,0:T(8,128)(2,1)S(1)} %copy-done.1, f32[1,512]{1,0:T(1,128)S(1)} %shard_map.119.scale_ref, bf16[512,128]{1,0:T(8,128)(2,1)S(1)} %copy-done), custom_call_target="tpu_custom_call" | custom-call | flops 655360 | bytes 524288 | tf_op jit(solution)/shard_map/pallas_call | solution.py:301
  (8 shorter events, 0.0 us)
Async XLA Ops:
  2.3 8.1 %copy-start.2 = (f32[1,512]{1,0:T(1,128)S(1)}, f32[1,512]{1,0:T(1,128)}, u32[]{:S(2)}) copy-start(f32[1,512]{1,0:T(1,128)} %get-tuple-element.9.refs_0_) | copy-start | bytes 6148
  2.3 23.9 %copy-start.3 = (bf16[2,256,256]{2,1,0:T(8,128)(2,1)S(1)}, bf16[2,256,256]{2,1,0:T(8,128)(2,1)}, u32[]{:S(2)}) copy-start(bf16[2,256,256]{2,1,0:T(8,128)(2,1)} %constant.16.clone.dft_ref) | copy-start | bytes 786436
  2.3 23.9 %copy-start.4 = (bf16[128,288]{1,0:T(8,128)(2,1)S(1)}, bf16[128,288]{1,0:T(8,128)(2,1)}, u32[]{:S(2)}) copy-start(bf16[128,288]{1,0:T(8,128)(2,1)} %constant.13.clone.last_ref) | copy-start | bytes 221188
  2.3 23.9 %copy-start.5 = (bf16[288,128]{1,0:T(8,128)(2,1)S(1)}, bf16[288,128]{1,0:T(8,128)(2,1)}, u32[]{:S(2)}) copy-start(bf16[288,128]{1,0:T(8,128)(2,1)} %constant.12.clone.first_ref) | copy-start | bytes 221188
  2.3 23.9 %copy-start.6 = (f32[2,9,512]{2,1,0:T(8,128)S(1)}, f32[2,9,512]{2,1,0:T(8,128)}, u32[]{:S(2)}) copy-start(f32[2,9,512]{2,1,0:T(8,128)} %constant.14.clone.twist_ref) | copy-start | bytes 110596
  2.4 23.9 %copy-start.7 = (bf16[128,128]{1,0:T(8,128)(2,1)S(1)}, bf16[128,128]{1,0:T(8,128)(2,1)}, u32[]{:S(2)}) copy-start(bf16[128,128]{1,0:T(8,128)(2,1)} %constant.17.clone.reverse_ref) | copy-start | bytes 98308
  2.4 23.9 %all-to-all-start = ((bf16[8,5,16,512]{3,2,1,0:T(8,128)(2,1)}), bf16[8,5,16,512]{3,2,1,0:T(8,128)(2,1)S(1)}, u32[]{:S(2)}, u32[]{:S(2)}) async-start(bf16[8,5,16,512]{3,2,1,0:T(8,128)(2,1)} %get-tuple-element.8), calls=%async_computation | async-start | bytes 1310720 | tf_op jit(solution)/shard_map/all_to_all | solution.py:312
  10.4 3.0 %collective-permute-start.2 = (f32[1,512]{1,0:T(1,128)S(1)}, f32[1,512]{1,0:T(1,128)S(1)}, u32[]{:S(2)}, u32[]{:S(2)}) collective-permute-start(f32[1,512]{1,0:T(1,128)S(1)} %copy-done.2), channel_id=1, source_target_pairs={{0,3},{1,2},{2,1},{3,0},{4,7},{5,6},{6,5},{7,4},{8,11},{9,10},{10,... | collective-permute-start | bytes 6152 | tf_op jit(solution)/shard_map/ppermute | solution.py:316
  10.7 3.6 %collective-permute-start.1 = (f32[1,512]{1,0:T(1,128)S(1)}, f32[1,512]{1,0:T(1,128)S(1)}, u32[]{:S(2)}, u32[]{:S(2)}) collective-permute-start(f32[1,512]{1,0:T(1,128)S(1)} %copy-done.2), channel_id=1, source_target_pairs={{0,2},{1,3},{2,0},{3,1},{4,6},{5,7},{6,4},{7,5},{8,10},{9,11},{10,... | collective-permute-start | bytes 6152 | tf_op jit(solution)/shard_map/ppermute | solution.py:316
  11.9 2.4 %collective-permute-start = (f32[1,512]{1,0:T(1,128)S(1)}, f32[1,512]{1,0:T(1,128)S(1)}, u32[]{:S(2)}, u32[]{:S(2)}) collective-permute-start(f32[1,512]{1,0:T(1,128)S(1)} %copy-done.2), channel_id=1, source_target_pairs={{0,1},{1,0},{2,3},{3,2},{4,5},{5,4},{6,7},{7,6},{8,9},{9,8},{10,11... | collective-permute-start | bytes 6152 | tf_op jit(solution)/shard_map/ppermute | solution.py:316
  14.3 11.9 %copy-start.8 = (f32[2,4,128]{2,1,0:T(4,128)S(1)}, f32[2,4,128]{2,1,0:T(4,128)}, u32[]{:S(2)}) copy-start(f32[2,4,128]{2,1,0:T(4,128)} %constant.15.clone.spin_ref) | copy-start | bytes 12292
  14.3 3.7 %collective-permute-start.3 = (f32[1,512]{1,0:T(1,128)S(1)}, f32[1,512]{1,0:T(1,128)S(1)}, u32[]{:S(2)}, u32[]{:S(2)}) collective-permute-start(f32[1,512]{1,0:T(1,128)S(1)} %shard_map.119.scale_ref), channel_id=1, source_target_pairs={{0,4},{4,0},{8,12},{12,8},{16,20},{20,16},{24,28},{28,24},{1,5},{5... | collective-permute-start | bytes 6152 | tf_op jit(solution)/shard_map/ppermute | solution.py:316
  18.1 5.6 %collective-permute-start.6 = (f32[2,512]{1,0:T(2,128)S(1)}, f32[2,512]{1,0:T(2,128)S(1)}, u32[]{:S(2)}, u32[]{:S(2)}) collective-permute-start(f32[2,512]{1,0:T(2,128)S(1)} %pad_maximum_fusion.refs_0_), channel_id=1, source_target_pairs={{0,24},{4,28},{8,16},{12,20},{16,8},{20,12},{24,0},{28,4},{1,25},{... | collective-permute-start | bytes 12296 | tf_op jit(solution)/shard_map/ppermute | solution.py:316
  19.6 5.8 %collective-permute-start.5 = (f32[2,512]{1,0:T(2,128)S(1)}, f32[2,512]{1,0:T(2,128)S(1)}, u32[]{:S(2)}, u32[]{:S(2)}) collective-permute-start(f32[2,512]{1,0:T(2,128)S(1)} %pad_maximum_fusion.refs_0_), channel_id=1, source_target_pairs={{0,16},{4,20},{8,24},{12,28},{16,0},{20,4},{24,8},{28,12},{1,17},{... | collective-permute-start | bytes 12296 | tf_op jit(solution)/shard_map/ppermute | solution.py:316
  20.4 4.9 %collective-permute-start.4 = (f32[2,512]{1,0:T(2,128)S(1)}, f32[2,512]{1,0:T(2,128)S(1)}, u32[]{:S(2)}, u32[]{:S(2)}) collective-permute-start(f32[2,512]{1,0:T(2,128)S(1)} %pad_maximum_fusion.refs_0_), channel_id=1, source_target_pairs={{0,8},{4,12},{8,0},{12,4},{16,24},{20,28},{24,16},{28,20},{1,9},{5... | collective-permute-start | bytes 12296 | tf_op jit(solution)/shard_map/ppermute | solution.py:316
  27.4 8.7 %copy-start = (bf16[512,128]{1,0:T(8,128)(2,1)S(1)}, bf16[512,128]{1,0:T(8,128)(2,1)}, u32[]{:S(2)}) copy-start(bf16[512,128]{1,0:T(8,128)(2,1)} %post_ref.1) | copy-start | bytes 393220
  27.4 8.7 %copy-start.1 = (bf16[128,512]{1,0:T(8,128)(2,1)S(1)}, bf16[128,512]{1,0:T(8,128)(2,1)}, u32[]{:S(2)}) copy-start(bf16[128,512]{1,0:T(8,128)(2,1)} %get-tuple-element.10.skipped_ref) | copy-start | bytes 393220

commit v13 on v12

--- a/solution.py
+++ b/solution.py
@@ -89,7 +89,7 @@
 
 
 def hops(places):
-    return [[apart, apart + 1] for apart in range(0, places, 2)]
+    return [[apart, apart ^ 2] for apart in range(places) if apart & 2 == 0]
 
 
 def prepare_kernel(
@@ -363,7 +363,7 @@
         functools.partial(scale_kernel, wide * groups), shape((1, rows), F32), 8 * rows, 32 * rows, squares, *others
     )
     if piled:
-        near = jnp.concatenate([scale, swap(scale, "seq", 1)])
+        near = jnp.concatenate([scale, swap(scale, "seq", 2)])
         scales = [near] + [swap(near, "seq", steps[0]) for steps in hops(places)[1:]]
     else:
         scales = [jnp.repeat(lax.all_gather(scale, "seq", axis=0, tiled=True), width, axis=0)]

time: 37.1 us -> 40.1 us (1.081)
  waiting for transfers between devices: 7.97 us -> 11.5 us
  starting transfers between devices: 15.8 us -> 14.9 us
  blocking collectives: 8.67 us -> 9.14 us
    ppermute x7, waiting for transfers between devices: 7.11 us -> 11.5 us  [swap(): lax.ppermute(value, axis, [(place, place ^ apart) for place in range(lax....]
    ppermute x7, starting transfers between devices: 7.86 us -> 6.9 us  [swap(): lax.ppermute(value, axis, [(place, place ^ apart) for place in range(lax....]
    all_to_all x1, waiting for transfers between devices: 0.87 us -> 0.01 us  [exchange(): lax.all_to_all(value, 'seq', split_axis=0, concat_axis=0, tiled=True, axi...]
    all_to_all x1, blocking collectives: 8.67 us -> 9.14 us  [exchange(): lax.all_to_all(value, 'seq', split_axis=0, concat_axis=0, tiled=True, axi...]
  transfers between devices with their start and end apart: 8 -> 8, of which waited for: 6 -> 5; matrix products, arithmetic and copies ran while one was open for 0% -> 0% of each run, Pallas kernels for 0% -> 0%
where the time goes in v13:
time: 40.1 us; the launch traced here: 39.9 us
  starting transfers between devices  14.9 us (37%)
  waiting for transfers between devices  11.5 us (29%)
  blocking collectives  9.14 us (23%)
  Pallas kernels  4.18 us (10%)
    ppermute x7, waiting for transfers between devices, swap(): lax.ppermute(value, axis, [(place, place ^ apart) for place in range(lax....  11.5 us
    all_to_all x1, blocking collectives, exchange(): lax.all_to_all(value, 'seq', split_axis=0, concat_axis=0, tiled=True, axi...  9.14 us
    all_to_all x1, starting transfers between devices, exchange(): lax.all_to_all(value, 'seq', split_axis=0, concat_axis=0, tiled=True, axi...  7.99 us
    ppermute x7, starting transfers between devices, swap(): lax.ppermute(value, axis, [(place, place ^ apart) for place in range(lax....  6.9 us
    pallas_call x4, Pallas kernels, call(): pl.pallas_call(kernel, out_shape=out_shape, compiler_params=pltpu.Compile...  4.18 us
  transfers between devices with their start and end apart: 8, of which 5 were waited for; matrix products, arithmetic and copies ran while one was open for 0% of the time, Pallas kernels for 0%

profile of v13, /device:TPU:0, one launch (start us, length us, event | category | flops | bytes accessed | tf_op | source)
XLA Modules:
  0.0 39.9 jit_solution(3886737953706805807)
XLA Ops:
  0.0 2.3 %shard_map.118 = (f32[1,512]{1,0:T(1,128)}, bf16[128,512]{1,0:T(8,128)(2,1)}, bf16[8,5,16,512]{3,2,1,0:T(8,128)(2,1)}) custom-call(bf16[512,128]{1,0:T(8,128)(2,1)} %features_ref.1, bf16[512,128]{1,0:T(8,128)(2,1)} %pre_ref.1, f32[1,128]{1,0:T(1,128)} %bitcast.4, f32[1,128]{1,0:T(1,128)} %bitcast.5, f32[2,2,512,128]{3,2,1,0:T(8,128)} %spectrum_ref.1), custom_call_target="tpu_custom_call" | custom-call | flops 655360 | bytes 2097152 | tf_op jit(solution)/shard_map/pallas_call | solution.py:301
  2.3 0.0 copy-start.2
  2.3 0.0 copy-start.3
  2.3 0.0 copy-start.4
  2.3 0.0 copy-start.5
  2.3 0.0 copy-start.6
  2.4 0.0 copy-start.7
  2.4 8.0 %all-to-all-start = ((bf16[8,5,16,512]{3,2,1,0:T(8,128)(2,1)}), bf16[8,5,16,512]{3,2,1,0:T(8,128)(2,1)S(1)}, u32[]{:S(2)}, u32[]{:S(2)}) async-start(bf16[8,5,16,512]{3,2,1,0:T(8,128)(2,1)} %get-tuple-element.8), calls=%async_computation | async-start | bytes 1310720 | tf_op jit(solution)/shard_map/all_to_all | solution.py:312
  10.4 0.0 copy-done.2
  10.4 0.4 collective-permute-start.2
  10.7 1.2 %collective-permute-start.1 = (f32[1,512]{1,0:T(1,128)S(1)}, f32[1,512]{1,0:T(1,128)S(1)}, u32[]{:S(2)}, u32[]{:S(2)}) collective-permute-start(f32[1,512]{1,0:T(1,128)S(1)} %copy-done.2), channel_id=1, source_target_pairs={{0,2},{1,3},{2,0},{3,1},{4,6},{5,7},{6,4},{7,5},{8,10},{9,11},{10,... | collective-permute-start | bytes 6152 | tf_op jit(solution)/shard_map/ppermute | solution.py:316
  11.9 0.3 collective-permute-start
  12.2 1.1 %collective-permute-done.2.refs_3_ = f32[1,512]{1,0:T(1,128)S(1)} collective-permute-done((f32[1,512]{1,0:T(1,128)S(1)}, f32[1,512]{1,0:T(1,128)S(1)}, u32[]{:S(2)}, u32[]{:S(2)}) %collective-permute-start.2) | collective-permute-done | bytes 2080 | tf_op jit(solution)/shard_map/ppermute | solution.py:316
  13.4 0.9 %collective-permute-done.1.refs_2_ = f32[1,512]{1,0:T(1,128)S(1)} collective-permute-done((f32[1,512]{1,0:T(1,128)S(1)}, f32[1,512]{1,0:T(1,128)S(1)}, u32[]{:S(2)}, u32[]{:S(2)}) %collective-permute-start.1) | collective-permute-done | bytes 2080 | tf_op jit(solution)/shard_map/ppermute | solution.py:316
  14.3 0.0 collective-permute-done.refs_1_
  14.3 0.0 copy-start.8
  14.3 0.6 %collective-permute-start.3 = (f32[1,512]{1,0:T(1,128)S(1)}, f32[1,512]{1,0:T(1,128)S(1)}, u32[]{:S(2)}, u32[]{:S(2)}) collective-permute-start(f32[1,512]{1,0:T(1,128)S(1)} %shard_map.119.scale_ref), channel_id=1, source_target_pairs={{0,8},{4,12},{8,0},{12,4},{16,24},{20,28},{24,16},{28,20},{1,9},{5... | collective-permute-start | bytes 6152 | tf_op jit(solution)/shard_map/ppermute | solution.py:316
  15.0 6.0 %collective-permute-done.3 = f32[1,512]{1,0:T(1,128)S(1)} collective-permute-done((f32[1,512]{1,0:T(1,128)S(1)}, f32[1,512]{1,0:T(1,128)S(1)}, u32[]{:S(2)}, u32[]{:S(2)}) %collective-permute-start.3) | collective-permute-done | bytes 2080 | tf_op jit(solution)/shard_map/ppermute | solution.py:316
  21.0 3.3 %collective-permute-start.6 = (f32[2,512]{1,0:T(2,128)S(1)}, f32[2,512]{1,0:T(2,128)S(1)}, u32[]{:S(2)}, u32[]{:S(2)}) collective-permute-start(f32[2,512]{1,0:T(2,128)S(1)} %pad_maximum_fusion.refs_0_), channel_id=1, source_target_pairs={{0,20},{4,16},{8,28},{12,24},{16,4},{20,0},{24,12},{28,8},{1,21},{... | collective-permute-start | bytes 12296 | tf_op jit(solution)/shard_map/ppermute | solution.py:316
  24.3 0.5 %collective-permute-start.5 = (f32[2,512]{1,0:T(2,128)S(1)}, f32[2,512]{1,0:T(2,128)S(1)}, u32[]{:S(2)}, u32[]{:S(2)}) collective-permute-start(f32[2,512]{1,0:T(2,128)S(1)} %pad_maximum_fusion.refs_0_), channel_id=1, source_target_pairs={{0,16},{4,20},{8,24},{12,28},{16,0},{20,4},{24,8},{28,12},{1,17},{... | collective-permute-start | bytes 12296 | tf_op jit(solution)/shard_map/ppermute | solution.py:316
  24.7 0.6 %collective-permute-start.4 = (f32[2,512]{1,0:T(2,128)S(1)}, f32[2,512]{1,0:T(2,128)S(1)}, u32[]{:S(2)}, u32[]{:S(2)}) collective-permute-start(f32[2,512]{1,0:T(2,128)S(1)} %pad_maximum_fusion.refs_0_), channel_id=1, source_target_pairs={{0,4},{4,0},{8,12},{12,8},{16,20},{20,16},{24,28},{28,24},{1,5},{5... | collective-permute-start | bytes 12296 | tf_op jit(solution)/shard_map/ppermute | solution.py:316
  25.4 1.7 %collective-permute-done.6.refs_3_ = f32[2,512]{1,0:T(2,128)S(1)} collective-permute-done((f32[2,512]{1,0:T(2,128)S(1)}, f32[2,512]{1,0:T(2,128)S(1)}, u32[]{:S(2)}, u32[]{:S(2)}) %collective-permute-start.6) | collective-permute-done | bytes 4128 | tf_op jit(solution)/shard_map/ppermute | solution.py:316
  27.1 1.7 %collective-permute-done.5.refs_2_ = f32[2,512]{1,0:T(2,128)S(1)} collective-permute-done((f32[2,512]{1,0:T(2,128)S(1)}, f32[2,512]{1,0:T(2,128)S(1)}, u32[]{:S(2)}, u32[]{:S(2)}) %collective-permute-start.5) | collective-permute-done | bytes 4128 | tf_op jit(solution)/shard_map/ppermute | solution.py:316
  28.8 0.0 collective-permute-done.4.refs_1_
  28.8 0.0 all-to-all-done.packed_ref
  28.8 0.0 copy-done.3
  28.8 1.1 %shard_map.120 = bf16[128,512]{1,0:T(8,128)(2,1)S(1)} custom-call(bf16[8,5,16,512]{3,2,1,0:T(8,128)(2,1)S(1)} %all-to-all-done.packed_ref, bf16[288,128]{1,0:T(8,128)(2,1)S(1)} %copy-done.5, bf16[128,288]{1,0:T(8,128)(2,1)S(1)} %copy-done.4, f32[2,9,512]{2,1,0:T(8,128)S(1)} %copy-done.6, f32[2,4,128]{2,1,0:T(4,128)S(1)} %copy-done.8, ...), custom_call_target="tpu_custom_call" | custom-call | flops 671088640 | bytes 1310720 | tf_op jit(solution)/shard_map/pallas_call | solution.py:301
  29.9 0.0 copy-start
  29.9 0.0 copy-start.1
  30.0 9.1 %all_to_all.10.conv_ref = bf16[8,16,512]{2,1,0:T(8,128)(2,1)S(1)} all-to-all(bf16[8,16,512]{2,1,0:T(8,128)(2,1)S(1)} %bitcast.3), channel_id=1, replica_groups={{20,4,12,24,8,16,0,28},{21,5,13,25,9,17,1,29},{22,6,14,26,10,18,2,30},{..., dimensions={0} | all-to-all | bytes 262144 | tf_op jit(solution)/shard_map/all_to_all | solution.py:312
  39.1 0.0 copy-done.1
  39.1 0.8 %shard_map.121 = bf16[512,128]{1,0:T(8,128)(2,1)} custom-call(bf16[8,16,512]{2,1,0:T(8,128)(2,1)S(1)} %all_to_all.10.conv_ref, bf16[128,512]{1,0:T(8,128)(2,1)S(1)} %copy-done.1, f32[1,512]{1,0:T(1,128)S(1)} %shard_map.119.scale_ref, bf16[512,128]{1,0:T(8,128)(2,1)S(1)} %copy-done), custom_call_target="tpu_custom_call" | custom-call | flops 655360 | bytes 524288 | tf_op jit(solution)/shard_map/pallas_call | solution.py:301
  (8 shorter events, 0.0 us)
Async XLA Ops:
  2.3 8.1 %copy-start.2 = (f32[1,512]{1,0:T(1,128)S(1)}, f32[1,512]{1,0:T(1,128)}, u32[]{:S(2)}) copy-start(f32[1,512]{1,0:T(1,128)} %get-tuple-element.9.refs_0_) | copy-start | bytes 6148
  2.3 26.5 %copy-start.3 = (bf16[2,256,256]{2,1,0:T(8,128)(2,1)S(1)}, bf16[2,256,256]{2,1,0:T(8,128)(2,1)}, u32[]{:S(2)}) copy-start(bf16[2,256,256]{2,1,0:T(8,128)(2,1)} %constant.16.clone.dft_ref) | copy-start | bytes 786436
  2.3 26.5 %copy-start.4 = (bf16[128,288]{1,0:T(8,128)(2,1)S(1)}, bf16[128,288]{1,0:T(8,128)(2,1)}, u32[]{:S(2)}) copy-start(bf16[128,288]{1,0:T(8,128)(2,1)} %constant.13.clone.last_ref) | copy-start | bytes 221188
  2.3 26.5 %copy-start.5 = (bf16[288,128]{1,0:T(8,128)(2,1)S(1)}, bf16[288,128]{1,0:T(8,128)(2,1)}, u32[]{:S(2)}) copy-start(bf16[288,128]{1,0:T(8,128)(2,1)} %constant.12.clone.first_ref) | copy-start | bytes 221188
  2.3 26.5 %copy-start.6 = (f32[2,9,512]{2,1,0:T(8,128)S(1)}, f32[2,9,512]{2,1,0:T(8,128)}, u32[]{:S(2)}) copy-start(f32[2,9,512]{2,1,0:T(8,128)} %constant.14.clone.twist_ref) | copy-start | bytes 110596
  2.4 26.5 %copy-start.7 = (bf16[128,128]{1,0:T(8,128)(2,1)S(1)}, bf16[128,128]{1,0:T(8,128)(2,1)}, u32[]{:S(2)}) copy-start(bf16[128,128]{1,0:T(8,128)(2,1)} %constant.17.clone.reverse_ref) | copy-start | bytes 98308
  2.4 26.4 %all-to-all-start = ((bf16[8,5,16,512]{3,2,1,0:T(8,128)(2,1)}), bf16[8,5,16,512]{3,2,1,0:T(8,128)(2,1)S(1)}, u32[]{:S(2)}, u32[]{:S(2)}) async-start(bf16[8,5,16,512]{3,2,1,0:T(8,128)(2,1)} %get-tuple-element.8), calls=%async_computation | async-start | bytes 1310720 | tf_op jit(solution)/shard_map/all_to_all | solution.py:312
  10.4 3.0 %collective-permute-start.2 = (f32[1,512]{1,0:T(1,128)S(1)}, f32[1,512]{1,0:T(1,128)S(1)}, u32[]{:S(2)}, u32[]{:S(2)}) collective-permute-start(f32[1,512]{1,0:T(1,128)S(1)} %copy-done.2), channel_id=1, source_target_pairs={{0,3},{1,2},{2,1},{3,0},{4,7},{5,6},{6,5},{7,4},{8,11},{9,10},{10,... | collective-permute-start | bytes 6152 | tf_op jit(solution)/shard_map/ppermute | solution.py:316
  10.7 3.6 %collective-permute-start.1 = (f32[1,512]{1,0:T(1,128)S(1)}, f32[1,512]{1,0:T(1,128)S(1)}, u32[]{:S(2)}, u32[]{:S(2)}) collective-permute-start(f32[1,512]{1,0:T(1,128)S(1)} %copy-done.2), channel_id=1, source_target_pairs={{0,2},{1,3},{2,0},{3,1},{4,6},{5,7},{6,4},{7,5},{8,10},{9,11},{10,... | collective-permute-start | bytes 6152 | tf_op jit(solution)/shard_map/ppermute | solution.py:316
  11.9 2.4 %collective-permute-start = (f32[1,512]{1,0:T(1,128)S(1)}, f32[1,512]{1,0:T(1,128)S(1)}, u32[]{:S(2)}, u32[]{:S(2)}) collective-permute-start(f32[1,512]{1,0:T(1,128)S(1)} %copy-done.2), channel_id=1, source_target_pairs={{0,1},{1,0},{2,3},{3,2},{4,5},{5,4},{6,7},{7,6},{8,9},{9,8},{10,11... | collective-permute-start | bytes 6152 | tf_op jit(solution)/shard_map/ppermute | solution.py:316
  14.3 14.5 %copy-start.8 = (f32[2,4,128]{2,1,0:T(4,128)S(1)}, f32[2,4,128]{2,1,0:T(4,128)}, u32[]{:S(2)}) copy-start(f32[2,4,128]{2,1,0:T(4,128)} %constant.15.clone.spin_ref) | copy-start | bytes 12292
  14.3 6.6 %collective-permute-start.3 = (f32[1,512]{1,0:T(1,128)S(1)}, f32[1,512]{1,0:T(1,128)S(1)}, u32[]{:S(2)}, u32[]{:S(2)}) collective-permute-start(f32[1,512]{1,0:T(1,128)S(1)} %shard_map.119.scale_ref), channel_id=1, source_target_pairs={{0,8},{4,12},{8,0},{12,4},{16,24},{20,28},{24,16},{28,20},{1,9},{5... | collective-permute-start | bytes 6152 | tf_op jit(solution)/shard_map/ppermute | solution.py:316
  21.0 6.1 %collective-permute-start.6 = (f32[2,512]{1,0:T(2,128)S(1)}, f32[2,512]{1,0:T(2,128)S(1)}, u32[]{:S(2)}, u32[]{:S(2)}) collective-permute-start(f32[2,512]{1,0:T(2,128)S(1)} %pad_maximum_fusion.refs_0_), channel_id=1, source_target_pairs={{0,20},{4,16},{8,28},{12,24},{16,4},{20,0},{24,12},{28,8},{1,21},{... | collective-permute-start | bytes 12296 | tf_op jit(solution)/shard_map/ppermute | solution.py:316
  24.3 4.5 %collective-permute-start.5 = (f32[2,512]{1,0:T(2,128)S(1)}, f32[2,512]{1,0:T(2,128)S(1)}, u32[]{:S(2)}, u32[]{:S(2)}) collective-permute-start(f32[2,512]{1,0:T(2,128)S(1)} %pad_maximum_fusion.refs_0_), channel_id=1, source_target_pairs={{0,16},{4,20},{8,24},{12,28},{16,0},{20,4},{24,8},{28,12},{1,17},{... | collective-permute-start | bytes 12296 | tf_op jit(solution)/shard_map/ppermute | solution.py:316
  24.7 4.0 %collective-permute-start.4 = (f32[2,512]{1,0:T(2,128)S(1)}, f32[2,512]{1,0:T(2,128)S(1)}, u32[]{:S(2)}, u32[]{:S(2)}) collective-permute-start(f32[2,512]{1,0:T(2,128)S(1)} %pad_maximum_fusion.refs_0_), channel_id=1, source_target_pairs={{0,4},{4,0},{8,12},{12,8},{16,20},{20,16},{24,28},{28,24},{1,5},{5... | collective-permute-start | bytes 12296 | tf_op jit(solution)/shard_map/ppermute | solution.py:316
  29.9 9.2 %copy-start = (bf16[512,128]{1,0:T(8,128)(2,1)S(1)}, bf16[512,128]{1,0:T(8,128)(2,1)}, u32[]{:S(2)}) copy-start(bf16[512,128]{1,0:T(8,128)(2,1)} %post_ref.1) | copy-start | bytes 393220
  29.9 9.2 %copy-start.1 = (bf16[128,512]{1,0:T(8,128)(2,1)S(1)}, bf16[128,512]{1,0:T(8,128)(2,1)}, u32[]{:S(2)}) copy-start(bf16[128,512]{1,0:T(8,128)(2,1)} %get-tuple-element.10.skipped_ref) | copy-start | bytes 393220

commit v14 on v12

--- a/solution.py
+++ b/solution.py
@@ -18,7 +18,7 @@
 def order_of(places, back=False):
     if places != 8:
         return tuple(range(places))
-    return (5, 1, 3, 6, 2, 4, 0, 7) if back else (4, 7, 3, 6, 2, 1, 5, 0)
+    return (5, 3, 6, 2, 4, 0, 7, 1) if back else (4, 7, 3, 6, 2, 1, 5, 0)
 
 
 def reverse_bits(index, levels):

time: 37.1 us -> 37.1 us (level)
  no operation moved by 1% of the time
where the time goes in v14:
time: 37.1 us; the launch traced here: 36.9 us
  starting transfers between devices  15.8 us (43%)
  blocking collectives  8.67 us (23%)
  waiting for transfers between devices  7.97 us (21%)
  Pallas kernels  4.18 us (11%)
    all_to_all x1, blocking collectives, exchange(): lax.all_to_all(value, 'seq', split_axis=0, concat_axis=0, tiled=True, axi...  8.67 us
    all_to_all x1, starting transfers between devices, exchange(): lax.all_to_all(value, 'seq', split_axis=0, concat_axis=0, tiled=True, axi...  7.99 us
    ppermute x7, starting transfers between devices, swap(): lax.ppermute(value, axis, [(place, place ^ apart) for place in range(lax....  7.86 us
    ppermute x7, waiting for transfers between devices, swap(): lax.ppermute(value, axis, [(place, place ^ apart) for place in range(lax....  7.11 us
    pallas_call x4, Pallas kernels, call(): pl.pallas_call(kernel, out_shape=out_shape, compiler_params=pltpu.Compile...  4.18 us
    all_to_all x1, waiting for transfers between devices, exchange(): lax.all_to_all(value, 'seq', split_axis=0, concat_axis=0, tiled=True, axi...  0.87 us
  transfers between devices with their start and end apart: 8, of which 6 were waited for; matrix products, arithmetic and copies ran while one was open for 0% of the time, Pallas kernels for 0%

profile of v14, /device:TPU:0, one launch (start us, length us, event | category | flops | bytes accessed | tf_op | source)
XLA Modules:
  0.0 36.9 jit_solution(10061544408115526952)
XLA Ops:
  0.0 2.3 %shard_map.118 = (f32[1,512]{1,0:T(1,128)}, bf16[128,512]{1,0:T(8,128)(2,1)}, bf16[8,5,16,512]{3,2,1,0:T(8,128)(2,1)}) custom-call(bf16[512,128]{1,0:T(8,128)(2,1)} %features_ref.1, bf16[512,128]{1,0:T(8,128)(2,1)} %pre_ref.1, f32[1,128]{1,0:T(1,128)} %bitcast.4, f32[1,128]{1,0:T(1,128)} %bitcast.5, f32[2,2,512,128]{3,2,1,0:T(8,128)} %spectrum_ref.1), custom_call_target="tpu_custom_call" | custom-call | flops 655360 | bytes 2097152 | tf_op jit(solution)/shard_map/pallas_call | solution.py:301
  2.3 0.0 copy-start.2
  2.3 0.0 copy-start.3
  2.3 0.0 copy-start.4
  2.3 0.0 copy-start.5
  2.3 0.0 copy-start.6
  2.4 0.0 copy-start.7
  2.4 8.0 %all-to-all-start = ((bf16[8,5,16,512]{3,2,1,0:T(8,128)(2,1)}), bf16[8,5,16,512]{3,2,1,0:T(8,128)(2,1)S(1)}, u32[]{:S(2)}, u32[]{:S(2)}) async-start(bf16[8,5,16,512]{3,2,1,0:T(8,128)(2,1)} %get-tuple-element.8), calls=%async_computation | async-start | bytes 1310720 | tf_op jit(solution)/shard_map/all_to_all | solution.py:312
  10.4 0.0 copy-done.2
  10.4 0.4 %collective-permute-start.2 = (f32[1,512]{1,0:T(1,128)S(1)}, f32[1,512]{1,0:T(1,128)S(1)}, u32[]{:S(2)}, u32[]{:S(2)}) collective-permute-start(f32[1,512]{1,0:T(1,128)S(1)} %copy-done.2), channel_id=1, source_target_pairs={{0,3},{1,2},{2,1},{3,0},{4,7},{5,6},{6,5},{7,4},{8,11},{9,10},{10,... | collective-permute-start | bytes 6152 | tf_op jit(solution)/shard_map/ppermute | solution.py:316
  10.7 1.2 %collective-permute-start.1 = (f32[1,512]{1,0:T(1,128)S(1)}, f32[1,512]{1,0:T(1,128)S(1)}, u32[]{:S(2)}, u32[]{:S(2)}) collective-permute-start(f32[1,512]{1,0:T(1,128)S(1)} %copy-done.2), channel_id=1, source_target_pairs={{0,2},{1,3},{2,0},{3,1},{4,6},{5,7},{6,4},{7,5},{8,10},{9,11},{10,... | collective-permute-start | bytes 6152 | tf_op jit(solution)/shard_map/ppermute | solution.py:316
  11.9 0.3 collective-permute-start
  12.2 1.1 %collective-permute-done.2.refs_3_ = f32[1,512]{1,0:T(1,128)S(1)} collective-permute-done((f32[1,512]{1,0:T(1,128)S(1)}, f32[1,512]{1,0:T(1,128)S(1)}, u32[]{:S(2)}, u32[]{:S(2)}) %collective-permute-start.2) | collective-permute-done | bytes 2080 | tf_op jit(solution)/shard_map/ppermute | solution.py:316
  13.4 0.9 %collective-permute-done.1.refs_2_ = f32[1,512]{1,0:T(1,128)S(1)} collective-permute-done((f32[1,512]{1,0:T(1,128)S(1)}, f32[1,512]{1,0:T(1,128)S(1)}, u32[]{:S(2)}, u32[]{:S(2)}) %collective-permute-start.1) | collective-permute-done | bytes 2080 | tf_op jit(solution)/shard_map/ppermute | solution.py:316
  14.3 0.0 collective-permute-done.refs_1_
  14.3 0.0 copy-start.8
  14.3 1.5 %collective-permute-start.3 = (f32[1,512]{1,0:T(1,128)S(1)}, f32[1,512]{1,0:T(1,128)S(1)}, u32[]{:S(2)}, u32[]{:S(2)}) collective-permute-start(f32[1,512]{1,0:T(1,128)S(1)} %shard_map.119.scale_ref), channel_id=1, source_target_pairs={{0,4},{4,0},{8,12},{12,8},{16,20},{20,16},{24,28},{28,24},{1,5},{5... | collective-permute-start | bytes 6152 | tf_op jit(solution)/shard_map/ppermute | solution.py:316
  15.9 2.2 %collective-permute-done.3 = f32[1,512]{1,0:T(1,128)S(1)} collective-permute-done((f32[1,512]{1,0:T(1,128)S(1)}, f32[1,512]{1,0:T(1,128)S(1)}, u32[]{:S(2)}, u32[]{:S(2)}) %collective-permute-start.3) | collective-permute-done | bytes 2080 | tf_op jit(solution)/shard_map/ppermute | solution.py:316
  18.1 1.5 %collective-permute-start.6 = (f32[2,512]{1,0:T(2,128)S(1)}, f32[2,512]{1,0:T(2,128)S(1)}, u32[]{:S(2)}, u32[]{:S(2)}) collective-permute-start(f32[2,512]{1,0:T(2,128)S(1)} %pad_maximum_fusion.refs_0_), channel_id=1, source_target_pairs={{0,24},{4,28},{8,16},{12,20},{16,8},{20,12},{24,0},{28,4},{1,25},{... | collective-permute-start | bytes 12296 | tf_op jit(solution)/shard_map/ppermute | solution.py:316
  19.6 0.8 %collective-permute-start.5 = (f32[2,512]{1,0:T(2,128)S(1)}, f32[2,512]{1,0:T(2,128)S(1)}, u32[]{:S(2)}, u32[]{:S(2)}) collective-permute-start(f32[2,512]{1,0:T(2,128)S(1)} %pad_maximum_fusion.refs_0_), channel_id=1, source_target_pairs={{0,16},{4,20},{8,24},{12,28},{16,0},{20,4},{24,8},{28,12},{1,17},{... | collective-permute-start | bytes 12296 | tf_op jit(solution)/shard_map/ppermute | solution.py:316
  20.4 2.1 %collective-permute-start.4 = (f32[2,512]{1,0:T(2,128)S(1)}, f32[2,512]{1,0:T(2,128)S(1)}, u32[]{:S(2)}, u32[]{:S(2)}) collective-permute-start(f32[2,512]{1,0:T(2,128)S(1)} %pad_maximum_fusion.refs_0_), channel_id=1, source_target_pairs={{0,8},{4,12},{8,0},{12,4},{16,24},{20,28},{24,16},{28,20},{1,9},{5... | collective-permute-start | bytes 12296 | tf_op jit(solution)/shard_map/ppermute | solution.py:316
  22.5 1.1 %collective-permute-done.6.refs_3_ = f32[2,512]{1,0:T(2,128)S(1)} collective-permute-done((f32[2,512]{1,0:T(2,128)S(1)}, f32[2,512]{1,0:T(2,128)S(1)}, u32[]{:S(2)}, u32[]{:S(2)}) %collective-permute-start.6) | collective-permute-done | bytes 4128 | tf_op jit(solution)/shard_map/ppermute | solution.py:316
  23.7 1.7 %collective-permute-done.5.refs_2_ = f32[2,512]{1,0:T(2,128)S(1)} collective-permute-done((f32[2,512]{1,0:T(2,128)S(1)}, f32[2,512]{1,0:T(2,128)S(1)}, u32[]{:S(2)}, u32[]{:S(2)}) %collective-permute-start.5) | collective-permute-done | bytes 4128 | tf_op jit(solution)/shard_map/ppermute | solution.py:316
  25.4 0.0 collective-permute-done.4.refs_1_
  25.4 0.9 %all-to-all-done.packed_ref = bf16[8,5,16,512]{3,2,1,0:T(8,128)(2,1)S(1)} async-done(((bf16[8,5,16,512]{3,2,1,0:T(8,128)(2,1)}), bf16[8,5,16,512]{3,2,1,0:T(8,128)(2,1)S(1)}, u32[]{:S(2)}, u32[]{:S(2)}) %all-to-all-start) | async-done | bytes 655392 | tf_op jit(solution)/shard_map/all_to_all | solution.py:312
  26.2 0.0 copy-done.3
  26.3 1.1 %shard_map.120 = bf16[128,512]{1,0:T(8,128)(2,1)S(1)} custom-call(bf16[8,5,16,512]{3,2,1,0:T(8,128)(2,1)S(1)} %all-to-all-done.packed_ref, bf16[288,128]{1,0:T(8,128)(2,1)S(1)} %copy-done.5, bf16[128,288]{1,0:T(8,128)(2,1)S(1)} %copy-done.4, f32[2,9,512]{2,1,0:T(8,128)S(1)} %copy-done.6, f32[2,4,128]{2,1,0:T(4,128)S(1)} %copy-done.8, ...), custom_call_target="tpu_custom_call" | custom-call | flops 671088640 | bytes 1310720 | tf_op jit(solution)/shard_map/pallas_call | solution.py:301
  27.4 0.0 copy-start
  27.4 0.0 copy-start.1
  27.4 8.7 %all_to_all.10.conv_ref = bf16[8,16,512]{2,1,0:T(8,128)(2,1)S(1)} all-to-all(bf16[8,16,512]{2,1,0:T(8,128)(2,1)S(1)} %bitcast.3), channel_id=1, replica_groups={{20,12,24,8,16,0,28,4},{21,13,25,9,17,1,29,5},{22,14,26,10,18,2,30,6},{..., dimensions={0} | all-to-all | bytes 262144 | tf_op jit(solution)/shard_map/all_to_all | solution.py:312
  36.1 0.0 copy-done.1
  36.1 0.8 %shard_map.121 = bf16[512,128]{1,0:T(8,128)(2,1)} custom-call(bf16[8,16,512]{2,1,0:T(8,128)(2,1)S(1)} %all_to_all.10.conv_ref, bf16[128,512]{1,0:T(8,128)(2,1)S(1)} %copy-done.1, f32[1,512]{1,0:T(1,128)S(1)} %shard_map.119.scale_ref, bf16[512,128]{1,0:T(8,128)(2,1)S(1)} %copy-done), custom_call_target="tpu_custom_call" | custom-call | flops 655360 | bytes 524288 | tf_op jit(solution)/shard_map/pallas_call | solution.py:301
  (8 shorter events, 0.0 us)
Async XLA Ops:
  2.3 8.1 %copy-start.2 = (f32[1,512]{1,0:T(1,128)S(1)}, f32[1,512]{1,0:T(1,128)}, u32[]{:S(2)}) copy-start(f32[1,512]{1,0:T(1,128)} %get-tuple-element.9.refs_0_) | copy-start | bytes 6148
  2.3 23.9 %copy-start.3 = (bf16[2,256,256]{2,1,0:T(8,128)(2,1)S(1)}, bf16[2,256,256]{2,1,0:T(8,128)(2,1)}, u32[]{:S(2)}) copy-start(bf16[2,256,256]{2,1,0:T(8,128)(2,1)} %constant.16.clone.dft_ref) | copy-start | bytes 786436
  2.3 23.9 %copy-start.4 = (bf16[128,288]{1,0:T(8,128)(2,1)S(1)}, bf16[128,288]{1,0:T(8,128)(2,1)}, u32[]{:S(2)}) copy-start(bf16[128,288]{1,0:T(8,128)(2,1)} %constant.13.clone.last_ref) | copy-start | bytes 221188
  2.3 23.9 %copy-start.5 = (bf16[288,128]{1,0:T(8,128)(2,1)S(1)}, bf16[288,128]{1,0:T(8,128)(2,1)}, u32[]{:S(2)}) copy-start(bf16[288,128]{1,0:T(8,128)(2,1)} %constant.12.clone.first_ref) | copy-start | bytes 221188
  2.3 23.9 %copy-start.6 = (f32[2,9,512]{2,1,0:T(8,128)S(1)}, f32[2,9,512]{2,1,0:T(8,128)}, u32[]{:S(2)}) copy-start(f32[2,9,512]{2,1,0:T(8,128)} %constant.14.clone.twist_ref) | copy-start | bytes 110596
  2.4 23.9 %copy-start.7 = (bf16[128,128]{1,0:T(8,128)(2,1)S(1)}, bf16[128,128]{1,0:T(8,128)(2,1)}, u32[]{:S(2)}) copy-start(bf16[128,128]{1,0:T(8,128)(2,1)} %constant.17.clone.reverse_ref) | copy-start | bytes 98308
  2.4 23.9 %all-to-all-start = ((bf16[8,5,16,512]{3,2,1,0:T(8,128)(2,1)}), bf16[8,5,16,512]{3,2,1,0:T(8,128)(2,1)S(1)}, u32[]{:S(2)}, u32[]{:S(2)}) async-start(bf16[8,5,16,512]{3,2,1,0:T(8,128)(2,1)} %get-tuple-element.8), calls=%async_computation | async-start | bytes 1310720 | tf_op jit(solution)/shard_map/all_to_all | solution.py:312
  10.4 3.0 %collective-permute-start.2 = (f32[1,512]{1,0:T(1,128)S(1)}, f32[1,512]{1,0:T(1,128)S(1)}, u32[]{:S(2)}, u32[]{:S(2)}) collective-permute-start(f32[1,512]{1,0:T(1,128)S(1)} %copy-done.2), channel_id=1, source_target_pairs={{0,3},{1,2},{2,1},{3,0},{4,7},{5,6},{6,5},{7,4},{8,11},{9,10},{10,... | collective-permute-start | bytes 6152 | tf_op jit(solution)/shard_map/ppermute | solution.py:316
  10.7 3.6 %collective-permute-start.1 = (f32[1,512]{1,0:T(1,128)S(1)}, f32[1,512]{1,0:T(1,128)S(1)}, u32[]{:S(2)}, u32[]{:S(2)}) collective-permute-start(f32[1,512]{1,0:T(1,128)S(1)} %copy-done.2), channel_id=1, source_target_pairs={{0,2},{1,3},{2,0},{3,1},{4,6},{5,7},{6,4},{7,5},{8,10},{9,11},{10,... | collective-permute-start | bytes 6152 | tf_op jit(solution)/shard_map/ppermute | solution.py:316
  11.9 2.4 %collective-permute-start = (f32[1,512]{1,0:T(1,128)S(1)}, f32[1,512]{1,0:T(1,128)S(1)}, u32[]{:S(2)}, u32[]{:S(2)}) collective-permute-start(f32[1,512]{1,0:T(1,128)S(1)} %copy-done.2), channel_id=1, source_target_pairs={{0,1},{1,0},{2,3},{3,2},{4,5},{5,4},{6,7},{7,6},{8,9},{9,8},{10,11... | collective-permute-start | bytes 6152 | tf_op jit(solution)/shard_map/ppermute | solution.py:316
  14.3 11.9 %copy-start.8 = (f32[2,4,128]{2,1,0:T(4,128)S(1)}, f32[2,4,128]{2,1,0:T(4,128)}, u32[]{:S(2)}) copy-start(f32[2,4,128]{2,1,0:T(4,128)} %constant.15.clone.spin_ref) | copy-start | bytes 12292
  14.3 3.7 %collective-permute-start.3 = (f32[1,512]{1,0:T(1,128)S(1)}, f32[1,512]{1,0:T(1,128)S(1)}, u32[]{:S(2)}, u32[]{:S(2)}) collective-permute-start(f32[1,512]{1,0:T(1,128)S(1)} %shard_map.119.scale_ref), channel_id=1, source_target_pairs={{0,4},{4,0},{8,12},{12,8},{16,20},{20,16},{24,28},{28,24},{1,5},{5... | collective-permute-start | bytes 6152 | tf_op jit(solution)/shard_map/ppermute | solution.py:316
  18.1 5.6 %collective-permute-start.6 = (f32[2,512]{1,0:T(2,128)S(1)}, f32[2,512]{1,0:T(2,128)S(1)}, u32[]{:S(2)}, u32[]{:S(2)}) collective-permute-start(f32[2,512]{1,0:T(2,128)S(1)} %pad_maximum_fusion.refs_0_), channel_id=1, source_target_pairs={{0,24},{4,28},{8,16},{12,20},{16,8},{20,12},{24,0},{28,4},{1,25},{... | collective-permute-start | bytes 12296 | tf_op jit(solution)/shard_map/ppermute | solution.py:316
  19.6 5.8 %collective-permute-start.5 = (f32[2,512]{1,0:T(2,128)S(1)}, f32[2,512]{1,0:T(2,128)S(1)}, u32[]{:S(2)}, u32[]{:S(2)}) collective-permute-start(f32[2,512]{1,0:T(2,128)S(1)} %pad_maximum_fusion.refs_0_), channel_id=1, source_target_pairs={{0,16},{4,20},{8,24},{12,28},{16,0},{20,4},{24,8},{28,12},{1,17},{... | collective-permute-start | bytes 12296 | tf_op jit(solution)/shard_map/ppermute | solution.py:316
  20.4 4.9 %collective-permute-start.4 = (f32[2,512]{1,0:T(2,128)S(1)}, f32[2,512]{1,0:T(2,128)S(1)}, u32[]{:S(2)}, u32[]{:S(2)}) collective-permute-start(f32[2,512]{1,0:T(2,128)S(1)} %pad_maximum_fusion.refs_0_), channel_id=1, source_target_pairs={{0,8},{4,12},{8,0},{12,4},{16,24},{20,28},{24,16},{28,20},{1,9},{5... | collective-permute-start | bytes 12296 | tf_op jit(solution)/shard_map/ppermute | solution.py:316
  27.4 8.7 %copy-start = (bf16[512,128]{1,0:T(8,128)(2,1)S(1)}, bf16[512,128]{1,0:T(8,128)(2,1)}, u32[]{:S(2)}) copy-start(bf16[512,128]{1,0:T(8,128)(2,1)} %post_ref.1) | copy-start | bytes 393220
  27.4 8.7 %copy-start.1 = (bf16[128,512]{1,0:T(8,128)(2,1)S(1)}, bf16[128,512]{1,0:T(8,128)(2,1)}, u32[]{:S(2)}) copy-start(bf16[128,512]{1,0:T(8,128)(2,1)} %get-tuple-element.10.skipped_ref) | copy-start | bytes 393220

commit v15 on v14

--- a/solution.py
+++ b/solution.py
@@ -18,7 +18,7 @@
 def order_of(places, back=False):
     if places != 8:
         return tuple(range(places))
-    return (5, 3, 6, 2, 4, 0, 7, 1) if back else (4, 7, 3, 6, 2, 1, 5, 0)
+    return (5, 1, 3, 6, 2, 4, 0, 7) if back else (5, 6, 2, 7, 3, 0, 4, 1)
 
 
 def reverse_bits(index, levels):

time: 37.1 us -> 37.8 us (1.019)
  waiting for transfers between devices: 7.97 us -> 9.04 us
    ppermute x7, waiting for transfers between devices: 7.11 us -> 9.04 us  [swap(): lax.ppermute(value, axis, [(place, place ^ apart) for place in range(lax....]
    ppermute x7, starting transfers between devices: 7.86 us -> 6.96 us  [swap(): lax.ppermute(value, axis, [(place, place ^ apart) for place in range(lax....]
    all_to_all x1, waiting for transfers between devices: 0.87 us -> 0.01 us  [exchange(): lax.all_to_all(value, 'seq', split_axis=0, concat_axis=0, tiled=True, axi...]
    all_to_all x1, starting transfers between devices: 7.99 us -> 8.6 us  [exchange(): lax.all_to_all(value, 'seq', split_axis=0, concat_axis=0, tiled=True, axi...]
  transfers between devices with their start and end apart: 8 -> 8, of which waited for: 6 -> 5; matrix products, arithmetic and copies ran while one was open for 0% -> 0% of each run, Pallas kernels for 0% -> 0%
where the time goes in v15:
time: 37.8 us; the launch traced here: 37.6 us
  starting transfers between devices  15.6 us (41%)
  waiting for transfers between devices  9.04 us (24%)
  blocking collectives  8.58 us (23%)
  Pallas kernels  4.18 us (11%)
    ppermute x7, waiting for transfers between devices, swap(): lax.ppermute(value, axis, [(place, place ^ apart) for place in range(lax....  9.04 us
    all_to_all x1, starting transfers between devices, exchange(): lax.all_to_all(value, 'seq', split_axis=0, concat_axis=0, tiled=True, axi...  8.6 us
    all_to_all x1, blocking collectives, exchange(): lax.all_to_all(value, 'seq', split_axis=0, concat_axis=0, tiled=True, axi...  8.58 us
    ppermute x7, starting transfers between devices, swap(): lax.ppermute(value, axis, [(place, place ^ apart) for place in range(lax....  6.96 us
    pallas_call x4, Pallas kernels, call(): pl.pallas_call(kernel, out_shape=out_shape, compiler_params=pltpu.Compile...  4.18 us
  transfers between devices with their start and end apart: 8, of which 5 were waited for; matrix products, arithmetic and copies ran while one was open for 0% of the time, Pallas kernels for 0%

profile of v15, /device:TPU:0, one launch (start us, length us, event | category | flops | bytes accessed | tf_op | source)
XLA Modules:
  0.0 37.6 jit_solution(8429529164701942772)
XLA Ops:
  0.0 2.3 %shard_map.118 = (f32[1,512]{1,0:T(1,128)}, bf16[128,512]{1,0:T(8,128)(2,1)}, bf16[8,5,16,512]{3,2,1,0:T(8,128)(2,1)}) custom-call(bf16[512,128]{1,0:T(8,128)(2,1)} %features_ref.1, bf16[512,128]{1,0:T(8,128)(2,1)} %pre_ref.1, f32[1,128]{1,0:T(1,128)} %bitcast.4, f32[1,128]{1,0:T(1,128)} %bitcast.5, f32[2,2,512,128]{3,2,1,0:T(8,128)} %spectrum_ref.1), custom_call_target="tpu_custom_call" | custom-call | flops 655360 | bytes 2097152 | tf_op jit(solution)/shard_map/pallas_call | solution.py:301
  2.3 0.0 copy-start.2
  2.3 0.0 copy-start.3
  2.3 0.0 copy-start.4
  2.3 0.0 copy-start.5
  2.3 0.0 copy-start.6
  2.4 0.0 copy-start.7
  2.4 8.6 %all-to-all-start = ((bf16[8,5,16,512]{3,2,1,0:T(8,128)(2,1)}), bf16[8,5,16,512]{3,2,1,0:T(8,128)(2,1)S(1)}, u32[]{:S(2)}, u32[]{:S(2)}) async-start(bf16[8,5,16,512]{3,2,1,0:T(8,128)(2,1)} %get-tuple-element.8), calls=%async_computation | async-start | bytes 1310720 | tf_op jit(solution)/shard_map/all_to_all | solution.py:312
  11.0 0.0 copy-done.2
  11.0 0.7 %collective-permute-start.2 = (f32[1,512]{1,0:T(1,128)S(1)}, f32[1,512]{1,0:T(1,128)S(1)}, u32[]{:S(2)}, u32[]{:S(2)}) collective-permute-start(f32[1,512]{1,0:T(1,128)S(1)} %copy-done.2), channel_id=1, source_target_pairs={{0,3},{1,2},{2,1},{3,0},{4,7},{5,6},{6,5},{7,4},{8,11},{9,10},{10,... | collective-permute-start | bytes 6152 | tf_op jit(solution)/shard_map/ppermute | solution.py:316
  11.6 0.9 %collective-permute-start.1 = (f32[1,512]{1,0:T(1,128)S(1)}, f32[1,512]{1,0:T(1,128)S(1)}, u32[]{:S(2)}, u32[]{:S(2)}) collective-permute-start(f32[1,512]{1,0:T(1,128)S(1)} %copy-done.2), channel_id=1, source_target_pairs={{0,2},{1,3},{2,0},{3,1},{4,6},{5,7},{6,4},{7,5},{8,10},{9,11},{10,... | collective-permute-start | bytes 6152 | tf_op jit(solution)/shard_map/ppermute | solution.py:316
  12.5 0.3 collective-permute-start
  12.8 1.1 %collective-permute-done.2.refs_3_ = f32[1,512]{1,0:T(1,128)S(1)} collective-permute-done((f32[1,512]{1,0:T(1,128)S(1)}, f32[1,512]{1,0:T(1,128)S(1)}, u32[]{:S(2)}, u32[]{:S(2)}) %collective-permute-start.2) | collective-permute-done | bytes 2080 | tf_op jit(solution)/shard_map/ppermute | solution.py:316
  14.0 1.2 %collective-permute-done.1.refs_2_ = f32[1,512]{1,0:T(1,128)S(1)} collective-permute-done((f32[1,512]{1,0:T(1,128)S(1)}, f32[1,512]{1,0:T(1,128)S(1)}, u32[]{:S(2)}, u32[]{:S(2)}) %collective-permute-start.1) | collective-permute-done | bytes 2080 | tf_op jit(solution)/shard_map/ppermute | solution.py:316
  15.2 0.0 collective-permute-done.refs_1_
  15.2 0.0 copy-start.8
  15.3 0.6 %collective-permute-start.3 = (f32[1,512]{1,0:T(1,128)S(1)}, f32[1,512]{1,0:T(1,128)S(1)}, u32[]{:S(2)}, u32[]{:S(2)}) collective-permute-start(f32[1,512]{1,0:T(1,128)S(1)} %shard_map.119.scale_ref), channel_id=1, source_target_pairs={{0,4},{4,0},{8,12},{12,8},{16,20},{20,16},{24,28},{28,24},{1,5},{5... | collective-permute-start | bytes 6152 | tf_op jit(solution)/shard_map/ppermute | solution.py:316
  15.9 3.2 %collective-permute-done.3 = f32[1,512]{1,0:T(1,128)S(1)} collective-permute-done((f32[1,512]{1,0:T(1,128)S(1)}, f32[1,512]{1,0:T(1,128)S(1)}, u32[]{:S(2)}, u32[]{:S(2)}) %collective-permute-start.3) | collective-permute-done | bytes 2080 | tf_op jit(solution)/shard_map/ppermute | solution.py:316
  19.1 1.4 %collective-permute-start.6 = (f32[2,512]{1,0:T(2,128)S(1)}, f32[2,512]{1,0:T(2,128)S(1)}, u32[]{:S(2)}, u32[]{:S(2)}) collective-permute-start(f32[2,512]{1,0:T(2,128)S(1)} %pad_maximum_fusion.refs_0_), channel_id=1, source_target_pairs={{0,24},{4,28},{8,16},{12,20},{16,8},{20,12},{24,0},{28,4},{1,25},{... | collective-permute-start | bytes 12296 | tf_op jit(solution)/shard_map/ppermute | solution.py:316
  20.5 0.6 %collective-permute-start.5 = (f32[2,512]{1,0:T(2,128)S(1)}, f32[2,512]{1,0:T(2,128)S(1)}, u32[]{:S(2)}, u32[]{:S(2)}) collective-permute-start(f32[2,512]{1,0:T(2,128)S(1)} %pad_maximum_fusion.refs_0_), channel_id=1, source_target_pairs={{0,16},{4,20},{8,24},{12,28},{16,0},{20,4},{24,8},{28,12},{1,17},{... | collective-permute-start | bytes 12296 | tf_op jit(solution)/shard_map/ppermute | solution.py:316
  21.0 2.5 %collective-permute-start.4 = (f32[2,512]{1,0:T(2,128)S(1)}, f32[2,512]{1,0:T(2,128)S(1)}, u32[]{:S(2)}, u32[]{:S(2)}) collective-permute-start(f32[2,512]{1,0:T(2,128)S(1)} %pad_maximum_fusion.refs_0_), channel_id=1, source_target_pairs={{0,8},{4,12},{8,0},{12,4},{16,24},{20,28},{24,16},{28,20},{1,9},{5... | collective-permute-start | bytes 12296 | tf_op jit(solution)/shard_map/ppermute | solution.py:316
  23.5 1.1 %collective-permute-done.6.refs_3_ = f32[2,512]{1,0:T(2,128)S(1)} collective-permute-done((f32[2,512]{1,0:T(2,128)S(1)}, f32[2,512]{1,0:T(2,128)S(1)}, u32[]{:S(2)}, u32[]{:S(2)}) %collective-permute-start.6) | collective-permute-done | bytes 4128 | tf_op jit(solution)/shard_map/ppermute | solution.py:316
  24.6 2.4 %collective-permute-done.5.refs_2_ = f32[2,512]{1,0:T(2,128)S(1)} collective-permute-done((f32[2,512]{1,0:T(2,128)S(1)}, f32[2,512]{1,0:T(2,128)S(1)}, u32[]{:S(2)}, u32[]{:S(2)}) %collective-permute-start.5) | collective-permute-done | bytes 4128 | tf_op jit(solution)/shard_map/ppermute | solution.py:316
  27.0 0.0 collective-permute-done.4.refs_1_
  27.0 0.0 all-to-all-done.packed_ref
  27.0 0.0 copy-done.3
  27.0 0.0 copy-done.4
  27.1 1.1 %shard_map.120 = bf16[128,512]{1,0:T(8,128)(2,1)S(1)} custom-call(bf16[8,5,16,512]{3,2,1,0:T(8,128)(2,1)S(1)} %all-to-all-done.packed_ref, bf16[288,128]{1,0:T(8,128)(2,1)S(1)} %copy-done.5, bf16[128,288]{1,0:T(8,128)(2,1)S(1)} %copy-done.4, f32[2,9,512]{2,1,0:T(8,128)S(1)} %copy-done.6, f32[2,4,128]{2,1,0:T(4,128)S(1)} %copy-done.8, ...), custom_call_target="tpu_custom_call" | custom-call | flops 671088640 | bytes 1310720 | tf_op jit(solution)/shard_map/pallas_call | solution.py:301
  28.2 0.0 copy-start
  28.2 0.0 copy-start.1
  28.2 8.6 %all_to_all.10.conv_ref = bf16[8,16,512]{2,1,0:T(8,128)(2,1)S(1)} all-to-all(bf16[8,16,512]{2,1,0:T(8,128)(2,1)S(1)} %bitcast.3), channel_id=1, replica_groups={{20,4,12,24,8,16,0,28},{21,5,13,25,9,17,1,29},{22,6,14,26,10,18,2,30},{..., dimensions={0} | all-to-all | bytes 262144 | tf_op jit(solution)/shard_map/all_to_all | solution.py:312
  36.8 0.8 %shard_map.121 = bf16[512,128]{1,0:T(8,128)(2,1)} custom-call(bf16[8,16,512]{2,1,0:T(8,128)(2,1)S(1)} %all_to_all.10.conv_ref, bf16[128,512]{1,0:T(8,128)(2,1)S(1)} %copy-done.1, f32[1,512]{1,0:T(1,128)S(1)} %shard_map.119.scale_ref, bf16[512,128]{1,0:T(8,128)(2,1)S(1)} %copy-done), custom_call_target="tpu_custom_call" | custom-call | flops 655360 | bytes 524288 | tf_op jit(solution)/shard_map/pallas_call | solution.py:301
  (8 shorter events, 0.0 us)
Async XLA Ops:
  2.3 8.7 %copy-start.2 = (f32[1,512]{1,0:T(1,128)S(1)}, f32[1,512]{1,0:T(1,128)}, u32[]{:S(2)}) copy-start(f32[1,512]{1,0:T(1,128)} %get-tuple-element.9.refs_0_) | copy-start | bytes 6148
  2.3 24.7 %copy-start.3 = (bf16[2,256,256]{2,1,0:T(8,128)(2,1)S(1)}, bf16[2,256,256]{2,1,0:T(8,128)(2,1)}, u32[]{:S(2)}) copy-start(bf16[2,256,256]{2,1,0:T(8,128)(2,1)} %constant.16.clone.dft_ref) | copy-start | bytes 786436
  2.3 24.7 %copy-start.4 = (bf16[128,288]{1,0:T(8,128)(2,1)S(1)}, bf16[128,288]{1,0:T(8,128)(2,1)}, u32[]{:S(2)}) copy-start(bf16[128,288]{1,0:T(8,128)(2,1)} %constant.13.clone.last_ref) | copy-start | bytes 221188
  2.3 24.7 %copy-start.5 = (bf16[288,128]{1,0:T(8,128)(2,1)S(1)}, bf16[288,128]{1,0:T(8,128)(2,1)}, u32[]{:S(2)}) copy-start(bf16[288,128]{1,0:T(8,128)(2,1)} %constant.12.clone.first_ref) | copy-start | bytes 221188
  2.3 24.7 %copy-start.6 = (f32[2,9,512]{2,1,0:T(8,128)S(1)}, f32[2,9,512]{2,1,0:T(8,128)}, u32[]{:S(2)}) copy-start(f32[2,9,512]{2,1,0:T(8,128)} %constant.14.clone.twist_ref) | copy-start | bytes 110596
  2.4 24.7 %copy-start.7 = (bf16[128,128]{1,0:T(8,128)(2,1)S(1)}, bf16[128,128]{1,0:T(8,128)(2,1)}, u32[]{:S(2)}) copy-start(bf16[128,128]{1,0:T(8,128)(2,1)} %constant.17.clone.reverse_ref) | copy-start | bytes 98308
  2.4 24.6 %all-to-all-start = ((bf16[8,5,16,512]{3,2,1,0:T(8,128)(2,1)}), bf16[8,5,16,512]{3,2,1,0:T(8,128)(2,1)S(1)}, u32[]{:S(2)}, u32[]{:S(2)}) async-start(bf16[8,5,16,512]{3,2,1,0:T(8,128)(2,1)} %get-tuple-element.8), calls=%async_computation | async-start | bytes 1310720 | tf_op jit(solution)/shard_map/all_to_all | solution.py:312
  11.0 3.0 %collective-permute-start.2 = (f32[1,512]{1,0:T(1,128)S(1)}, f32[1,512]{1,0:T(1,128)S(1)}, u32[]{:S(2)}, u32[]{:S(2)}) collective-permute-start(f32[1,512]{1,0:T(1,128)S(1)} %copy-done.2), channel_id=1, source_target_pairs={{0,3},{1,2},{2,1},{3,0},{4,7},{5,6},{6,5},{7,4},{8,11},{9,10},{10,... | collective-permute-start | bytes 6152 | tf_op jit(solution)/shard_map/ppermute | solution.py:316
  11.6 3.6 %collective-permute-start.1 = (f32[1,512]{1,0:T(1,128)S(1)}, f32[1,512]{1,0:T(1,128)S(1)}, u32[]{:S(2)}, u32[]{:S(2)}) collective-permute-start(f32[1,512]{1,0:T(1,128)S(1)} %copy-done.2), channel_id=1, source_target_pairs={{0,2},{1,3},{2,0},{3,1},{4,6},{5,7},{6,4},{7,5},{8,10},{9,11},{10,... | collective-permute-start | bytes 6152 | tf_op jit(solution)/shard_map/ppermute | solution.py:316
  12.5 2.7 %collective-permute-start = (f32[1,512]{1,0:T(1,128)S(1)}, f32[1,512]{1,0:T(1,128)S(1)}, u32[]{:S(2)}, u32[]{:S(2)}) collective-permute-start(f32[1,512]{1,0:T(1,128)S(1)} %copy-done.2), channel_id=1, source_target_pairs={{0,1},{1,0},{2,3},{3,2},{4,5},{5,4},{6,7},{7,6},{8,9},{9,8},{10,11... | collective-permute-start | bytes 6152 | tf_op jit(solution)/shard_map/ppermute | solution.py:316
  15.2 11.8 %copy-start.8 = (f32[2,4,128]{2,1,0:T(4,128)S(1)}, f32[2,4,128]{2,1,0:T(4,128)}, u32[]{:S(2)}) copy-start(f32[2,4,128]{2,1,0:T(4,128)} %constant.15.clone.spin_ref) | copy-start | bytes 12292
  15.3 3.8 %collective-permute-start.3 = (f32[1,512]{1,0:T(1,128)S(1)}, f32[1,512]{1,0:T(1,128)S(1)}, u32[]{:S(2)}, u32[]{:S(2)}) collective-permute-start(f32[1,512]{1,0:T(1,128)S(1)} %shard_map.119.scale_ref), channel_id=1, source_target_pairs={{0,4},{4,0},{8,12},{12,8},{16,20},{20,16},{24,28},{28,24},{1,5},{5... | collective-permute-start | bytes 6152 | tf_op jit(solution)/shard_map/ppermute | solution.py:316
  19.1 5.6 %collective-permute-start.6 = (f32[2,512]{1,0:T(2,128)S(1)}, f32[2,512]{1,0:T(2,128)S(1)}, u32[]{:S(2)}, u32[]{:S(2)}) collective-permute-start(f32[2,512]{1,0:T(2,128)S(1)} %pad_maximum_fusion.refs_0_), channel_id=1, source_target_pairs={{0,24},{4,28},{8,16},{12,20},{16,8},{20,12},{24,0},{28,4},{1,25},{... | collective-permute-start | bytes 12296 | tf_op jit(solution)/shard_map/ppermute | solution.py:316
  20.5 6.5 %collective-permute-start.5 = (f32[2,512]{1,0:T(2,128)S(1)}, f32[2,512]{1,0:T(2,128)S(1)}, u32[]{:S(2)}, u32[]{:S(2)}) collective-permute-start(f32[2,512]{1,0:T(2,128)S(1)} %pad_maximum_fusion.refs_0_), channel_id=1, source_target_pairs={{0,16},{4,20},{8,24},{12,28},{16,0},{20,4},{24,8},{28,12},{1,17},{... | collective-permute-start | bytes 12296 | tf_op jit(solution)/shard_map/ppermute | solution.py:316
  21.0 6.0 %collective-permute-start.4 = (f32[2,512]{1,0:T(2,128)S(1)}, f32[2,512]{1,0:T(2,128)S(1)}, u32[]{:S(2)}, u32[]{:S(2)}) collective-permute-start(f32[2,512]{1,0:T(2,128)S(1)} %pad_maximum_fusion.refs_0_), channel_id=1, source_target_pairs={{0,8},{4,12},{8,0},{12,4},{16,24},{20,28},{24,16},{28,20},{1,9},{5... | collective-permute-start | bytes 12296 | tf_op jit(solution)/shard_map/ppermute | solution.py:316
  28.2 8.6 %copy-start = (bf16[512,128]{1,0:T(8,128)(2,1)S(1)}, bf16[512,128]{1,0:T(8,128)(2,1)}, u32[]{:S(2)}) copy-start(bf16[512,128]{1,0:T(8,128)(2,1)} %post_ref.1) | copy-start | bytes 393220
  28.2 8.6 %copy-start.1 = (bf16[128,512]{1,0:T(8,128)(2,1)S(1)}, bf16[128,512]{1,0:T(8,128)(2,1)}, u32[]{:S(2)}) copy-start(bf16[128,512]{1,0:T(8,128)(2,1)} %get-tuple-element.10.skipped_ref) | copy-start | bytes 393220

commit v16 on v12

--- a/solution.py
+++ b/solution.py
@@ -358,7 +358,7 @@
     if not piled:
         packed = packed.reshape(5, places, width, rows).transpose(1, 0, 2, 3)
     gathered = exchange(packed)
-    others = [swap(squares, "chan", apart) for apart in range(1, groups)]
+    others = [swap(squares, "chan", apart) for apart in range(groups - 1, 0, -1)]
     scale = call(
         functools.partial(scale_kernel, wide * groups), shape((1, rows), F32), 8 * rows, 32 * rows, squares, *others
     )

time: 37.1 us -> 37.1 us (level)
  no operation moved by 1% of the time
where the time goes in v16:
time: 37.1 us; the launch traced here: 36.9 us
  starting transfers between devices  15.8 us (43%)
  blocking collectives  8.67 us (23%)
  waiting for transfers between devices  8 us (22%)
  Pallas kernels  4.18 us (11%)
    all_to_all x1, blocking collectives, exchange(): lax.all_to_all(value, 'seq', split_axis=0, concat_axis=0, tiled=True, axi...  8.67 us
    all_to_all x1, starting transfers between devices, exchange(): lax.all_to_all(value, 'seq', split_axis=0, concat_axis=0, tiled=True, axi...  7.99 us
    ppermute x7, starting transfers between devices, swap(): lax.ppermute(value, axis, [(place, place ^ apart) for place in range(lax....  7.84 us
    ppermute x7, waiting for transfers between devices, swap(): lax.ppermute(value, axis, [(place, place ^ apart) for place in range(lax....  7.13 us
    pallas_call x4, Pallas kernels, call(): pl.pallas_call(kernel, out_shape=out_shape, compiler_params=pltpu.Compile...  4.18 us
    all_to_all x1, waiting for transfers between devices, exchange(): lax.all_to_all(value, 'seq', split_axis=0, concat_axis=0, tiled=True, axi...  0.87 us
  transfers between devices with their start and end apart: 8, of which 6 were waited for; matrix products, arithmetic and copies ran while one was open for 0% of the time, Pallas kernels for 0%

profile of v16, /device:TPU:0, one launch (start us, length us, event | category | flops | bytes accessed | tf_op | source)
XLA Modules:
  0.0 36.9 jit_solution(853964327652411100)
XLA Ops:
  0.0 2.3 %shard_map.118 = (f32[1,512]{1,0:T(1,128)}, bf16[128,512]{1,0:T(8,128)(2,1)}, bf16[8,5,16,512]{3,2,1,0:T(8,128)(2,1)}) custom-call(bf16[512,128]{1,0:T(8,128)(2,1)} %features_ref.1, bf16[512,128]{1,0:T(8,128)(2,1)} %pre_ref.1, f32[1,128]{1,0:T(1,128)} %bitcast.4, f32[1,128]{1,0:T(1,128)} %bitcast.5, f32[2,2,512,128]{3,2,1,0:T(8,128)} %spectrum_ref.1), custom_call_target="tpu_custom_call" | custom-call | flops 655360 | bytes 2097152 | tf_op jit(solution)/shard_map/pallas_call | solution.py:301
  2.3 0.0 copy-start.2
  2.3 0.0 copy-start.3
  2.3 0.0 copy-start.4
  2.3 0.0 copy-start.5
  2.3 0.0 copy-start.6
  2.4 0.0 copy-start.7
  2.4 8.0 %all-to-all-start = ((bf16[8,5,16,512]{3,2,1,0:T(8,128)(2,1)}), bf16[8,5,16,512]{3,2,1,0:T(8,128)(2,1)S(1)}, u32[]{:S(2)}, u32[]{:S(2)}) async-start(bf16[8,5,16,512]{3,2,1,0:T(8,128)(2,1)} %get-tuple-element.8), calls=%async_computation | async-start | bytes 1310720 | tf_op jit(solution)/shard_map/all_to_all | solution.py:312
  10.4 0.0 copy-done.2
  10.4 0.0 collective-permute-start.2
  10.4 1.6 %collective-permute-start.1 = (f32[1,512]{1,0:T(1,128)S(1)}, f32[1,512]{1,0:T(1,128)S(1)}, u32[]{:S(2)}, u32[]{:S(2)}) collective-permute-start(f32[1,512]{1,0:T(1,128)S(1)} %copy-done.2), channel_id=1, source_target_pairs={{0,2},{1,3},{2,0},{3,1},{4,6},{5,7},{6,4},{7,5},{8,10},{9,11},{10,... | collective-permute-start | bytes 6152 | tf_op jit(solution)/shard_map/ppermute | solution.py:316
  11.9 0.3 collective-permute-start
  12.2 0.0 collective-permute-done.2.refs_3_
  12.2 1.8 %collective-permute-done.1.refs_2_ = f32[1,512]{1,0:T(1,128)S(1)} collective-permute-done((f32[1,512]{1,0:T(1,128)S(1)}, f32[1,512]{1,0:T(1,128)S(1)}, u32[]{:S(2)}, u32[]{:S(2)}) %collective-permute-start.1) | collective-permute-done | bytes 2080 | tf_op jit(solution)/shard_map/ppermute | solution.py:316
  14.0 0.9 %collective-permute-done.refs_1_ = f32[1,512]{1,0:T(1,128)S(1)} collective-permute-done((f32[1,512]{1,0:T(1,128)S(1)}, f32[1,512]{1,0:T(1,128)S(1)}, u32[]{:S(2)}, u32[]{:S(2)}) %collective-permute-start) | collective-permute-done | bytes 2080 | tf_op jit(solution)/shard_map/ppermute | solution.py:316
  15.0 1.5 %collective-permute-start.3 = (f32[1,512]{1,0:T(1,128)S(1)}, f32[1,512]{1,0:T(1,128)S(1)}, u32[]{:S(2)}, u32[]{:S(2)}) collective-permute-start(f32[1,512]{1,0:T(1,128)S(1)} %shard_map.119.scale_ref), channel_id=1, source_target_pairs={{0,4},{4,0},{8,12},{12,8},{16,20},{20,16},{24,28},{28,24},{1,5},{5... | collective-permute-start | bytes 6152 | tf_op jit(solution)/shard_map/ppermute | solution.py:316
  16.5 2.3 %collective-permute-done.3 = f32[1,512]{1,0:T(1,128)S(1)} collective-permute-done((f32[1,512]{1,0:T(1,128)S(1)}, f32[1,512]{1,0:T(1,128)S(1)}, u32[]{:S(2)}, u32[]{:S(2)}) %collective-permute-start.3) | collective-permute-done | bytes 2080 | tf_op jit(solution)/shard_map/ppermute | solution.py:316
  18.8 1.4 %collective-permute-start.6 = (f32[2,512]{1,0:T(2,128)S(1)}, f32[2,512]{1,0:T(2,128)S(1)}, u32[]{:S(2)}, u32[]{:S(2)}) collective-permute-start(f32[2,512]{1,0:T(2,128)S(1)} %pad_maximum_fusion.refs_0_), channel_id=1, source_target_pairs={{0,24},{4,28},{8,16},{12,20},{16,8},{20,12},{24,0},{28,4},{1,25},{... | collective-permute-start | bytes 12296 | tf_op jit(solution)/shard_map/ppermute | solution.py:316
  20.2 0.5 %collective-permute-start.5 = (f32[2,512]{1,0:T(2,128)S(1)}, f32[2,512]{1,0:T(2,128)S(1)}, u32[]{:S(2)}, u32[]{:S(2)}) collective-permute-start(f32[2,512]{1,0:T(2,128)S(1)} %pad_maximum_fusion.refs_0_), channel_id=1, source_target_pairs={{0,16},{4,20},{8,24},{12,28},{16,0},{20,4},{24,8},{28,12},{1,17},{... | collective-permute-start | bytes 12296 | tf_op jit(solution)/shard_map/ppermute | solution.py:316
  20.7 2.5 %collective-permute-start.4 = (f32[2,512]{1,0:T(2,128)S(1)}, f32[2,512]{1,0:T(2,128)S(1)}, u32[]{:S(2)}, u32[]{:S(2)}) collective-permute-start(f32[2,512]{1,0:T(2,128)S(1)} %pad_maximum_fusion.refs_0_), channel_id=1, source_target_pairs={{0,8},{4,12},{8,0},{12,4},{16,24},{20,28},{24,16},{28,20},{1,9},{5... | collective-permute-start | bytes 12296 | tf_op jit(solution)/shard_map/ppermute | solution.py:316
  23.2 1.1 %collective-permute-done.6.refs_3_ = f32[2,512]{1,0:T(2,128)S(1)} collective-permute-done((f32[2,512]{1,0:T(2,128)S(1)}, f32[2,512]{1,0:T(2,128)S(1)}, u32[]{:S(2)}, u32[]{:S(2)}) %collective-permute-start.6) | collective-permute-done | bytes 4128 | tf_op jit(solution)/shard_map/ppermute | solution.py:316
  24.4 1.0 %collective-permute-done.5.refs_2_ = f32[2,512]{1,0:T(2,128)S(1)} collective-permute-done((f32[2,512]{1,0:T(2,128)S(1)}, f32[2,512]{1,0:T(2,128)S(1)}, u32[]{:S(2)}, u32[]{:S(2)}) %collective-permute-start.5) | collective-permute-done | bytes 4128 | tf_op jit(solution)/shard_map/ppermute | solution.py:316
  25.4 0.0 collective-permute-done.4.refs_1_
  25.4 0.9 %all-to-all-done.packed_ref = bf16[8,5,16,512]{3,2,1,0:T(8,128)(2,1)S(1)} async-done(((bf16[8,5,16,512]{3,2,1,0:T(8,128)(2,1)}), bf16[8,5,16,512]{3,2,1,0:T(8,128)(2,1)S(1)}, u32[]{:S(2)}, u32[]{:S(2)}) %all-to-all-start) | async-done | bytes 655392 | tf_op jit(solution)/shard_map/all_to_all | solution.py:312
  26.2 0.0 copy-done.3
  26.2 0.0 copy-done.4
  26.2 0.0 copy-done.5
  26.3 1.1 %shard_map.120 = bf16[128,512]{1,0:T(8,128)(2,1)S(1)} custom-call(bf16[8,5,16,512]{3,2,1,0:T(8,128)(2,1)S(1)} %all-to-all-done.packed_ref, bf16[288,128]{1,0:T(8,128)(2,1)S(1)} %copy-done.5, bf16[128,288]{1,0:T(8,128)(2,1)S(1)} %copy-done.4, f32[2,9,512]{2,1,0:T(8,128)S(1)} %copy-done.6, f32[2,4,128]{2,1,0:T(4,128)S(1)} %copy-done.8, ...), custom_call_target="tpu_custom_call" | custom-call | flops 671088640 | bytes 1310720 | tf_op jit(solution)/shard_map/pallas_call | solution.py:301
  27.4 0.0 copy-start
  27.4 0.0 copy-start.1
  27.4 8.7 %all_to_all.10.conv_ref = bf16[8,16,512]{2,1,0:T(8,128)(2,1)S(1)} all-to-all(bf16[8,16,512]{2,1,0:T(8,128)(2,1)S(1)} %bitcast.3), channel_id=1, replica_groups={{20,4,12,24,8,16,0,28},{21,5,13,25,9,17,1,29},{22,6,14,26,10,18,2,30},{..., dimensions={0} | all-to-all | bytes 262144 | tf_op jit(solution)/shard_map/all_to_all | solution.py:312
  36.1 0.8 %shard_map.121 = bf16[512,128]{1,0:T(8,128)(2,1)} custom-call(bf16[8,16,512]{2,1,0:T(8,128)(2,1)S(1)} %all_to_all.10.conv_ref, bf16[128,512]{1,0:T(8,128)(2,1)S(1)} %copy-done.1, f32[1,512]{1,0:T(1,128)S(1)} %shard_map.119.scale_ref, bf16[512,128]{1,0:T(8,128)(2,1)S(1)} %copy-done), custom_call_target="tpu_custom_call" | custom-call | flops 655360 | bytes 524288 | tf_op jit(solution)/shard_map/pallas_call | solution.py:301
  (8 shorter events, 0.0 us)
Async XLA Ops:
  2.3 8.1 %copy-start.2 = (f32[1,512]{1,0:T(1,128)S(1)}, f32[1,512]{1,0:T(1,128)}, u32[]{:S(2)}) copy-start(f32[1,512]{1,0:T(1,128)} %get-tuple-element.9.refs_0_) | copy-start | bytes 6148
  2.3 23.9 %copy-start.3 = (bf16[2,256,256]{2,1,0:T(8,128)(2,1)S(1)}, bf16[2,256,256]{2,1,0:T(8,128)(2,1)}, u32[]{:S(2)}) copy-start(bf16[2,256,256]{2,1,0:T(8,128)(2,1)} %constant.16.clone.dft_ref) | copy-start | bytes 786436
  2.3 23.9 %copy-start.4 = (bf16[128,288]{1,0:T(8,128)(2,1)S(1)}, bf16[128,288]{1,0:T(8,128)(2,1)}, u32[]{:S(2)}) copy-start(bf16[128,288]{1,0:T(8,128)(2,1)} %constant.13.clone.last_ref) | copy-start | bytes 221188
  2.3 23.9 %copy-start.5 = (bf16[288,128]{1,0:T(8,128)(2,1)S(1)}, bf16[288,128]{1,0:T(8,128)(2,1)}, u32[]{:S(2)}) copy-start(bf16[288,128]{1,0:T(8,128)(2,1)} %constant.12.clone.first_ref) | copy-start | bytes 221188
  2.3 23.9 %copy-start.6 = (f32[2,9,512]{2,1,0:T(8,128)S(1)}, f32[2,9,512]{2,1,0:T(8,128)}, u32[]{:S(2)}) copy-start(f32[2,9,512]{2,1,0:T(8,128)} %constant.14.clone.twist_ref) | copy-start | bytes 110596
  2.4 23.9 %copy-start.7 = (bf16[128,128]{1,0:T(8,128)(2,1)S(1)}, bf16[128,128]{1,0:T(8,128)(2,1)}, u32[]{:S(2)}) copy-start(bf16[128,128]{1,0:T(8,128)(2,1)} %constant.17.clone.reverse_ref) | copy-start | bytes 98308
  2.4 23.9 %all-to-all-start = ((bf16[8,5,16,512]{3,2,1,0:T(8,128)(2,1)}), bf16[8,5,16,512]{3,2,1,0:T(8,128)(2,1)S(1)}, u32[]{:S(2)}, u32[]{:S(2)}) async-start(bf16[8,5,16,512]{3,2,1,0:T(8,128)(2,1)} %get-tuple-element.8), calls=%async_computation | async-start | bytes 1310720 | tf_op jit(solution)/shard_map/all_to_all | solution.py:312
  10.4 1.9 %collective-permute-start.2 = (f32[1,512]{1,0:T(1,128)S(1)}, f32[1,512]{1,0:T(1,128)S(1)}, u32[]{:S(2)}, u32[]{:S(2)}) collective-permute-start(f32[1,512]{1,0:T(1,128)S(1)} %copy-done.2), channel_id=1, source_target_pairs={{0,1},{1,0},{2,3},{3,2},{4,5},{5,4},{6,7},{7,6},{8,9},{9,8},{10,11... | collective-permute-start | bytes 6152 | tf_op jit(solution)/shard_map/ppermute | solution.py:316
  10.4 3.7 %collective-permute-start.1 = (f32[1,512]{1,0:T(1,128)S(1)}, f32[1,512]{1,0:T(1,128)S(1)}, u32[]{:S(2)}, u32[]{:S(2)}) collective-permute-start(f32[1,512]{1,0:T(1,128)S(1)} %copy-done.2), channel_id=1, source_target_pairs={{0,2},{1,3},{2,0},{3,1},{4,6},{5,7},{6,4},{7,5},{8,10},{9,11},{10,... | collective-permute-start | bytes 6152 | tf_op jit(solution)/shard_map/ppermute | solution.py:316
  11.9 3.0 %collective-permute-start = (f32[1,512]{1,0:T(1,128)S(1)}, f32[1,512]{1,0:T(1,128)S(1)}, u32[]{:S(2)}, u32[]{:S(2)}) collective-permute-start(f32[1,512]{1,0:T(1,128)S(1)} %copy-done.2), channel_id=1, source_target_pairs={{0,3},{1,2},{2,1},{3,0},{4,7},{5,6},{6,5},{7,4},{8,11},{9,10},{10,... | collective-permute-start | bytes 6152 | tf_op jit(solution)/shard_map/ppermute | solution.py:316
  14.9 11.3 %copy-start.8 = (f32[2,4,128]{2,1,0:T(4,128)S(1)}, f32[2,4,128]{2,1,0:T(4,128)}, u32[]{:S(2)}) copy-start(f32[2,4,128]{2,1,0:T(4,128)} %constant.15.clone.spin_ref) | copy-start | bytes 12292
  15.0 3.8 %collective-permute-start.3 = (f32[1,512]{1,0:T(1,128)S(1)}, f32[1,512]{1,0:T(1,128)S(1)}, u32[]{:S(2)}, u32[]{:S(2)}) collective-permute-start(f32[1,512]{1,0:T(1,128)S(1)} %shard_map.119.scale_ref), channel_id=1, source_target_pairs={{0,4},{4,0},{8,12},{12,8},{16,20},{20,16},{24,28},{28,24},{1,5},{5... | collective-permute-start | bytes 6152 | tf_op jit(solution)/shard_map/ppermute | solution.py:316
  18.8 5.6 %collective-permute-start.6 = (f32[2,512]{1,0:T(2,128)S(1)}, f32[2,512]{1,0:T(2,128)S(1)}, u32[]{:S(2)}, u32[]{:S(2)}) collective-permute-start(f32[2,512]{1,0:T(2,128)S(1)} %pad_maximum_fusion.refs_0_), channel_id=1, source_target_pairs={{0,24},{4,28},{8,16},{12,20},{16,8},{20,12},{24,0},{28,4},{1,25},{... | collective-permute-start | bytes 12296 | tf_op jit(solution)/shard_map/ppermute | solution.py:316
  20.2 5.2 %collective-permute-start.5 = (f32[2,512]{1,0:T(2,128)S(1)}, f32[2,512]{1,0:T(2,128)S(1)}, u32[]{:S(2)}, u32[]{:S(2)}) collective-permute-start(f32[2,512]{1,0:T(2,128)S(1)} %pad_maximum_fusion.refs_0_), channel_id=1, source_target_pairs={{0,16},{4,20},{8,24},{12,28},{16,0},{20,4},{24,8},{28,12},{1,17},{... | collective-permute-start | bytes 12296 | tf_op jit(solution)/shard_map/ppermute | solution.py:316
  20.7 4.7 %collective-permute-start.4 = (f32[2,512]{1,0:T(2,128)S(1)}, f32[2,512]{1,0:T(2,128)S(1)}, u32[]{:S(2)}, u32[]{:S(2)}) collective-permute-start(f32[2,512]{1,0:T(2,128)S(1)} %pad_maximum_fusion.refs_0_), channel_id=1, source_target_pairs={{0,8},{4,12},{8,0},{12,4},{16,24},{20,28},{24,16},{28,20},{1,9},{5... | collective-permute-start | bytes 12296 | tf_op jit(solution)/shard_map/ppermute | solution.py:316
  27.4 8.7 %copy-start = (bf16[512,128]{1,0:T(8,128)(2,1)S(1)}, bf16[512,128]{1,0:T(8,128)(2,1)}, u32[]{:S(2)}) copy-start(bf16[512,128]{1,0:T(8,128)(2,1)} %post_ref.1) | copy-start | bytes 393220
  27.4 8.7 %copy-start.1 = (bf16[128,512]{1,0:T(8,128)(2,1)S(1)}, bf16[128,512]{1,0:T(8,128)(2,1)}, u32[]{:S(2)}) copy-start(bf16[128,512]{1,0:T(8,128)(2,1)} %get-tuple-element.10.skipped_ref) | copy-start | bytes 393220

commit v17 on v12

--- a/solution.py
+++ b/solution.py
@@ -187,7 +187,7 @@
     order = order_of(places)
     direct, mirrors = pair_rows(places)
     quarters = [pl.ds(turn * block, block) for turn in range(4)]
-    groups = [range(begin, min(begin + 3, places + 1)) for begin in range(0, places + 1, 3)]
+    groups = [range(begin, min(begin + 5, places + 1)) for begin in range(0, places + 1, 5)]
     for row, holder in enumerate(mirrors[1:places]):
         for part in range(2):
             for turn in range(4):

time: 37.1 us -> 37 us (level)
  no operation moved by 1% of the time
where the time goes in v17:
time: 37 us; the launch traced here: 36.8 us
  starting transfers between devices  15.8 us (43%)
  blocking collectives  8.67 us (23%)
  waiting for transfers between devices  7.97 us (22%)
  Pallas kernels  4.1 us (11%)
    all_to_all x1, blocking collectives, exchange(): lax.all_to_all(value, 'seq', split_axis=0, concat_axis=0, tiled=True, axi...  8.67 us
    all_to_all x1, starting transfers between devices, exchange(): lax.all_to_all(value, 'seq', split_axis=0, concat_axis=0, tiled=True, axi...  7.99 us
    ppermute x7, starting transfers between devices, swap(): lax.ppermute(value, axis, [(place, place ^ apart) for place in range(lax....  7.86 us
    ppermute x7, waiting for transfers between devices, swap(): lax.ppermute(value, axis, [(place, place ^ apart) for place in range(lax....  7.11 us
    pallas_call x4, Pallas kernels, call(): pl.pallas_call(kernel, out_shape=out_shape, compiler_params=pltpu.Compile...  4.1 us
    all_to_all x1, waiting for transfers between devices, exchange(): lax.all_to_all(value, 'seq', split_axis=0, concat_axis=0, tiled=True, axi...  0.87 us
  transfers between devices with their start and end apart: 8, of which 6 were waited for; matrix products, arithmetic and copies ran while one was open for 0% of the time, Pallas kernels for 0%

profile of v17, /device:TPU:0, one launch (start us, length us, event | category | flops | bytes accessed | tf_op | source)
XLA Modules:
  0.0 36.8 jit_solution(12109244722622303965)
XLA Ops:
  0.0 2.3 %shard_map.118 = (f32[1,512]{1,0:T(1,128)}, bf16[128,512]{1,0:T(8,128)(2,1)}, bf16[8,5,16,512]{3,2,1,0:T(8,128)(2,1)}) custom-call(bf16[512,128]{1,0:T(8,128)(2,1)} %features_ref.1, bf16[512,128]{1,0:T(8,128)(2,1)} %pre_ref.1, f32[1,128]{1,0:T(1,128)} %bitcast.4, f32[1,128]{1,0:T(1,128)} %bitcast.5, f32[2,2,512,128]{3,2,1,0:T(8,128)} %spectrum_ref.1), custom_call_target="tpu_custom_call" | custom-call | flops 655360 | bytes 2097152 | tf_op jit(solution)/shard_map/pallas_call | solution.py:301
  2.3 0.0 copy-start.2
  2.3 0.0 copy-start.3
  2.3 0.0 copy-start.4
  2.3 0.0 copy-start.5
  2.3 0.0 copy-start.6
  2.4 0.0 copy-start.7
  2.4 8.0 %all-to-all-start = ((bf16[8,5,16,512]{3,2,1,0:T(8,128)(2,1)}), bf16[8,5,16,512]{3,2,1,0:T(8,128)(2,1)S(1)}, u32[]{:S(2)}, u32[]{:S(2)}) async-start(bf16[8,5,16,512]{3,2,1,0:T(8,128)(2,1)} %get-tuple-element.8), calls=%async_computation | async-start | bytes 1310720 | tf_op jit(solution)/shard_map/all_to_all | solution.py:312
  10.4 0.0 copy-done.2
  10.4 0.4 %collective-permute-start.2 = (f32[1,512]{1,0:T(1,128)S(1)}, f32[1,512]{1,0:T(1,128)S(1)}, u32[]{:S(2)}, u32[]{:S(2)}) collective-permute-start(f32[1,512]{1,0:T(1,128)S(1)} %copy-done.2), channel_id=1, source_target_pairs={{0,3},{1,2},{2,1},{3,0},{4,7},{5,6},{6,5},{7,4},{8,11},{9,10},{10,... | collective-permute-start | bytes 6152 | tf_op jit(solution)/shard_map/ppermute | solution.py:316
  10.7 1.2 %collective-permute-start.1 = (f32[1,512]{1,0:T(1,128)S(1)}, f32[1,512]{1,0:T(1,128)S(1)}, u32[]{:S(2)}, u32[]{:S(2)}) collective-permute-start(f32[1,512]{1,0:T(1,128)S(1)} %copy-done.2), channel_id=1, source_target_pairs={{0,2},{1,3},{2,0},{3,1},{4,6},{5,7},{6,4},{7,5},{8,10},{9,11},{10,... | collective-permute-start | bytes 6152 | tf_op jit(solution)/shard_map/ppermute | solution.py:316
  11.9 0.3 collective-permute-start
  12.2 1.1 %collective-permute-done.2.refs_3_ = f32[1,512]{1,0:T(1,128)S(1)} collective-permute-done((f32[1,512]{1,0:T(1,128)S(1)}, f32[1,512]{1,0:T(1,128)S(1)}, u32[]{:S(2)}, u32[]{:S(2)}) %collective-permute-start.2) | collective-permute-done | bytes 2080 | tf_op jit(solution)/shard_map/ppermute | solution.py:316
  13.4 0.9 %collective-permute-done.1.refs_2_ = f32[1,512]{1,0:T(1,128)S(1)} collective-permute-done((f32[1,512]{1,0:T(1,128)S(1)}, f32[1,512]{1,0:T(1,128)S(1)}, u32[]{:S(2)}, u32[]{:S(2)}) %collective-permute-start.1) | collective-permute-done | bytes 2080 | tf_op jit(solution)/shard_map/ppermute | solution.py:316
  14.3 0.0 collective-permute-done.refs_1_
  14.3 0.0 copy-start.8
  14.3 1.5 %collective-permute-start.3 = (f32[1,512]{1,0:T(1,128)S(1)}, f32[1,512]{1,0:T(1,128)S(1)}, u32[]{:S(2)}, u32[]{:S(2)}) collective-permute-start(f32[1,512]{1,0:T(1,128)S(1)} %shard_map.119.scale_ref), channel_id=1, source_target_pairs={{0,4},{4,0},{8,12},{12,8},{16,20},{20,16},{24,28},{28,24},{1,5},{5... | collective-permute-start | bytes 6152 | tf_op jit(solution)/shard_map/ppermute | solution.py:316
  15.9 2.2 %collective-permute-done.3 = f32[1,512]{1,0:T(1,128)S(1)} collective-permute-done((f32[1,512]{1,0:T(1,128)S(1)}, f32[1,512]{1,0:T(1,128)S(1)}, u32[]{:S(2)}, u32[]{:S(2)}) %collective-permute-start.3) | collective-permute-done | bytes 2080 | tf_op jit(solution)/shard_map/ppermute | solution.py:316
  18.1 1.5 %collective-permute-start.6 = (f32[2,512]{1,0:T(2,128)S(1)}, f32[2,512]{1,0:T(2,128)S(1)}, u32[]{:S(2)}, u32[]{:S(2)}) collective-permute-start(f32[2,512]{1,0:T(2,128)S(1)} %pad_maximum_fusion.refs_0_), channel_id=1, source_target_pairs={{0,24},{4,28},{8,16},{12,20},{16,8},{20,12},{24,0},{28,4},{1,25},{... | collective-permute-start | bytes 12296 | tf_op jit(solution)/shard_map/ppermute | solution.py:316
  19.6 0.8 %collective-permute-start.5 = (f32[2,512]{1,0:T(2,128)S(1)}, f32[2,512]{1,0:T(2,128)S(1)}, u32[]{:S(2)}, u32[]{:S(2)}) collective-permute-start(f32[2,512]{1,0:T(2,128)S(1)} %pad_maximum_fusion.refs_0_), channel_id=1, source_target_pairs={{0,16},{4,20},{8,24},{12,28},{16,0},{20,4},{24,8},{28,12},{1,17},{... | collective-permute-start | bytes 12296 | tf_op jit(solution)/shard_map/ppermute | solution.py:316
  20.4 2.1 %collective-permute-start.4 = (f32[2,512]{1,0:T(2,128)S(1)}, f32[2,512]{1,0:T(2,128)S(1)}, u32[]{:S(2)}, u32[]{:S(2)}) collective-permute-start(f32[2,512]{1,0:T(2,128)S(1)} %pad_maximum_fusion.refs_0_), channel_id=1, source_target_pairs={{0,8},{4,12},{8,0},{12,4},{16,24},{20,28},{24,16},{28,20},{1,9},{5... | collective-permute-start | bytes 12296 | tf_op jit(solution)/shard_map/ppermute | solution.py:316
  22.5 1.1 %collective-permute-done.6.refs_3_ = f32[2,512]{1,0:T(2,128)S(1)} collective-permute-done((f32[2,512]{1,0:T(2,128)S(1)}, f32[2,512]{1,0:T(2,128)S(1)}, u32[]{:S(2)}, u32[]{:S(2)}) %collective-permute-start.6) | collective-permute-done | bytes 4128 | tf_op jit(solution)/shard_map/ppermute | solution.py:316
  23.7 1.7 %collective-permute-done.5.refs_2_ = f32[2,512]{1,0:T(2,128)S(1)} collective-permute-done((f32[2,512]{1,0:T(2,128)S(1)}, f32[2,512]{1,0:T(2,128)S(1)}, u32[]{:S(2)}, u32[]{:S(2)}) %collective-permute-start.5) | collective-permute-done | bytes 4128 | tf_op jit(solution)/shard_map/ppermute | solution.py:316
  25.4 0.0 collective-permute-done.4.refs_1_
  25.4 0.9 %all-to-all-done.packed_ref = bf16[8,5,16,512]{3,2,1,0:T(8,128)(2,1)S(1)} async-done(((bf16[8,5,16,512]{3,2,1,0:T(8,128)(2,1)}), bf16[8,5,16,512]{3,2,1,0:T(8,128)(2,1)S(1)}, u32[]{:S(2)}, u32[]{:S(2)}) %all-to-all-start) | async-done | bytes 655392 | tf_op jit(solution)/shard_map/all_to_all | solution.py:312
  26.2 0.0 copy-done.3
  26.3 1.0 %shard_map.120 = bf16[128,512]{1,0:T(8,128)(2,1)S(1)} custom-call(bf16[8,5,16,512]{3,2,1,0:T(8,128)(2,1)S(1)} %all-to-all-done.packed_ref, bf16[288,128]{1,0:T(8,128)(2,1)S(1)} %copy-done.5, bf16[128,288]{1,0:T(8,128)(2,1)S(1)} %copy-done.4, f32[2,9,512]{2,1,0:T(8,128)S(1)} %copy-done.6, f32[2,4,128]{2,1,0:T(4,128)S(1)} %copy-done.8, ...), custom_call_target="tpu_custom_call" | custom-call | flops 671088640 | bytes 1310720 | tf_op jit(solution)/shard_map/pallas_call | solution.py:301
  27.3 0.0 copy-start
  27.3 0.0 copy-start.1
  27.3 8.7 %all_to_all.10.conv_ref = bf16[8,16,512]{2,1,0:T(8,128)(2,1)S(1)} all-to-all(bf16[8,16,512]{2,1,0:T(8,128)(2,1)S(1)} %bitcast.3), channel_id=1, replica_groups={{20,4,12,24,8,16,0,28},{21,5,13,25,9,17,1,29},{22,6,14,26,10,18,2,30},{..., dimensions={0} | all-to-all | bytes 262144 | tf_op jit(solution)/shard_map/all_to_all | solution.py:312
  36.0 0.0 copy-done
  36.0 0.8 %shard_map.121 = bf16[512,128]{1,0:T(8,128)(2,1)} custom-call(bf16[8,16,512]{2,1,0:T(8,128)(2,1)S(1)} %all_to_all.10.conv_ref, bf16[128,512]{1,0:T(8,128)(2,1)S(1)} %copy-done.1, f32[1,512]{1,0:T(1,128)S(1)} %shard_map.119.scale_ref, bf16[512,128]{1,0:T(8,128)(2,1)S(1)} %copy-done), custom_call_target="tpu_custom_call" | custom-call | flops 655360 | bytes 524288 | tf_op jit(solution)/shard_map/pallas_call | solution.py:301
  (8 shorter events, 0.0 us)
Async XLA Ops:
  2.3 8.1 %copy-start.2 = (f32[1,512]{1,0:T(1,128)S(1)}, f32[1,512]{1,0:T(1,128)}, u32[]{:S(2)}) copy-start(f32[1,512]{1,0:T(1,128)} %get-tuple-element.9.refs_0_) | copy-start | bytes 6148
  2.3 23.9 %copy-start.3 = (bf16[2,256,256]{2,1,0:T(8,128)(2,1)S(1)}, bf16[2,256,256]{2,1,0:T(8,128)(2,1)}, u32[]{:S(2)}) copy-start(bf16[2,256,256]{2,1,0:T(8,128)(2,1)} %constant.16.clone.dft_ref) | copy-start | bytes 786436
  2.3 23.9 %copy-start.4 = (bf16[128,288]{1,0:T(8,128)(2,1)S(1)}, bf16[128,288]{1,0:T(8,128)(2,1)}, u32[]{:S(2)}) copy-start(bf16[128,288]{1,0:T(8,128)(2,1)} %constant.13.clone.last_ref) | copy-start | bytes 221188
  2.3 23.9 %copy-start.5 = (bf16[288,128]{1,0:T(8,128)(2,1)S(1)}, bf16[288,128]{1,0:T(8,128)(2,1)}, u32[]{:S(2)}) copy-start(bf16[288,128]{1,0:T(8,128)(2,1)} %constant.12.clone.first_ref) | copy-start | bytes 221188
  2.3 23.9 %copy-start.6 = (f32[2,9,512]{2,1,0:T(8,128)S(1)}, f32[2,9,512]{2,1,0:T(8,128)}, u32[]{:S(2)}) copy-start(f32[2,9,512]{2,1,0:T(8,128)} %constant.14.clone.twist_ref) | copy-start | bytes 110596
  2.4 23.9 %copy-start.7 = (bf16[128,128]{1,0:T(8,128)(2,1)S(1)}, bf16[128,128]{1,0:T(8,128)(2,1)}, u32[]{:S(2)}) copy-start(bf16[128,128]{1,0:T(8,128)(2,1)} %constant.17.clone.reverse_ref) | copy-start | bytes 98308
  2.4 23.9 %all-to-all-start = ((bf16[8,5,16,512]{3,2,1,0:T(8,128)(2,1)}), bf16[8,5,16,512]{3,2,1,0:T(8,128)(2,1)S(1)}, u32[]{:S(2)}, u32[]{:S(2)}) async-start(bf16[8,5,16,512]{3,2,1,0:T(8,128)(2,1)} %get-tuple-element.8), calls=%async_computation | async-start | bytes 1310720 | tf_op jit(solution)/shard_map/all_to_all | solution.py:312
  10.4 3.0 %collective-permute-start.2 = (f32[1,512]{1,0:T(1,128)S(1)}, f32[1,512]{1,0:T(1,128)S(1)}, u32[]{:S(2)}, u32[]{:S(2)}) collective-permute-start(f32[1,512]{1,0:T(1,128)S(1)} %copy-done.2), channel_id=1, source_target_pairs={{0,3},{1,2},{2,1},{3,0},{4,7},{5,6},{6,5},{7,4},{8,11},{9,10},{10,... | collective-permute-start | bytes 6152 | tf_op jit(solution)/shard_map/ppermute | solution.py:316
  10.7 3.6 %collective-permute-start.1 = (f32[1,512]{1,0:T(1,128)S(1)}, f32[1,512]{1,0:T(1,128)S(1)}, u32[]{:S(2)}, u32[]{:S(2)}) collective-permute-start(f32[1,512]{1,0:T(1,128)S(1)} %copy-done.2), channel_id=1, source_target_pairs={{0,2},{1,3},{2,0},{3,1},{4,6},{5,7},{6,4},{7,5},{8,10},{9,11},{10,... | collective-permute-start | bytes 6152 | tf_op jit(solution)/shard_map/ppermute | solution.py:316
  11.9 2.4 %collective-permute-start = (f32[1,512]{1,0:T(1,128)S(1)}, f32[1,512]{1,0:T(1,128)S(1)}, u32[]{:S(2)}, u32[]{:S(2)}) collective-permute-start(f32[1,512]{1,0:T(1,128)S(1)} %copy-done.2), channel_id=1, source_target_pairs={{0,1},{1,0},{2,3},{3,2},{4,5},{5,4},{6,7},{7,6},{8,9},{9,8},{10,11... | collective-permute-start | bytes 6152 | tf_op jit(solution)/shard_map/ppermute | solution.py:316
  14.3 11.9 %copy-start.8 = (f32[2,4,128]{2,1,0:T(4,128)S(1)}, f32[2,4,128]{2,1,0:T(4,128)}, u32[]{:S(2)}) copy-start(f32[2,4,128]{2,1,0:T(4,128)} %constant.15.clone.spin_ref) | copy-start | bytes 12292
  14.3 3.7 %collective-permute-start.3 = (f32[1,512]{1,0:T(1,128)S(1)}, f32[1,512]{1,0:T(1,128)S(1)}, u32[]{:S(2)}, u32[]{:S(2)}) collective-permute-start(f32[1,512]{1,0:T(1,128)S(1)} %shard_map.119.scale_ref), channel_id=1, source_target_pairs={{0,4},{4,0},{8,12},{12,8},{16,20},{20,16},{24,28},{28,24},{1,5},{5... | collective-permute-start | bytes 6152 | tf_op jit(solution)/shard_map/ppermute | solution.py:316
  18.1 5.6 %collective-permute-start.6 = (f32[2,512]{1,0:T(2,128)S(1)}, f32[2,512]{1,0:T(2,128)S(1)}, u32[]{:S(2)}, u32[]{:S(2)}) collective-permute-start(f32[2,512]{1,0:T(2,128)S(1)} %pad_maximum_fusion.refs_0_), channel_id=1, source_target_pairs={{0,24},{4,28},{8,16},{12,20},{16,8},{20,12},{24,0},{28,4},{1,25},{... | collective-permute-start | bytes 12296 | tf_op jit(solution)/shard_map/ppermute | solution.py:316
  19.6 5.8 %collective-permute-start.5 = (f32[2,512]{1,0:T(2,128)S(1)}, f32[2,512]{1,0:T(2,128)S(1)}, u32[]{:S(2)}, u32[]{:S(2)}) collective-permute-start(f32[2,512]{1,0:T(2,128)S(1)} %pad_maximum_fusion.refs_0_), channel_id=1, source_target_pairs={{0,16},{4,20},{8,24},{12,28},{16,0},{20,4},{24,8},{28,12},{1,17},{... | collective-permute-start | bytes 12296 | tf_op jit(solution)/shard_map/ppermute | solution.py:316
  20.4 4.9 %collective-permute-start.4 = (f32[2,512]{1,0:T(2,128)S(1)}, f32[2,512]{1,0:T(2,128)S(1)}, u32[]{:S(2)}, u32[]{:S(2)}) collective-permute-start(f32[2,512]{1,0:T(2,128)S(1)} %pad_maximum_fusion.refs_0_), channel_id=1, source_target_pairs={{0,8},{4,12},{8,0},{12,4},{16,24},{20,28},{24,16},{28,20},{1,9},{5... | collective-permute-start | bytes 12296 | tf_op jit(solution)/shard_map/ppermute | solution.py:316
  27.3 8.7 %copy-start = (bf16[512,128]{1,0:T(8,128)(2,1)S(1)}, bf16[512,128]{1,0:T(8,128)(2,1)}, u32[]{:S(2)}) copy-start(bf16[512,128]{1,0:T(8,128)(2,1)} %post_ref.1) | copy-start | bytes 393220
  27.3 8.7 %copy-start.1 = (bf16[128,512]{1,0:T(8,128)(2,1)S(1)}, bf16[128,512]{1,0:T(8,128)(2,1)}, u32[]{:S(2)}) copy-start(bf16[128,512]{1,0:T(8,128)(2,1)} %get-tuple-element.10.skipped_ref) | copy-start | bytes 393220

commit v18 on v17

--- a/solution.py
+++ b/solution.py
@@ -358,7 +358,7 @@
     if not piled:
         packed = packed.reshape(5, places, width, rows).transpose(1, 0, 2, 3)
     gathered = exchange(packed)
-    others = [swap(squares, "chan", apart) for apart in range(1, groups)]
+    others = [swap(squares, "chan", apart) for apart in range(groups - 1, 0, -1)]
     scale = call(
         functools.partial(scale_kernel, wide * groups), shape((1, rows), F32), 8 * rows, 32 * rows, squares, *others
     )

time: 37 us -> 37 us (level)
  no operation moved by 1% of the time
where the time goes in v18:
time: 37 us; the launch traced here: 36.8 us
  starting transfers between devices  15.8 us (43%)
  blocking collectives  8.67 us (23%)
  waiting for transfers between devices  8 us (22%)
  Pallas kernels  4.1 us (11%)
    all_to_all x1, blocking collectives, exchange(): lax.all_to_all(value, 'seq', split_axis=0, concat_axis=0, tiled=True, axi...  8.67 us
    all_to_all x1, starting transfers between devices, exchange(): lax.all_to_all(value, 'seq', split_axis=0, concat_axis=0, tiled=True, axi...  7.99 us
    ppermute x7, starting transfers between devices, swap(): lax.ppermute(value, axis, [(place, place ^ apart) for place in range(lax....  7.84 us
    ppermute x7, waiting for transfers between devices, swap(): lax.ppermute(value, axis, [(place, place ^ apart) for place in range(lax....  7.13 us
    pallas_call x4, Pallas kernels, call(): pl.pallas_call(kernel, out_shape=out_shape, compiler_params=pltpu.Compile...  4.1 us
    all_to_all x1, waiting for transfers between devices, exchange(): lax.all_to_all(value, 'seq', split_axis=0, concat_axis=0, tiled=True, axi...  0.87 us
  transfers between devices with their start and end apart: 8, of which 6 were waited for; matrix products, arithmetic and copies ran while one was open for 0% of the time, Pallas kernels for 0%

profile of v18, /device:TPU:0, one launch (start us, length us, event | category | flops | bytes accessed | tf_op | source)
XLA Modules:
  0.0 36.8 jit_solution(11111993797671912486)
XLA Ops:
  0.0 2.3 %shard_map.118 = (f32[1,512]{1,0:T(1,128)}, bf16[128,512]{1,0:T(8,128)(2,1)}, bf16[8,5,16,512]{3,2,1,0:T(8,128)(2,1)}) custom-call(bf16[512,128]{1,0:T(8,128)(2,1)} %features_ref.1, bf16[512,128]{1,0:T(8,128)(2,1)} %pre_ref.1, f32[1,128]{1,0:T(1,128)} %bitcast.4, f32[1,128]{1,0:T(1,128)} %bitcast.5, f32[2,2,512,128]{3,2,1,0:T(8,128)} %spectrum_ref.1), custom_call_target="tpu_custom_call" | custom-call | flops 655360 | bytes 2097152 | tf_op jit(solution)/shard_map/pallas_call | solution.py:301
  2.3 0.0 copy-start.2
  2.3 0.0 copy-start.3
  2.3 0.0 copy-start.4
  2.3 0.0 copy-start.5
  2.3 0.0 copy-start.6
  2.4 0.0 copy-start.7
  2.4 8.0 %all-to-all-start = ((bf16[8,5,16,512]{3,2,1,0:T(8,128)(2,1)}), bf16[8,5,16,512]{3,2,1,0:T(8,128)(2,1)S(1)}, u32[]{:S(2)}, u32[]{:S(2)}) async-start(bf16[8,5,16,512]{3,2,1,0:T(8,128)(2,1)} %get-tuple-element.8), calls=%async_computation | async-start | bytes 1310720 | tf_op jit(solution)/shard_map/all_to_all | solution.py:312
  10.4 0.0 copy-done.2
  10.4 0.0 collective-permute-start.2
  10.4 1.6 %collective-permute-start.1 = (f32[1,512]{1,0:T(1,128)S(1)}, f32[1,512]{1,0:T(1,128)S(1)}, u32[]{:S(2)}, u32[]{:S(2)}) collective-permute-start(f32[1,512]{1,0:T(1,128)S(1)} %copy-done.2), channel_id=1, source_target_pairs={{0,2},{1,3},{2,0},{3,1},{4,6},{5,7},{6,4},{7,5},{8,10},{9,11},{10,... | collective-permute-start | bytes 6152 | tf_op jit(solution)/shard_map/ppermute | solution.py:316
  11.9 0.3 collective-permute-start
  12.2 0.0 collective-permute-done.2.refs_3_
  12.2 1.8 %collective-permute-done.1.refs_2_ = f32[1,512]{1,0:T(1,128)S(1)} collective-permute-done((f32[1,512]{1,0:T(1,128)S(1)}, f32[1,512]{1,0:T(1,128)S(1)}, u32[]{:S(2)}, u32[]{:S(2)}) %collective-permute-start.1) | collective-permute-done | bytes 2080 | tf_op jit(solution)/shard_map/ppermute | solution.py:316
  14.0 0.9 %collective-permute-done.refs_1_ = f32[1,512]{1,0:T(1,128)S(1)} collective-permute-done((f32[1,512]{1,0:T(1,128)S(1)}, f32[1,512]{1,0:T(1,128)S(1)}, u32[]{:S(2)}, u32[]{:S(2)}) %collective-permute-start) | collective-permute-done | bytes 2080 | tf_op jit(solution)/shard_map/ppermute | solution.py:316
  15.0 1.5 %collective-permute-start.3 = (f32[1,512]{1,0:T(1,128)S(1)}, f32[1,512]{1,0:T(1,128)S(1)}, u32[]{:S(2)}, u32[]{:S(2)}) collective-permute-start(f32[1,512]{1,0:T(1,128)S(1)} %shard_map.119.scale_ref), channel_id=1, source_target_pairs={{0,4},{4,0},{8,12},{12,8},{16,20},{20,16},{24,28},{28,24},{1,5},{5... | collective-permute-start | bytes 6152 | tf_op jit(solution)/shard_map/ppermute | solution.py:316
  16.5 2.3 %collective-permute-done.3 = f32[1,512]{1,0:T(1,128)S(1)} collective-permute-done((f32[1,512]{1,0:T(1,128)S(1)}, f32[1,512]{1,0:T(1,128)S(1)}, u32[]{:S(2)}, u32[]{:S(2)}) %collective-permute-start.3) | collective-permute-done | bytes 2080 | tf_op jit(solution)/shard_map/ppermute | solution.py:316
  18.8 1.4 %collective-permute-start.6 = (f32[2,512]{1,0:T(2,128)S(1)}, f32[2,512]{1,0:T(2,128)S(1)}, u32[]{:S(2)}, u32[]{:S(2)}) collective-permute-start(f32[2,512]{1,0:T(2,128)S(1)} %pad_maximum_fusion.refs_0_), channel_id=1, source_target_pairs={{0,24},{4,28},{8,16},{12,20},{16,8},{20,12},{24,0},{28,4},{1,25},{... | collective-permute-start | bytes 12296 | tf_op jit(solution)/shard_map/ppermute | solution.py:316
  20.2 0.5 %collective-permute-start.5 = (f32[2,512]{1,0:T(2,128)S(1)}, f32[2,512]{1,0:T(2,128)S(1)}, u32[]{:S(2)}, u32[]{:S(2)}) collective-permute-start(f32[2,512]{1,0:T(2,128)S(1)} %pad_maximum_fusion.refs_0_), channel_id=1, source_target_pairs={{0,16},{4,20},{8,24},{12,28},{16,0},{20,4},{24,8},{28,12},{1,17},{... | collective-permute-start | bytes 12296 | tf_op jit(solution)/shard_map/ppermute | solution.py:316
  20.7 2.5 %collective-permute-start.4 = (f32[2,512]{1,0:T(2,128)S(1)}, f32[2,512]{1,0:T(2,128)S(1)}, u32[]{:S(2)}, u32[]{:S(2)}) collective-permute-start(f32[2,512]{1,0:T(2,128)S(1)} %pad_maximum_fusion.refs_0_), channel_id=1, source_target_pairs={{0,8},{4,12},{8,0},{12,4},{16,24},{20,28},{24,16},{28,20},{1,9},{5... | collective-permute-start | bytes 12296 | tf_op jit(solution)/shard_map/ppermute | solution.py:316
  23.2 1.1 %collective-permute-done.6.refs_3_ = f32[2,512]{1,0:T(2,128)S(1)} collective-permute-done((f32[2,512]{1,0:T(2,128)S(1)}, f32[2,512]{1,0:T(2,128)S(1)}, u32[]{:S(2)}, u32[]{:S(2)}) %collective-permute-start.6) | collective-permute-done | bytes 4128 | tf_op jit(solution)/shard_map/ppermute | solution.py:316
  24.4 1.0 %collective-permute-done.5.refs_2_ = f32[2,512]{1,0:T(2,128)S(1)} collective-permute-done((f32[2,512]{1,0:T(2,128)S(1)}, f32[2,512]{1,0:T(2,128)S(1)}, u32[]{:S(2)}, u32[]{:S(2)}) %collective-permute-start.5) | collective-permute-done | bytes 4128 | tf_op jit(solution)/shard_map/ppermute | solution.py:316
  25.4 0.0 collective-permute-done.4.refs_1_
  25.4 0.9 %all-to-all-done.packed_ref = bf16[8,5,16,512]{3,2,1,0:T(8,128)(2,1)S(1)} async-done(((bf16[8,5,16,512]{3,2,1,0:T(8,128)(2,1)}), bf16[8,5,16,512]{3,2,1,0:T(8,128)(2,1)S(1)}, u32[]{:S(2)}, u32[]{:S(2)}) %all-to-all-start) | async-done | bytes 655392 | tf_op jit(solution)/shard_map/all_to_all | solution.py:312
  26.2 0.0 copy-done.3
  26.2 0.0 copy-done.4
  26.3 1.0 %shard_map.120 = bf16[128,512]{1,0:T(8,128)(2,1)S(1)} custom-call(bf16[8,5,16,512]{3,2,1,0:T(8,128)(2,1)S(1)} %all-to-all-done.packed_ref, bf16[288,128]{1,0:T(8,128)(2,1)S(1)} %copy-done.5, bf16[128,288]{1,0:T(8,128)(2,1)S(1)} %copy-done.4, f32[2,9,512]{2,1,0:T(8,128)S(1)} %copy-done.6, f32[2,4,128]{2,1,0:T(4,128)S(1)} %copy-done.8, ...), custom_call_target="tpu_custom_call" | custom-call | flops 671088640 | bytes 1310720 | tf_op jit(solution)/shard_map/pallas_call | solution.py:301
  27.3 0.0 copy-start
  27.3 0.0 copy-start.1
  27.3 8.7 %all_to_all.10.conv_ref = bf16[8,16,512]{2,1,0:T(8,128)(2,1)S(1)} all-to-all(bf16[8,16,512]{2,1,0:T(8,128)(2,1)S(1)} %bitcast.3), channel_id=1, replica_groups={{20,4,12,24,8,16,0,28},{21,5,13,25,9,17,1,29},{22,6,14,26,10,18,2,30},{..., dimensions={0} | all-to-all | bytes 262144 | tf_op jit(solution)/shard_map/all_to_all | solution.py:312
  36.0 0.0 copy-done
  36.0 0.8 %shard_map.121 = bf16[512,128]{1,0:T(8,128)(2,1)} custom-call(bf16[8,16,512]{2,1,0:T(8,128)(2,1)S(1)} %all_to_all.10.conv_ref, bf16[128,512]{1,0:T(8,128)(2,1)S(1)} %copy-done.1, f32[1,512]{1,0:T(1,128)S(1)} %shard_map.119.scale_ref, bf16[512,128]{1,0:T(8,128)(2,1)S(1)} %copy-done), custom_call_target="tpu_custom_call" | custom-call | flops 655360 | bytes 524288 | tf_op jit(solution)/shard_map/pallas_call | solution.py:301
  (8 shorter events, 0.0 us)
Async XLA Ops:
  2.3 8.1 %copy-start.2 = (f32[1,512]{1,0:T(1,128)S(1)}, f32[1,512]{1,0:T(1,128)}, u32[]{:S(2)}) copy-start(f32[1,512]{1,0:T(1,128)} %get-tuple-element.9.refs_0_) | copy-start | bytes 6148
  2.3 23.9 %copy-start.3 = (bf16[2,256,256]{2,1,0:T(8,128)(2,1)S(1)}, bf16[2,256,256]{2,1,0:T(8,128)(2,1)}, u32[]{:S(2)}) copy-start(bf16[2,256,256]{2,1,0:T(8,128)(2,1)} %constant.16.clone.dft_ref) | copy-start | bytes 786436
  2.3 23.9 %copy-start.4 = (bf16[128,288]{1,0:T(8,128)(2,1)S(1)}, bf16[128,288]{1,0:T(8,128)(2,1)}, u32[]{:S(2)}) copy-start(bf16[128,288]{1,0:T(8,128)(2,1)} %constant.13.clone.last_ref) | copy-start | bytes 221188
  2.3 23.9 %copy-start.5 = (bf16[288,128]{1,0:T(8,128)(2,1)S(1)}, bf16[288,128]{1,0:T(8,128)(2,1)}, u32[]{:S(2)}) copy-start(bf16[288,128]{1,0:T(8,128)(2,1)} %constant.12.clone.first_ref) | copy-start | bytes 221188
  2.3 23.9 %copy-start.6 = (f32[2,9,512]{2,1,0:T(8,128)S(1)}, f32[2,9,512]{2,1,0:T(8,128)}, u32[]{:S(2)}) copy-start(f32[2,9,512]{2,1,0:T(8,128)} %constant.14.clone.twist_ref) | copy-start | bytes 110596
  2.4 23.9 %copy-start.7 = (bf16[128,128]{1,0:T(8,128)(2,1)S(1)}, bf16[128,128]{1,0:T(8,128)(2,1)}, u32[]{:S(2)}) copy-start(bf16[128,128]{1,0:T(8,128)(2,1)} %constant.17.clone.reverse_ref) | copy-start | bytes 98308
  2.4 23.9 %all-to-all-start = ((bf16[8,5,16,512]{3,2,1,0:T(8,128)(2,1)}), bf16[8,5,16,512]{3,2,1,0:T(8,128)(2,1)S(1)}, u32[]{:S(2)}, u32[]{:S(2)}) async-start(bf16[8,5,16,512]{3,2,1,0:T(8,128)(2,1)} %get-tuple-element.8), calls=%async_computation | async-start | bytes 1310720 | tf_op jit(solution)/shard_map/all_to_all | solution.py:312
  10.4 1.9 %collective-permute-start.2 = (f32[1,512]{1,0:T(1,128)S(1)}, f32[1,512]{1,0:T(1,128)S(1)}, u32[]{:S(2)}, u32[]{:S(2)}) collective-permute-start(f32[1,512]{1,0:T(1,128)S(1)} %copy-done.2), channel_id=1, source_target_pairs={{0,1},{1,0},{2,3},{3,2},{4,5},{5,4},{6,7},{7,6},{8,9},{9,8},{10,11... | collective-permute-start | bytes 6152 | tf_op jit(solution)/shard_map/ppermute | solution.py:316
  10.4 3.7 %collective-permute-start.1 = (f32[1,512]{1,0:T(1,128)S(1)}, f32[1,512]{1,0:T(1,128)S(1)}, u32[]{:S(2)}, u32[]{:S(2)}) collective-permute-start(f32[1,512]{1,0:T(1,128)S(1)} %copy-done.2), channel_id=1, source_target_pairs={{0,2},{1,3},{2,0},{3,1},{4,6},{5,7},{6,4},{7,5},{8,10},{9,11},{10,... | collective-permute-start | bytes 6152 | tf_op jit(solution)/shard_map/ppermute | solution.py:316
  11.9 3.0 %collective-permute-start = (f32[1,512]{1,0:T(1,128)S(1)}, f32[1,512]{1,0:T(1,128)S(1)}, u32[]{:S(2)}, u32[]{:S(2)}) collective-permute-start(f32[1,512]{1,0:T(1,128)S(1)} %copy-done.2), channel_id=1, source_target_pairs={{0,3},{1,2},{2,1},{3,0},{4,7},{5,6},{6,5},{7,4},{8,11},{9,10},{10,... | collective-permute-start | bytes 6152 | tf_op jit(solution)/shard_map/ppermute | solution.py:316
  14.9 11.3 %copy-start.8 = (f32[2,4,128]{2,1,0:T(4,128)S(1)}, f32[2,4,128]{2,1,0:T(4,128)}, u32[]{:S(2)}) copy-start(f32[2,4,128]{2,1,0:T(4,128)} %constant.15.clone.spin_ref) | copy-start | bytes 12292
  15.0 3.8 %collective-permute-start.3 = (f32[1,512]{1,0:T(1,128)S(1)}, f32[1,512]{1,0:T(1,128)S(1)}, u32[]{:S(2)}, u32[]{:S(2)}) collective-permute-start(f32[1,512]{1,0:T(1,128)S(1)} %shard_map.119.scale_ref), channel_id=1, source_target_pairs={{0,4},{4,0},{8,12},{12,8},{16,20},{20,16},{24,28},{28,24},{1,5},{5... | collective-permute-start | bytes 6152 | tf_op jit(solution)/shard_map/ppermute | solution.py:316
  18.8 5.6 %collective-permute-start.6 = (f32[2,512]{1,0:T(2,128)S(1)}, f32[2,512]{1,0:T(2,128)S(1)}, u32[]{:S(2)}, u32[]{:S(2)}) collective-permute-start(f32[2,512]{1,0:T(2,128)S(1)} %pad_maximum_fusion.refs_0_), channel_id=1, source_target_pairs={{0,24},{4,28},{8,16},{12,20},{16,8},{20,12},{24,0},{28,4},{1,25},{... | collective-permute-start | bytes 12296 | tf_op jit(solution)/shard_map/ppermute | solution.py:316
  20.2 5.2 %collective-permute-start.5 = (f32[2,512]{1,0:T(2,128)S(1)}, f32[2,512]{1,0:T(2,128)S(1)}, u32[]{:S(2)}, u32[]{:S(2)}) collective-permute-start(f32[2,512]{1,0:T(2,128)S(1)} %pad_maximum_fusion.refs_0_), channel_id=1, source_target_pairs={{0,16},{4,20},{8,24},{12,28},{16,0},{20,4},{24,8},{28,12},{1,17},{... | collective-permute-start | bytes 12296 | tf_op jit(solution)/shard_map/ppermute | solution.py:316
  20.7 4.7 %collective-permute-start.4 = (f32[2,512]{1,0:T(2,128)S(1)}, f32[2,512]{1,0:T(2,128)S(1)}, u32[]{:S(2)}, u32[]{:S(2)}) collective-permute-start(f32[2,512]{1,0:T(2,128)S(1)} %pad_maximum_fusion.refs_0_), channel_id=1, source_target_pairs={{0,8},{4,12},{8,0},{12,4},{16,24},{20,28},{24,16},{28,20},{1,9},{5... | collective-permute-start | bytes 12296 | tf_op jit(solution)/shard_map/ppermute | solution.py:316
  27.3 8.7 %copy-start = (bf16[512,128]{1,0:T(8,128)(2,1)S(1)}, bf16[512,128]{1,0:T(8,128)(2,1)}, u32[]{:S(2)}) copy-start(bf16[512,128]{1,0:T(8,128)(2,1)} %post_ref.1) | copy-start | bytes 393220
  27.3 8.7 %copy-start.1 = (bf16[128,512]{1,0:T(8,128)(2,1)S(1)}, bf16[128,512]{1,0:T(8,128)(2,1)}, u32[]{:S(2)}) copy-start(bf16[128,512]{1,0:T(8,128)(2,1)} %get-tuple-element.10.skipped_ref) | copy-start | bytes 393220
